TPU v7x, 32 devices: a whole 2x2x4 slice. The times are simulated.
32 devices in a mesh: sy: 4 (over z), sx: 2 (over y), tp: 4 (over x, core).
Axes of the slice: x: 2, y: 2, z: 4, core: 2. Of those that a mesh axis runs over, the one named last changes fastest.
Arguments:
- tokens: bfloat16 [3200, 3072], P(('sy', 'sx')), may hold values from -8 to 8
- mod_shift: float32 [3072], replicated, may hold values from -3 to 3
- mod_scale: float32 [3072], replicated, may hold values from -0.5 to 0.5
- mod_gate: float32 [3072], replicated, may hold values from 0.5 to 1.5
- w_qkv: bfloat16 [3072, 3, 1536], P('sx', None, 'tp'), as said below
- w_mlp_in: bfloat16 [3072, 6144], P('sx', 'tp'), may hold values from -0.109375 to 0.109375
- q_gain: float32 [12, 128], P('tp'), may hold values from 0 to 7, as said below
- k_gain: float32 [12, 128], P('tp'), may hold values from 0 to 7, as said below
- w_attn_out: bfloat16 [1536, 3072], P('tp', 'sx'), may hold values from -0.0625 to 0.0625
- w_mlp_out: bfloat16 [6144, 3072], P('tp', 'sx'), may hold values from -0.0625 to 0.0625
Outputs:
- result: bfloat16 [3200, 3072], P(('sy', 'sx'), 'tp')
Inputs may be any that keep to these rules, and one draw needn't show every extreme that they name: `w_qkv`: mean-zero entries of about 3072 to the power -0.5 in size. `q_gain`: positive. `k_gain`: positive.
All inputs are finite; a program needn't handle non-finite values.
Results may differ from a plain program's by a relative error of at most 0.0085.
Values may be sent and summed in bfloat16 or wider, within the bound.
No kernel may reach another device: no remote copies, remote signals or barrier semaphores. Data moves between devices by JAX's collectives and lax.ppermute only.
A program may use at most 128 MiB of HBM per device.

v0:
```python
import jax
import jax.numpy as jnp
from jax import lax
from jax.sharding import PartitionSpec as P

TILE = 20


def with_halo(cells, sides, width):
    for axis, dim in sides:
        count = lax.axis_size(axis)
        ends = count - 1
        head = lax.slice_in_dim(cells, 0, width, axis=dim)
        tail = lax.slice_in_dim(cells, cells.shape[dim] - width, cells.shape[dim], axis=dim)
        cells = jnp.concatenate(
            [
                lax.ppermute(tail, axis, [(i, (i + 1) % count) for i in range(ends)]),
                cells,
                lax.ppermute(head, axis, [((i + 1) % count, i) for i in range(ends)]),
            ],
            axis=dim,
        )
    return cells


def layer_norm(vector):
    centered = vector - jnp.mean(vector, axis=-1, keepdims=True)
    variance = jnp.mean(centered * centered, axis=-1, keepdims=True)
    return centered * lax.rsqrt(variance + 1e-06)


def rms_gain(vector, scaling):
    mean_square = jnp.mean(vector * vector, axis=-1, keepdims=True)
    return vector * lax.rsqrt(mean_square + 1e-06) * scaling


def shards(
    tokens, mod_shift, mod_scale, mod_gate, w_qkv, w_mlp_in, q_gain, k_gain, w_attn_out, w_mlp_out
):
    tok_rows, model_width = tokens.shape
    tile_side = TILE
    half_side = TILE // 2
    inputs = tokens.astype(jnp.float32)
    modded = (layer_norm(inputs) * (1.0 + mod_scale) + mod_shift).astype(jnp.bfloat16)
    local_heads, head_dim = q_gain.shape
    local_width = local_heads * head_dim
    pieces = (
        lax.all_gather(w_qkv, "sx", axis=0, tiled=True),
        lax.all_gather(w_mlp_in, "sx", axis=0, tiled=True),
    )
    piece_rows = pieces[0].shape[0]
    qkv_sum = jnp.dot(
        modded, pieces[0].reshape(piece_rows, 3 * local_width), preferred_element_type=jnp.float32
    )
    mlp_sum = jnp.dot(modded, pieces[1], preferred_element_type=jnp.float32)
    qkv_parts = qkv_sum.reshape(tok_rows, 3, local_heads, head_dim)
    queries = rms_gain(qkv_parts[:, 0], q_gain).astype(jnp.bfloat16)
    key_rows = rms_gain(qkv_parts[:, 1], k_gain).astype(jnp.bfloat16)
    value_rows = qkv_parts[:, 2].astype(jnp.bfloat16)
    key_value = jnp.concatenate(
        [key_rows.reshape(tok_rows, local_width), value_rows.reshape(tok_rows, local_width)], axis=1
    )
    key_value = key_value.reshape(tile_side, tile_side, 2 * local_width)
    extended = with_halo(key_value, (("sy", 0), ("sx", 1)), half_side)
    window = extended.reshape(4 * tok_rows, 2 * local_width)
    window_keys = window[:, :local_width].reshape(4 * tok_rows, local_heads, head_dim)
    window_values = window[:, local_width:].reshape(4 * tok_rows, local_heads, head_dim)
    offsets = jnp.arange(2 * tile_side, dtype=jnp.int32)
    row_pos = lax.axis_index("sy") * tile_side - half_side + offsets
    col_pos = lax.axis_index("sx") * tile_side - half_side + offsets
    row_ok = (row_pos >= 0) & (row_pos < tile_side * lax.axis_size("sy"))
    col_ok = (col_pos >= 0) & (col_pos < tile_side * lax.axis_size("sx"))
    in_grid = (row_ok[:, None] & col_ok[None, :]).reshape(4 * tok_rows)
    scores = jnp.einsum(
        "qhd,khd->hqk", queries, window_keys, preferred_element_type=jnp.float32
    ) * head_dim ** (-0.5)
    scores = jnp.where(in_grid[None, None, :], scores, -jnp.inf)
    row_max = jnp.max(scores, axis=-1, keepdims=True)
    numerators = jnp.exp(scores - row_max)
    weights = (numerators / jnp.sum(numerators, axis=-1, keepdims=True)).astype(jnp.bfloat16)
    attended = jnp.einsum(
        "hqk,khd->qhd", weights, window_values, preferred_element_type=jnp.float32
    )
    attended = attended.astype(jnp.bfloat16).reshape(tok_rows, local_width)
    activated = jax.nn.gelu(mlp_sum, approximate=True).astype(jnp.bfloat16)
    pieces = (
        lax.all_gather(w_attn_out, "sx", axis=1, tiled=True),
        lax.all_gather(w_mlp_out, "sx", axis=1, tiled=True),
    )
    product_term = jnp.dot(attended, pieces[0], preferred_element_type=jnp.float32)
    product_term = product_term + jnp.dot(activated, pieces[1], preferred_element_type=jnp.float32)
    reduced = lax.psum_scatter(
        product_term.astype(jnp.bfloat16), "tp", scatter_dimension=1, tiled=True
    ).astype(jnp.float32)
    block_width = model_width // lax.axis_size("tp")
    first_col = lax.axis_index("tp") * block_width
    residual_part = lax.dynamic_slice_in_dim(inputs, first_col, block_width, 1)
    gate_part = lax.dynamic_slice_in_dim(mod_gate, first_col, block_width, 0)
    return (residual_part + gate_part * reduced).astype(jnp.bfloat16)


def solution(mesh):
    placed = (
        P(("sy", "sx"), None),
        P(),
        P(),
        P(),
        P("sx", None, "tp"),
        P("sx", "tp"),
        P("tp", None),
        P("tp", None),
        P("tp", "sx"),
        P("tp", "sx"),
    )
    return jax.shard_map(
        shards, mesh=mesh, in_specs=placed, out_specs=P(("sy", "sx"), "tp"), check_vma=False
    )
```

profile of v0, /device:TPU:0, one launch (start us, length us, event | category | flops | bytes accessed | tf_op | source)
XLA Modules:
  0.0 443.5 jit_solution(1568275324761217008)
XLA Ops:
  6.5 6.1 %copy.23 = bf16[1536,3,384]{0,2,1:T(8,128)(2,1)} copy(bf16[1536,3,384]{2,0,1:T(8,128)(2,1)} %param.14) | data formatting | bytes 7077888 | tf_op args[4]
  12.6 0.0 all-gather.5.cloned.1.call-update
  12.7 0.0 all-gather.11.cloned.1.call-start
  12.7 0.7 all-gather.11.cloned.1.call-update
  13.4 0.0 copy-start
  13.4 0.0 all-gather.9.cloned.1.call-start
  13.5 0.7 all-gather.9.cloned.1.call-update
  14.2 0.0 all-gather.7.cloned.1.call-start
  14.2 0.9 copy-done
  15.1 0.4 convert_reduce_fusion
  15.5 0.8 multiply_reduce_fusion
  16.3 88.4 %all-gather.5.cloned.1.call-done = bf16[3072,3,384]{0,2,1:T(8,128)(2,1)} async-done(((bf16[1536,3,384]{0,2,1:T(8,128)(2,1)}), bf16[3072,3,384]{0,2,1:T(8,128)(2,1)}) %all-gather.5.cloned.1.call-update) | async-done | bytes 7077904 | tf_op jit(solution)/shard_map/all_gather | solution.py:48
  104.8 6.3 %fusion.14 = f32[400,3,3,128]{3,0,2,1:T(8,128)S(1)} fusion(bf16[3,3,128,3072]{3,2,1,0:T(8,128)(2,1)} %bitcast.78, bf16[400,3072]{1,0:T(8,128)(2,1)S(1)} %copy-done, f32[3072]{0:T(1024)S(1)} %copy-done.7, f32[3072]{0:T(1024)S(1)} %broadcast_add_fusion, f32[400]{0:T(512)S(1)} %add_rsqrt_fusion.2, f32[400]{0:T(512)S(1)} %broadcast_multiply_fusion), kind=kOutput, calls=%fused_computation.23 | convolution fusion | flops 2838528000 | bytes 11406464 | tf_op jit(solution)/shard_map/dot_general | solution.py:52
  111.1 0.9 slice.72
  112.0 0.5 copy-done.4
  112.5 1.0 fusion.40
  113.4 0.1 copy.25
  113.6 1.5 copy.24
  115.1 1.2 copy.26
  116.3 0.7 copy-done.2
  117.1 0.5 mul.126
  117.6 0.9 copy-done.1
  118.5 0.1 fusion.27
  118.6 0.9 fusion.28
  119.5 1.8 slice.38
  121.3 1.3 collective-permute-start.1
  122.6 1.8 slice.36
  124.4 5.3 %collective-permute-start = (bf16[10,20,768]{2,1,0:T(8,128)(2,1)}, bf16[10,20,768]{2,1,0:T(8,128)(2,1)}, u32[]{:S(2)}, u32[]{:S(2)}) collective-permute-start(bf16[10,20,768]{2,1,0:T(8,128)(2,1)} %slice.36), channel_id=1, source_target_pairs={{0,8},{8,16},{16,24},{1,9},{9,17},{17,25},{2,10},{10,18},{18,26},{... | collective-permute-start | bytes 921608 | tf_op jit(solution)/shard_map/ppermute | solution.py:17
  129.7 0.0 all-gather.7.cloned.1.call-update
  129.8 0.0 reduce-scatter.2.cloned.1.call-start
  129.8 2.0 convert_element_type.54
  131.8 1.2 squeeze.10
  133.0 2.3 mul.132
  135.3 1.4 multiply_convert_fusion
  136.8 0.1 collective-permute-done
  136.9 1.2 pad_maximum_fusion.1
  138.1 0.4 fusion.41
  138.5 1.0 copy.30
  139.5 1.3 collective-permute-start.3
  140.8 1.0 copy.29
  141.8 6.2 %collective-permute-start.2 = (bf16[40,10,768]{2,0,1:T(8,128)(2,1)}, bf16[40,10,768]{2,0,1:T(8,128)(2,1)}, u32[]{:S(2)}, u32[]{:S(2)}) collective-permute-start(bf16[40,10,768]{2,0,1:T(8,128)(2,1)} %copy.29), channel_id=1, source_target_pairs={{0,4},{1,5},{2,6},{3,7},{8,12},{9,13},{10,14},{11,15},{16,20},{17,... | collective-permute-start | bytes 1843208 | tf_op jit(solution)/shard_map/ppermute | solution.py:17
  148.0 0.1 broadcast_and_fusion
  148.1 0.1 and.42
  148.2 1.4 multiply_reduce_fusion.1
  149.6 21.4 %collective-permute-done.3 = bf16[40,10,768]{2,0,1:T(8,128)(2,1)} collective-permute-done((bf16[40,10,768]{2,0,1:T(8,128)(2,1)}, bf16[40,10,768]{2,0,1:T(8,128)(2,1)}, u32[]{:S(2)}, u32[]{:S(2)}) %collective-permute-start.3) | collective-permute-done | bytes 614432 | tf_op jit(solution)/shard_map/ppermute | solution.py:19
  171.0 1.2 copy.32
  172.2 2.0 collective-permute-done.2
  174.2 1.2 copy.31
  175.4 3.1 pad_maximum_fusion
  178.5 1.7 fusion.39
  180.2 2.5 copy.41
  182.7 2.5 copy.42
  185.2 7.3 %fusion.42 = (f32[3,400]{1,0:T(4,128)S(1)}, f32[3,400,1600]{2,1,0:T(8,128)}) fusion(pred[1600]{0:T(1024)(128)(4,1)S(1)} %and.42, bf16[1600,3,128]{0,2,1:T(8,128)(2,1)} %bitcast.74, f32[400,3,3,128]{3,0,2,1:T(8,128)} %copy-done.4, f32[3,128]{1,0:T(4,128)S(1)} %copy-done.8, f32[400,3]{0,1:T(4,128)S(1)} %add_rsqrt_fusion), kind=kOutput, calls=%fused_computation.70 | convolution fusion | flops 499662400 | bytes 9585088 | tf_op jit(solution)/shard_map/sub | solution.py:79
  192.5 5.0 %fusion.25 = bf16[3,50,8,128]{3,2,1,0:T(8,128)(2,1)S(1)} fusion(bf16[1600,3,128]{0,2,1:T(8,128)(2,1)} %bitcast.73, f32[3,400,1600]{2,1,0:T(8,128)} %get-tuple-element.14, f32[3,400]{1,0:T(4,128)S(1)} %get-tuple-element.13), kind=kOutput, calls=%fused_computation.34 | convolution fusion | flops 495513600 | bytes 9220800 | tf_op jit(solution)/shard_map/hqk,khd->qhd/dot_general | solution.py:81
  197.5 40.0 %all-gather.11.cloned.1.call-done = bf16[1536,3072]{1,0:T(8,128)(2,1)} async-done(((bf16[1536,1536]{1,0:T(8,128)(2,1)}), bf16[1536,3072]{1,0:T(8,128)(2,1)}) %all-gather.11.cloned.1.call-update) | async-done | bytes 9437200 | tf_op jit(solution)/shard_map/all_gather | solution.py:88
  237.5 119.6 %all-gather.9.cloned.1.call-done = bf16[3072,1536]{1,0:T(8,128)(2,1)} async-done(((bf16[1536,1536]{1,0:T(8,128)(2,1)}), bf16[3072,1536]{1,0:T(8,128)(2,1)}) %all-gather.9.cloned.1.call-update) | async-done | bytes 9437200 | tf_op jit(solution)/shard_map/all_gather | solution.py:49
  357.1 16.7 %fusion.18 = f32[400,3072]{1,0:T(8,128)} fusion(bf16[1536,3072]{1,0:T(8,128)(2,1)} %all-gather.11.cloned.1.call-done, bf16[3072,1536]{1,0:T(8,128)(2,1)} %all-gather.9.cloned.1.call-done, bf16[400,3072]{1,0:T(8,128)(2,1)S(1)} %copy-done, f32[3072]{0:T(1024)S(1)} %copy-done.7, f32[3072]{0:T(1024)S(1)} %broadcast_add_fusion, f32[400]{0:T(512)S(1)} %add_rsqrt_fusion.2, ...), kind=kOutput, calls=%fused_computation.27 | convolution fusion | flops 7562649600 | bytes 26274944 | tf_op jit(solution)/shard_map/dot_general | solution.py:91
  373.8 20.8 %all-gather.7.cloned.1.call-done = bf16[384,3072]{1,0:T(8,128)(2,1)} async-done(((bf16[384,1536]{1,0:T(8,128)(2,1)}), bf16[384,3072]{1,0:T(8,128)(2,1)}) %all-gather.7.cloned.1.call-update) | async-done | bytes 2359312 | tf_op jit(solution)/shard_map/all_gather | solution.py:87
  394.6 6.0 %add_convert_fusion = bf16[400,3072]{1,0:T(8,128)(2,1)} fusion(f32[400,3072]{1,0:T(8,128)} %fusion.18, bf16[384,3072]{1,0:T(8,128)(2,1)} %all-gather.7.cloned.1.call-done, bf16[3,50,8,128]{3,2,1,0:T(8,128)(2,1)S(1)} %fusion.25), kind=kOutput, calls=%fused_computation.5 | convolution fusion | flops 946176000 | bytes 10039296 | tf_op jit(solution)/shard_map/dot_general | solution.py:90
  400.6 0.0 reduce-scatter.2.cloned.1.call-update
  400.7 2.8 convert_element_type.48
  403.5 0.8 dynamic_slice.7
  404.2 30.3 %reduce-scatter.2.cloned.1.call-done = bf16[400,768]{1,0:T(8,128)(2,1)} async-done(((bf16[400,3072]{1,0:T(8,128)(2,1)}), bf16[400,768]{1,0:T(8,128)(2,1)}) %reduce-scatter.2.cloned.1.call-update) | async-done | bytes 614416 | tf_op jit(solution)/shard_map/reduce_scatter | solution.py:92
  434.5 2.4 add_convert_fusion.2
  (22 shorter events, 0.1 us)
Async XLA Ops:
  6.5 98.2 %all-gather.5.cloned.1.call-start = ((), (), s32[]{:S(2)}) async-start(), calls=%async_computation.1 | async-start | bytes 10616832 | tf_op jit(solution)/shard_map/all_gather | solution.py:48
  12.7 224.8 %all-gather.11.cloned.1.call-start = ((), (), s32[]{:S(2)}) async-start(), calls=%async_computation.4 | async-start | bytes 14155776 | tf_op jit(solution)/shard_map/all_gather | solution.py:88
  13.4 1.7 copy-start
  13.4 343.7 %all-gather.9.cloned.1.call-start = ((), (), s32[]{:S(2)}) async-start(), calls=%async_computation.3 | async-start | bytes 14155776 | tf_op jit(solution)/shard_map/all_gather | solution.py:49
  14.2 2.2 copy-start.5
  14.2 90.6 %copy-start.7 = (f32[3072]{0:T(1024)S(1)}, f32[3072]{0:T(1024)}, u32[]{:S(2)}) copy-start(f32[3072]{0:T(1024)} %param.11) | copy-start | bytes 36868
  14.2 380.4 %all-gather.7.cloned.1.call-start = ((), (), s32[]{:S(2)}) async-start(), calls=%async_computation.2 | async-start | bytes 3538944 | tf_op jit(solution)/shard_map/all_gather | solution.py:87
  111.1 1.4 copy-start.4
  111.1 7.4 %copy-start.6 = (f32[3,128]{1,0:T(4,128)S(1)}, f32[3,128]{1,0:T(4,128)}, u32[]{:S(2)}) copy-start(f32[3,128]{1,0:T(4,128)} %param.17) | copy-start | bytes 4612
  116.3 0.8 copy-start.2
  117.6 0.9 copy-start.1
  121.3 15.4 %collective-permute-start.1 = (bf16[10,20,768]{2,1,0:T(8,128)(2,1)}, bf16[10,20,768]{2,1,0:T(8,128)(2,1)}, u32[]{:S(2)}, u32[]{:S(2)}) collective-permute-start(bf16[10,20,768]{2,1,0:T(8,128)(2,1)} %slice.38), channel_id=1, source_target_pairs={{8,0},{16,8},{24,16},{9,1},{17,9},{25,17},{10,2},{18,10},{26,18},{... | collective-permute-start | bytes 921608 | tf_op jit(solution)/shard_map/ppermute | solution.py:19
  124.4 12.4 %collective-permute-start = (bf16[10,20,768]{2,1,0:T(8,128)(2,1)}, bf16[10,20,768]{2,1,0:T(8,128)(2,1)}, u32[]{:S(2)}, u32[]{:S(2)}) collective-permute-start(bf16[10,20,768]{2,1,0:T(8,128)(2,1)} %slice.36), channel_id=1, source_target_pairs={{0,8},{8,16},{16,24},{1,9},{9,17},{17,25},{2,10},{10,18},{18,26},{... | collective-permute-start | bytes 921608 | tf_op jit(solution)/shard_map/ppermute | solution.py:17
  129.8 304.7 %reduce-scatter.2.cloned.1.call-start = ((), (), s32[]{:S(2)}) async-start(), calls=%async_computation.5 | async-start | bytes 3072000 | tf_op jit(solution)/shard_map/reduce_scatter | solution.py:92
  133.0 3.9 copy-start.3
  139.5 31.5 %collective-permute-start.3 = (bf16[40,10,768]{2,0,1:T(8,128)(2,1)}, bf16[40,10,768]{2,0,1:T(8,128)(2,1)}, u32[]{:S(2)}, u32[]{:S(2)}) collective-permute-start(bf16[40,10,768]{2,0,1:T(8,128)(2,1)} %copy.30), channel_id=1, source_target_pairs={{4,0},{5,1},{6,2},{7,3},{12,8},{13,9},{14,10},{15,11},{20,16},{21,... | collective-permute-start | bytes 1843208 | tf_op jit(solution)/shard_map/ppermute | solution.py:19
  141.8 32.4 %collective-permute-start.2 = (bf16[40,10,768]{2,0,1:T(8,128)(2,1)}, bf16[40,10,768]{2,0,1:T(8,128)(2,1)}, u32[]{:S(2)}, u32[]{:S(2)}) collective-permute-start(bf16[40,10,768]{2,0,1:T(8,128)(2,1)} %copy.29), channel_id=1, source_target_pairs={{0,4},{1,5},{2,6},{3,7},{8,12},{9,13},{10,14},{11,15},{16,20},{17,... | collective-permute-start | bytes 1843208 | tf_op jit(solution)/shard_map/ppermute | solution.py:17
  180.2 5.1 %copy-start.8 = (f32[3,128]{1,0:T(4,128)S(1)}, f32[3,128]{1,0:T(4,128)}, u32[]{:S(2)}) copy-start(f32[3,128]{1,0:T(4,128)} %param.16) | copy-start | bytes 4612
Sparse Core Ops, SparseCore 0:
  12.8 91.9 all-gather.4
  106.3 131.1 all-gather.10
  239.1 117.9 all-gather.8
  358.5 36.0 all-gather.6
  400.8 33.6 reduce-scatter.1
where the time goes:
time: 444 us; the launch traced here: 443 us
  waiting for transfers between devices  324 us (73%)
  matrix products  41.4 us (9%)
  local copies, waits for them, and re-layouts  35 us (8%)
  other arithmetic  15.6 us (4%)
  starting transfers between devices  14.2 us (3%)
  between operations  13.3 us (3%)
    all_gather x1, waiting for transfers between devices, shards(): lax.all_gather(w_mlp_in, 'sx', axis=0, tiled=True)  120 us
    all_gather x1, waiting for transfers between devices, shards(): lax.all_gather(w_qkv, 'sx', axis=0, tiled=True)  88.4 us
    all_gather x1, waiting for transfers between devices, shards(): lax.all_gather(w_mlp_out, 'sx', axis=1, tiled=True)  40 us
    reduce_scatter x1, waiting for transfers between devices, shards(): lax.psum_scatter(product_term.astype(jnp.bfloat16), 'tp', scatter_dimensi...  30.3 us
    ppermute x2, waiting for transfers between devices, with_halo(): lax.ppermute(head, axis, [((i + 1) % count, i) for i in range(ends)])  21.4 us
    all_gather x1, waiting for transfers between devices, shards(): lax.all_gather(w_attn_out, 'sx', axis=1, tiled=True)  20.8 us
    dot_general x1, matrix products, shards(): jnp.dot(activated, pieces[1], preferred_element_type=jnp.float32)  16.7 us
    unnamed x22, local copies, waits for them, and re-layouts  14.3 us
  transfers between devices with their start and end apart: 9, of which 8 were waited for; matrix products, arithmetic and copies ran while one was open for 17% of the time, Pallas kernels for 0%

commit v1 on v0

--- a/solution.py
+++ b/solution.py
@@ -34,7 +34,7 @@
     return vector * lax.rsqrt(mean_square + 1e-06) * scaling
 
 
-def shards(
+def gathered_plan(
     tokens, mod_shift, mod_scale, mod_gate, w_qkv, w_mlp_in, q_gain, k_gain, w_attn_out, w_mlp_out
 ):
     tok_rows, model_width = tokens.shape
@@ -99,6 +99,156 @@
     return (residual_part + gate_part * reduced).astype(jnp.bfloat16)
 
 
+def swap(cells, axis, bit):
+    count = lax.axis_size(axis)
+    return lax.ppermute(cells, axis, [(i, i ^ bit) for i in range(count)])
+
+
+def shift(cells, axis, step):
+    count = lax.axis_size(axis)
+    return lax.ppermute(
+        cells, axis, [(i, i + step) for i in range(count) if 0 <= i + step < count]
+    )
+
+
+def dot(left, right):
+    return jnp.dot(left, right, preferred_element_type=jnp.float32)
+
+
+def in_order(bit, mine, other):
+    return jnp.where(bit == 0, mine, other), jnp.where(bit == 0, other, mine)
+
+
+def border_pick(side, tile_side, rows, dtype):
+    half = tile_side // 2
+    taken = lax.broadcasted_iota(jnp.int32, (tile_side * half, rows), 0)
+    token = lax.broadcasted_iota(jnp.int32, (tile_side * half, rows), 1)
+    first = jnp.where(side == 0, half, 0)
+    return (taken // half * tile_side + taken % half + first == token).astype(dtype)
+
+
+def paired_plan(
+    tokens, mod_shift, mod_scale, mod_gate, w_qkv, w_mlp_in, q_gain, k_gain, w_attn_out, w_mlp_out
+):
+    tok_rows, model_width = tokens.shape
+    half_width = w_mlp_in.shape[0]
+    heads, head_dim = q_gain.shape
+    width = heads * head_dim
+    side = lax.axis_index("sx")
+    part = lax.axis_index("tp")
+    core, far = part % 2, part // 2
+    bf16 = jnp.bfloat16
+
+    quarter = half_width // 4
+    sent = lax.dynamic_slice_in_dim(tokens, (1 - side) * half_width + part * quarter, quarter, 1)
+    piece = swap(sent, "sx", 1)
+    pieces = jnp.concatenate(in_order(far, piece, swap(piece, "tp", 2)), axis=1)
+    near = swap(pieces, "tp", 1)
+    even, odd = in_order(core, pieces, near)
+    other_tokens = jnp.concatenate(
+        [even[:, :quarter], odd[:, :quarter], even[:, quarter:], odd[:, quarter:]], axis=1
+    )
+
+    inputs = tokens.astype(jnp.float32)
+    mean = jnp.mean(inputs, axis=-1, keepdims=True)
+    centered = inputs - mean
+    scaling = lax.rsqrt(jnp.mean(centered * centered, axis=-1, keepdims=True) + 1e-06)
+    stats = jnp.concatenate([mean, scaling], axis=1)
+    other_stats = swap(stats, "sx", 1)
+    first = side * half_width
+    gain_part = 1.0 + lax.dynamic_slice_in_dim(mod_scale, first, half_width, 0)
+    shift_part = lax.dynamic_slice_in_dim(mod_shift, first, half_width, 0)
+
+    def modulate(cells, moments):
+        cells = (cells.astype(jnp.float32) - moments[:, :1]) * moments[:, 1:]
+        return (cells * gain_part + shift_part).astype(bf16)
+
+    own = modulate(lax.dynamic_slice_in_dim(tokens, first, half_width, 1), stats)
+    other = modulate(other_tokens, other_stats)
+    own_border = dot(border_pick(side, TILE, tok_rows, bf16), own).astype(bf16)
+    other_border = dot(border_pick(1 - side, TILE, tok_rows, bf16), other).astype(bf16)
+
+    w_heads = w_qkv.reshape(half_width, 3 * width)
+    w_keys = w_heads[:, width:]
+    own_border_kv = dot(own_border, w_keys)
+    other_border_kv = dot(other_border, w_keys)
+    own_qkv = dot(own, w_heads)
+    other_qkv = dot(other, w_heads)
+    own_hidden = dot(own, w_mlp_in)
+    other_hidden = dot(other, w_mlp_in)
+
+    border_kv = other_border_kv + swap(own_border_kv.astype(bf16), "sx", 1).astype(jnp.float32)
+    qkv = own_qkv + swap(other_qkv.astype(bf16), "sx", 1).astype(jnp.float32)
+    hidden_other = other_hidden + swap(own_hidden.astype(bf16), "sx", 1).astype(jnp.float32)
+    hidden_own = own_hidden + swap(other_hidden.astype(bf16), "sx", 1).astype(jnp.float32)
+
+    def columns(cells, head, base=0):
+        return cells[:, base + head * head_dim : base + (head + 1) * head_dim]
+
+    queries = [rms_gain(columns(qkv, h), q_gain[h]).astype(bf16) for h in range(heads)]
+
+    def keys_values(cells, base):
+        keys = [rms_gain(columns(cells, h, base), k_gain[h]).astype(bf16) for h in range(heads)]
+        return jnp.concatenate(keys + [cells[:, base + width : base + 2 * width].astype(bf16)], axis=1)
+
+    own_kv = keys_values(qkv, width)
+    border = keys_values(border_kv, 0)
+    half_rows, half_border = own_kv.shape[0] // 2, border.shape[0] // 2
+    above = shift(jnp.concatenate([own_kv[half_rows:], border[half_border:]], axis=0), "sy", 1)
+    below = shift(jnp.concatenate([own_kv[:half_rows], border[:half_border]], axis=0), "sy", -1)
+    window = jnp.concatenate([own_kv, border, above, below], axis=0)
+    place = jnp.arange(window.shape[0], dtype=jnp.int32)
+    start_above = own_kv.shape[0] + border.shape[0]
+    start_below = start_above + above.shape[0]
+    row = lax.axis_index("sy")
+    in_grid = (place < start_above) | jnp.where(
+        place < start_below, row > 0, row < lax.axis_size("sy") - 1
+    )
+    attended = []
+    for h in range(heads):
+        scores = dot(queries[h], columns(window, h).T) * head_dim ** (-0.5)
+        scores = jnp.where(in_grid[None, :], scores, -jnp.inf)
+        numerators = jnp.exp(scores - jnp.max(scores, axis=-1, keepdims=True))
+        weights = (numerators / jnp.sum(numerators, axis=-1, keepdims=True)).astype(bf16)
+        attended.append(dot(weights, columns(window, h, width)).astype(bf16))
+    attended = jnp.concatenate(attended, axis=1)
+    other_attended = swap(attended, "sx", 1)
+
+    activated_own = jax.nn.gelu(hidden_own, approximate=True).astype(bf16)
+    activated_other = jax.nn.gelu(hidden_other, approximate=True).astype(bf16)
+
+    def branch(heads_part, hidden_part):
+        return dot(heads_part, w_attn_out) + dot(hidden_part, w_mlp_out)
+
+    block = half_width // 2
+
+    def halves(cells):
+        left, right = cells[:, :block], cells[:, block:]
+        return jnp.where(core == 0, left, right), jnp.where(core == 0, right, left)
+
+    def core_sum(cells):
+        keep, send = halves(cells)
+        return keep + swap(send.astype(bf16), "tp", 1).astype(jnp.float32)
+
+    other_sum = core_sum(branch(other_attended, activated_other))
+    own_sum = core_sum(branch(attended, activated_own))
+    got = swap(other_sum.astype(bf16), "sx", 1).astype(jnp.float32)
+    keep = jnp.where(far == side, own_sum, got)
+    send = jnp.where(far == side, got, own_sum)
+    reduced = keep + swap(send.astype(bf16), "tp", 2).astype(jnp.float32)
+
+    first_col = part * block
+    residual_part = lax.dynamic_slice_in_dim(tokens, first_col, block, 1).astype(jnp.float32)
+    gate_part = lax.dynamic_slice_in_dim(mod_gate, first_col, block, 0)
+    return (residual_part + gate_part * reduced).astype(bf16)
+
+
+def shards(*arrays):
+    if lax.axis_size("sx") == 2 and lax.axis_size("tp") == 4:
+        return paired_plan(*arrays)
+    return gathered_plan(*arrays)
+
+
 def solution(mesh):
     placed = (
         P(("sy", "sx"), None),

time: 444 us -> 161 us (0.36)
  waiting for transfers between devices: 324 us -> 59.1 us
  local copies, waits for them, and re-layouts: 35 us -> 21.3 us
  between operations: 13.3 us -> 0.47 us
  starting transfers between devices: 14.2 us -> 20.7 us
    all_gather x4 -> x0, waiting for transfers between devices: 269 us -> none  [the longest x1 120 us: shards(): lax.all_gather(w_mlp_in, 'sx', axis=0, tiled=True)]
    ppermute x4 -> x15, waiting for transfers between devices: 23.5 us -> 59.1 us  [the longest x13 53.5 us: swap(): return lax.ppermute(cells, axis, [(i, i ^ bit) for i in range(count)])]
    reduce_scatter x1 -> x0, waiting for transfers between devices: 30.3 us -> none  [shards(): lax.psum_scatter(product_term.astype(jnp.bfloat16), 'tp', scatter_dimensi...]
    concatenate x0 -> x1, local copies, waits for them, and re-layouts: none -> 11.3 us  [paired_plan(): window = jnp.concatenate([own_kv, border, above, below], axis=0)]
    dot_general x4 -> x16, matrix products: 34.1 us -> 44.3 us  [dot(): return jnp.dot(left, right, preferred_element_type=jnp.float32)]
    slice x8 -> x6, local copies, waits for them, and re-layouts: 10 us -> 0.32 us  [the longest x1 0.18 us: paired_plan(): even[:, :quarter]]
    sub x1 -> x0, matrix products: 7.28 us -> none  [shards(): numerators = jnp.exp(scores - row_max)]
    ppermute x4 -> x15, starting transfers between devices: 14.1 us -> 20.7 us  [the longest x13 14 us: swap(): return lax.ppermute(cells, axis, [(i, i ^ bit) for i in range(count)])]
  transfers between devices with their start and end apart: 9 -> 15, of which waited for: 8 -> 9; matrix products, arithmetic and copies ran while one was open for 17% -> 45% of each run, Pallas kernels for 0% -> 0%
where the time goes in v1:
time: 161 us; the launch traced here: 160 us
  waiting for transfers between devices  59.1 us (37%)
  matrix products  44.3 us (28%)
  local copies, waits for them, and re-layouts  21.3 us (13%)
  starting transfers between devices  20.7 us (13%)
  other arithmetic  14.7 us (9%)
    ppermute x13, waiting for transfers between devices, swap(): return lax.ppermute(cells, axis, [(i, i ^ bit) for i in range(count)])  53.5 us
    dot_general x16, matrix products, dot(): return jnp.dot(left, right, preferred_element_type=jnp.float32)  44.3 us
    ppermute x13, starting transfers between devices, swap(): return lax.ppermute(cells, axis, [(i, i ^ bit) for i in range(count)])  14 us
    concatenate x1, local copies, waits for them, and re-layouts, paired_plan(): window = jnp.concatenate([own_kv, border, above, below], axis=0)  11.3 us
    unnamed x33, local copies, waits for them, and re-layouts  7.73 us
    ppermute x2, starting transfers between devices, shift(): lax.ppermute(cells, axis, [(i, i + step) for i in range(count) if 0 <= i...  6.61 us
    ppermute x2, waiting for transfers between devices, shift(): lax.ppermute(cells, axis, [(i, i + step) for i in range(count) if 0 <= i...  5.59 us
    convert_element_type x1, other arithmetic, paired_plan(): return (residual_part + gate_part * reduced).astype(bf16)  3.33 us
  transfers between devices with their start and end apart: 15, of which 9 were waited for; matrix products, arithmetic and copies ran while one was open for 45% of the time, Pallas kernels for 0%

profile of v1, /device:TPU:0, one launch (start us, length us, event | category | flops | bytes accessed | tf_op | source)
XLA Modules:
  0.0 160.5 jit_solution(9656711721534234050)
XLA Ops:
  0.0 1.1 constant_dynamic-slice_fusion
  1.1 3.0 %collective-permute-start = (bf16[400,384]{1,0:T(8,128)(2,1)S(1)}, bf16[400,384]{1,0:T(8,128)(2,1)S(1)}, u32[]{:S(2)}, u32[]{:S(2)}) collective-permute-start(bf16[400,384]{1,0:T(8,128)(2,1)S(1)} %constant_dynamic-slice_fusion), channel_id=1, source_target_pairs={{0,4},{4,0},{1,5},{5,1},{2,6},{6,2},{3,7},{7,3},{8,12},{12,8},{9,1... | collective-permute-start | bytes 921608 | tf_op jit(solution)/shard_map/ppermute | solution.py:104
  4.2 2.1 %convert_reduce_fusion = f32[400]{0:T(512)S(1)} fusion(bf16[400,3072]{1,0:T(8,128)(2,1)} %param.10), kind=kLoop, calls=%fused_computation.1 | loop fusion | flops 2457200 | bytes 2459200 | tf_op jit(solution)/shard_map/reduce_sum | solution.py:153
  6.3 0.1 dynamic-slice_add_fusion
  6.4 0.1 dynamic_slice.22
  6.5 2.5 %fusion.1 = f32[400]{0:T(512)S(1)} fusion(bf16[400,3072]{1,0:T(8,128)(2,1)} %param.10, f32[400]{0:T(512)S(1)} %broadcast_multiply_fusion), kind=kLoop, calls=%fused_computation.3 | loop fusion | flops 4914800 | bytes 2460800 | tf_op jit(solution)/shard_map/reduce_sum | solution.py:155
  8.9 6.1 %copy.11 = bf16[1536,3,384]{0,2,1:T(8,128)(2,1)} copy(bf16[1536,3,384]{2,0,1:T(8,128)(2,1)} %param.14) | data formatting | bytes 7077888 | tf_op args[4]
  15.0 4.2 %fusion.47 = bf16[200,768]{1,0:T(8,128)(2,1)} fusion(bf16[1536,1152]{0,1:T(8,128)(2,1)} %bitcast.26, s32[]{:T(128)S(6)} %select_n.134, s32[200]{0:T(256)S(1)} %get-tuple-element.55, s32[200]{0:T(256)S(1)} %get-tuple-element.56, s32[200]{0:T(256)S(1)} %get-tuple-element.54, s32[200]{0:T(256)S(1)} %get-tuple-element.57, ...), kind=kOutput, calls=%fused_computation.70 | convolution fusion | flops 722246400 | bytes 3914392 | tf_op jit(solution)/shard_map/dot_general | solution.py:115
  19.2 2.1 %collective-permute-start.3 = (f32[400,2]{0,1:T(2,128)S(1)}, f32[400,2]{0,1:T(2,128)S(1)}, u32[]{:S(2)}, u32[]{:S(2)}) collective-permute-start(f32[400,2]{0,1:T(2,128)S(1)} %pad_maximum_fusion.6), channel_id=1, source_target_pairs={{0,4},{4,0},{1,5},{5,1},{2,6},{6,2},{3,7},{7,3},{8,12},{12,8},{9,1... | collective-permute-start | bytes 9608 | tf_op jit(solution)/shard_map/ppermute | solution.py:104
  21.3 6.7 %fusion.119 = (bf16[400,1536]{1,0:T(8,128)(2,1)}, f32[400,1536]{1,0:T(8,128)}) fusion(bf16[1536,1536]{1,0:T(8,128)(2,1)} %param.15, f32[1536]{0:T(1024)S(1)} %dynamic_slice.22, f32[1536]{0:T(1024)S(1)} %dynamic-slice_add_fusion, f32[400]{0:T(512)S(1)} %add_rsqrt_fusion.6, f32[400]{0:T(512)S(1)} %broadcast_multiply_fusion, bf16[400,3072]{1,0:T(8,128)(2,1)} %param.10, ...), kind=kOutput, calls=%fused_computation.186 | convolution fusion | flops 1891737600 | bytes 9649284 | tf_op jit(solution)/shard_map/dot_general | solution.py:115
  28.0 2.0 %collective-permute-start.1 = (bf16[400,384]{1,0:T(8,128)(2,1)S(1)}, bf16[400,384]{1,0:T(8,128)(2,1)S(1)}, u32[]{:S(2)}, u32[]{:S(2)}) collective-permute-start(bf16[400,384]{1,0:T(8,128)(2,1)S(1)} %collective-permute-done), channel_id=1, source_target_pairs={{0,2},{1,3},{2,0},{3,1},{4,6},{5,7},{6,4},{7,5},{8,10},{9,11},{10,... | collective-permute-start | bytes 921608 | tf_op jit(solution)/shard_map/ppermute | solution.py:104
  30.0 5.5 %fusion.112 = f32[400,1152]{1,0:T(8,128)} fusion(bf16[1536,1152]{0,1:T(8,128)(2,1)} %bitcast.27, f32[1536]{0:T(1024)S(1)} %dynamic_slice.22, f32[1536]{0:T(1024)S(1)} %dynamic-slice_add_fusion, f32[400]{0:T(512)S(1)} %add_rsqrt_fusion.6, f32[400]{0:T(512)S(1)} %broadcast_multiply_fusion, bf16[400,3072]{1,0:T(8,128)(2,1)} %param.10, s32[]{:T(128)S(6)} %select_n.124), kind=kOutput, calls=%fused_computation.179 | convolution fusion | flops 1419264000 | bytes 6626436 | tf_op jit(solution)/shard_map/dot_general | solution.py:115
  35.5 0.7 collective-permute-done.1
  36.4 0.1 collective-permute-start.2
  36.6 1.9 %collective-permute-done.2 = bf16[400,768]{1,0:T(8,128)(2,1)S(1)} collective-permute-done((bf16[400,768]{1,0:T(8,128)(2,1)S(1)}, bf16[400,768]{1,0:T(8,128)(2,1)S(1)}, u32[]{:S(2)}, u32[]{:S(2)}) %collective-permute-start.2) | collective-permute-done | bytes 614432 | tf_op jit(solution)/shard_map/ppermute | solution.py:104
  38.5 0.2 broadcast_select_fusion.1
  38.7 0.2 fusion.115
  38.9 3.1 %fusion.28 = f32[200,768]{1,0:T(8,128)S(1)} fusion(bf16[1536,1152]{0,1:T(8,128)(2,1)} %bitcast.28, bf16[200,768]{1,0:T(8,128)(2,1)} %collective-permute-done.5, s32[]{:T(128)S(6)} %select_n.133, s32[200]{0:T(256)S(1)} %get-tuple-element.55, s32[200]{0:T(256)S(1)} %get-tuple-element.56, s32[200]{0:T(256)S(1)} %get-tuple-element.54, ...), kind=kOutput, calls=%fused_computation.51 | convolution fusion | flops 726700800 | bytes 4528788 | tf_op jit(solution)/shard_map/dot_general | solution.py:115
  42.1 0.2 multiply_reduce_fusion.8
  42.3 4.0 %convolution_convert_fusion = bf16[400,1152]{1,0:T(8,128)(2,1)S(1)} fusion(bf16[1536,1152]{0,1:T(8,128)(2,1)} %bitcast.29, bf16[400,384]{1,0:T(8,128)(2,1)S(1)} %get-tuple-element.52, bf16[400,384]{1,0:T(8,128)(2,1)S(1)} %get-tuple-element.25, bf16[400,384]{1,0:T(8,128)(2,1)S(1)} %get-tuple-element.53, bf16[400,384]{1,0:T(8,128)(2,1)S(1)} %get-tuple-element.24, ...), kind=kOutput, calls=%fused_computation.14 | convolution fusion | flops 1424025600 | bytes 5704832 | tf_op jit(solution)/shard_map/dot_general | solution.py:115
  46.3 5.7 %fusion.123 = (bf16[400,1536]{1,0:T(8,128)(2,1)}, f32[400,1536]{1,0:T(8,128)S(1)}) fusion(bf16[1536,1536]{1,0:T(8,128)(2,1)} %param.15, bf16[400,384]{1,0:T(8,128)(2,1)S(1)} %get-tuple-element.52, bf16[400,384]{1,0:T(8,128)(2,1)S(1)} %get-tuple-element.25, bf16[400,384]{1,0:T(8,128)(2,1)S(1)} %get-tuple-element.53, ...), kind=kOutput, calls=%fused_computation.190 | convolution fusion | flops 1896038400 | bytes 9649280 | tf_op jit(solution)/shard_map/dot_general | solution.py:115
  52.0 1.7 %collective-permute-start.4 = (bf16[400,1152]{1,0:T(8,128)(2,1)S(1)}, bf16[400,1152]{1,0:T(8,128)(2,1)S(1)}, u32[]{:S(2)}, u32[]{:S(2)}) collective-permute-start(bf16[400,1152]{1,0:T(8,128)(2,1)S(1)} %convolution_convert_fusion), channel_id=1, source_target_pairs={{0,4},{4,0},{1,5},{5,1},{2,6},{6,2},{3,7},{7,3},{8,12},{12,8},{9,1... | collective-permute-start | bytes 2764808 | tf_op jit(solution)/shard_map/ppermute | solution.py:104
  53.6 0.3 collective-permute-start.8
  54.0 0.2 multiply_convert_fusion.11
  54.3 3.4 %collective-permute-done.11 = bf16[400,1536]{1,0:T(8,128)(2,1)} collective-permute-done((bf16[400,1536]{1,0:T(8,128)(2,1)}, bf16[400,1536]{1,0:T(8,128)(2,1)}, u32[]{:S(2)}, u32[]{:S(2)}) %collective-permute-start.11) | collective-permute-done | bytes 1228832 | tf_op jit(solution)/shard_map/ppermute | solution.py:104
  57.6 5.3 %fusion.36 = f32[400,1536]{1,0:T(8,128)} fusion(bf16[1536,1536]{1,0:T(8,128)(2,1)S(1)} %bitcast.39, f32[400,1536]{1,0:T(8,128)S(1)} %get-tuple-element.49, bf16[400,1536]{1,0:T(8,128)(2,1)} %collective-permute-done.11), kind=kOutput, calls=%fused_computation.57 | convolution fusion | flops 1894195200 | bytes 10862592 | tf_op jit(solution)/shard_map/dot_general | solution.py:115
  62.9 14.4 %collective-permute-done.4 = bf16[400,1152]{1,0:T(8,128)(2,1)S(1)} collective-permute-done((bf16[400,1152]{1,0:T(8,128)(2,1)S(1)}, bf16[400,1152]{1,0:T(8,128)(2,1)S(1)}, u32[]{:S(2)}, u32[]{:S(2)}) %collective-permute-start.4) | collective-permute-done | bytes 921632 | tf_op jit(solution)/shard_map/ppermute | solution.py:104
  77.3 0.2 convert_add_fusion
  77.5 0.7 multiply_reduce_fusion.5
  78.2 0.2 multiply_convert_fusion.4
  78.5 0.1 pad_maximum_fusion.1
  78.6 0.8 copy-done.2
  79.5 1.3 collective-permute-start.7
  80.8 5.3 %collective-permute-start.6 = (bf16[300,768]{1,0:T(8,128)(2,1)S(1)}, bf16[300,768]{1,0:T(8,128)(2,1)}, u32[]{:S(2)}, u32[]{:S(2)}) collective-permute-start(bf16[300,768]{1,0:T(8,128)(2,1)S(1)} %pad_maximum_fusion.2), channel_id=1, source_target_pairs={{0,8},{8,16},{16,24},{1,9},{9,17},{17,25},{2,10},{10,18},{18,26},{... | collective-permute-start | bytes 1382408 | tf_op jit(solution)/shard_map/ppermute | solution.py:109
  86.1 5.1 %collective-permute-done.7 = bf16[300,768]{1,0:T(8,128)(2,1)S(1)} collective-permute-done((bf16[300,768]{1,0:T(8,128)(2,1)S(1)}, bf16[300,768]{1,0:T(8,128)(2,1)S(1)}, u32[]{:S(2)}, u32[]{:S(2)}) %collective-permute-start.7) | collective-permute-done | bytes 460832 | tf_op jit(solution)/shard_map/ppermute | solution.py:109
  91.3 0.8 copy-done.6
  92.1 0.4 collective-permute-done.6
  92.5 11.3 %concatenate.34 = bf16[1200,768]{1,0:T(8,128)(2,1)} concatenate(bf16[400,768]{1,0:T(8,128)(2,1)} %copy-done.2, bf16[200,768]{1,0:T(8,128)(2,1)S(1)} %pad_maximum_fusion.4, bf16[300,768]{1,0:T(8,128)(2,1)} %collective-permute-done.6, bf16[300,768]{1,0:T(8,128)(2,1)} %copy-done.6), dimensions={0} | concatenate | bytes 3686400 | tf_op jit(solution)/shard_map/concatenate | solution.py:199
  103.8 1.7 %fusion.122 = (f32[400]{0:T(512)S(1)}, f32[400,1200]{1,0:T(8,128)S(1)}) fusion(bf16[1200,768]{1,0:T(8,128)(2,1)} %concatenate.34, f32[400,1152]{1,0:T(8,128)S(1)} %convert_add_fusion, f32[128]{0:T(128)S(1)} %get-tuple-element.34, f32[400]{0:T(512)S(1)} %add_rsqrt_fusion.5, pred[1200]{0:T(1024)(128)(4,1)S(1)} %fusion.94), kind=kOutput, calls=%fused_computation.189 | convolution fusion | flops 124473200 | bytes 2438208 | tf_op jit(solution)/shard_map/dot_general | solution.py:115
  105.5 0.4 fusion.25
  105.9 0.6 convolution_convert_fusion.5
  106.5 0.6 fusion.121
  107.1 0.4 fusion.26
  107.5 0.6 convolution_convert_fusion.4
  108.1 0.6 fusion.120
  108.7 0.4 fusion.27
  109.1 0.6 convolution_convert_fusion.3
  109.7 1.3 collective-permute-start.10
  111.0 0.8 fusion.110
  111.8 4.8 %collective-permute-done.10 = bf16[400,384]{1,0:T(8,128)(2,1)S(1)} collective-permute-done((bf16[400,384]{1,0:T(8,128)(2,1)S(1)}, bf16[400,384]{1,0:T(8,128)(2,1)S(1)}, u32[]{:S(2)}, u32[]{:S(2)}) %collective-permute-start.10) | collective-permute-done | bytes 307232 | tf_op jit(solution)/shard_map/ppermute | solution.py:104
  116.7 0.8 convolution_add_fusion
  117.5 0.1 select_convert_fusion
  117.6 0.1 collective-permute-start.12
  117.7 3.7 %convolution_add_fusion.1 = f32[400,1536]{1,0:T(8,128)S(1)} fusion(f32[400,1536]{1,0:T(8,128)S(1)} %fusion.110, bf16[1536,1536]{1,0:T(8,128)(2,1)S(1)} %bitcast.41, f32[400,1536]{1,0:T(8,128)S(1)} %copy-done.11, bf16[400,1536]{1,0:T(8,128)(2,1)} %collective-permute-done.8), kind=kOutput, calls=%fused_computation.13 | convolution fusion | flops 1894809600 | bytes 13320192 | tf_op jit(solution)/shard_map/dot_general | solution.py:115
  121.4 0.1 select_convert_fusion.1
  121.6 0.5 collective-permute-start.9
  122.1 1.1 add_convert_fusion.2
  123.2 1.2 collective-permute-start.13
  124.4 15.2 %collective-permute-done.13 = bf16[400,768]{1,0:T(8,128)(2,1)S(1)} collective-permute-done((bf16[400,768]{1,0:T(8,128)(2,1)}, bf16[400,768]{1,0:T(8,128)(2,1)S(1)}, u32[]{:S(2)}, u32[]{:S(2)}) %collective-permute-start.13) | collective-permute-done | bytes 614432 | tf_op jit(solution)/shard_map/ppermute | solution.py:104
  139.6 2.0 %fusion.35 = bf16[400,768]{1,0:T(8,128)(2,1)S(1)} fusion(bf16[400,768]{1,0:T(8,128)(2,1)S(1)} %collective-permute-done.13, pred[]{:T(512)S(6)} %eq.33, bf16[400,768]{1,0:T(8,128)(2,1)S(1)} %collective-permute-done.9, f32[400,1536]{1,0:T(8,128)} %copy-done.1, pred[]{:T(512)S(6)} %eq.34), kind=kLoop, calls=%fused_computation.56 | loop fusion | flops 1843200 | bytes 4300802 | tf_op jit(solution)/shard_map/convert_element_type | solution.py:238
  141.6 1.7 %collective-permute-start.14 = (bf16[400,768]{1,0:T(8,128)(2,1)S(1)}, bf16[400,768]{1,0:T(8,128)(2,1)}, u32[]{:S(2)}, u32[]{:S(2)}) collective-permute-start(bf16[400,768]{1,0:T(8,128)(2,1)S(1)} %fusion.35), channel_id=1, source_target_pairs={{0,2},{1,3},{2,0},{3,1},{4,6},{5,7},{6,4},{7,5},{8,10},{9,11},{10,... | collective-permute-start | bytes 1843208 | tf_op jit(solution)/shard_map/ppermute | solution.py:104
  143.3 0.8 dynamic_slice.19
  144.1 13.1 %collective-permute-done.14 = bf16[400,768]{1,0:T(8,128)(2,1)} collective-permute-done((bf16[400,768]{1,0:T(8,128)(2,1)S(1)}, bf16[400,768]{1,0:T(8,128)(2,1)}, u32[]{:S(2)}, u32[]{:S(2)}) %collective-permute-start.14) | collective-permute-done | bytes 614432 | tf_op jit(solution)/shard_map/ppermute | solution.py:104
  157.1 3.3 %fusion.34 = bf16[400,768]{1,0:T(8,128)(2,1)} fusion(bf16[400,768]{1,0:T(8,128)(2,1)S(1)} %collective-permute-done.13, bf16[400,768]{1,0:T(8,128)(2,1)} %collective-permute-done.14, f32[768]{0:T(1024)S(1)} %dynamic_slice.19, bf16[400,3072]{1,0:T(8,128)(2,1)} %param.10, s32[]{:T(128)S(6)} %select_n.118, pred[]{:T(512)S(6)} %eq.33, ...), kind=kLoop, calls=%fused_computation.55 | loop fusion | flops 3379200 | bytes 5532678 | tf_op jit(solution)/shard_map/convert_element_type | solution.py:243
  (69 shorter events, 0.6 us)
Async XLA Ops:
  0.0 111.0 %copy-start = (bf16[384,1536]{1,0:T(8,128)(2,1)S(1)}, bf16[384,1536]{1,0:T(8,128)(2,1)}, u32[]{:S(2)}) copy-start(bf16[384,1536]{1,0:T(8,128)(2,1)} %param.18) | copy-start | bytes 3538948
  0.0 6.3 %copy-start.7 = (f32[3072]{0:T(1024)S(1)}, f32[3072]{0:T(1024)}, u32[]{:S(2)}) copy-start(f32[3072]{0:T(1024)} %param.12) | copy-start | bytes 36868
  0.0 6.4 %copy-start.8 = (f32[3072]{0:T(1024)S(1)}, f32[3072]{0:T(1024)}, u32[]{:S(2)}) copy-start(f32[3072]{0:T(1024)} %param.11) | copy-start | bytes 36868
  1.1 26.9 %collective-permute-start = (bf16[400,384]{1,0:T(8,128)(2,1)S(1)}, bf16[400,384]{1,0:T(8,128)(2,1)S(1)}, u32[]{:S(2)}, u32[]{:S(2)}) collective-permute-start(bf16[400,384]{1,0:T(8,128)(2,1)S(1)} %constant_dynamic-slice_fusion), channel_id=1, source_target_pairs={{0,4},{4,0},{1,5},{5,1},{2,6},{6,2},{3,7},{7,3},{8,12},{12,8},{9,1... | collective-permute-start | bytes 921608 | tf_op jit(solution)/shard_map/ppermute | solution.py:104
  19.2 19.7 %collective-permute-start.5 = (bf16[200,768]{1,0:T(8,128)(2,1)}, bf16[200,768]{1,0:T(8,128)(2,1)}, u32[]{:S(2)}, u32[]{:S(2)}) collective-permute-start(bf16[200,768]{1,0:T(8,128)(2,1)} %fusion.47), channel_id=1, source_target_pairs={{0,4},{4,0},{1,5},{5,1},{2,6},{6,2},{3,7},{7,3},{8,12},{12,8},{9,1... | collective-permute-start | bytes 921608 | tf_op jit(solution)/shard_map/ppermute | solution.py:104
  19.2 17.3 %collective-permute-start.3 = (f32[400,2]{0,1:T(2,128)S(1)}, f32[400,2]{0,1:T(2,128)S(1)}, u32[]{:S(2)}, u32[]{:S(2)}) collective-permute-start(f32[400,2]{0,1:T(2,128)S(1)} %pad_maximum_fusion.6), channel_id=1, source_target_pairs={{0,4},{4,0},{1,5},{5,1},{2,6},{6,2},{3,7},{7,3},{8,12},{12,8},{9,1... | collective-permute-start | bytes 9608 | tf_op jit(solution)/shard_map/ppermute | solution.py:104
  28.0 29.6 %collective-permute-start.11 = (bf16[400,1536]{1,0:T(8,128)(2,1)}, bf16[400,1536]{1,0:T(8,128)(2,1)}, u32[]{:S(2)}, u32[]{:S(2)}) collective-permute-start(bf16[400,1536]{1,0:T(8,128)(2,1)} %get-tuple-element.40), channel_id=1, source_target_pairs={{0,4},{4,0},{1,5},{5,1},{2,6},{6,2},{3,7},{7,3},{8,12},{12,8},{9,1... | collective-permute-start | bytes 3686408 | tf_op jit(solution)/shard_map/ppermute | solution.py:104
  28.0 8.2 %collective-permute-start.1 = (bf16[400,384]{1,0:T(8,128)(2,1)S(1)}, bf16[400,384]{1,0:T(8,128)(2,1)S(1)}, u32[]{:S(2)}, u32[]{:S(2)}) collective-permute-start(bf16[400,384]{1,0:T(8,128)(2,1)S(1)} %collective-permute-done), channel_id=1, source_target_pairs={{0,2},{1,3},{2,0},{3,1},{4,6},{5,7},{6,4},{7,5},{8,10},{9,11},{10,... | collective-permute-start | bytes 921608 | tf_op jit(solution)/shard_map/ppermute | solution.py:104
  35.5 0.9 copy-start.9
  35.5 0.9 copy-start.10
  36.4 2.1 %collective-permute-start.2 = (bf16[400,768]{1,0:T(8,128)(2,1)S(1)}, bf16[400,768]{1,0:T(8,128)(2,1)S(1)}, u32[]{:S(2)}, u32[]{:S(2)}) collective-permute-start(bf16[400,768]{1,0:T(8,128)(2,1)S(1)} %pad_maximum_fusion), channel_id=1, source_target_pairs={{0,1},{1,0},{2,3},{3,2},{4,5},{5,4},{6,7},{7,6},{8,9},{9,8},{10,11... | collective-permute-start | bytes 1843208 | tf_op jit(solution)/shard_map/ppermute | solution.py:104
  42.3 15.4 %slice-start = ((s8[4718592]{0:T(1024)(128)(4,1)}), s8[524288]{0:T(1024)(128)(4,1)S(1)}, s32[]{:S(2)}) async-start(s8[4718592]{0:T(1024)(128)(4,1)} %bitcast.38), calls=%async_computation | async-start | bytes 1048576
  46.3 11.4 %slice-start.1 = ((s8[4718592]{0:T(1024)(128)(4,1)}), s8[4194304]{0:T(1024)(128)(4,1)S(1)}, s32[]{:S(2)}) async-start(s8[4718592]{0:T(1024)(128)(4,1)} %bitcast.38), calls=%async_computation.1 | async-start | bytes 8388608
  52.0 25.3 %collective-permute-start.4 = (bf16[400,1152]{1,0:T(8,128)(2,1)S(1)}, bf16[400,1152]{1,0:T(8,128)(2,1)S(1)}, u32[]{:S(2)}, u32[]{:S(2)}) collective-permute-start(bf16[400,1152]{1,0:T(8,128)(2,1)S(1)} %convolution_convert_fusion), channel_id=1, source_target_pairs={{0,4},{4,0},{1,5},{5,1},{2,6},{6,2},{3,7},{7,3},{8,12},{12,8},{9,1... | collective-permute-start | bytes 2764808 | tf_op jit(solution)/shard_map/ppermute | solution.py:104
  53.6 64.0 %collective-permute-start.8 = (bf16[400,1536]{1,0:T(8,128)(2,1)}, bf16[400,1536]{1,0:T(8,128)(2,1)}, u32[]{:S(2)}, u32[]{:S(2)}) collective-permute-start(bf16[400,1536]{1,0:T(8,128)(2,1)} %get-tuple-element.48), channel_id=1, source_target_pairs={{0,4},{4,0},{1,5},{5,1},{2,6},{6,2},{3,7},{7,3},{8,12},{12,8},{9,1... | collective-permute-start | bytes 3686408 | tf_op jit(solution)/shard_map/ppermute | solution.py:104
  57.6 19.6 %copy-start.5 = (f32[400,1152]{1,0:T(8,128)S(1)}, f32[400,1152]{1,0:T(8,128)}, u32[]{:S(2)}) copy-start(f32[400,1152]{1,0:T(8,128)} %fusion.112) | copy-start | bytes 5529604
  78.6 0.8 copy-start.2
  79.5 11.8 %collective-permute-start.7 = (bf16[300,768]{1,0:T(8,128)(2,1)S(1)}, bf16[300,768]{1,0:T(8,128)(2,1)S(1)}, u32[]{:S(2)}, u32[]{:S(2)}) collective-permute-start(bf16[300,768]{1,0:T(8,128)(2,1)S(1)} %pad_maximum_fusion.3), channel_id=1, source_target_pairs={{8,0},{16,8},{24,16},{9,1},{17,9},{25,17},{10,2},{18,10},{26,18},{... | collective-permute-start | bytes 1382408 | tf_op jit(solution)/shard_map/ppermute | solution.py:109
  80.8 11.7 %collective-permute-start.6 = (bf16[300,768]{1,0:T(8,128)(2,1)S(1)}, bf16[300,768]{1,0:T(8,128)(2,1)}, u32[]{:S(2)}, u32[]{:S(2)}) collective-permute-start(bf16[300,768]{1,0:T(8,128)(2,1)S(1)} %pad_maximum_fusion.2), channel_id=1, source_target_pairs={{0,8},{8,16},{16,24},{1,9},{9,17},{17,25},{2,10},{10,18},{18,26},{... | collective-permute-start | bytes 1382408 | tf_op jit(solution)/shard_map/ppermute | solution.py:109
  91.3 0.8 copy-start.6
  103.8 2.1 %copy-start.3 = (bf16[1200,768]{1,0:T(8,128)(2,1)S(1)}, bf16[1200,768]{1,0:T(8,128)(2,1)}, u32[]{:S(2)}) copy-start(bf16[1200,768]{1,0:T(8,128)(2,1)} %concatenate.34) | copy-start | bytes 5529604
  109.7 6.9 %copy-start.4 = (f32[400,1536]{1,0:T(8,128)S(1)}, f32[400,1536]{1,0:T(8,128)}, u32[]{:S(2)}) copy-start(f32[400,1536]{1,0:T(8,128)} %fusion.36) | copy-start | bytes 7372804
  109.7 6.9 %collective-permute-start.10 = (bf16[400,384]{1,0:T(8,128)(2,1)S(1)}, bf16[400,384]{1,0:T(8,128)(2,1)S(1)}, u32[]{:S(2)}, u32[]{:S(2)}) collective-permute-start(bf16[400,384]{1,0:T(8,128)(2,1)S(1)} %pad_maximum_fusion.5), channel_id=1, source_target_pairs={{0,4},{4,0},{1,5},{5,1},{2,6},{6,2},{3,7},{7,3},{8,12},{12,8},{9,1... | collective-permute-start | bytes 921608 | tf_op jit(solution)/shard_map/ppermute | solution.py:104
  111.0 6.7 %slice-start.2 = ((s8[4718592]{0:T(1024)(128)(4,1)}), s8[4194304]{0:T(1024)(128)(4,1)S(1)}, s32[]{:S(2)}) async-start(s8[4718592]{0:T(1024)(128)(4,1)} %bitcast.40), calls=%async_computation.2 | async-start | bytes 8388608
  111.8 5.9 %slice-start.3 = ((s8[4718592]{0:T(1024)(128)(4,1)}), s8[524288]{0:T(1024)(128)(4,1)S(1)}, s32[]{:S(2)}) async-start(s8[4718592]{0:T(1024)(128)(4,1)} %bitcast.40), calls=%async_computation.3 | async-start | bytes 1048576
  111.8 5.9 %copy-start.11 = (f32[400,1536]{1,0:T(8,128)S(1)}, f32[400,1536]{1,0:T(8,128)}, u32[]{:S(2)}) copy-start(f32[400,1536]{1,0:T(8,128)} %get-tuple-element.41) | copy-start | bytes 7372804
  117.6 4.5 %collective-permute-start.12 = (bf16[400,768]{1,0:T(8,128)(2,1)S(1)}, bf16[400,768]{1,0:T(8,128)(2,1)S(1)}, u32[]{:S(2)}, u32[]{:S(2)}) collective-permute-start(bf16[400,768]{1,0:T(8,128)(2,1)S(1)} %select_convert_fusion), channel_id=1, source_target_pairs={{0,1},{1,0},{2,3},{3,2},{4,5},{5,4},{6,7},{7,6},{8,9},{9,8},{10,11... | collective-permute-start | bytes 1843208 | tf_op jit(solution)/shard_map/ppermute | solution.py:104
  121.4 1.7 %copy-start.1 = (f32[400,1536]{1,0:T(8,128)}, f32[400,1536]{1,0:T(8,128)S(1)}, u32[]{:S(2)}) copy-start(f32[400,1536]{1,0:T(8,128)S(1)} %convolution_add_fusion.1) | copy-start | bytes 7372804
  121.6 2.8 %collective-permute-start.9 = (bf16[400,768]{1,0:T(8,128)(2,1)S(1)}, bf16[400,768]{1,0:T(8,128)(2,1)S(1)}, u32[]{:S(2)}, u32[]{:S(2)}) collective-permute-start(bf16[400,768]{1,0:T(8,128)(2,1)S(1)} %select_convert_fusion.1), channel_id=1, source_target_pairs={{0,1},{1,0},{2,3},{3,2},{4,5},{5,4},{6,7},{7,6},{8,9},{9,8},{10,11... | collective-permute-start | bytes 1843208 | tf_op jit(solution)/shard_map/ppermute | solution.py:104
  123.2 16.4 %collective-permute-start.13 = (bf16[400,768]{1,0:T(8,128)(2,1)}, bf16[400,768]{1,0:T(8,128)(2,1)S(1)}, u32[]{:S(2)}, u32[]{:S(2)}) collective-permute-start(bf16[400,768]{1,0:T(8,128)(2,1)} %add_convert_fusion.2), channel_id=1, source_target_pairs={{0,4},{4,0},{1,5},{5,1},{2,6},{6,2},{3,7},{7,3},{8,12},{12,8},{9,1... | collective-permute-start | bytes 1843208 | tf_op jit(solution)/shard_map/ppermute | solution.py:104
  141.6 15.6 %collective-permute-start.14 = (bf16[400,768]{1,0:T(8,128)(2,1)S(1)}, bf16[400,768]{1,0:T(8,128)(2,1)}, u32[]{:S(2)}, u32[]{:S(2)}) collective-permute-start(bf16[400,768]{1,0:T(8,128)(2,1)S(1)} %fusion.35), channel_id=1, source_target_pairs={{0,2},{1,3},{2,0},{3,1},{4,6},{5,7},{6,4},{7,5},{8,10},{9,11},{10,... | collective-permute-start | bytes 1843208 | tf_op jit(solution)/shard_map/ppermute | solution.py:104

commit v2 on v0

--- a/solution.py
+++ b/solution.py
@@ -1,6 +1,9 @@
 import jax
 import jax.numpy as jnp
+import numpy as np
 from jax import lax
+from jax.experimental import pallas as pl
+from jax.experimental.pallas import tpu as pltpu
 from jax.sharding import PartitionSpec as P
 
 TILE = 20
@@ -34,7 +37,7 @@
     return vector * lax.rsqrt(mean_square + 1e-06) * scaling
 
 
-def shards(
+def gathered_plan(
     tokens, mod_shift, mod_scale, mod_gate, w_qkv, w_mlp_in, q_gain, k_gain, w_attn_out, w_mlp_out
 ):
     tok_rows, model_width = tokens.shape
@@ -99,6 +102,337 @@
     return (residual_part + gate_part * reduced).astype(jnp.bfloat16)
 
 
+def swap(cells, axis, bit):
+    count = lax.axis_size(axis)
+    return lax.ppermute(cells, axis, [(i, i ^ bit) for i in range(count)])
+
+
+def shift(cells, axis, step):
+    count = lax.axis_size(axis)
+    return lax.ppermute(
+        cells, axis, [(i, i + step) for i in range(count) if 0 <= i + step < count]
+    )
+
+
+def dot(left, right):
+    return jnp.dot(left, right, preferred_element_type=jnp.float32)
+
+
+BF16, F32 = jnp.bfloat16, jnp.float32
+LANES = 128
+
+
+def width_of(total, most):
+    return max(w for w in range(LANES, most + 1, LANES) if total % w == 0)
+
+
+def call(body, grid, ins, outs, scratch=(), after=(), vmem=16, cost=(1000, 1000)):
+    n_in, n_after = len(ins), len(after)
+
+    def kernel(*refs):
+        body(*refs[:n_in], *refs[n_in + n_after :])
+
+    def spec(block, index):
+        if block is None:
+            return pl.BlockSpec(memory_space=index)
+        return pl.BlockSpec(block, index)
+
+    return pl.pallas_call(
+        kernel,
+        grid=(grid,),
+        in_specs=[spec(b, i) for _, b, i in ins] + [pl.BlockSpec(memory_space=pl.ANY)] * n_after,
+        out_specs=[spec(b, i) for _, _, b, i in outs],
+        out_shape=[jax.ShapeDtypeStruct(s, d) for s, d, _, _ in outs],
+        scratch_shapes=list(scratch),
+        compiler_params=pltpu.CompilerParams(vmem_limit_bytes=vmem * 2**20),
+        cost_estimate=pl.CostEstimate(flops=cost[0], bytes_accessed=cost[1], transcendentals=0),
+    )(*[a for a, _, _ in ins], *after)
+
+
+def in_order(bit, mine, other):
+    return jnp.where(bit == 0, mine, other), jnp.where(bit == 0, other, mine)
+
+
+def hold(cells, *earlier, cost=0):
+    return pl.pallas_call(
+        lambda *refs: None,
+        in_specs=[pl.BlockSpec(memory_space=pl.ANY)] * (1 + len(earlier)),
+        out_specs=pl.BlockSpec(memory_space=pl.ANY),
+        out_shape=jax.ShapeDtypeStruct(cells.shape, cells.dtype),
+        input_output_aliases={0: 0},
+        compiler_params=pltpu.CompilerParams(vmem_limit_bytes=2**20),
+        cost_estimate=pl.CostEstimate(flops=0, bytes_accessed=cost, transcendentals=0),
+    )(cells, *earlier)
+
+
+def at(*place):
+    return lambda *_: place
+
+
+def border_rows(tile_side):
+    half = tile_side // 2
+    return (half * half + 15) // 16 * 16
+
+
+def border_picks(tile_side, side):
+    half, rows = tile_side // 2, border_rows(tile_side)
+    picks = np.zeros((2, 2 * rows, tile_side * tile_side), np.float32)
+    for which in range(2):
+        for low in range(2):
+            for i in range(half):
+                for j in range(half):
+                    token = (low * half + i) * tile_side + j + (half if which == 0 else 0)
+                    picks[which, low * rows + i * half + j, token] = 1
+    left, right = jnp.asarray(picks[0], BF16), jnp.asarray(picks[1], BF16)
+    return jnp.where(side == 0, left, right), jnp.where(side == 0, right, left)
+
+
+def rest_of_first(own, other, pick, heads_weights, hidden_weights, cut, after=()):
+    rows, depth = own.shape
+    width, hidden = heads_weights[0].shape[1], hidden_weights.shape[1]
+    border = pick.shape[0]
+    block = width_of(hidden, 384)
+
+    def body(own_ref, other_ref, pick_ref, wq_ref, wk_ref, wv_ref, w_ref, qkv_ref, border_ref, sums_ref, a_ref, b_ref):
+        @pl.when(pl.program_id(0) == 0)
+        def _():
+            taken = dot(pick_ref[...], other_ref[...]).astype(BF16)
+            for i, ref in enumerate((wq_ref, wk_ref, wv_ref)):
+                qkv_ref[:, i * width : (i + 1) * width] = dot(own_ref[...], ref[...])
+            for i, ref in enumerate((wk_ref, wv_ref)):
+                border_ref[:, i * width : (i + 1) * width] = dot(taken, ref[...])
+
+        sums = dot(other_ref[...], w_ref[...])
+        sums_ref[...] = sums
+        a_ref[...] = sums[:cut].astype(BF16)
+        b_ref[...] = sums[cut:].astype(BF16)
+
+    whole = at(0, 0)
+    column = lambda j: (0, j)
+    return call(
+        body, hidden // block,
+        [(own, own.shape, whole), (other, other.shape, whole), (pick, pick.shape, whole)]
+        + [(w, w.shape, whole) for w in heads_weights]
+        + [(hidden_weights, (depth, block), column)],
+        [
+            ((rows, 3 * width), F32, (rows, 3 * width), whole),
+            ((border, 2 * width), F32, (border, 2 * width), whole),
+            ((rows, hidden), F32, (rows, block), column),
+            ((cut, hidden), BF16, (cut, block), column),
+            ((rows - cut, hidden), BF16, (rows - cut, block), column),
+        ],
+        after=after, vmem=28,
+        cost=(
+            2 * depth * (rows * 3 * width + border * 2 * width + rows * hidden),
+            2 * depth * (2 * rows + 3 * width + hidden) + 4 * (3 * rows + 2 * border) * width + 6 * rows * hidden,
+        ),
+    )
+
+
+def norm_heads(mine, got, border_mine, border_got, q_gain, k_gain, after=()):
+    rows, heads, head_dim = mine.shape[0], q_gain.shape[0], q_gain.shape[2]
+    half_border = border_mine.shape[0] // 2
+    sent_own = (rows // 2 + 15) // 16 * 16
+    sent = sent_own + half_border
+
+    def body(*refs):
+        q, k, v, q2, k2, v2, bk, bv, bk2, bv2, qg, kg = [r[...].astype(F32) for r in refs[:12]]
+        queries_ref, own_ref, border_ref, lower_ref, upper_ref = refs[12:]
+        queries_ref[...] = rms_gain(q + q2, qg[0]).astype(BF16)
+        own = jnp.concatenate([rms_gain(k + k2, kg[0]), v + v2], axis=1).astype(BF16)
+        border = jnp.concatenate([rms_gain(bk + bk2, kg[0]), bv + bv2], axis=1).astype(BF16)
+        own_ref[...] = own
+        border_ref[...] = border
+        upper_ref[:sent_own] = own[:sent_own]
+        upper_ref[sent_own:] = border[:half_border]
+        lower_ref[:sent_own] = own[rows - sent_own :]
+        lower_ref[sent_own:] = border[half_border:]
+
+    def third(array, group):
+        return (array, (array.shape[0], head_dim), lambda h: (0, group * heads + h))
+
+    def beside(count):
+        return ((count, 2 * heads * head_dim), BF16, (count, 2 * head_dim), lambda h: (0, h))
+
+    gain = lambda h: (h, 0, 0)
+    return call(
+        body, heads,
+        [third(mine, g) for g in range(3)] + [third(got, g) for g in range(3)]
+        + [third(border_mine, g) for g in range(2)] + [third(border_got, g) for g in range(2)]
+        + [(q_gain, (1, 1, head_dim), gain), (k_gain, (1, 1, head_dim), gain)],
+        [
+            ((rows, heads * head_dim), BF16, (rows, head_dim), lambda h: (0, h)),
+            beside(rows), beside(2 * half_border), beside(sent), beside(sent),
+        ],
+        after=after,
+    )
+
+
+def attend(queries, keys_values, bias, heads, after=()):
+    rows, head_dim = queries.shape[0], queries.shape[1] // heads
+    spare = bias.shape[1] - sum(k.shape[0] for k in keys_values)
+
+    def body(queries_ref, bias_ref, *refs):
+        blocks = [r[...] for r in refs[:-1]]
+        if spare:
+            blocks.append(jnp.zeros((spare, 2 * head_dim), BF16))
+        both = jnp.concatenate(blocks, axis=0)
+        keys, values = both[:, :head_dim], both[:, head_dim:]
+        scores = lax.dot_general(queries_ref[...], keys, (((1,), (1,)), ((), ())), preferred_element_type=F32)
+        scores = scores * head_dim ** (-0.5) + bias_ref[...]
+        numerators = jnp.exp(scores - jnp.max(scores, axis=-1, keepdims=True))
+        total = jnp.sum(numerators, axis=-1, keepdims=True)
+        refs[-1][...] = (dot(numerators.astype(BF16), values) / total).astype(BF16)
+
+    head = lambda h: (0, h)
+    return call(
+        body, heads,
+        [(queries, (rows, head_dim), head), (bias, bias.shape, at(0, 0))]
+        + [(k, (k.shape[0], 2 * head_dim), head) for k in keys_values],
+        [((rows, heads * head_dim), BF16, (rows, head_dim), head)],
+        after=after,
+    )[0]
+
+
+def paired_plan(
+    tokens, mod_shift, mod_scale, mod_gate, w_qkv, w_mlp_in, q_gain, k_gain, w_attn_out, w_mlp_out
+):
+    tok_rows, model_width = tokens.shape
+    half_width, hidden = w_mlp_in.shape
+    heads, head_dim = q_gain.shape
+    width = heads * head_dim
+    side = lax.axis_index("sx")
+    part = lax.axis_index("tp")
+    core, far = part % 2, part // 2
+    mid = hidden // 2
+    block = half_width // 2
+    own_pick, other_pick = border_picks(TILE, side)
+    q_gain, k_gain = q_gain[:, None, :], k_gain[:, None, :]
+
+    piece_width = half_width // 2
+    other_first = (1 - side) * half_width + core * piece_width
+    sent = lax.dynamic_slice_in_dim(tokens, other_first, piece_width, 1)
+    piece = swap(sent, "sx", 1)
+    cells = tokens.astype(F32)
+    mean = jnp.mean(cells, axis=-1, keepdims=True)
+    centered = cells - mean
+    scaling = lax.rsqrt(jnp.mean(centered * centered, axis=-1, keepdims=True) + 1e-06)
+    stats = jnp.concatenate([mean, scaling], axis=1)
+    other_stats = swap(stats, "sx", 1)
+    first = side * half_width
+    gain_part = 1.0 + lax.dynamic_slice_in_dim(mod_scale, first, half_width, 0)
+    shift_part = lax.dynamic_slice_in_dim(mod_shift, first, half_width, 0)
+
+    def modulate(cells, pair):
+        cells = (cells.astype(F32) - pair[:, :1]) * pair[:, 1:]
+        return (cells * gain_part + shift_part).astype(BF16)
+
+    def projected(cells, weights):
+        sums = dot(cells, weights)
+        return sums, sums.astype(BF16)
+
+    w_queries, w_keys, w_values = [w_qkv[:, group] for group in range(3)]
+
+    def heads_of(cells):
+        return jnp.concatenate([dot(cells, w) for w in (w_queries, w_keys, w_values)], axis=1)
+
+    def border_of(pick, cells):
+        cells = dot(pick, cells).astype(BF16)
+        return jnp.concatenate([dot(cells, w) for w in (w_keys, w_values)], axis=1)
+
+    own = modulate(lax.dynamic_slice_in_dim(tokens, first, half_width, 1), stats)
+    own_border = border_of(own_pick, own).astype(BF16)
+    got_border = swap(own_border, "sx", 1)
+    own = hold(own, own_border)
+    own_sums, own_sent = projected(own, w_mlp_in)
+    piece = hold(piece, own_sent)
+    near = swap(piece, "tp", 1)
+    other = modulate(jnp.concatenate(in_order(core, piece, near), axis=1), other_stats)
+    other_qkv = heads_of(other).astype(BF16)
+    got_qkv = swap(other_qkv, "sx", 1)
+    got_own = swap(hold(own_sent, other_qkv), "sx", 1)
+    cut = (tok_rows // 2 + 15) // 16 * 16
+    own_qkv, other_border, other_sums, other_a, other_b = rest_of_first(
+        own, other, other_pick, (w_queries, w_keys, w_values), w_mlp_in, cut, [other_qkv, got_border]
+    )
+
+    queries, own_kv, border_kv, lower, upper = norm_heads(
+        own_qkv, got_qkv, other_border, got_border, q_gain, k_gain, [other_a]
+    )
+    above = shift(lower, "sy", 1)
+    below = shift(upper, "sy", -1)
+
+    def gelu_dot(sums, got, rows):
+        return dot(jax.nn.gelu(sums + got.astype(F32), approximate=True).astype(BF16), rows)
+
+    row = lax.axis_index("sy")
+    extra = tok_rows // 2
+    half_border, taken = border_kv.shape[0] // 2, (TILE // 2) ** 2
+    sent_own = lower.shape[0] - half_border
+    inside = np.zeros(((own_kv.shape[0] + 2 * half_border + 2 * lower.shape[0] + 127) // 128 * 128,), np.int32)
+    inside[:tok_rows] = 1
+    for start in (tok_rows, tok_rows + half_border):
+        inside[start : start + taken] = 1
+    start = tok_rows + 2 * half_border
+    inside[start + sent_own - extra : start + sent_own] = 2
+    inside[start + sent_own : start + sent_own + taken] = 2
+    start += lower.shape[0]
+    inside[start : start + extra] = 3
+    inside[start + sent_own : start + sent_own + taken] = 3
+    there = (inside == 1) | ((inside == 2) & (row > 0)) | ((inside == 3) & (row < lax.axis_size("sy") - 1))
+    bias = jnp.where(there, 0.0, -jnp.inf).astype(F32)[None]
+    attended = attend(queries, [own_kv, border_kv, above, below], bias, heads)
+    got_attended = swap(attended, "sx", 1)
+    got_other_a = swap(other_a, "sx", 1)
+    other_sums = hold(other_sums, attended)
+    other_branch = gelu_dot(other_sums, got_own, w_mlp_out)
+    got_other_a = swap(other_a, "sx", 1)
+    got_other_b = swap(hold(other_b, other_branch), "sx", 1)
+
+    def split(cells):
+        left, right = cells[:, :block], cells[:, block:]
+        return jnp.where(core == 0, right, left).astype(BF16), jnp.where(core == 0, left, right)
+
+    def core_sum(cells, *earlier):
+        send, keep = split(cells)
+        return keep + swap(hold(send, *earlier), "tp", 1).astype(F32)
+
+    own_sums = hold(own_sums, other_branch)
+    own_part = gelu_dot(own_sums[:cut], got_other_a, w_mlp_out) + dot(attended[:cut], w_attn_out)
+    other_branch = hold(other_branch, own_part)
+    other_sum = core_sum(other_branch + dot(got_attended, w_attn_out))
+    half_rows = tok_rows // 2
+    send = lax.dynamic_slice_in_dim(other_sum, (1 - far) * half_rows, half_rows, 0).astype(BF16)
+    keep = lax.dynamic_slice_in_dim(other_sum, far * half_rows, half_rows, 0)
+    crossing = (keep + swap(send, "tp", 2).astype(F32)).astype(BF16)
+    got = swap(crossing, "sx", 1)
+    own_sum_a = core_sum(own_part)
+    own_sums = hold(own_sums, own_part, crossing)
+    own_sum_b = core_sum(gelu_dot(own_sums[cut:], got_other_b, w_mlp_out) + dot(attended[cut:], w_attn_out), got)
+
+    others = lax.axis_size("tp") // 2
+    homes = [(s * 2 * others + (1 - s) * 2 + c, s * 2 * others + s * 2 + c) for s in range(2) for c in range(2)]
+    to_home = lambda cells: lax.ppermute(cells, ("sx", "tp"), homes)
+    from_home = lambda cells: lax.ppermute(cells, ("sx", "tp"), [(b, a) for a, b in homes])
+    come_a = to_home(own_sum_a.astype(BF16))
+    come_b = to_home(own_sum_b.astype(BF16))
+    got = hold(got, come_a)
+    rest = from_home(got)
+    own_sum = jnp.concatenate([own_sum_a + come_a.astype(F32), own_sum_b + come_b.astype(F32)], axis=0)
+    reduced = jnp.where(far == side, own_sum, jnp.concatenate(in_order(far, got, rest), axis=0).astype(F32))
+
+    first_col = hold(part[None], other_sum)[0] * block
+    gate_part = lax.dynamic_slice_in_dim(mod_gate, first_col, block, 0)
+    residual_part = lax.dynamic_slice_in_dim(tokens, first_col, block, 1).astype(F32)
+    return (residual_part + gate_part * reduced).astype(BF16)
+
+
+def shards(*arrays):
+    if lax.axis_size("sx") == 2 and lax.axis_size("tp") == 4:
+        return paired_plan(*arrays)
+    return gathered_plan(*arrays)
+
+
 def solution(mesh):
     placed = (
         P(("sy", "sx"), None),

time: 444 us -> 144 us (0.32)
  waiting for transfers between devices: 324 us -> 54.3 us
  local copies, waits for them, and re-layouts: 35 us -> 10.9 us
  matrix products: 41.4 us -> 19.7 us
  Pallas kernels: 0 us -> 16 us
  between operations: 13.3 us -> 1.19 us
  starting transfers between devices: 14.2 us -> 22.9 us
    all_gather x4 -> x0, waiting for transfers between devices: 269 us -> none  [the longest x1 120 us: shards(): lax.all_gather(w_mlp_in, 'sx', axis=0, tiled=True)]
    ppermute x4 -> x19, waiting for transfers between devices: 23.5 us -> 54.3 us  [the longest x14 37 us: swap(): return lax.ppermute(cells, axis, [(i, i ^ bit) for i in range(count)])]
    reduce_scatter x1 -> x0, waiting for transfers between devices: 30.3 us -> none  [shards(): lax.psum_scatter(product_term.astype(jnp.bfloat16), 'tp', scatter_dimensi...]
    pallas_call x0 -> x16, Pallas kernels: none -> 16 us  [the longest x3 15.4 us: call(): pl.pallas_call(kernel, grid=(grid,), in_specs=[spec(b, i) for _, b, i in...]
    dot_general x4 -> x13, matrix products: 34.1 us -> 19.7 us  [dot(): return jnp.dot(left, right, preferred_element_type=jnp.float32)]
    slice x8 -> x1, local copies, waits for them, and re-layouts: 10 us -> 0.01 us  [modulate(): cells = (cells.astype(F32) - pair[:, :1]) * pair[:, 1:]]
    ppermute x4 -> x19, starting transfers between devices: 14.1 us -> 22.9 us  [the longest x14 10.8 us: swap(): return lax.ppermute(cells, axis, [(i, i ^ bit) for i in range(count)])]
    sub x1 -> x0, matrix products: 7.28 us -> none  [shards(): numerators = jnp.exp(scores - row_max)]
  transfers between devices with their start and end apart: 9 -> 19, of which waited for: 8 -> 13; matrix products, arithmetic and copies ran while one was open for 17% -> 25% of each run, Pallas kernels for 0% -> 11%
where the time goes in v2:
time: 144 us
  waiting for transfers between devices  54.3 us (38%)
  starting transfers between devices  22.9 us (16%)
  matrix products  19.7 us (14%)
  other arithmetic  18.6 us (13%)
  Pallas kernels  16 us (11%)
  local copies, waits for them, and re-layouts  10.9 us (8%)
    ppermute x14, waiting for transfers between devices, swap(): return lax.ppermute(cells, axis, [(i, i ^ bit) for i in range(count)])  37 us
    dot_general x13, matrix products, dot(): return jnp.dot(left, right, preferred_element_type=jnp.float32)  19.7 us
    pallas_call x3, Pallas kernels, call(): pl.pallas_call(kernel, grid=(grid,), in_specs=[spec(b, i) for _, b, i in...  15.4 us
    ppermute x2, waiting for transfers between devices, shift(): lax.ppermute(cells, axis, [(i, i + step) for i in range(count) if 0 <= i...  11.2 us
    ppermute x14, starting transfers between devices, swap(): return lax.ppermute(cells, axis, [(i, i ^ bit) for i in range(count)])  10.8 us
    unnamed x80, local copies, waits for them, and re-layouts  7.57 us
    ppermute x2, waiting for transfers between devices, paired_plan(): to_home = lambda cells: lax.ppermute(cells, ('sx', 'tp'), homes)  6.02 us
    ppermute x2, starting transfers between devices, shift(): lax.ppermute(cells, axis, [(i, i + step) for i in range(count) if 0 <= i...  4.97 us
  transfers between devices with their start and end apart: 19, of which 13 were waited for; matrix products, arithmetic and copies ran while one was open for 25% of the time, Pallas kernels for 11%

profile of v2, /device:TPU:0, one launch (start us, length us, event | category | flops | bytes accessed | tf_op | source)
XLA Modules:
  0.0 143.5 jit_solution(15809598518429276100)
XLA Ops:
  0.0 2.0 %constant_dynamic-slice_fusion = bf16[400,768]{1,0:T(8,128)(2,1)} fusion(bf16[400,3072]{1,0:T(8,128)(2,1)} %param.15, s32[]{:T(128)S(6)} %select_n.114), kind=kLoop, calls=%fused_computation.93 | loop fusion | bytes 1228804 | tf_op jit(solution)/shard_map/dynamic_slice | solution.py:314
  2.0 3.0 %collective-permute-start = (bf16[400,768]{1,0:T(8,128)(2,1)}, bf16[400,768]{1,0:T(8,128)(2,1)S(1)}, u32[]{:S(2)}, u32[]{:S(2)}) collective-permute-start(bf16[400,768]{1,0:T(8,128)(2,1)} %constant_dynamic-slice_fusion), channel_id=1, source_target_pairs={{0,4},{4,0},{1,5},{5,1},{2,6},{6,2},{3,7},{7,3},{8,12},{12,8},{9,1... | collective-permute-start | bytes 1843208 | tf_op jit(solution)/shard_map/ppermute | solution.py:107
  5.0 2.1 %convert_reduce_fusion = f32[400]{0:T(512)S(1)} fusion(bf16[400,3072]{1,0:T(8,128)(2,1)} %param.15), kind=kLoop, calls=%fused_computation.1 | loop fusion | flops 2457200 | bytes 2459200 | tf_op jit(solution)/shard_map/reduce_sum | solution.py:317
  7.3 2.6 %fusion.1 = f32[400]{0:T(512)S(1)} fusion(bf16[400,3072]{1,0:T(8,128)(2,1)} %param.15, f32[400]{0:T(512)S(1)} %broadcast_multiply_fusion), kind=kLoop, calls=%fused_computation.3 | loop fusion | flops 4914800 | bytes 2460800 | tf_op jit(solution)/shard_map/reduce_sum | solution.py:319
  10.0 0.5 add_convert_fusion.1.refs_0_
  10.5 0.5 convolution_convert_fusion
  11.1 0.5 convolution_convert_fusion.4
  11.6 0.5 convolution_convert_fusion.5
  12.1 0.8 pad_maximum_fusion.1.refs_1_
  12.9 3.9 %fusion.66 = (bf16[400,1536]{1,0:T(8,128)(2,1)}, f32[400,1536]{1,0:T(8,128)}) fusion(bf16[400,1536]{1,0:T(8,128)(2,1)S(1)} %shard_map.145.refs_0_, bf16[1536,1536]{1,0:T(8,128)(2,1)S(1)} %bitcast.33), kind=kOutput, calls=%fused_computation.108 | convolution fusion | flops 1888051200 | bytes 9633792 | tf_op jit(solution)/shard_map/dot_general | solution.py:118
  16.8 2.3 %collective-permute-done.refs_0_ = bf16[400,768]{1,0:T(8,128)(2,1)S(1)} collective-permute-done((bf16[400,768]{1,0:T(8,128)(2,1)}, bf16[400,768]{1,0:T(8,128)(2,1)S(1)}, u32[]{:S(2)}, u32[]{:S(2)}) %collective-permute-start) | collective-permute-done | bytes 614432 | tf_op jit(solution)/shard_map/ppermute | solution.py:107
  19.1 1.8 %collective-permute-start.2 = (f32[400,2]{0,1:T(2,128)S(1)}, f32[400,2]{0,1:T(2,128)S(1)}, u32[]{:S(2)}, u32[]{:S(2)}) collective-permute-start(f32[400,2]{0,1:T(2,128)S(1)} %pad_maximum_fusion.2), channel_id=1, source_target_pairs={{0,4},{4,0},{1,5},{5,1},{2,6},{6,2},{3,7},{7,3},{8,12},{12,8},{9,1... | collective-permute-start | bytes 9608 | tf_op jit(solution)/shard_map/ppermute | solution.py:107
  21.2 1.6 %collective-permute-done.2 = f32[400,2]{0,1:T(2,128)S(1)} collective-permute-done((f32[400,2]{0,1:T(2,128)S(1)}, f32[400,2]{0,1:T(2,128)S(1)}, u32[]{:S(2)}, u32[]{:S(2)}) %collective-permute-start.2) | collective-permute-done | bytes 3232 | tf_op jit(solution)/shard_map/ppermute | solution.py:107
  22.8 1.3 broadcast_select_fusion.1
  24.1 0.5 add_convert_fusion.refs_1_
  24.6 0.3 copy-done.20
  25.0 0.8 convolution_convert_fusion.1
  25.8 0.8 convolution_convert_fusion.2
  26.6 0.8 convolution_convert_fusion.3
  27.5 1.8 %collective-permute-start.4 = (bf16[400,1152]{1,0:T(8,128)(2,1)S(1)}, bf16[400,1152]{1,0:T(8,128)(2,1)S(1)}, u32[]{:S(2)}, u32[]{:S(2)}) collective-permute-start(bf16[400,1152]{1,0:T(8,128)(2,1)S(1)} %pad_maximum_fusion.refs_7_.refs_1_), channel_id=1, source_target_pairs={{0,4},{4,0},{1,5},{5,1},{2,6},{6,2},{3,7},{7,3},{8,12},{12,8},{9,1... | collective-permute-start | bytes 2764808 | tf_op jit(solution)/shard_map/ppermute | solution.py:107
  29.7 0.4 slice_bitcast_fusion.1
  30.6 1.4 collective-permute-done.3.refs_8_.refs_9_
  32.0 7.2 %shard_map.147 = (f32[400,1152]{1,0:T(8,128)S(1)}, f32[224,768]{1,0:T(8,128)S(1)}, f32[400,1536]{1,0:T(8,128)S(1)}, bf16[208,1536]{1,0:T(8,128)(2,1)S(1)}, bf16[192,1536]{1,0:T(8,128)(2,1)S(1)}) custom-call(bf16[400,1536]{1,0:T(8,128)(2,1)S(1)} %shard_map.145.refs_0_, bf16[400,1536]{1,0:T(8,128)(2,1)S(1)} %add_convert_fusion.refs_1_, ...), custom_call_target="tpu_custom_call" | custom-call | flops 3831496704 | bytes 16932864 | tf_op jit(solution)/shard_map/pallas_call | solution.py:140
  39.2 12.5 %collective-permute-done.4.refs_3_.refs_4_.refs_5_ = bf16[400,1152]{1,0:T(8,128)(2,1)S(1)} collective-permute-done((bf16[400,1152]{1,0:T(8,128)(2,1)S(1)}, bf16[400,1152]{1,0:T(8,128)(2,1)S(1)}, u32[]{:S(2)}, u32[]{:S(2)}) %collective-permute-start.4) | collective-permute-done | bytes 921632 | tf_op jit(solution)/shard_map/ppermute | solution.py:107
  51.8 2.5 %shard_map.148 = (bf16[400,384]{1,0:T(8,128)(2,1)S(1)}, bf16[400,768]{1,0:T(8,128)(2,1)S(1)}, bf16[224,768]{1,0:T(8,128)(2,1)S(1)}, bf16[320,768]{1,0:T(8,128)(2,1)}, bf16[320,768]{1,0:T(8,128)(2,1)}) custom-call(f32[400,1152]{1,0:T(8,128)S(1)} %get-tuple-element.16.refs_0_.refs_1_.refs_2_, f32[400,1152]{1,0:T(8,128)S(1)} %get-tuple-element.16.refs_0_.refs_1_.refs_2_, ...), custom_call_target="tpu_custom_call" | custom-call | flops 1000 | bytes 1000 | tf_op jit(solution)/shard_map/pallas_call | solution.py:140
  54.2 0.7 copy-done.11
  55.0 0.7 copy-done.13
  55.7 3.5 %collective-permute-start.5 = (bf16[320,768]{1,0:T(8,128)(2,1)}, bf16[320,768]{1,0:T(8,128)(2,1)S(1)}, u32[]{:S(2)}, u32[]{:S(2)}) collective-permute-start(bf16[320,768]{1,0:T(8,128)(2,1)} %get-tuple-element.22), channel_id=1, source_target_pairs={{0,8},{8,16},{16,24},{1,9},{9,17},{17,25},{2,10},{10,18},{18,26},{... | collective-permute-start | bytes 1474568 | tf_op jit(solution)/shard_map/ppermute | solution.py:112
  59.2 1.5 %collective-permute-start.6 = (bf16[320,768]{1,0:T(8,128)(2,1)}, bf16[320,768]{1,0:T(8,128)(2,1)}, u32[]{:S(2)}, u32[]{:S(2)}) collective-permute-start(bf16[320,768]{1,0:T(8,128)(2,1)} %get-tuple-element.23), channel_id=1, source_target_pairs={{8,0},{16,8},{24,16},{9,1},{17,9},{25,17},{10,2},{18,10},{26,18},{... | collective-permute-start | bytes 1474568 | tf_op jit(solution)/shard_map/ppermute | solution.py:112
  60.7 1.0 collective-permute-start.8
  61.7 7.1 %collective-permute-done.5.refs_4_ = bf16[320,768]{1,0:T(8,128)(2,1)S(1)} collective-permute-done((bf16[320,768]{1,0:T(8,128)(2,1)}, bf16[320,768]{1,0:T(8,128)(2,1)S(1)}, u32[]{:S(2)}, u32[]{:S(2)}) %collective-permute-start.5) | collective-permute-done | bytes 491552 | tf_op jit(solution)/shard_map/ppermute | solution.py:112
  68.8 4.1 %collective-permute-done.6.refs_5_ = bf16[320,768]{1,0:T(8,128)(2,1)} collective-permute-done((bf16[320,768]{1,0:T(8,128)(2,1)}, bf16[320,768]{1,0:T(8,128)(2,1)}, u32[]{:S(2)}, u32[]{:S(2)}) %collective-permute-start.6) | collective-permute-done | bytes 491552 | tf_op jit(solution)/shard_map/ppermute | solution.py:112
  73.0 1.0 copy-done.12
  73.9 1.0 copy-done.14
  74.9 5.8 %shard_map.149.refs_1_ = bf16[400,384]{1,0:T(8,128)(2,1)S(1)} custom-call(bf16[400,384]{1,0:T(8,128)(2,1)S(1)} %copy-done.14, f32[1,1280]{1,0:T(1,128)S(1)} %broadcast_in_dim.32.refs_1_, bf16[400,768]{1,0:T(8,128)(2,1)S(1)} %get-tuple-element.20.refs_2_, bf16[224,768]{1,0:T(8,128)(2,1)S(1)} %copy-done.12, ...), custom_call_target="tpu_custom_call" | custom-call | flops 1000 | bytes 1000 | tf_op jit(solution)/shard_map/pallas_call | solution.py:140
  81.0 5.2 %fusion.18.refs_1_.refs_0_ = f32[400,1536]{1,0:T(8,128)S(1)} fusion(bf16[1536,1536]{1,0:T(8,128)(2,1)} %param.24, f32[400,1536]{1,0:T(8,128)S(1)} %shard_map.150, bf16[400,1536]{1,0:T(8,128)(2,1)} %collective-permute-done.7), kind=kOutput, calls=%fused_computation.30 | convolution fusion | flops 1894195200 | bytes 10862592 | tf_op jit(solution)/shard_map/dot_general | solution.py:118
  86.2 1.9 %copy-done.1 = f32[400,1536]{1,0:T(8,128)S(1)} copy-done((f32[400,1536]{1,0:T(8,128)S(1)}, f32[400,1536]{1,0:T(8,128)}, u32[]{:S(2)}) %copy-start.1) | copy-done | bytes 2457624
  88.1 0.5 fusion.47
  88.6 3.2 %collective-permute-done.8 = bf16[208,1536]{1,0:T(8,128)(2,1)S(1)} collective-permute-done((bf16[208,1536]{1,0:T(8,128)(2,1)S(1)}, bf16[208,1536]{1,0:T(8,128)(2,1)S(1)}, u32[]{:S(2)}, u32[]{:S(2)}) %collective-permute-start.8) | collective-permute-done | bytes 639008 | tf_op jit(solution)/shard_map/ppermute | solution.py:107
  91.8 1.3 convolution_add_fusion.1.refs_1_
  93.2 4.5 %collective-permute-done.9 = bf16[400,384]{1,0:T(8,128)(2,1)S(1)} collective-permute-done((bf16[400,384]{1,0:T(8,128)(2,1)S(1)}, bf16[400,384]{1,0:T(8,128)(2,1)S(1)}, u32[]{:S(2)}, u32[]{:S(2)}) %collective-permute-start.9) | collective-permute-done | bytes 307232 | tf_op jit(solution)/shard_map/ppermute | solution.py:107
  97.7 0.8 convolution_add_fusion
  98.6 1.3 copy-done.16
  99.9 0.4 collective-permute-start.14
  100.7 1.4 collective-permute-done.10
  102.1 2.0 %convert_add_fusion.refs_1_ = f32[400,768]{1,0:T(8,128)S(1)} fusion(bf16[400,768]{1,0:T(8,128)(2,1)} %collective-permute-done.10, f32[400,1536]{1,0:T(8,128)} %copy-done.16, pred[]{:T(512)S(6)} %eq.10), kind=kLoop, calls=%fused_computation.35 | loop fusion | flops 921600 | bytes 4300801 | tf_op jit(solution)/shard_map/add | solution.py:398
  104.2 1.6 %collective-permute-start.13 = (bf16[200,768]{1,0:T(8,128)(2,1)S(1)}, bf16[200,768]{1,0:T(8,128)(2,1)S(1)}, u32[]{:S(2)}, u32[]{:S(2)}) collective-permute-start(bf16[200,768]{1,0:T(8,128)(2,1)S(1)} %dynamic-slice_convert_fusion), channel_id=1, source_target_pairs={{0,2},{1,3},{2,0},{3,1},{4,6},{5,7},{6,4},{7,5},{8,10},{9,11},{10,... | collective-permute-start | bytes 921608 | tf_op jit(solution)/shard_map/ppermute | solution.py:107
  105.8 0.5 fusion.49
  106.2 0.8 fusion.51
  107.1 1.4 collective-permute-start.12
  108.5 5.9 %collective-permute-done.13 = bf16[200,768]{1,0:T(8,128)(2,1)S(1)} collective-permute-done((bf16[200,768]{1,0:T(8,128)(2,1)S(1)}, bf16[200,768]{1,0:T(8,128)(2,1)S(1)}, u32[]{:S(2)}, u32[]{:S(2)}) %collective-permute-start.13) | collective-permute-done | bytes 307232 | tf_op jit(solution)/shard_map/ppermute | solution.py:107
  114.5 1.5 %collective-permute-done.14 = bf16[192,1536]{1,0:T(8,128)(2,1)S(1)} collective-permute-done((bf16[192,1536]{1,0:T(8,128)(2,1)}, bf16[192,1536]{1,0:T(8,128)(2,1)S(1)}, u32[]{:S(2)}, u32[]{:S(2)}) %collective-permute-start.14) | collective-permute-done | bytes 589856 | tf_op jit(solution)/shard_map/ppermute | solution.py:107
  116.1 3.6 %convolution_add_fusion.2 = f32[192,1536]{1,0:T(8,128)S(1)} fusion(f32[192,1536]{1,0:T(8,128)S(1)} %fusion.49, bf16[1536,1536]{1,0:T(8,128)(2,1)} %param.24, f32[400,1536]{1,0:T(8,128)S(1)} %shard_map.157, bf16[192,1536]{1,0:T(8,128)(2,1)S(1)} %collective-permute-done.14), kind=kOutput, calls=%fused_computation.7 | convolution fusion | flops 909508608 | bytes 8847360 | tf_op jit(solution)/shard_map/dot_general | solution.py:118
  119.7 2.7 %collective-permute-done.15.refs_1_.refs_0_ = bf16[200,768]{1,0:T(8,128)(2,1)S(1)} collective-permute-done((bf16[200,768]{1,0:T(8,128)(2,1)S(1)}, bf16[200,768]{1,0:T(8,128)(2,1)S(1)}, u32[]{:S(2)}, u32[]{:S(2)}) %collective-permute-start.15) | collective-permute-done | bytes 307232 | tf_op jit(solution)/shard_map/ppermute | solution.py:107
  122.5 4.3 %collective-permute-start.18 = (bf16[200,768]{1,0:T(8,128)(2,1)S(1)}, bf16[200,768]{1,0:T(8,128)(2,1)}, u32[]{:S(2)}, u32[]{:S(2)}) collective-permute-start(bf16[200,768]{1,0:T(8,128)(2,1)S(1)} %shard_map.160), channel_id=1, source_target_pairs={{0,2},{1,3},{6,4},{7,5},{8,10},{9,11},{14,12},{15,13},{16,18},{17,... | collective-permute-start | bytes 921608 | tf_op jit(solution)/shard_map/ppermute | solution.py:416
  126.8 2.1 %fusion.52 = bf16[192,768]{1,0:T(8,128)(2,1)} fusion(bf16[192,768]{1,0:T(8,128)(2,1)} %collective-permute-done.16, f32[192,1536]{1,0:T(8,128)} %copy-done.17, pred[]{:T(512)S(6)} %eq.10), kind=kLoop, calls=%fused_computation.90 | loop fusion | flops 589824 | bytes 1769473 | tf_op jit(solution)/shard_map/convert_element_type | solution.py:418
  128.9 1.4 collective-permute-start.17
  130.3 1.0 convert_add_fusion.1
  131.3 0.5 shard_map.155
  132.4 0.8 dynamic_slice.29
  133.2 1.0 broadcast_select_fusion.3
  134.2 6.0 %collective-permute-done.17 = bf16[192,768]{1,0:T(8,128)(2,1)S(1)} collective-permute-done((bf16[192,768]{1,0:T(8,128)(2,1)}, bf16[192,768]{1,0:T(8,128)(2,1)S(1)}, u32[]{:S(2)}, u32[]{:S(2)}) %collective-permute-start.17) | collective-permute-done | bytes 294944 | tf_op jit(solution)/shard_map/ppermute | solution.py:415
  140.3 1.1 convert_add_fusion.3
  141.3 2.2 %fusion.22 = bf16[400,768]{1,0:T(8,128)(2,1)} fusion(f32[192,768]{1,0:T(8,128)S(1)} %convert_add_fusion.3, f32[208,768]{1,0:T(8,128)S(1)} %copy-done.21, bf16[200,768]{1,0:T(8,128)(2,1)S(1)} %get-tuple-element.31, bf16[200,768]{1,0:T(8,128)(2,1)S(1)} %get-tuple-element.30, f32[768]{0:T(1024)S(1)} %dynamic_slice.29, bf16[400,3072]{1,0:T(8,128)(2,1)} %param.15, ...), kind=kLoop, calls=%fused_computation.34 | loop fusion | flops 3072000 | bytes 3075077 | tf_op jit(solution)/shard_map/convert_element_type | solution.py:427
  (119 shorter events, 2.5 us)
Async XLA Ops:
  0.0 88.1 %copy-start = (bf16[384,1536]{1,0:T(8,128)(2,1)S(1)}, bf16[384,1536]{1,0:T(8,128)(2,1)}, u32[]{:S(2)}) copy-start(bf16[384,1536]{1,0:T(8,128)(2,1)} %param.23) | copy-start | bytes 3538948
  2.0 5.1 %copy-start.27 = (f32[3072]{0:T(1024)S(1)}, f32[3072]{0:T(1024)}, u32[]{:S(2)}) copy-start(f32[3072]{0:T(1024)} %param.17) | copy-start | bytes 36868
  2.0 5.2 %copy-start.28 = (f32[3072]{0:T(1024)S(1)}, f32[3072]{0:T(1024)}, u32[]{:S(2)}) copy-start(f32[3072]{0:T(1024)} %param.16) | copy-start | bytes 36868
  2.0 17.0 %collective-permute-start = (bf16[400,768]{1,0:T(8,128)(2,1)}, bf16[400,768]{1,0:T(8,128)(2,1)S(1)}, u32[]{:S(2)}, u32[]{:S(2)}) collective-permute-start(bf16[400,768]{1,0:T(8,128)(2,1)} %constant_dynamic-slice_fusion), channel_id=1, source_target_pairs={{0,4},{4,0},{1,5},{5,1},{2,6},{6,2},{3,7},{7,3},{8,12},{12,8},{9,1... | collective-permute-start | bytes 1843208 | tf_op jit(solution)/shard_map/ppermute | solution.py:107
  5.0 5.5 %copy-start.24 = (bf16[224,400]{1,0:T(8,128)(2,1)S(1)}, bf16[224,400]{1,0:T(8,128)(2,1)}, u32[]{:S(2)}) copy-start(bf16[224,400]{1,0:T(8,128)(2,1)} %constant.89.clone) | copy-start | bytes 537604
  7.2 2.8 %copy-start.15 = (bf16[400,3072]{1,0:T(8,128)(2,1)S(1)}, bf16[400,3072]{1,0:T(8,128)(2,1)}, u32[]{:S(2)}) copy-start(bf16[400,3072]{1,0:T(8,128)(2,1)} %param.15) | copy-start | bytes 7372804
  7.3 3.7 %copy-start.19 = (bf16[1536,3,384]{2,0,1:T(8,128)(2,1)S(1)}, bf16[1536,3,384]{2,0,1:T(8,128)(2,1)}, u32[]{:S(2)}) copy-start(bf16[1536,3,384]{2,0,1:T(8,128)(2,1)} %param.19) | copy-start | bytes 10616836
  10.0 2.9 %slice-start = ((s8[4718592]{0:T(1024)(128)(4,1)}), s8[4194304]{0:T(1024)(128)(4,1)S(1)}, s32[]{:S(2)}) async-start(s8[4718592]{0:T(1024)(128)(4,1)} %bitcast.32), calls=%async_computation | async-start | bytes 8388608
  11.1 1.8 %slice-start.1 = ((s8[4718592]{0:T(1024)(128)(4,1)}), s8[524288]{0:T(1024)(128)(4,1)S(1)}, s32[]{:S(2)}) async-start(s8[4718592]{0:T(1024)(128)(4,1)} %bitcast.32), calls=%async_computation.1 | async-start | bytes 1048576
  19.1 3.7 %collective-permute-start.1 = (bf16[400,768]{1,0:T(8,128)(2,1)S(1)}, bf16[400,768]{1,0:T(8,128)(2,1)}, u32[]{:S(2)}, u32[]{:S(2)}) collective-permute-start(bf16[400,768]{1,0:T(8,128)(2,1)S(1)} %shard_map.146), channel_id=1, source_target_pairs={{0,1},{1,0},{2,3},{3,2},{4,5},{5,4},{6,7},{7,6},{8,9},{9,8},{10,11... | collective-permute-start | bytes 1843208 | tf_op jit(solution)/shard_map/ppermute | solution.py:107
  19.1 3.7 %collective-permute-start.2 = (f32[400,2]{0,1:T(2,128)S(1)}, f32[400,2]{0,1:T(2,128)S(1)}, u32[]{:S(2)}, u32[]{:S(2)}) collective-permute-start(f32[400,2]{0,1:T(2,128)S(1)} %pad_maximum_fusion.2), channel_id=1, source_target_pairs={{0,4},{4,0},{1,5},{5,1},{2,6},{6,2},{3,7},{7,3},{8,12},{12,8},{9,1... | collective-permute-start | bytes 9608 | tf_op jit(solution)/shard_map/ppermute | solution.py:107
  20.9 11.1 %collective-permute-start.3 = (bf16[224,768]{1,0:T(8,128)(2,1)}, bf16[224,768]{1,0:T(8,128)(2,1)S(1)}, u32[]{:S(2)}, u32[]{:S(2)}) collective-permute-start(bf16[224,768]{1,0:T(8,128)(2,1)} %pad_maximum_fusion.1.refs_1_), channel_id=1, source_target_pairs={{0,4},{4,0},{1,5},{5,1},{2,6},{6,2},{3,7},{7,3},{8,12},{12,8},{9,1... | collective-permute-start | bytes 1032200 | tf_op jit(solution)/shard_map/ppermute | solution.py:107
  22.8 2.2 %copy-start.20 = (bf16[1536,3,384]{2,0,1:T(8,128)(2,1)S(1)}, bf16[1536,3,384]{2,0,1:T(8,128)(2,1)}, u32[]{:S(2)}) copy-start(bf16[1536,3,384]{2,0,1:T(8,128)(2,1)} %param.19) | copy-start | bytes 10616836
  27.5 24.3 %collective-permute-start.4 = (bf16[400,1152]{1,0:T(8,128)(2,1)S(1)}, bf16[400,1152]{1,0:T(8,128)(2,1)S(1)}, u32[]{:S(2)}, u32[]{:S(2)}) collective-permute-start(bf16[400,1152]{1,0:T(8,128)(2,1)S(1)} %pad_maximum_fusion.refs_7_.refs_1_), channel_id=1, source_target_pairs={{0,4},{4,0},{1,5},{5,1},{2,6},{6,2},{3,7},{7,3},{8,12},{12,8},{9,1... | collective-permute-start | bytes 2764808 | tf_op jit(solution)/shard_map/ppermute | solution.py:107
  29.3 2.7 %slice-start.2 = ((s8[4718592]{0:T(1024)(128)(4,1)}), s8[4194304]{0:T(1024)(128)(4,1)S(1)}, s32[]{:S(2)}) async-start(s8[4718592]{0:T(1024)(128)(4,1)} %bitcast.34), calls=%async_computation.2 | async-start | bytes 8388608
  29.3 0.8 copy-start.32
  29.3 0.8 copy-start.33
  29.3 1.1 copy-start.25
  29.3 1.2 copy-start.26
  29.3 2.7 %slice-start.3 = ((s8[4718592]{0:T(1024)(128)(4,1)}), s8[524288]{0:T(1024)(128)(4,1)S(1)}, s32[]{:S(2)}) async-start(s8[4718592]{0:T(1024)(128)(4,1)} %bitcast.34), calls=%async_computation.3 | async-start | bytes 1048576
  29.4 51.6 %collective-permute-start.7 = (bf16[400,1536]{1,0:T(8,128)(2,1)}, bf16[400,1536]{1,0:T(8,128)(2,1)}, u32[]{:S(2)}, u32[]{:S(2)}) collective-permute-start(bf16[400,1536]{1,0:T(8,128)(2,1)} %shard_map.151), channel_id=1, source_target_pairs={{0,4},{4,0},{1,5},{5,1},{2,6},{6,2},{3,7},{7,3},{8,12},{12,8},{9,1... | collective-permute-start | bytes 3686408 | tf_op jit(solution)/shard_map/ppermute | solution.py:107
  39.2 15.0 %copy-start.6 = (f32[400,1536]{1,0:T(8,128)}, f32[400,1536]{1,0:T(8,128)S(1)}, u32[]{:S(2)}) copy-start(f32[400,1536]{1,0:T(8,128)S(1)} %get-tuple-element.15.refs_0_) | copy-start | bytes 7372804
  39.2 15.0 %copy-start.8 = (bf16[192,1536]{1,0:T(8,128)(2,1)}, bf16[192,1536]{1,0:T(8,128)(2,1)S(1)}, u32[]{:S(2)}) copy-start(bf16[192,1536]{1,0:T(8,128)(2,1)S(1)} %get-tuple-element.24.refs_0_) | copy-start | bytes 1769476
  51.8 8.9 %copy-start.29 = (pred[1280]{0:T(1024)(128)(4,1)S(1)}, pred[1280]{0:T(1024)(128)(4,1)}, u32[]{:S(2)}) copy-start(pred[1280]{0:T(1024)(128)(4,1)} %constant.91.clone) | copy-start | bytes 3844
  51.8 8.9 %copy-start.30 = (pred[1280]{0:T(1024)(128)(4,1)S(1)}, pred[1280]{0:T(1024)(128)(4,1)}, u32[]{:S(2)}) copy-start(pred[1280]{0:T(1024)(128)(4,1)} %constant.92.clone) | copy-start | bytes 3844
  51.8 9.0 %copy-start.31 = (pred[1280]{0:T(1024)(128)(4,1)S(1)}, pred[1280]{0:T(1024)(128)(4,1)}, u32[]{:S(2)}) copy-start(pred[1280]{0:T(1024)(128)(4,1)} %constant.93.clone) | copy-start | bytes 3844
  54.2 0.7 copy-start.11
  55.0 0.7 copy-start.13
  55.7 13.1 %collective-permute-start.5 = (bf16[320,768]{1,0:T(8,128)(2,1)}, bf16[320,768]{1,0:T(8,128)(2,1)S(1)}, u32[]{:S(2)}, u32[]{:S(2)}) collective-permute-start(bf16[320,768]{1,0:T(8,128)(2,1)} %get-tuple-element.22), channel_id=1, source_target_pairs={{0,8},{8,16},{16,24},{1,9},{9,17},{17,25},{2,10},{10,18},{18,26},{... | collective-permute-start | bytes 1474568 | tf_op jit(solution)/shard_map/ppermute | solution.py:112
  59.2 13.8 %collective-permute-start.6 = (bf16[320,768]{1,0:T(8,128)(2,1)}, bf16[320,768]{1,0:T(8,128)(2,1)}, u32[]{:S(2)}, u32[]{:S(2)}) collective-permute-start(bf16[320,768]{1,0:T(8,128)(2,1)} %get-tuple-element.23), channel_id=1, source_target_pairs={{8,0},{16,8},{24,16},{9,1},{17,9},{25,17},{10,2},{18,10},{26,18},{... | collective-permute-start | bytes 1474568 | tf_op jit(solution)/shard_map/ppermute | solution.py:112
  60.7 31.0 %collective-permute-start.8 = (bf16[208,1536]{1,0:T(8,128)(2,1)S(1)}, bf16[208,1536]{1,0:T(8,128)(2,1)S(1)}, u32[]{:S(2)}, u32[]{:S(2)}) collective-permute-start(bf16[208,1536]{1,0:T(8,128)(2,1)S(1)} %get-tuple-element.18.refs_12_), channel_id=1, source_target_pairs={{0,4},{4,0},{1,5},{5,1},{2,6},{6,2},{3,7},{7,3},{8,12},{12,8},{9,1... | collective-permute-start | bytes 1916936 | tf_op jit(solution)/shard_map/ppermute | solution.py:107
  73.0 1.0 copy-start.12
  73.9 1.0 copy-start.14
  74.9 6.0 %copy-start.7 = (f32[400,1536]{1,0:T(8,128)S(1)}, f32[400,1536]{1,0:T(8,128)}, u32[]{:S(2)}) copy-start(f32[400,1536]{1,0:T(8,128)} %copy-done.6) | copy-start | bytes 7372804
  80.7 16.9 %collective-permute-start.9 = (bf16[400,384]{1,0:T(8,128)(2,1)S(1)}, bf16[400,384]{1,0:T(8,128)(2,1)S(1)}, u32[]{:S(2)}, u32[]{:S(2)}) collective-permute-start(bf16[400,384]{1,0:T(8,128)(2,1)S(1)} %shard_map.149.refs_1_), channel_id=1, source_target_pairs={{0,4},{4,0},{1,5},{5,1},{2,6},{6,2},{3,7},{7,3},{8,12},{12,8},{9,1... | collective-permute-start | bytes 921608 | tf_op jit(solution)/shard_map/ppermute | solution.py:107
  81.0 5.2 %copy-start.9 = (bf16[192,1536]{1,0:T(8,128)(2,1)S(1)}, bf16[192,1536]{1,0:T(8,128)(2,1)}, u32[]{:S(2)}) copy-start(bf16[192,1536]{1,0:T(8,128)(2,1)} %copy-done.8) | copy-start | bytes 1769476
  86.2 1.9 %copy-start.1 = (f32[400,1536]{1,0:T(8,128)S(1)}, f32[400,1536]{1,0:T(8,128)}, u32[]{:S(2)}) copy-start(f32[400,1536]{1,0:T(8,128)} %get-tuple-element.35.refs_0_) | copy-start | bytes 7372804
  86.2 5.6 %slice-start.4 = ((s8[4718592]{0:T(1024)(128)(4,1)}), s8[4194304]{0:T(1024)(128)(4,1)S(1)}, s32[]{:S(2)}) async-start(s8[4718592]{0:T(1024)(128)(4,1)} %bitcast.40), calls=%async_computation.4 | async-start | bytes 8388608
  86.2 1.9 %copy-start.10 = (bf16[192,1536]{1,0:T(8,128)(2,1)}, bf16[192,1536]{1,0:T(8,128)(2,1)S(1)}, u32[]{:S(2)}) copy-start(bf16[192,1536]{1,0:T(8,128)(2,1)S(1)} %shard_map.158) | copy-start | bytes 1769476
  88.1 3.7 %slice-start.5 = ((s8[4718592]{0:T(1024)(128)(4,1)}), s8[524288]{0:T(1024)(128)(4,1)S(1)}, s32[]{:S(2)}) async-start(s8[4718592]{0:T(1024)(128)(4,1)} %bitcast.40), calls=%async_computation.5 | async-start | bytes 1048576
  88.1 3.7 %copy-start.2 = (f32[400,1536]{1,0:T(8,128)}, f32[400,1536]{1,0:T(8,128)S(1)}, u32[]{:S(2)}) copy-start(f32[400,1536]{1,0:T(8,128)S(1)} %shard_map.152.refs_0_) | copy-start | bytes 7372804
  98.5 1.5 %copy-start.16 = (f32[400,1536]{1,0:T(8,128)}, f32[400,1536]{1,0:T(8,128)S(1)}, u32[]{:S(2)}) copy-start(f32[400,1536]{1,0:T(8,128)S(1)} %convolution_add_fusion) | copy-start | bytes 7372804
  99.9 2.2 %collective-permute-start.10 = (bf16[400,768]{1,0:T(8,128)(2,1)S(1)}, bf16[400,768]{1,0:T(8,128)(2,1)}, u32[]{:S(2)}, u32[]{:S(2)}) collective-permute-start(bf16[400,768]{1,0:T(8,128)(2,1)S(1)} %shard_map.154), channel_id=1, source_target_pairs={{0,1},{1,0},{2,3},{3,2},{4,5},{5,4},{6,7},{7,6},{8,9},{9,8},{10,11... | collective-permute-start | bytes 1843208 | tf_op jit(solution)/shard_map/ppermute | solution.py:107
  99.9 16.1 %collective-permute-start.14 = (bf16[192,1536]{1,0:T(8,128)(2,1)}, bf16[192,1536]{1,0:T(8,128)(2,1)S(1)}, u32[]{:S(2)}, u32[]{:S(2)}) collective-permute-start(bf16[192,1536]{1,0:T(8,128)(2,1)} %copy-done.10), channel_id=1, source_target_pairs={{0,4},{4,0},{1,5},{5,1},{2,6},{6,2},{3,7},{7,3},{8,12},{12,8},{9,1... | collective-permute-start | bytes 1769480 | tf_op jit(solution)/shard_map/ppermute | solution.py:107
  100.4 5.8 %collective-permute-start.11 = (bf16[208,768]{1,0:T(8,128)(2,1)S(1)}, bf16[208,768]{1,0:T(8,128)(2,1)S(1)}, u32[]{:S(2)}, u32[]{:S(2)}) collective-permute-start(bf16[208,768]{1,0:T(8,128)(2,1)S(1)} %shard_map.156), channel_id=1, source_target_pairs={{0,1},{1,0},{2,3},{3,2},{4,5},{5,4},{6,7},{7,6},{8,9},{9,8},{10,11... | collective-permute-start | bytes 958472 | tf_op jit(solution)/shard_map/ppermute | solution.py:107
  104.1 10.2 %copy-start.4 = (f32[400,768]{1,0:T(8,128)}, f32[400,768]{1,0:T(8,128)S(1)}, u32[]{:S(2)}) copy-start(f32[400,768]{1,0:T(8,128)S(1)} %convert_add_fusion.refs_1_) | copy-start | bytes 3686404
  104.2 10.2 %collective-permute-start.13 = (bf16[200,768]{1,0:T(8,128)(2,1)S(1)}, bf16[200,768]{1,0:T(8,128)(2,1)S(1)}, u32[]{:S(2)}, u32[]{:S(2)}) collective-permute-start(bf16[200,768]{1,0:T(8,128)(2,1)S(1)} %dynamic-slice_convert_fusion), channel_id=1, source_target_pairs={{0,2},{1,3},{2,0},{3,1},{4,6},{5,7},{6,4},{7,5},{8,10},{9,11},{10,... | collective-permute-start | bytes 921608 | tf_op jit(solution)/shard_map/ppermute | solution.py:107
  106.2 8.2 %copy-start.3 = (f32[400,1536]{1,0:T(8,128)S(1)}, f32[400,1536]{1,0:T(8,128)}, u32[]{:S(2)}) copy-start(f32[400,1536]{1,0:T(8,128)} %copy-done.2) | copy-start | bytes 7372804
  106.2 2.3 %copy-start.22 = (bf16[208,768]{1,0:T(8,128)(2,1)}, bf16[208,768]{1,0:T(8,128)(2,1)S(1)}, u32[]{:S(2)}) copy-start(bf16[208,768]{1,0:T(8,128)(2,1)S(1)} %collective-permute-done.11) | copy-start | bytes 958468
  107.1 15.4 %collective-permute-start.12 = (bf16[208,768]{1,0:T(8,128)(2,1)}, bf16[208,768]{1,0:T(8,128)(2,1)S(1)}, u32[]{:S(2)}, u32[]{:S(2)}) collective-permute-start(bf16[208,768]{1,0:T(8,128)(2,1)} %fusion.51), channel_id=1, source_target_pairs={{2,0},{3,1},{4,6},{5,7},{10,8},{11,9},{12,14},{13,15},{18,16},{19,... | collective-permute-start | bytes 958472 | tf_op jit(solution)/shard_map/ppermute | solution.py:415
  114.5 8.0 %collective-permute-start.15 = (bf16[200,768]{1,0:T(8,128)(2,1)S(1)}, bf16[200,768]{1,0:T(8,128)(2,1)S(1)}, u32[]{:S(2)}, u32[]{:S(2)}) collective-permute-start(bf16[200,768]{1,0:T(8,128)(2,1)S(1)} %add_convert_fusion.2.refs_2_), channel_id=1, source_target_pairs={{0,4},{4,0},{1,5},{5,1},{2,6},{6,2},{3,7},{7,3},{8,12},{12,8},{9,1... | collective-permute-start | bytes 921608 | tf_op jit(solution)/shard_map/ppermute | solution.py:107
  119.7 2.8 %copy-start.17 = (f32[192,1536]{1,0:T(8,128)}, f32[192,1536]{1,0:T(8,128)S(1)}, u32[]{:S(2)}) copy-start(f32[192,1536]{1,0:T(8,128)S(1)} %convolution_add_fusion.2) | copy-start | bytes 3538948
  122.5 4.3 %collective-permute-start.16 = (bf16[192,768]{1,0:T(8,128)(2,1)S(1)}, bf16[192,768]{1,0:T(8,128)(2,1)}, u32[]{:S(2)}, u32[]{:S(2)}) collective-permute-start(bf16[192,768]{1,0:T(8,128)(2,1)S(1)} %shard_map.159), channel_id=1, source_target_pairs={{0,1},{1,0},{2,3},{3,2},{4,5},{5,4},{6,7},{7,6},{8,9},{9,8},{10,11... | collective-permute-start | bytes 884744 | tf_op jit(solution)/shard_map/ppermute | solution.py:107
  122.5 7.9 %copy-start.23 = (bf16[208,768]{1,0:T(8,128)(2,1)S(1)}, bf16[208,768]{1,0:T(8,128)(2,1)}, u32[]{:S(2)}) copy-start(bf16[208,768]{1,0:T(8,128)(2,1)} %copy-done.22) | copy-start | bytes 958468
  122.5 10.7 %collective-permute-start.18 = (bf16[200,768]{1,0:T(8,128)(2,1)S(1)}, bf16[200,768]{1,0:T(8,128)(2,1)}, u32[]{:S(2)}, u32[]{:S(2)}) collective-permute-start(bf16[200,768]{1,0:T(8,128)(2,1)S(1)} %shard_map.160), channel_id=1, source_target_pairs={{0,2},{1,3},{6,4},{7,5},{8,10},{9,11},{14,12},{15,13},{16,18},{17,... | collective-permute-start | bytes 921608 | tf_op jit(solution)/shard_map/ppermute | solution.py:416
  128.9 2.4 %copy-start.5 = (f32[400,768]{1,0:T(8,128)S(1)}, f32[400,768]{1,0:T(8,128)}, u32[]{:S(2)}) copy-start(f32[400,768]{1,0:T(8,128)} %copy-done.4) | copy-start | bytes 3686404
  128.9 11.3 %collective-permute-start.17 = (bf16[192,768]{1,0:T(8,128)(2,1)}, bf16[192,768]{1,0:T(8,128)(2,1)S(1)}, u32[]{:S(2)}, u32[]{:S(2)}) collective-permute-start(bf16[192,768]{1,0:T(8,128)(2,1)} %fusion.52), channel_id=1, source_target_pairs={{2,0},{3,1},{4,6},{5,7},{10,8},{11,9},{12,14},{13,15},{18,16},{19,... | collective-permute-start | bytes 884744 | tf_op jit(solution)/shard_map/ppermute | solution.py:415
  131.3 8.9 %copy-start.18 = (f32[192,1536]{1,0:T(8,128)S(1)}, f32[192,1536]{1,0:T(8,128)}, u32[]{:S(2)}) copy-start(f32[192,1536]{1,0:T(8,128)} %copy-done.17) | copy-start | bytes 3538948
  134.2 7.1 %copy-start.21 = (f32[208,768]{1,0:T(8,128)S(1)}, f32[208,768]{1,0:T(8,128)}, u32[]{:S(2)}) copy-start(f32[208,768]{1,0:T(8,128)} %convert_add_fusion.1) | copy-start | bytes 1916932

commit v3 on v2

--- a/solution.py
+++ b/solution.py
@@ -120,6 +120,7 @@
 
 BF16, F32 = jnp.bfloat16, jnp.float32
 LANES = 128
+EARLY = 20_000_000
 
 
 def width_of(total, most):
@@ -193,7 +194,7 @@
     border = pick.shape[0]
     block = width_of(hidden, 384)
 
-    def body(own_ref, other_ref, pick_ref, wq_ref, wk_ref, wv_ref, w_ref, qkv_ref, border_ref, sums_ref, a_ref, b_ref):
+    def body(own_ref, other_ref, pick_ref, wq_ref, wk_ref, wv_ref, w_ref, qkv_ref, border_ref, a_ref, b_ref):
         @pl.when(pl.program_id(0) == 0)
         def _():
             taken = dot(pick_ref[...], other_ref[...]).astype(BF16)
@@ -203,7 +204,6 @@
                 border_ref[:, i * width : (i + 1) * width] = dot(taken, ref[...])
 
         sums = dot(other_ref[...], w_ref[...])
-        sums_ref[...] = sums
         a_ref[...] = sums[:cut].astype(BF16)
         b_ref[...] = sums[cut:].astype(BF16)
 
@@ -217,14 +217,13 @@
         [
             ((rows, 3 * width), F32, (rows, 3 * width), whole),
             ((border, 2 * width), F32, (border, 2 * width), whole),
-            ((rows, hidden), F32, (rows, block), column),
             ((cut, hidden), BF16, (cut, block), column),
             ((rows - cut, hidden), BF16, (rows - cut, block), column),
         ],
         after=after, vmem=28,
         cost=(
             2 * depth * (rows * 3 * width + border * 2 * width + rows * hidden),
-            2 * depth * (2 * rows + 3 * width + hidden) + 4 * (3 * rows + 2 * border) * width + 6 * rows * hidden,
+            2 * depth * (2 * rows + 3 * width + hidden) + 4 * (3 * rows + 2 * border) * width + 2 * rows * hidden,
         ),
     )
 
@@ -319,17 +318,13 @@
     scaling = lax.rsqrt(jnp.mean(centered * centered, axis=-1, keepdims=True) + 1e-06)
     stats = jnp.concatenate([mean, scaling], axis=1)
     other_stats = swap(stats, "sx", 1)
-    first = side * half_width
+    first = hold(side[None], sent)[0] * half_width
     gain_part = 1.0 + lax.dynamic_slice_in_dim(mod_scale, first, half_width, 0)
     shift_part = lax.dynamic_slice_in_dim(mod_shift, first, half_width, 0)
 
     def modulate(cells, pair):
         cells = (cells.astype(F32) - pair[:, :1]) * pair[:, 1:]
         return (cells * gain_part + shift_part).astype(BF16)
-
-    def projected(cells, weights):
-        sums = dot(cells, weights)
-        return sums, sums.astype(BF16)
 
     w_queries, w_keys, w_values = [w_qkv[:, group] for group in range(3)]
 
@@ -344,15 +339,16 @@
     own_border = border_of(own_pick, own).astype(BF16)
     got_border = swap(own_border, "sx", 1)
     own = hold(own, own_border)
-    own_sums, own_sent = projected(own, w_mlp_in)
-    piece = hold(piece, own_sent)
+    own_hidden = dot(own, w_mlp_in).astype(BF16)
+    piece = hold(piece, own_hidden)
     near = swap(piece, "tp", 1)
     other = modulate(jnp.concatenate(in_order(core, piece, near), axis=1), other_stats)
     other_qkv = heads_of(other).astype(BF16)
     got_qkv = swap(other_qkv, "sx", 1)
-    got_own = swap(hold(own_sent, other_qkv), "sx", 1)
-    cut = (tok_rows // 2 + 15) // 16 * 16
-    own_qkv, other_border, other_sums, other_a, other_b = rest_of_first(
+    own_hidden = hold(own_hidden, other_qkv)
+    got_own = swap(own_hidden, "sx", 1)
+    cut = tok_rows // 2
+    own_qkv, other_border, other_a, other_b = rest_of_first(
         own, other, other_pick, (w_queries, w_keys, w_values), w_mlp_in, cut, [other_qkv, got_border]
     )
 
@@ -362,8 +358,15 @@
     above = shift(lower, "sy", 1)
     below = shift(upper, "sy", -1)
 
-    def gelu_dot(sums, got, rows):
-        return dot(jax.nn.gelu(sums + got.astype(F32), approximate=True).astype(BF16), rows)
+    sent_mlp, kept_mlp, sent_attn, kept_attn = (
+        lax.dynamic_slice_in_dim(w, first * block, block, 1)
+        for w in (w_mlp_out, w_attn_out)
+        for first in (1 - core, core)
+    )
+
+    def activate(mine, got, *earlier):
+        got = hold(got, *earlier)
+        return hold(jax.nn.gelu(mine.astype(F32) + got.astype(F32), approximate=True).astype(BF16))
 
     row = lax.axis_index("sy")
     extra = tok_rows // 2
@@ -384,47 +387,56 @@
     attended = attend(queries, [own_kv, border_kv, above, below], bias, heads)
     got_attended = swap(attended, "sx", 1)
     got_other_a = swap(other_a, "sx", 1)
-    other_sums = hold(other_sums, attended)
-    other_branch = gelu_dot(other_sums, got_own, w_mlp_out)
+    other_active = activate(jnp.concatenate([other_a, other_b], axis=0), got_own, attended)
+    other_sent, other_kept = dot(other_active, sent_mlp), dot(other_active, kept_mlp)
     got_other_a = swap(other_a, "sx", 1)
-    got_other_b = swap(hold(other_b, other_branch), "sx", 1)
-
-    def split(cells):
-        left, right = cells[:, :block], cells[:, block:]
-        return jnp.where(core == 0, right, left).astype(BF16), jnp.where(core == 0, left, right)
-
-    def core_sum(cells, *earlier):
-        send, keep = split(cells)
-        return keep + swap(hold(send, *earlier), "tp", 1).astype(F32)
-
-    own_sums = hold(own_sums, other_branch)
-    own_part = gelu_dot(own_sums[:cut], got_other_a, w_mlp_out) + dot(attended[:cut], w_attn_out)
-    other_branch = hold(other_branch, own_part)
-    other_sum = core_sum(other_branch + dot(got_attended, w_attn_out))
-    half_rows = tok_rows // 2
-    send = lax.dynamic_slice_in_dim(other_sum, (1 - far) * half_rows, half_rows, 0).astype(BF16)
-    keep = lax.dynamic_slice_in_dim(other_sum, far * half_rows, half_rows, 0)
-    crossing = (keep + swap(send, "tp", 2).astype(F32)).astype(BF16)
+    got_other_b = swap(hold(other_b, other_sent), "sx", 1)
+
+    def own_part(begin, end, got, *earlier):
+        active, heads_part = activate(own_hidden[begin:end], got, *earlier), attended[begin:end]
+        return (
+            (dot(active, sent_mlp) + dot(heads_part, sent_attn)).astype(BF16),
+            dot(active, kept_mlp) + dot(heads_part, kept_attn),
+        )
+
+    got_attended = hold(got_attended, other_sent, other_kept, got_other_a)
+    other_sent = (other_sent + dot(got_attended, sent_attn)).astype(BF16)
+    other_kept = other_kept + dot(got_attended, kept_attn)
+    other_come = swap(other_sent, "tp", 1)
+    own_sent_a, own_kept_a = own_part(0, cut, got_other_a, other_sent, other_kept)
+
+    def rows_of(half):
+        kept = jnp.where(half == 0, other_kept[:cut], other_kept[cut:])
+        return kept + jnp.where(half == 0, other_come[:cut], other_come[cut:]).astype(F32)
+
+    passed = rows_of(1 - far).astype(BF16)
+    passed = hold(swap(passed, "tp", 2), own_sent_a, own_kept_a)
+    crossing = (rows_of(far) + passed.astype(F32)).astype(BF16)
     got = swap(crossing, "sx", 1)
-    own_sum_a = core_sum(own_part)
-    own_sums = hold(own_sums, own_part, crossing)
-    own_sum_b = core_sum(gelu_dot(own_sums[cut:], got_other_b, w_mlp_out) + dot(attended[cut:], w_attn_out), got)
-
-    others = lax.axis_size("tp") // 2
-    homes = [(s * 2 * others + (1 - s) * 2 + c, s * 2 * others + s * 2 + c) for s in range(2) for c in range(2)]
-    to_home = lambda cells: lax.ppermute(cells, ("sx", "tp"), homes)
-    from_home = lambda cells: lax.ppermute(cells, ("sx", "tp"), [(b, a) for a, b in homes])
-    come_a = to_home(own_sum_a.astype(BF16))
-    come_b = to_home(own_sum_b.astype(BF16))
-    got = hold(got, come_a)
-    rest = from_home(got)
-    own_sum = jnp.concatenate([own_sum_a + come_a.astype(F32), own_sum_b + come_b.astype(F32)], axis=0)
-    reduced = jnp.where(far == side, own_sum, jnp.concatenate(in_order(far, got, rest), axis=0).astype(F32))
-
-    first_col = hold(part[None], other_sum)[0] * block
+    own_sum_a = own_kept_a + swap(own_sent_a, "tp", 1).astype(F32)
+    come_a = swap(own_sum_a.astype(BF16), "tp", 2)
+    own_sent_b, own_kept_b = own_part(cut, tok_rows, got_other_b, crossing)
+    own_sum_b = hold(own_kept_b, got, come_a, cost=EARLY) + swap(own_sent_b, "tp", 1).astype(F32)
+
+    home = far == side
+    come_b = swap(jnp.where(home, got, own_sum_b.astype(BF16)), "tp", 2)
+    wide = got.astype(F32)
+    known = jnp.concatenate(
+        [
+            jnp.where(home, own_sum_a + come_a.astype(F32), jnp.where(far == 0, wide, 0.0)),
+            jnp.where(home, own_sum_b, jnp.where(far == 0, 0.0, wide)),
+        ],
+        axis=0,
+    )
+    first_col = hold(part[None], own_sent_a)[0] * block
     gate_part = lax.dynamic_slice_in_dim(mod_gate, first_col, block, 0)
     residual_part = lax.dynamic_slice_in_dim(tokens, first_col, block, 1).astype(F32)
-    return (residual_part + gate_part * reduced).astype(BF16)
+    known = hold(residual_part + gate_part * known)
+    late_first = jnp.where(home, 1, 1 - far) * cut
+    place = lax.broadcasted_iota(jnp.int32, (tok_rows, 1), 0)
+    late = (place >= late_first) & (place < late_first + cut)
+    late_part = jnp.concatenate([come_b, come_b], axis=0).astype(F32)
+    return (known + jnp.where(late, gate_part * late_part, 0.0)).astype(BF16)
 
 
 def shards(*arrays):

time: 144 us -> 132 us (0.917)
  waiting for transfers between devices: 54.3 us -> 41.4 us
  other arithmetic: 18.6 us -> 16.9 us
    ppermute x3 -> x0, starting transfers between devices: 7.11 us -> none  [the longest x1 4.29 us: paired_plan(): lax.ppermute(cells, ('sx', 'tp'), [(b, a) for a, b in homes])]
    ppermute x14 -> x16, waiting for transfers between devices: 37 us -> 30.7 us  [swap(): return lax.ppermute(cells, axis, [(i, i ^ bit) for i in range(count)])]
    ppermute x3 -> x0, waiting for transfers between devices: 6.02 us -> none  [the longest x2 6.02 us: paired_plan(): to_home = lambda cells: lax.ppermute(cells, ('sx', 'tp'), homes)]
    ppermute x14 -> x16, starting transfers between devices: 10.8 us -> 16.1 us  [swap(): return lax.ppermute(cells, axis, [(i, i ^ bit) for i in range(count)])]
    add x3 -> x1, other arithmetic: 4.1 us -> 1.23 us  [paired_plan(): known = hold(residual_part + gate_part * known)]
    unnamed x80 -> x72, local copies, waits for them, and re-layouts: 7.57 us -> 9.74 us
    convert_element_type x7 -> x6, other arithmetic: 5.4 us -> 6.71 us  [the longest x3 4.53 us: activate(): jax.nn.gelu(mine.astype(F32) + got.astype(F32), approximate=True)]
    dot_general x13 -> x19, matrix products: 19.7 us -> 20.3 us  [dot(): return jnp.dot(left, right, preferred_element_type=jnp.float32)]
  transfers between devices with their start and end apart: 19 -> 18, of which waited for: 13 -> 10; matrix products, arithmetic and copies ran while one was open for 25% -> 28% of each run, Pallas kernels for 11% -> 13%
where the time goes in v3:
time: 132 us; the launch traced here: 131 us
  waiting for transfers between devices  41.4 us (31%)
  starting transfers between devices  21.9 us (17%)
  matrix products  20.3 us (15%)
  other arithmetic  16.9 us (13%)
  Pallas kernels  16.8 us (13%)
  local copies, waits for them, and re-layouts  12.2 us (9%)
  between operations  1.97 us (1%)
    ppermute x16, waiting for transfers between devices, swap(): return lax.ppermute(cells, axis, [(i, i ^ bit) for i in range(count)])  30.7 us
    dot_general x19, matrix products, dot(): return jnp.dot(left, right, preferred_element_type=jnp.float32)  20.3 us
    ppermute x16, starting transfers between devices, swap(): return lax.ppermute(cells, axis, [(i, i ^ bit) for i in range(count)])  16.1 us
    pallas_call x3, Pallas kernels, call(): pl.pallas_call(kernel, grid=(grid,), in_specs=[spec(b, i) for _, b, i in...  15.8 us
    ppermute x2, waiting for transfers between devices, shift(): lax.ppermute(cells, axis, [(i, i + step) for i in range(count) if 0 <= i...  10.7 us
    unnamed x72, local copies, waits for them, and re-layouts  9.74 us
    ppermute x2, starting transfers between devices, shift(): lax.ppermute(cells, axis, [(i, i + step) for i in range(count) if 0 <= i...  5.72 us
    convert_element_type x3, other arithmetic, activate(): jax.nn.gelu(mine.astype(F32) + got.astype(F32), approximate=True)  4.53 us
  transfers between devices with their start and end apart: 18, of which 10 were waited for; matrix products, arithmetic and copies ran while one was open for 28% of the time, Pallas kernels for 13%

profile of v3, /device:TPU:0, one launch (start us, length us, event | category | flops | bytes accessed | tf_op | source)
XLA Modules:
  0.0 131.5 jit_solution(386188731042834335)
XLA Ops:
  0.0 1.2 constant_dynamic-slice_fusion.refs_1_
  1.2 3.0 %collective-permute-start = (bf16[400,768]{1,0:T(8,128)(2,1)S(1)}, bf16[400,768]{1,0:T(8,128)(2,1)}, u32[]{:S(2)}, u32[]{:S(2)}) collective-permute-start(bf16[400,768]{1,0:T(8,128)(2,1)S(1)} %constant_dynamic-slice_fusion.refs_1_), channel_id=1, source_target_pairs={{0,4},{4,0},{1,5},{5,1},{2,6},{6,2},{3,7},{7,3},{8,12},{12,8},{9,1... | collective-permute-start | bytes 1843208 | tf_op jit(solution)/shard_map/ppermute | solution.py:107
  4.2 0.5 shard_map.145
  5.5 2.1 %convert_reduce_fusion = f32[400]{0:T(512)S(1)} fusion(bf16[400,3072]{1,0:T(8,128)(2,1)} %param.15), kind=kLoop, calls=%fused_computation.1 | loop fusion | flops 2457200 | bytes 2459200 | tf_op jit(solution)/shard_map/reduce_sum | solution.py:316
  7.8 2.6 %fusion.1 = f32[400]{0:T(512)S(1)} fusion(bf16[400,3072]{1,0:T(8,128)(2,1)} %param.15, f32[400]{0:T(512)S(1)} %broadcast_multiply_fusion), kind=kLoop, calls=%fused_computation.3 | loop fusion | flops 4914800 | bytes 2460800 | tf_op jit(solution)/shard_map/reduce_sum | solution.py:318
  10.5 0.5 add_convert_fusion.1.refs_0_
  11.0 0.5 convolution_convert_fusion.1
  11.5 0.5 convolution_convert_fusion.5
  12.1 0.5 convolution_convert_fusion.6
  13.0 2.1 %convolution_convert_fusion.refs_1_.refs_0_ = bf16[400,1536]{1,0:T(8,128)(2,1)S(1)} fusion(bf16[400,1536]{1,0:T(8,128)(2,1)S(1)} %shard_map.146.refs_0_, bf16[1536,1536]{1,0:T(8,128)(2,1)S(1)} %bitcast.36), kind=kOutput, calls=%fused_computation.5 | convolution fusion | flops 1888051200 | bytes 7176192 | tf_op jit(solution)/shard_map/dot_general | solution.py:118
  15.0 3.2 %collective-permute-done.refs_0_ = bf16[400,768]{1,0:T(8,128)(2,1)} collective-permute-done((bf16[400,768]{1,0:T(8,128)(2,1)S(1)}, bf16[400,768]{1,0:T(8,128)(2,1)}, u32[]{:S(2)}, u32[]{:S(2)}) %collective-permute-start) | collective-permute-done | bytes 614432 | tf_op jit(solution)/shard_map/ppermute | solution.py:107
  18.2 1.8 %collective-permute-start.2 = (f32[400,2]{0,1:T(2,128)S(1)}, f32[400,2]{0,1:T(2,128)S(1)}, u32[]{:S(2)}, u32[]{:S(2)}) collective-permute-start(f32[400,2]{0,1:T(2,128)S(1)} %pad_maximum_fusion.2), channel_id=1, source_target_pairs={{0,4},{4,0},{1,5},{5,1},{2,6},{6,2},{3,7},{7,3},{8,12},{12,8},{9,1... | collective-permute-start | bytes 9608 | tf_op jit(solution)/shard_map/ppermute | solution.py:107
  20.3 1.6 %collective-permute-done.2 = f32[400,2]{0,1:T(2,128)S(1)} collective-permute-done((f32[400,2]{0,1:T(2,128)S(1)}, f32[400,2]{0,1:T(2,128)S(1)}, u32[]{:S(2)}, u32[]{:S(2)}) %collective-permute-start.2) | collective-permute-done | bytes 3232 | tf_op jit(solution)/shard_map/ppermute | solution.py:107
  21.9 1.5 %broadcast_select_fusion.1 = (bf16[400,768]{1,0:T(8,128)(2,1)S(1)}, bf16[400,768]{1,0:T(8,128)(2,1)S(1)}) fusion(bf16[400,768]{1,0:T(8,128)(2,1)} %shard_map.147, bf16[400,768]{1,0:T(8,128)(2,1)} %collective-permute-done.1, pred[]{:T(512)S(6)} %eq.24), kind=kLoop, calls=%fused_computation.77 | loop fusion | flops 614400 | bytes 2457601 | tf_op jit(solution)/shard_map/jit(_where)/select_n | solution.py:154
  23.4 0.5 add_convert_fusion.refs_1_
  24.3 0.8 convolution_convert_fusion.2
  25.1 0.8 convolution_convert_fusion.3
  25.9 0.8 convolution_convert_fusion.4
  26.8 1.8 %collective-permute-start.6 = (bf16[400,1152]{1,0:T(8,128)(2,1)S(1)}, bf16[400,1152]{1,0:T(8,128)(2,1)S(1)}, u32[]{:S(2)}, u32[]{:S(2)}) collective-permute-start(bf16[400,1152]{1,0:T(8,128)(2,1)S(1)} %pad_maximum_fusion.refs_1_.refs_7_), channel_id=1, source_target_pairs={{0,4},{4,0},{1,5},{5,1},{2,6},{6,2},{3,7},{7,3},{8,12},{12,8},{9,1... | collective-permute-start | bytes 2764808 | tf_op jit(solution)/shard_map/ppermute | solution.py:107
  30.2 0.7 collective-permute-done.3.refs_8_.refs_9_
  30.9 0.7 copy-done.6
  31.7 1.0 copy-done.7
  32.6 7.6 %shard_map.149 = (f32[400,1152]{1,0:T(8,128)S(1)}, f32[224,768]{1,0:T(8,128)S(1)}, bf16[200,1536]{1,0:T(8,128)(2,1)S(1)}, bf16[200,1536]{1,0:T(8,128)(2,1)}) custom-call(bf16[400,1536]{1,0:T(8,128)(2,1)S(1)} %copy-done.5, bf16[400,1536]{1,0:T(8,128)(2,1)S(1)} %add_convert_fusion.refs_1_, bf16[224,400]{1,0:T(8,128)(2,1)S(1)} %broadcast_select_fusion.2.refs_2_, ...), custom_call_target="tpu_custom_call" | custom-call | flops 3831496704 | bytes 14475264 | tf_op jit(solution)/shard_map/pallas_call | solution.py:141
  40.2 10.4 %collective-permute-done.6.refs_3_.refs_4_.refs_5_ = bf16[400,1152]{1,0:T(8,128)(2,1)S(1)} collective-permute-done((bf16[400,1152]{1,0:T(8,128)(2,1)S(1)}, bf16[400,1152]{1,0:T(8,128)(2,1)S(1)}, u32[]{:S(2)}, u32[]{:S(2)}) %collective-permute-start.6) | collective-permute-done | bytes 921632 | tf_op jit(solution)/shard_map/ppermute | solution.py:107
  50.7 2.5 %shard_map.150 = (bf16[400,384]{1,0:T(8,128)(2,1)S(1)}, bf16[400,768]{1,0:T(8,128)(2,1)S(1)}, bf16[224,768]{1,0:T(8,128)(2,1)S(1)}, bf16[320,768]{1,0:T(8,128)(2,1)}, bf16[320,768]{1,0:T(8,128)(2,1)}) custom-call(f32[400,1152]{1,0:T(8,128)S(1)} %get-tuple-element.16.refs_0_.refs_1_.refs_2_, f32[400,1152]{1,0:T(8,128)S(1)} %get-tuple-element.16.refs_0_.refs_1_.refs_2_, ...), custom_call_target="tpu_custom_call" | custom-call | flops 1000 | bytes 1000 | tf_op jit(solution)/shard_map/pallas_call | solution.py:141
  53.1 0.8 copy-done.8
  54.0 0.7 copy-done.10
  54.7 0.7 copy-done.12
  55.4 4.3 %collective-permute-start.7 = (bf16[320,768]{1,0:T(8,128)(2,1)}, bf16[320,768]{1,0:T(8,128)(2,1)}, u32[]{:S(2)}, u32[]{:S(2)}) collective-permute-start(bf16[320,768]{1,0:T(8,128)(2,1)} %get-tuple-element.21), channel_id=1, source_target_pairs={{0,8},{8,16},{16,24},{1,9},{9,17},{17,25},{2,10},{10,18},{18,26},{... | collective-permute-start | bytes 1474568 | tf_op jit(solution)/shard_map/ppermute | solution.py:112
  59.7 1.5 %collective-permute-start.8 = (bf16[320,768]{1,0:T(8,128)(2,1)}, bf16[320,768]{1,0:T(8,128)(2,1)}, u32[]{:S(2)}, u32[]{:S(2)}) collective-permute-start(bf16[320,768]{1,0:T(8,128)(2,1)} %get-tuple-element.22), channel_id=1, source_target_pairs={{8,0},{16,8},{24,16},{9,1},{17,9},{25,17},{10,2},{18,10},{26,18},{... | collective-permute-start | bytes 1474568 | tf_op jit(solution)/shard_map/ppermute | solution.py:112
  61.3 1.4 %collective-permute-start.4 = (bf16[200,1536]{1,0:T(8,128)(2,1)S(1)}, bf16[200,1536]{1,0:T(8,128)(2,1)S(1)}, u32[]{:S(2)}, u32[]{:S(2)}) collective-permute-start(bf16[200,1536]{1,0:T(8,128)(2,1)S(1)} %get-tuple-element.14.refs_12_), channel_id=1, source_target_pairs={{0,4},{4,0},{1,5},{5,1},{2,6},{6,2},{3,7},{7,3},{8,12},{12,8},{9,1... | collective-permute-start | bytes 1843208 | tf_op jit(solution)/shard_map/ppermute | solution.py:107
  62.7 5.8 %collective-permute-done.7.refs_4_ = bf16[320,768]{1,0:T(8,128)(2,1)} collective-permute-done((bf16[320,768]{1,0:T(8,128)(2,1)}, bf16[320,768]{1,0:T(8,128)(2,1)}, u32[]{:S(2)}, u32[]{:S(2)}) %collective-permute-start.7) | collective-permute-done | bytes 491552 | tf_op jit(solution)/shard_map/ppermute | solution.py:112
  68.6 4.9 %collective-permute-done.8.refs_5_ = bf16[320,768]{1,0:T(8,128)(2,1)} collective-permute-done((bf16[320,768]{1,0:T(8,128)(2,1)}, bf16[320,768]{1,0:T(8,128)(2,1)}, u32[]{:S(2)}, u32[]{:S(2)}) %collective-permute-start.8) | collective-permute-done | bytes 491552 | tf_op jit(solution)/shard_map/ppermute | solution.py:112
  73.4 1.1 copy-done.9
  74.5 1.0 copy-done.11
  75.5 1.0 copy-done.13
  76.5 5.7 %shard_map.151.refs_1_ = bf16[400,384]{1,0:T(8,128)(2,1)S(1)} custom-call(bf16[400,384]{1,0:T(8,128)(2,1)S(1)} %copy-done.13, f32[1,1280]{1,0:T(1,128)S(1)} %broadcast_in_dim.55.refs_1_, bf16[400,768]{1,0:T(8,128)(2,1)S(1)} %copy-done.9, bf16[224,768]{1,0:T(8,128)(2,1)S(1)} %copy-done.11, bf16[320,768]{1,0:T(8,128)(2,1)} %collective-permute-done.7.refs_4_, ...), custom_call_target="tpu_custom_call" | custom-call | flops 1000 | bytes 1000 | tf_op jit(solution)/shard_map/pallas_call | solution.py:141
  82.3 2.4 %fusion.9.refs_0_ = bf16[400,1536]{1,0:T(8,128)(2,1)S(1)} fusion(bf16[400,1536]{1,0:T(8,128)(2,1)} %shard_map.152, bf16[200,1536]{1,0:T(8,128)(2,1)} %get-tuple-element.15.refs_0_, bf16[200,1536]{1,0:T(8,128)(2,1)S(1)} %get-tuple-element.14.refs_12_), kind=kLoop, calls=%fused_computation.14 | loop fusion | flops 9216000 | bytes 3686400 | tf_op jit(solution)/shard_map/convert_element_type | solution.py:369
  84.8 2.9 %fusion.20.refs_1_ = f32[400,768]{1,0:T(8,128)S(1)} fusion(bf16[400,1536]{1,0:T(8,128)(2,1)S(1)} %shard_map.153, bf16[1536,1536]{1,0:T(8,128)(2,1)} %param.24, s32[]{:T(128)S(6)} %select_n.127), kind=kOutput, calls=%fused_computation.29 | convolution fusion | flops 943718400 | bytes 4816900 | tf_op jit(solution)/shard_map/dot_general | solution.py:118
  87.7 2.1 %collective-permute-start.15 = (bf16[200,1536]{1,0:T(8,128)(2,1)}, bf16[200,1536]{1,0:T(8,128)(2,1)}, u32[]{:S(2)}, u32[]{:S(2)}) collective-permute-start(bf16[200,1536]{1,0:T(8,128)(2,1)} %shard_map.159), channel_id=1, source_target_pairs={{0,4},{4,0},{1,5},{5,1},{2,6},{6,2},{3,7},{7,3},{8,12},{12,8},{9,1... | collective-permute-start | bytes 1843208 | tf_op jit(solution)/shard_map/ppermute | solution.py:107
  89.8 1.1 fusion.14.refs_2_
  91.0 5.8 %collective-permute-done.9.refs_0_ = bf16[400,384]{1,0:T(8,128)(2,1)S(1)} collective-permute-done((bf16[400,384]{1,0:T(8,128)(2,1)S(1)}, bf16[400,384]{1,0:T(8,128)(2,1)S(1)}, u32[]{:S(2)}, u32[]{:S(2)}) %collective-permute-start.9) | collective-permute-done | bytes 307232 | tf_op jit(solution)/shard_map/ppermute | solution.py:107
  96.8 0.5 fusion.22.refs_1_
  97.2 0.5 convolution_add_fusion.refs_2_
  97.8 1.2 copy-done.2
  99.0 0.5 fusion.30.refs_0_
  99.6 0.7 fusion.18
  100.7 0.9 add_convert_fusion.4
  101.6 1.5 %collective-permute-start.13 = (bf16[200,768]{1,0:T(8,128)(2,1)}, bf16[200,768]{1,0:T(8,128)(2,1)S(1)}, u32[]{:S(2)}, u32[]{:S(2)}) collective-permute-start(bf16[200,768]{1,0:T(8,128)(2,1)} %add_convert_fusion.4), channel_id=1, source_target_pairs={{0,2},{1,3},{2,0},{3,1},{4,6},{5,7},{6,4},{7,5},{8,10},{9,11},{10,... | collective-permute-start | bytes 921608 | tf_op jit(solution)/shard_map/ppermute | solution.py:107
  103.1 1.5 %fusion.12 = f32[200,768]{1,0:T(8,128)} fusion(bf16[200,1536]{1,0:T(8,128)(2,1)S(1)} %shard_map.156, bf16[1536,1536]{1,0:T(8,128)(2,1)S(1)} %bitcast.40, s32[]{:T(128)S(6)} %select_n.128), kind=kOutput, calls=%fused_computation.21 | convolution fusion | flops 471859200 | bytes 3588100 | tf_op jit(solution)/shard_map/dot_general | solution.py:118
  104.6 0.5 shard_map.157
  105.7 0.8 dynamic_slice.39
  106.5 1.5 %fusion.50 = (bf16[200,768]{1,0:T(8,128)(2,1)S(1)}, f32[200,768]{1,0:T(8,128)S(1)}) fusion(bf16[200,768]{1,0:T(8,128)(2,1)} %collective-permute-done.10, f32[200,768]{1,0:T(8,128)} %fusion.12, bf16[384,1536]{1,0:T(8,128)(2,1)S(1)} %copy-done, s32[]{:T(128)S(6)} %select_n.128, bf16[400,384]{1,0:T(8,128)(2,1)S(1)} %shard_map.151.refs_1_), kind=kOutput, calls=%fused_computation.84 | convolution fusion | flops 118579200 | bytes 2586628 | tf_op jit(solution)/shard_map/dot_general | solution.py:118
  108.0 0.6 collective-permute-start.11
  108.6 3.3 %collective-permute-done.13.refs_0_ = bf16[200,768]{1,0:T(8,128)(2,1)S(1)} collective-permute-done((bf16[200,768]{1,0:T(8,128)(2,1)}, bf16[200,768]{1,0:T(8,128)(2,1)S(1)}, u32[]{:S(2)}, u32[]{:S(2)}) %collective-permute-start.13) | collective-permute-done | bytes 307232 | tf_op jit(solution)/shard_map/ppermute | solution.py:107
  112.1 1.4 %collective-permute-start.14 = (bf16[200,768]{1,0:T(8,128)(2,1)S(1)}, bf16[200,768]{1,0:T(8,128)(2,1)S(1)}, u32[]{:S(2)}, u32[]{:S(2)}) collective-permute-start(bf16[200,768]{1,0:T(8,128)(2,1)S(1)} %add_convert_fusion.3.refs_1_), channel_id=1, source_target_pairs={{0,4},{4,0},{1,5},{5,1},{2,6},{6,2},{3,7},{7,3},{8,12},{12,8},{9,1... | collective-permute-start | bytes 921608 | tf_op jit(solution)/shard_map/ppermute | solution.py:107
  113.5 1.6 %fusion.38.refs_0_ = bf16[200,1536]{1,0:T(8,128)(2,1)S(1)} fusion(bf16[200,1536]{1,0:T(8,128)(2,1)} %shard_map.160, bf16[400,1536]{1,0:T(8,128)(2,1)S(1)} %copy-done.3), kind=kLoop, calls=%fused_computation.53 | loop fusion | flops 3686400 | bytes 1843200 | tf_op jit(solution)/shard_map/convert_element_type | solution.py:369
  115.1 2.3 %fusion.16 = f32[200,768]{1,0:T(8,128)S(1)} fusion(bf16[200,1536]{1,0:T(8,128)(2,1)S(1)} %shard_map.161, bf16[1536,1536]{1,0:T(8,128)(2,1)} %param.24, s32[]{:T(128)S(6)} %select_n.127), kind=kOutput, calls=%fused_computation.25 | convolution fusion | flops 471859200 | bytes 3588100 | tf_op jit(solution)/shard_map/dot_general | solution.py:118
  117.8 2.3 %fusion.10 = f32[200,768]{1,0:T(8,128)S(1)} fusion(bf16[200,1536]{1,0:T(8,128)(2,1)S(1)} %shard_map.161, bf16[1536,1536]{1,0:T(8,128)(2,1)} %param.24, s32[]{:T(128)S(6)} %select_n.128), kind=kOutput, calls=%fused_computation.19 | convolution fusion | flops 471859200 | bytes 3588100 | tf_op jit(solution)/shard_map/dot_general | solution.py:118
  120.8 1.6 %collective-permute-start.17 = (bf16[200,768]{1,0:T(8,128)(2,1)S(1)}, bf16[200,768]{1,0:T(8,128)(2,1)S(1)}, u32[]{:S(2)}, u32[]{:S(2)}) collective-permute-start(bf16[200,768]{1,0:T(8,128)(2,1)S(1)} %fusion.52), channel_id=1, source_target_pairs={{0,2},{1,3},{2,0},{3,1},{4,6},{5,7},{6,4},{7,5},{8,10},{9,11},{10,... | collective-permute-start | bytes 921608 | tf_op jit(solution)/shard_map/ppermute | solution.py:107
  122.3 1.2 fusion.42
  123.6 1.2 fusion.39.refs_0_
  124.8 5.6 %collective-permute-done.17 = bf16[200,768]{1,0:T(8,128)(2,1)S(1)} collective-permute-done((bf16[200,768]{1,0:T(8,128)(2,1)S(1)}, bf16[200,768]{1,0:T(8,128)(2,1)S(1)}, u32[]{:S(2)}, u32[]{:S(2)}) %collective-permute-start.17) | collective-permute-done | bytes 307232 | tf_op jit(solution)/shard_map/ppermute | solution.py:107
  130.4 1.1 add_convert_fusion.2
  (116 shorter events, 4.7 us)
Async XLA Ops:
  0.0 96.8 %copy-start = (bf16[384,1536]{1,0:T(8,128)(2,1)S(1)}, bf16[384,1536]{1,0:T(8,128)(2,1)}, u32[]{:S(2)}) copy-start(bf16[384,1536]{1,0:T(8,128)(2,1)} %param.23) | copy-start | bytes 3538948
  1.2 17.0 %collective-permute-start = (bf16[400,768]{1,0:T(8,128)(2,1)S(1)}, bf16[400,768]{1,0:T(8,128)(2,1)}, u32[]{:S(2)}, u32[]{:S(2)}) collective-permute-start(bf16[400,768]{1,0:T(8,128)(2,1)S(1)} %constant_dynamic-slice_fusion.refs_1_), channel_id=1, source_target_pairs={{0,4},{4,0},{1,5},{5,1},{2,6},{6,2},{3,7},{7,3},{8,12},{12,8},{9,1... | collective-permute-start | bytes 1843208 | tf_op jit(solution)/shard_map/ppermute | solution.py:107
  5.4 2.2 %copy-start.23 = (f32[3072]{0:T(1024)S(1)}, f32[3072]{0:T(1024)}, u32[]{:S(2)}) copy-start(f32[3072]{0:T(1024)} %param.17) | copy-start | bytes 36868
  5.4 2.3 %copy-start.24 = (f32[3072]{0:T(1024)S(1)}, f32[3072]{0:T(1024)}, u32[]{:S(2)}) copy-start(f32[3072]{0:T(1024)} %param.16) | copy-start | bytes 36868
  5.4 5.5 %copy-start.19 = (bf16[224,400]{1,0:T(8,128)(2,1)S(1)}, bf16[224,400]{1,0:T(8,128)(2,1)}, u32[]{:S(2)}) copy-start(bf16[224,400]{1,0:T(8,128)(2,1)} %constant.85.clone) | copy-start | bytes 537604
  5.5 5.5 %copy-start.21 = (bf16[224,400]{1,0:T(8,128)(2,1)S(1)}, bf16[224,400]{1,0:T(8,128)(2,1)}, u32[]{:S(2)}) copy-start(bf16[224,400]{1,0:T(8,128)(2,1)} %constant.86.clone) | copy-start | bytes 537604
  7.8 2.6 %copy-start.14 = (bf16[400,3072]{1,0:T(8,128)(2,1)S(1)}, bf16[400,3072]{1,0:T(8,128)(2,1)}, u32[]{:S(2)}) copy-start(bf16[400,3072]{1,0:T(8,128)(2,1)} %param.15) | copy-start | bytes 7372804
  7.8 3.7 %copy-start.15 = (bf16[1536,3,384]{2,0,1:T(8,128)(2,1)S(1)}, bf16[1536,3,384]{2,0,1:T(8,128)(2,1)}, u32[]{:S(2)}) copy-start(bf16[1536,3,384]{2,0,1:T(8,128)(2,1)} %param.19) | copy-start | bytes 10616836
  10.4 2.2 %slice-start = ((s8[4718592]{0:T(1024)(128)(4,1)}), s8[4194304]{0:T(1024)(128)(4,1)S(1)}, s32[]{:S(2)}) async-start(s8[4718592]{0:T(1024)(128)(4,1)} %bitcast.35), calls=%async_computation | async-start | bytes 8388608
  11.5 1.4 %slice-start.1 = ((s8[4718592]{0:T(1024)(128)(4,1)}), s8[524288]{0:T(1024)(128)(4,1)S(1)}, s32[]{:S(2)}) async-start(s8[4718592]{0:T(1024)(128)(4,1)} %bitcast.35), calls=%async_computation.1 | async-start | bytes 1048576
  13.0 2.1 %copy-start.4 = (bf16[400,1536]{1,0:T(8,128)(2,1)}, bf16[400,1536]{1,0:T(8,128)(2,1)S(1)}, u32[]{:S(2)}) copy-start(bf16[400,1536]{1,0:T(8,128)(2,1)S(1)} %shard_map.146.refs_0_) | copy-start | bytes 3686404
  18.2 3.7 %collective-permute-start.1 = (bf16[400,768]{1,0:T(8,128)(2,1)}, bf16[400,768]{1,0:T(8,128)(2,1)}, u32[]{:S(2)}, u32[]{:S(2)}) collective-permute-start(bf16[400,768]{1,0:T(8,128)(2,1)} %shard_map.147), channel_id=1, source_target_pairs={{0,1},{1,0},{2,3},{3,2},{4,5},{5,4},{6,7},{7,6},{8,9},{9,8},{10,11... | collective-permute-start | bytes 1843208 | tf_op jit(solution)/shard_map/ppermute | solution.py:107
  18.2 3.7 %collective-permute-start.2 = (f32[400,2]{0,1:T(2,128)S(1)}, f32[400,2]{0,1:T(2,128)S(1)}, u32[]{:S(2)}, u32[]{:S(2)}) collective-permute-start(f32[400,2]{0,1:T(2,128)S(1)} %pad_maximum_fusion.2), channel_id=1, source_target_pairs={{0,4},{4,0},{1,5},{5,1},{2,6},{6,2},{3,7},{7,3},{8,12},{12,8},{9,1... | collective-permute-start | bytes 9608 | tf_op jit(solution)/shard_map/ppermute | solution.py:107
  20.0 10.9 %collective-permute-start.3 = (bf16[224,768]{1,0:T(8,128)(2,1)S(1)}, bf16[224,768]{1,0:T(8,128)(2,1)S(1)}, u32[]{:S(2)}, u32[]{:S(2)}) collective-permute-start(bf16[224,768]{1,0:T(8,128)(2,1)S(1)} %pad_maximum_fusion.1.refs_1_), channel_id=1, source_target_pairs={{0,4},{4,0},{1,5},{5,1},{2,6},{6,2},{3,7},{7,3},{8,12},{12,8},{9,1... | collective-permute-start | bytes 1032200 | tf_op jit(solution)/shard_map/ppermute | solution.py:107
  21.9 2.4 %copy-start.16 = (bf16[1536,3,384]{2,0,1:T(8,128)(2,1)S(1)}, bf16[1536,3,384]{2,0,1:T(8,128)(2,1)}, u32[]{:S(2)}) copy-start(bf16[1536,3,384]{2,0,1:T(8,128)(2,1)} %param.19) | copy-start | bytes 10616836
  25.9 5.8 %slice-start.2 = ((s8[4718592]{0:T(1024)(128)(4,1)}), s8[4194304]{0:T(1024)(128)(4,1)S(1)}, s32[]{:S(2)}) async-start(s8[4718592]{0:T(1024)(128)(4,1)} %bitcast.37), calls=%async_computation.2 | async-start | bytes 8388608
  26.8 4.8 %slice-start.3 = ((s8[4718592]{0:T(1024)(128)(4,1)}), s8[524288]{0:T(1024)(128)(4,1)S(1)}, s32[]{:S(2)}) async-start(s8[4718592]{0:T(1024)(128)(4,1)} %bitcast.37), calls=%async_computation.3 | async-start | bytes 1048576
  26.8 23.8 %collective-permute-start.6 = (bf16[400,1152]{1,0:T(8,128)(2,1)S(1)}, bf16[400,1152]{1,0:T(8,128)(2,1)S(1)}, u32[]{:S(2)}, u32[]{:S(2)}) collective-permute-start(bf16[400,1152]{1,0:T(8,128)(2,1)S(1)} %pad_maximum_fusion.refs_1_.refs_7_), channel_id=1, source_target_pairs={{0,4},{4,0},{1,5},{5,1},{2,6},{6,2},{3,7},{7,3},{8,12},{12,8},{9,1... | collective-permute-start | bytes 2764808 | tf_op jit(solution)/shard_map/ppermute | solution.py:107
  28.6 1.1 copy-start.1
  28.6 1.1 copy-start.28
  28.6 1.1 copy-start.29
  28.6 1.3 copy-start.20
  28.7 1.5 %copy-start.22 = (bf16[224,400]{1,0:T(8,128)(2,1)S(1)}, bf16[224,400]{1,0:T(8,128)(2,1)}, u32[]{:S(2)}) copy-start(bf16[224,400]{1,0:T(8,128)(2,1)} %constant.86.clone) | copy-start | bytes 537604
  28.7 3.0 %copy-start.5 = (bf16[400,1536]{1,0:T(8,128)(2,1)S(1)}, bf16[400,1536]{1,0:T(8,128)(2,1)}, u32[]{:S(2)}) copy-start(bf16[400,1536]{1,0:T(8,128)(2,1)} %copy-done.4) | copy-start | bytes 3686404
  28.7 53.6 %collective-permute-start.5 = (bf16[400,1536]{1,0:T(8,128)(2,1)S(1)}, bf16[400,1536]{1,0:T(8,128)(2,1)}, u32[]{:S(2)}, u32[]{:S(2)}) collective-permute-start(bf16[400,1536]{1,0:T(8,128)(2,1)S(1)} %shard_map.148), channel_id=1, source_target_pairs={{0,4},{4,0},{1,5},{5,1},{2,6},{6,2},{3,7},{7,3},{8,12},{12,8},{9,1... | collective-permute-start | bytes 3686408 | tf_op jit(solution)/shard_map/ppermute | solution.py:107
  30.9 0.7 copy-start.6
  31.7 1.0 copy-start.7
  50.7 10.5 %copy-start.25 = (pred[1280]{0:T(1024)(128)(4,1)S(1)}, pred[1280]{0:T(1024)(128)(4,1)}, u32[]{:S(2)}) copy-start(pred[1280]{0:T(1024)(128)(4,1)} %constant.87.clone) | copy-start | bytes 3844
  50.7 10.5 %copy-start.26 = (pred[1280]{0:T(1024)(128)(4,1)S(1)}, pred[1280]{0:T(1024)(128)(4,1)}, u32[]{:S(2)}) copy-start(pred[1280]{0:T(1024)(128)(4,1)} %constant.88.clone) | copy-start | bytes 3844
  50.7 10.5 %copy-start.27 = (pred[1280]{0:T(1024)(128)(4,1)S(1)}, pred[1280]{0:T(1024)(128)(4,1)}, u32[]{:S(2)}) copy-start(pred[1280]{0:T(1024)(128)(4,1)} %constant.89.clone) | copy-start | bytes 3844
  53.1 0.8 copy-start.8
  54.0 0.7 copy-start.10
  54.7 0.7 copy-start.12
  55.4 13.1 %collective-permute-start.7 = (bf16[320,768]{1,0:T(8,128)(2,1)}, bf16[320,768]{1,0:T(8,128)(2,1)}, u32[]{:S(2)}, u32[]{:S(2)}) collective-permute-start(bf16[320,768]{1,0:T(8,128)(2,1)} %get-tuple-element.21), channel_id=1, source_target_pairs={{0,8},{8,16},{16,24},{1,9},{9,17},{17,25},{2,10},{10,18},{18,26},{... | collective-permute-start | bytes 1474568 | tf_op jit(solution)/shard_map/ppermute | solution.py:112
  59.7 13.8 %collective-permute-start.8 = (bf16[320,768]{1,0:T(8,128)(2,1)}, bf16[320,768]{1,0:T(8,128)(2,1)}, u32[]{:S(2)}, u32[]{:S(2)}) collective-permute-start(bf16[320,768]{1,0:T(8,128)(2,1)} %get-tuple-element.22), channel_id=1, source_target_pairs={{8,0},{16,8},{24,16},{9,1},{17,9},{25,17},{10,2},{18,10},{26,18},{... | collective-permute-start | bytes 1474568 | tf_op jit(solution)/shard_map/ppermute | solution.py:112
  61.3 29.7 %collective-permute-start.4 = (bf16[200,1536]{1,0:T(8,128)(2,1)S(1)}, bf16[200,1536]{1,0:T(8,128)(2,1)S(1)}, u32[]{:S(2)}, u32[]{:S(2)}) collective-permute-start(bf16[200,1536]{1,0:T(8,128)(2,1)S(1)} %get-tuple-element.14.refs_12_), channel_id=1, source_target_pairs={{0,4},{4,0},{1,5},{5,1},{2,6},{6,2},{3,7},{7,3},{8,12},{12,8},{9,1... | collective-permute-start | bytes 1843208 | tf_op jit(solution)/shard_map/ppermute | solution.py:107
  73.4 1.1 copy-start.9
  74.5 1.0 copy-start.11
  75.5 1.0 copy-start.13
  82.2 14.6 %collective-permute-start.9 = (bf16[400,384]{1,0:T(8,128)(2,1)S(1)}, bf16[400,384]{1,0:T(8,128)(2,1)S(1)}, u32[]{:S(2)}, u32[]{:S(2)}) collective-permute-start(bf16[400,384]{1,0:T(8,128)(2,1)S(1)} %shard_map.151.refs_1_), channel_id=1, source_target_pairs={{0,4},{4,0},{1,5},{5,1},{2,6},{6,2},{3,7},{7,3},{8,12},{12,8},{9,1... | collective-permute-start | bytes 921608 | tf_op jit(solution)/shard_map/ppermute | solution.py:107
  84.7 5.1 %slice-start.4 = ((s8[4718592]{0:T(1024)(128)(4,1)}), s8[4194304]{0:T(1024)(128)(4,1)S(1)}, s32[]{:S(2)}) async-start(s8[4718592]{0:T(1024)(128)(4,1)} %bitcast.39), calls=%async_computation.4 | async-start | bytes 8388608
  84.8 5.0 %slice-start.5 = ((s8[4718592]{0:T(1024)(128)(4,1)}), s8[524288]{0:T(1024)(128)(4,1)S(1)}, s32[]{:S(2)}) async-start(s8[4718592]{0:T(1024)(128)(4,1)} %bitcast.39), calls=%async_computation.5 | async-start | bytes 1048576
  87.7 25.8 %collective-permute-start.15 = (bf16[200,1536]{1,0:T(8,128)(2,1)}, bf16[200,1536]{1,0:T(8,128)(2,1)}, u32[]{:S(2)}, u32[]{:S(2)}) collective-permute-start(bf16[200,1536]{1,0:T(8,128)(2,1)} %shard_map.159), channel_id=1, source_target_pairs={{0,4},{4,0},{1,5},{5,1},{2,6},{6,2},{3,7},{7,3},{8,12},{12,8},{9,1... | collective-permute-start | bytes 1843208 | tf_op jit(solution)/shard_map/ppermute | solution.py:107
  97.8 1.3 copy-start.2
  97.8 2.9 %collective-permute-start.12 = (bf16[400,768]{1,0:T(8,128)(2,1)S(1)}, bf16[400,768]{1,0:T(8,128)(2,1)S(1)}, u32[]{:S(2)}, u32[]{:S(2)}) collective-permute-start(bf16[400,768]{1,0:T(8,128)(2,1)S(1)} %fusion.22.refs_1_), channel_id=1, source_target_pairs={{0,1},{1,0},{2,3},{3,2},{4,5},{5,4},{6,7},{7,6},{8,9},{9,8},{10,11... | collective-permute-start | bytes 1843208 | tf_op jit(solution)/shard_map/ppermute | solution.py:107
  100.6 6.0 %collective-permute-start.10 = (bf16[200,768]{1,0:T(8,128)(2,1)S(1)}, bf16[200,768]{1,0:T(8,128)(2,1)}, u32[]{:S(2)}, u32[]{:S(2)}) collective-permute-start(bf16[200,768]{1,0:T(8,128)(2,1)S(1)} %fusion.40.refs_1_), channel_id=1, source_target_pairs={{0,1},{1,0},{2,3},{3,2},{4,5},{5,4},{6,7},{7,6},{8,9},{9,8},{10,11... | collective-permute-start | bytes 921608 | tf_op jit(solution)/shard_map/ppermute | solution.py:107
  100.7 3.9 %copy-start.17 = (bf16[400,768]{1,0:T(8,128)(2,1)}, bf16[400,768]{1,0:T(8,128)(2,1)S(1)}, u32[]{:S(2)}) copy-start(bf16[400,768]{1,0:T(8,128)(2,1)S(1)} %collective-permute-done.12) | copy-start | bytes 1843204
  101.6 10.3 %collective-permute-start.13 = (bf16[200,768]{1,0:T(8,128)(2,1)}, bf16[200,768]{1,0:T(8,128)(2,1)S(1)}, u32[]{:S(2)}, u32[]{:S(2)}) collective-permute-start(bf16[200,768]{1,0:T(8,128)(2,1)} %add_convert_fusion.4), channel_id=1, source_target_pairs={{0,2},{1,3},{2,0},{3,1},{4,6},{5,7},{6,4},{7,5},{8,10},{9,11},{10,... | collective-permute-start | bytes 921608 | tf_op jit(solution)/shard_map/ppermute | solution.py:107
  108.0 3.9 %copy-start.18 = (bf16[400,768]{1,0:T(8,128)(2,1)S(1)}, bf16[400,768]{1,0:T(8,128)(2,1)}, u32[]{:S(2)}) copy-start(bf16[400,768]{1,0:T(8,128)(2,1)} %copy-done.17) | copy-start | bytes 1843204
  108.0 12.5 %collective-permute-start.11 = (bf16[200,768]{1,0:T(8,128)(2,1)S(1)}, bf16[200,768]{1,0:T(8,128)(2,1)S(1)}, u32[]{:S(2)}, u32[]{:S(2)}) collective-permute-start(bf16[200,768]{1,0:T(8,128)(2,1)S(1)} %get-tuple-element.32), channel_id=1, source_target_pairs={{0,2},{1,3},{2,0},{3,1},{4,6},{5,7},{6,4},{7,5},{8,10},{9,11},{10,... | collective-permute-start | bytes 921608 | tf_op jit(solution)/shard_map/ppermute | solution.py:107
  112.1 1.4 %copy-start.3 = (bf16[400,1536]{1,0:T(8,128)(2,1)S(1)}, bf16[400,1536]{1,0:T(8,128)(2,1)}, u32[]{:S(2)}) copy-start(bf16[400,1536]{1,0:T(8,128)(2,1)} %copy-done.1) | copy-start | bytes 3686404
  112.1 8.6 %collective-permute-start.14 = (bf16[200,768]{1,0:T(8,128)(2,1)S(1)}, bf16[200,768]{1,0:T(8,128)(2,1)S(1)}, u32[]{:S(2)}, u32[]{:S(2)}) collective-permute-start(bf16[200,768]{1,0:T(8,128)(2,1)S(1)} %add_convert_fusion.3.refs_1_), channel_id=1, source_target_pairs={{0,4},{4,0},{1,5},{5,1},{2,6},{6,2},{3,7},{7,3},{8,12},{12,8},{9,1... | collective-permute-start | bytes 921608 | tf_op jit(solution)/shard_map/ppermute | solution.py:107
  117.8 2.9 %collective-permute-start.16 = (bf16[200,768]{1,0:T(8,128)(2,1)S(1)}, bf16[200,768]{1,0:T(8,128)(2,1)S(1)}, u32[]{:S(2)}, u32[]{:S(2)}) collective-permute-start(bf16[200,768]{1,0:T(8,128)(2,1)S(1)} %fusion.41), channel_id=1, source_target_pairs={{0,1},{1,0},{2,3},{3,2},{4,5},{5,4},{6,7},{7,6},{8,9},{9,8},{10,11... | collective-permute-start | bytes 921608 | tf_op jit(solution)/shard_map/ppermute | solution.py:107
  120.8 9.6 %collective-permute-start.17 = (bf16[200,768]{1,0:T(8,128)(2,1)S(1)}, bf16[200,768]{1,0:T(8,128)(2,1)S(1)}, u32[]{:S(2)}, u32[]{:S(2)}) collective-permute-start(bf16[200,768]{1,0:T(8,128)(2,1)S(1)} %fusion.52), channel_id=1, source_target_pairs={{0,2},{1,3},{2,0},{3,1},{4,6},{5,7},{6,4},{7,5},{8,10},{9,11},{10,... | collective-permute-start | bytes 921608 | tf_op jit(solution)/shard_map/ppermute | solution.py:107

commit v4 on v3

--- a/solution.py
+++ b/solution.py
@@ -308,9 +308,9 @@
     own_pick, other_pick = border_picks(TILE, side)
     q_gain, k_gain = q_gain[:, None, :], k_gain[:, None, :]
 
-    piece_width = half_width // 2
-    other_first = (1 - side) * half_width + core * piece_width
-    sent = lax.dynamic_slice_in_dim(tokens, other_first, piece_width, 1)
+    quarter = half_width // 4
+    other_first = (1 - side) * half_width + part * quarter
+    sent = lax.dynamic_slice_in_dim(tokens, other_first, quarter, 1)
     piece = swap(sent, "sx", 1)
     cells = tokens.astype(F32)
     mean = jnp.mean(cells, axis=-1, keepdims=True)
@@ -339,17 +339,24 @@
     own_border = border_of(own_pick, own).astype(BF16)
     got_border = swap(own_border, "sx", 1)
     own = hold(own, own_border)
-    own_hidden = dot(own, w_mlp_in).astype(BF16)
-    piece = hold(piece, own_hidden)
-    near = swap(piece, "tp", 1)
-    other = modulate(jnp.concatenate(in_order(core, piece, near), axis=1), other_stats)
+    piece = hold(piece, own_border)
+    pieces = in_order(far, piece, swap(piece, "tp", 2))
+    first_part = width_of(hidden // 3, hidden)
+    own_first = dot(own, w_mlp_in[:, :first_part]).astype(BF16)
+    own = hold(own, own_first)
+    own_rest = dot(own, w_mlp_in[:, first_part:]).astype(BF16)
+    got_first = swap(own_first, "sx", 1)
+    pieces = hold(jnp.concatenate(pieces, axis=1), got_border, own_first)
+    even, odd = in_order(core, pieces, swap(pieces, "tp", 1))
+    other = jnp.concatenate([even[:, :quarter], odd[:, :quarter], even[:, quarter:], odd[:, quarter:]], axis=1)
+    other = modulate(other, other_stats)
     other_qkv = heads_of(other).astype(BF16)
     got_qkv = swap(other_qkv, "sx", 1)
-    own_hidden = hold(own_hidden, other_qkv)
-    got_own = swap(own_hidden, "sx", 1)
+    own_rest = hold(own_rest, other_qkv)
+    got_rest = swap(own_rest, "sx", 1)
     cut = tok_rows // 2
     own_qkv, other_border, other_a, other_b = rest_of_first(
-        own, other, other_pick, (w_queries, w_keys, w_values), w_mlp_in, cut, [other_qkv, got_border]
+        own, other, other_pick, (w_queries, w_keys, w_values), w_mlp_in, cut, [other_qkv, got_first]
     )
 
     queries, own_kv, border_kv, lower, upper = norm_heads(
@@ -365,7 +372,7 @@
     )
 
     def activate(mine, got, *earlier):
-        got = hold(got, *earlier)
+        got = hold(got, *earlier) if earlier else got
         return hold(jax.nn.gelu(mine.astype(F32) + got.astype(F32), approximate=True).astype(BF16))
 
     row = lax.axis_index("sy")
@@ -387,9 +394,10 @@
     attended = attend(queries, [own_kv, border_kv, above, below], bias, heads)
     got_attended = swap(attended, "sx", 1)
     got_other_a = swap(other_a, "sx", 1)
-    other_active = activate(jnp.concatenate([other_a, other_b], axis=0), got_own, attended)
+    got_own = jnp.concatenate([got_first, hold(got_rest, attended)], axis=1)
+    own_hidden = jnp.concatenate([own_first, own_rest], axis=1)
+    other_active = activate(jnp.concatenate([other_a, other_b], axis=0), got_own)
     other_sent, other_kept = dot(other_active, sent_mlp), dot(other_active, kept_mlp)
-    got_other_a = swap(other_a, "sx", 1)
     got_other_b = swap(hold(other_b, other_sent), "sx", 1)
 
     def own_part(begin, end, got, *earlier):
@@ -440,7 +448,8 @@
 
 
 def shards(*arrays):
-    if lax.axis_size("sx") == 2 and lax.axis_size("tp") == 4:
+    local_heads = arrays[6].shape[0]
+    if lax.axis_size("sx") == 2 and lax.axis_size("tp") == 4 and local_heads % 2 and local_heads > 1:
         return paired_plan(*arrays)
     return gathered_plan(*arrays)
 

time: 132 us -> 128 us (0.970)
  waiting for transfers between devices: 41.4 us -> 33.1 us
  starting transfers between devices: 21.9 us -> 24.4 us
  other arithmetic: 16.9 us -> 19.3 us
    ppermute x16 -> x18, waiting for transfers between devices: 30.7 us -> 25.6 us  [swap(): return lax.ppermute(cells, axis, [(i, i ^ bit) for i in range(count)])]
    ppermute x2, waiting for transfers between devices: 10.7 us -> 7.53 us  [shift(): lax.ppermute(cells, axis, [(i, i + step) for i in range(count) if 0 <= i...]
    unnamed x72 -> x70, local copies, waits for them, and re-layouts: 9.74 us -> 7.99 us
    ppermute x16 -> x18, starting transfers between devices: 16.1 us -> 17.7 us  [swap(): return lax.ppermute(cells, axis, [(i, i ^ bit) for i in range(count)])]
    squeeze x1, local copies, waits for them, and re-layouts: 0.35 us -> 1.88 us  [paired_plan(): w_queries, w_keys, w_values = [w_qkv[:, group] for group in range(3)]]
    dot_general x19 -> x20, matrix products: 20.3 us -> 20.3 us  [dot(): return jnp.dot(left, right, preferred_element_type=jnp.float32)]
  transfers between devices with their start and end apart: 18 -> 20, of which waited for: 10 -> 9; matrix products, arithmetic and copies ran while one was open for 28% -> 32% of each run, Pallas kernels for 13% -> 13%
where the time goes in v4:
time: 128 us
  waiting for transfers between devices  33.1 us (26%)
  starting transfers between devices  24.4 us (19%)
  matrix products  20.3 us (16%)
  other arithmetic  19.3 us (15%)
  Pallas kernels  16.7 us (13%)
  local copies, waits for them, and re-layouts  12 us (9%)
  between operations  1.88 us (1%)
    ppermute x18, waiting for transfers between devices, swap(): return lax.ppermute(cells, axis, [(i, i ^ bit) for i in range(count)])  25.6 us
    dot_general x20, matrix products, dot(): return jnp.dot(left, right, preferred_element_type=jnp.float32)  20.3 us
    ppermute x18, starting transfers between devices, swap(): return lax.ppermute(cells, axis, [(i, i ^ bit) for i in range(count)])  17.7 us
    pallas_call x3, Pallas kernels, call(): pl.pallas_call(kernel, grid=(grid,), in_specs=[spec(b, i) for _, b, i in...  15.7 us
    unnamed x70, local copies, waits for them, and re-layouts  7.99 us
    ppermute x2, waiting for transfers between devices, shift(): lax.ppermute(cells, axis, [(i, i + step) for i in range(count) if 0 <= i...  7.53 us
    ppermute x2, starting transfers between devices, shift(): lax.ppermute(cells, axis, [(i, i + step) for i in range(count) if 0 <= i...  6.63 us
    convert_element_type x3, other arithmetic, activate(): jax.nn.gelu(mine.astype(F32) + got.astype(F32), approximate=True)  5.49 us
  transfers between devices with their start and end apart: 20, of which 9 were waited for; matrix products, arithmetic and copies ran while one was open for 32% of the time, Pallas kernels for 13%

profile of v4, /device:TPU:0, one launch (start us, length us, event | category | flops | bytes accessed | tf_op | source)
XLA Modules:
  0.0 127.7 jit_solution(17494061313168318802)
XLA Ops:
  0.0 1.1 constant_dynamic-slice_fusion.refs_1_
  1.1 3.0 %collective-permute-start = (bf16[400,384]{1,0:T(8,128)(2,1)S(1)}, bf16[400,384]{1,0:T(8,128)(2,1)S(1)}, u32[]{:S(2)}, u32[]{:S(2)}) collective-permute-start(bf16[400,384]{1,0:T(8,128)(2,1)S(1)} %constant_dynamic-slice_fusion.refs_1_), channel_id=1, source_target_pairs={{0,4},{4,0},{1,5},{5,1},{2,6},{6,2},{3,7},{7,3},{8,12},{12,8},{9,1... | collective-permute-start | bytes 921608 | tf_op jit(solution)/shard_map/ppermute | solution.py:107
  5.3 2.1 %convert_reduce_fusion = f32[400]{0:T(512)S(1)} fusion(bf16[400,3072]{1,0:T(8,128)(2,1)} %param.15), kind=kLoop, calls=%fused_computation.1 | loop fusion | flops 2457200 | bytes 2459200 | tf_op jit(solution)/shard_map/reduce_sum | solution.py:316
  7.6 2.6 %fusion.1 = f32[400]{0:T(512)S(1)} fusion(bf16[400,3072]{1,0:T(8,128)(2,1)} %param.15, f32[400]{0:T(512)S(1)} %broadcast_multiply_fusion), kind=kLoop, calls=%fused_computation.3 | loop fusion | flops 4914800 | bytes 2460800 | tf_op jit(solution)/shard_map/reduce_sum | solution.py:318
  10.8 0.5 convolution_convert_fusion
  11.3 0.9 copy-done.13
  12.8 0.5 convolution_convert_fusion.5
  13.3 0.8 pad_maximum_fusion.3.refs_1_
  14.1 2.0 %collective-permute-start.1 = (bf16[400,384]{1,0:T(8,128)(2,1)S(1)}, bf16[400,384]{1,0:T(8,128)(2,1)S(1)}, u32[]{:S(2)}, u32[]{:S(2)}) collective-permute-start(bf16[400,384]{1,0:T(8,128)(2,1)S(1)} %shard_map.148), channel_id=1, source_target_pairs={{0,2},{1,3},{2,0},{3,1},{4,6},{5,7},{6,4},{7,5},{8,10},{9,11},{10,... | collective-permute-start | bytes 921608 | tf_op jit(solution)/shard_map/ppermute | solution.py:107
  16.1 1.6 %collective-permute-start.4 = (f32[400,2]{0,1:T(2,128)S(1)}, f32[400,2]{0,1:T(2,128)S(1)}, u32[]{:S(2)}, u32[]{:S(2)}) collective-permute-start(f32[400,2]{0,1:T(2,128)S(1)} %pad_maximum_fusion.4), channel_id=1, source_target_pairs={{0,4},{4,0},{1,5},{5,1},{2,6},{6,2},{3,7},{7,3},{8,12},{12,8},{9,1... | collective-permute-start | bytes 9608 | tf_op jit(solution)/shard_map/ppermute | solution.py:107
  17.7 3.0 %fusion.30.refs_1_.refs_2_ = bf16[400,512]{1,0:T(8,128)(2,1)} fusion(bf16[400,1536]{1,0:T(8,128)(2,1)S(1)} %shard_map.146.refs_0_, bf16[1536,1536]{1,0:T(8,128)(2,1)} %refs_6_.1), kind=kOutput, calls=%fused_computation.42 | convolution fusion | flops 629350400 | bytes 3211264 | tf_op jit(solution)/shard_map/dot_general | solution.py:118
  21.2 1.7 %collective-permute-done.1 = bf16[400,384]{1,0:T(8,128)(2,1)S(1)} collective-permute-done((bf16[400,384]{1,0:T(8,128)(2,1)S(1)}, bf16[400,384]{1,0:T(8,128)(2,1)S(1)}, u32[]{:S(2)}, u32[]{:S(2)}) %collective-permute-start.1) | collective-permute-done | bytes 307232 | tf_op jit(solution)/shard_map/ppermute | solution.py:107
  23.0 2.3 %collective-permute-done.2.refs_1_.refs_8_.refs_9_ = bf16[224,768]{1,0:T(8,128)(2,1)S(1)} collective-permute-done((bf16[224,768]{1,0:T(8,128)(2,1)}, bf16[224,768]{1,0:T(8,128)(2,1)S(1)}, u32[]{:S(2)}, u32[]{:S(2)}) %collective-permute-start.2) | collective-permute-done | bytes 344096 | tf_op jit(solution)/shard_map/ppermute | solution.py:107
  25.3 1.9 %slice_bitcast_fusion.1 = (bf16[1536,384]{1,0:T(8,128)(2,1)}, bf16[1536,384]{1,0:T(8,128)(2,1)}, bf16[1536,384]{1,0:T(8,128)(2,1)}) fusion(bf16[1536,3,384]{2,0,1:T(8,128)(2,1)S(1)} %copy-done.14), kind=kLoop, calls=%fused_computation.70 | loop fusion | bytes 7077888 | tf_op jit(solution)/shard_map/squeeze | solution.py:329
  27.2 0.7 copy-done.27
  27.9 1.2 broadcast_select_fusion.1
  29.3 0.5 add_convert_fusion.refs_1_
  29.8 1.3 copy-done.15
  31.1 0.8 convolution_convert_fusion.1
  31.9 0.8 convolution_convert_fusion.2
  32.7 0.8 convolution_convert_fusion.3
  33.6 1.5 %collective-permute-start.8 = (bf16[400,1152]{1,0:T(8,128)(2,1)S(1)}, bf16[400,1152]{1,0:T(8,128)(2,1)S(1)}, u32[]{:S(2)}, u32[]{:S(2)}) collective-permute-start(bf16[400,1152]{1,0:T(8,128)(2,1)S(1)} %pad_maximum_fusion.refs_1_.refs_7_), channel_id=1, source_target_pairs={{0,4},{4,0},{1,5},{5,1},{2,6},{6,2},{3,7},{7,3},{8,12},{12,8},{9,1... | collective-permute-start | bytes 2764808 | tf_op jit(solution)/shard_map/ppermute | solution.py:107
  35.2 1.4 %fusion.26.refs_0_ = bf16[400,1024]{1,0:T(8,128)(2,1)S(1)} fusion(bf16[400,1536]{1,0:T(8,128)(2,1)S(1)} %shard_map.147.refs_0_, bf16[1536,1536]{1,0:T(8,128)(2,1)S(1)} %bitcast.36), kind=kOutput, calls=%fused_computation.36 | convolution fusion | flops 1258700800 | bytes 5193728 | tf_op jit(solution)/shard_map/dot_general | solution.py:118
  36.6 0.9 collective-permute-start.7
  38.2 7.6 %shard_map.151 = (f32[400,1152]{1,0:T(8,128)S(1)}, f32[224,768]{1,0:T(8,128)S(1)}, bf16[200,1536]{1,0:T(8,128)(2,1)S(1)}, bf16[200,1536]{1,0:T(8,128)(2,1)}) custom-call(bf16[400,1536]{1,0:T(8,128)(2,1)S(1)} %shard_map.147.refs_0_, bf16[400,1536]{1,0:T(8,128)(2,1)S(1)} %add_convert_fusion.refs_1_, bf16[224,400]{1,0:T(8,128)(2,1)S(1)} %broadcast_select_fusion.4.refs_2_, ...), custom_call_target="tpu_custom_call" | custom-call | flops 3831496704 | bytes 14475264 | tf_op jit(solution)/shard_map/pallas_call | solution.py:141
  45.8 11.1 %collective-permute-done.8.refs_3_.refs_4_.refs_5_ = bf16[400,1152]{1,0:T(8,128)(2,1)S(1)} collective-permute-done((bf16[400,1152]{1,0:T(8,128)(2,1)S(1)}, bf16[400,1152]{1,0:T(8,128)(2,1)S(1)}, u32[]{:S(2)}, u32[]{:S(2)}) %collective-permute-start.8) | collective-permute-done | bytes 921632 | tf_op jit(solution)/shard_map/ppermute | solution.py:107
  57.0 2.5 %shard_map.152 = (bf16[400,384]{1,0:T(8,128)(2,1)S(1)}, bf16[400,768]{1,0:T(8,128)(2,1)S(1)}, bf16[224,768]{1,0:T(8,128)(2,1)S(1)}, bf16[320,768]{1,0:T(8,128)(2,1)}, bf16[320,768]{1,0:T(8,128)(2,1)}) custom-call(f32[400,1152]{1,0:T(8,128)S(1)} %get-tuple-element.16.refs_0_.refs_1_.refs_2_, f32[400,1152]{1,0:T(8,128)S(1)} %get-tuple-element.16.refs_0_.refs_1_.refs_2_, ...), custom_call_target="tpu_custom_call" | custom-call | flops 1000 | bytes 1000 | tf_op jit(solution)/shard_map/pallas_call | solution.py:141
  59.4 0.7 copy-done.8
  60.2 0.7 copy-done.10
  60.9 1.3 %collective-permute-start.10 = (bf16[320,768]{1,0:T(8,128)(2,1)}, bf16[320,768]{1,0:T(8,128)(2,1)S(1)}, u32[]{:S(2)}, u32[]{:S(2)}) collective-permute-start(bf16[320,768]{1,0:T(8,128)(2,1)} %get-tuple-element.22), channel_id=1, source_target_pairs={{8,0},{16,8},{24,16},{9,1},{17,9},{25,17},{10,2},{18,10},{26,18},{... | collective-permute-start | bytes 1474568 | tf_op jit(solution)/shard_map/ppermute | solution.py:112
  62.2 5.3 %collective-permute-start.9 = (bf16[320,768]{1,0:T(8,128)(2,1)}, bf16[320,768]{1,0:T(8,128)(2,1)}, u32[]{:S(2)}, u32[]{:S(2)}) collective-permute-start(bf16[320,768]{1,0:T(8,128)(2,1)} %get-tuple-element.21), channel_id=1, source_target_pairs={{0,8},{8,16},{16,24},{1,9},{9,17},{17,25},{2,10},{10,18},{18,26},{... | collective-permute-start | bytes 1474568 | tf_op jit(solution)/shard_map/ppermute | solution.py:112
  67.6 1.6 %collective-permute-start.6 = (bf16[200,1536]{1,0:T(8,128)(2,1)}, bf16[200,1536]{1,0:T(8,128)(2,1)S(1)}, u32[]{:S(2)}, u32[]{:S(2)}) collective-permute-start(bf16[200,1536]{1,0:T(8,128)(2,1)} %copy-done.3), channel_id=1, source_target_pairs={{0,4},{4,0},{1,5},{5,1},{2,6},{6,2},{3,7},{7,3},{8,12},{12,8},{9,1... | collective-permute-start | bytes 1843208 | tf_op jit(solution)/shard_map/ppermute | solution.py:107
  69.2 6.2 %collective-permute-done.10.refs_5_ = bf16[320,768]{1,0:T(8,128)(2,1)S(1)} collective-permute-done((bf16[320,768]{1,0:T(8,128)(2,1)}, bf16[320,768]{1,0:T(8,128)(2,1)S(1)}, u32[]{:S(2)}, u32[]{:S(2)}) %collective-permute-start.10) | collective-permute-done | bytes 491552 | tf_op jit(solution)/shard_map/ppermute | solution.py:112
  75.4 1.3 %collective-permute-done.9.refs_4_ = bf16[320,768]{1,0:T(8,128)(2,1)} collective-permute-done((bf16[320,768]{1,0:T(8,128)(2,1)}, bf16[320,768]{1,0:T(8,128)(2,1)}, u32[]{:S(2)}, u32[]{:S(2)}) %collective-permute-start.9) | collective-permute-done | bytes 491552 | tf_op jit(solution)/shard_map/ppermute | solution.py:112
  76.7 1.0 copy-done.9
  77.7 1.0 copy-done.11
  78.7 5.6 %shard_map.153.refs_1_ = bf16[400,384]{1,0:T(8,128)(2,1)S(1)} custom-call(bf16[400,384]{1,0:T(8,128)(2,1)S(1)} %copy-done.11, f32[1,1280]{1,0:T(1,128)S(1)} %broadcast_in_dim.55.refs_1_, bf16[400,768]{1,0:T(8,128)(2,1)S(1)} %get-tuple-element.19.refs_2_, bf16[224,768]{1,0:T(8,128)(2,1)S(1)} %copy-done.9, bf16[320,768]{1,0:T(8,128)(2,1)} %collective-permute-done.9.refs_4_, ...), custom_call_target="tpu_custom_call" | custom-call | flops 1000 | bytes 1000 | tf_op jit(solution)/shard_map/pallas_call | solution.py:141
  84.4 1.0 copy-done.4
  85.4 2.4 %fusion.11.refs_0_ = bf16[400,1536]{1,0:T(8,128)(2,1)S(1)} fusion(bf16[200,1536]{1,0:T(8,128)(2,1)} %get-tuple-element.15.refs_0_, bf16[200,1536]{1,0:T(8,128)(2,1)S(1)} %copy-done.4, bf16[400,1024]{1,0:T(8,128)(2,1)} %shard_map.154, bf16[400,512]{1,0:T(8,128)(2,1)} %collective-permute-done.5.refs_8_), kind=kLoop, calls=%fused_computation.15 | loop fusion | flops 11059200 | bytes 3686400 | tf_op jit(solution)/shard_map/convert_element_type | solution.py:376
  87.8 2.9 %fusion.22.refs_1_ = f32[400,768]{1,0:T(8,128)S(1)} fusion(bf16[400,1536]{1,0:T(8,128)(2,1)S(1)} %shard_map.155, bf16[1536,1536]{1,0:T(8,128)(2,1)} %param.24, s32[]{:T(128)S(6)} %select_n.143), kind=kOutput, calls=%fused_computation.30 | convolution fusion | flops 943718400 | bytes 4816900 | tf_op jit(solution)/shard_map/dot_general | solution.py:118
  90.8 1.1 collective-permute-start.17
  91.9 1.1 fusion.16.refs_2_
  93.1 1.5 %collective-permute-done.11.refs_0_ = bf16[400,384]{1,0:T(8,128)(2,1)S(1)} collective-permute-done((bf16[400,384]{1,0:T(8,128)(2,1)S(1)}, bf16[400,384]{1,0:T(8,128)(2,1)S(1)}, u32[]{:S(2)}, u32[]{:S(2)}) %collective-permute-start.11) | collective-permute-done | bytes 307232 | tf_op jit(solution)/shard_map/ppermute | solution.py:107
  95.7 1.4 %fusion.40.refs_0_ = bf16[200,1536]{1,0:T(8,128)(2,1)S(1)} fusion(bf16[200,1536]{1,0:T(8,128)(2,1)S(1)} %shard_map.157, bf16[400,512]{1,0:T(8,128)(2,1)} %fusion.30.refs_1_.refs_2_, bf16[400,1024]{1,0:T(8,128)(2,1)S(1)} %shard_map.150), kind=kLoop, calls=%fused_computation.50 | loop fusion | flops 4608000 | bytes 2457600 | tf_op jit(solution)/shard_map/convert_element_type | solution.py:376
  97.1 0.7 fusion.20
  97.8 1.1 fusion.50.refs_1_
  99.3 1.0 add_convert_fusion.4
  100.3 1.5 %collective-permute-start.15 = (bf16[200,768]{1,0:T(8,128)(2,1)}, bf16[200,768]{1,0:T(8,128)(2,1)}, u32[]{:S(2)}, u32[]{:S(2)}) collective-permute-start(bf16[200,768]{1,0:T(8,128)(2,1)} %add_convert_fusion.4), channel_id=1, source_target_pairs={{0,2},{1,3},{2,0},{3,1},{4,6},{5,7},{6,4},{7,5},{8,10},{9,11},{10,... | collective-permute-start | bytes 921608 | tf_op jit(solution)/shard_map/ppermute | solution.py:107
  101.8 1.5 %fusion.14 = f32[200,768]{1,0:T(8,128)} fusion(bf16[200,1536]{1,0:T(8,128)(2,1)S(1)} %shard_map.158, bf16[1536,1536]{1,0:T(8,128)(2,1)S(1)} %bitcast.38, s32[]{:T(128)S(6)} %select_n.144), kind=kOutput, calls=%fused_computation.22 | convolution fusion | flops 471859200 | bytes 3588100 | tf_op jit(solution)/shard_map/dot_general | solution.py:118
  104.4 0.8 dynamic_slice.39
  105.2 1.6 %fusion.61 = (bf16[200,768]{1,0:T(8,128)(2,1)S(1)}, f32[200,768]{1,0:T(8,128)S(1)}) fusion(bf16[200,768]{1,0:T(8,128)(2,1)} %collective-permute-done.12, f32[200,768]{1,0:T(8,128)} %fusion.14, bf16[384,1536]{1,0:T(8,128)(2,1)S(1)} %copy-done, s32[]{:T(128)S(6)} %select_n.144, bf16[400,384]{1,0:T(8,128)(2,1)S(1)} %shard_map.153.refs_1_), kind=kOutput, calls=%fused_computation.94 | convolution fusion | flops 118579200 | bytes 2586628 | tf_op jit(solution)/shard_map/dot_general | solution.py:118
  106.8 0.6 collective-permute-start.13
  107.5 2.8 %collective-permute-done.15.refs_0_ = bf16[200,768]{1,0:T(8,128)(2,1)} collective-permute-done((bf16[200,768]{1,0:T(8,128)(2,1)}, bf16[200,768]{1,0:T(8,128)(2,1)}, u32[]{:S(2)}, u32[]{:S(2)}) %collective-permute-start.15) | collective-permute-done | bytes 307232 | tf_op jit(solution)/shard_map/ppermute | solution.py:107
  110.2 1.2 add_convert_fusion.3.refs_1_
  111.4 1.2 collective-permute-start.16
  112.6 1.6 %fusion.48.refs_0_ = bf16[200,1536]{1,0:T(8,128)(2,1)S(1)} fusion(bf16[200,1536]{1,0:T(8,128)(2,1)} %shard_map.162, bf16[400,1024]{1,0:T(8,128)(2,1)S(1)} %shard_map.150, bf16[400,512]{1,0:T(8,128)(2,1)} %fusion.30.refs_1_.refs_2_), kind=kLoop, calls=%fused_computation.58 | loop fusion | flops 4608000 | bytes 2457600 | tf_op jit(solution)/shard_map/convert_element_type | solution.py:376
  114.2 0.7 fusion.18
  115.3 0.7 fusion.12
  116.3 3.1 %collective-permute-done.16.refs_1_ = bf16[200,768]{1,0:T(8,128)(2,1)S(1)} collective-permute-done((bf16[200,768]{1,0:T(8,128)(2,1)S(1)}, bf16[200,768]{1,0:T(8,128)(2,1)S(1)}, u32[]{:S(2)}, u32[]{:S(2)}) %collective-permute-start.16) | collective-permute-done | bytes 307232 | tf_op jit(solution)/shard_map/ppermute | solution.py:107
  119.5 1.5 %collective-permute-start.19 = (bf16[200,768]{1,0:T(8,128)(2,1)S(1)}, bf16[200,768]{1,0:T(8,128)(2,1)S(1)}, u32[]{:S(2)}, u32[]{:S(2)}) collective-permute-start(bf16[200,768]{1,0:T(8,128)(2,1)S(1)} %fusion.63), channel_id=1, source_target_pairs={{0,2},{1,3},{2,0},{3,1},{4,6},{5,7},{6,4},{7,5},{8,10},{9,11},{10,... | collective-permute-start | bytes 921608 | tf_op jit(solution)/shard_map/ppermute | solution.py:107
  121.1 1.2 fusion.52
  122.3 1.2 fusion.49.refs_0_
  123.5 3.1 %collective-permute-done.19 = bf16[200,768]{1,0:T(8,128)(2,1)S(1)} collective-permute-done((bf16[200,768]{1,0:T(8,128)(2,1)S(1)}, bf16[200,768]{1,0:T(8,128)(2,1)S(1)}, u32[]{:S(2)}, u32[]{:S(2)}) %collective-permute-start.19) | collective-permute-done | bytes 307232 | tf_op jit(solution)/shard_map/ppermute | solution.py:107
  126.6 1.1 add_convert_fusion.2
  (124 shorter events, 6.5 us)
Async XLA Ops:
  0.0 94.6 %copy-start = (bf16[384,1536]{1,0:T(8,128)(2,1)S(1)}, bf16[384,1536]{1,0:T(8,128)(2,1)}, u32[]{:S(2)}) copy-start(bf16[384,1536]{1,0:T(8,128)(2,1)} %param.23) | copy-start | bytes 3538948
  1.1 13.0 %collective-permute-start = (bf16[400,384]{1,0:T(8,128)(2,1)S(1)}, bf16[400,384]{1,0:T(8,128)(2,1)S(1)}, u32[]{:S(2)}, u32[]{:S(2)}) collective-permute-start(bf16[400,384]{1,0:T(8,128)(2,1)S(1)} %constant_dynamic-slice_fusion.refs_1_), channel_id=1, source_target_pairs={{0,4},{4,0},{1,5},{5,1},{2,6},{6,2},{3,7},{7,3},{8,12},{12,8},{9,1... | collective-permute-start | bytes 921608 | tf_op jit(solution)/shard_map/ppermute | solution.py:107
  5.3 2.1 %copy-start.22 = (f32[3072]{0:T(1024)S(1)}, f32[3072]{0:T(1024)}, u32[]{:S(2)}) copy-start(f32[3072]{0:T(1024)} %param.17) | copy-start | bytes 36868
  5.3 2.2 %copy-start.23 = (f32[3072]{0:T(1024)S(1)}, f32[3072]{0:T(1024)}, u32[]{:S(2)}) copy-start(f32[3072]{0:T(1024)} %param.16) | copy-start | bytes 36868
  7.6 2.6 %copy-start.12 = (bf16[400,3072]{1,0:T(8,128)(2,1)S(1)}, bf16[400,3072]{1,0:T(8,128)(2,1)}, u32[]{:S(2)}) copy-start(bf16[400,3072]{1,0:T(8,128)(2,1)} %param.15) | copy-start | bytes 7372804
  7.6 3.2 %copy-start.18 = (bf16[224,400]{1,0:T(8,128)(2,1)S(1)}, bf16[224,400]{1,0:T(8,128)(2,1)}, u32[]{:S(2)}) copy-start(bf16[224,400]{1,0:T(8,128)(2,1)} %constant.87.clone) | copy-start | bytes 537604
  7.6 3.2 %copy-start.20 = (bf16[224,400]{1,0:T(8,128)(2,1)S(1)}, bf16[224,400]{1,0:T(8,128)(2,1)}, u32[]{:S(2)}) copy-start(bf16[224,400]{1,0:T(8,128)(2,1)} %constant.88.clone) | copy-start | bytes 537604
  10.3 2.0 %copy-start.13 = (bf16[1536,3,384]{2,0,1:T(8,128)(2,1)S(1)}, bf16[1536,3,384]{2,0,1:T(8,128)(2,1)}, u32[]{:S(2)}) copy-start(bf16[1536,3,384]{2,0,1:T(8,128)(2,1)} %param.19) | copy-start | bytes 10616836
  14.1 11.2 %collective-permute-start.2 = (bf16[224,768]{1,0:T(8,128)(2,1)}, bf16[224,768]{1,0:T(8,128)(2,1)S(1)}, u32[]{:S(2)}, u32[]{:S(2)}) collective-permute-start(bf16[224,768]{1,0:T(8,128)(2,1)} %pad_maximum_fusion.3.refs_1_), channel_id=1, source_target_pairs={{0,4},{4,0},{1,5},{5,1},{2,6},{6,2},{3,7},{7,3},{8,12},{12,8},{9,1... | collective-permute-start | bytes 1032200 | tf_op jit(solution)/shard_map/ppermute | solution.py:107
  14.1 8.7 %collective-permute-start.1 = (bf16[400,384]{1,0:T(8,128)(2,1)S(1)}, bf16[400,384]{1,0:T(8,128)(2,1)S(1)}, u32[]{:S(2)}, u32[]{:S(2)}) collective-permute-start(bf16[400,384]{1,0:T(8,128)(2,1)S(1)} %shard_map.148), channel_id=1, source_target_pairs={{0,2},{1,3},{2,0},{3,1},{4,6},{5,7},{6,4},{7,5},{8,10},{9,11},{10,... | collective-permute-start | bytes 921608 | tf_op jit(solution)/shard_map/ppermute | solution.py:107
  16.1 11.8 %collective-permute-start.4 = (f32[400,2]{0,1:T(2,128)S(1)}, f32[400,2]{0,1:T(2,128)S(1)}, u32[]{:S(2)}, u32[]{:S(2)}) collective-permute-start(f32[400,2]{0,1:T(2,128)S(1)} %pad_maximum_fusion.4), channel_id=1, source_target_pairs={{0,4},{4,0},{1,5},{5,1},{2,6},{6,2},{3,7},{7,3},{8,12},{12,8},{9,1... | collective-permute-start | bytes 9608 | tf_op jit(solution)/shard_map/ppermute | solution.py:107
  20.7 16.9 %collective-permute-start.5 = (bf16[400,512]{1,0:T(8,128)(2,1)}, bf16[400,512]{1,0:T(8,128)(2,1)}, u32[]{:S(2)}, u32[]{:S(2)}) collective-permute-start(bf16[400,512]{1,0:T(8,128)(2,1)} %fusion.30.refs_1_.refs_2_), channel_id=1, source_target_pairs={{0,4},{4,0},{1,5},{5,1},{2,6},{6,2},{3,7},{7,3},{8,12},{12,8},{9,1... | collective-permute-start | bytes 1228808 | tf_op jit(solution)/shard_map/ppermute | solution.py:107
  22.9 2.4 %copy-start.14 = (bf16[1536,3,384]{2,0,1:T(8,128)(2,1)S(1)}, bf16[1536,3,384]{2,0,1:T(8,128)(2,1)}, u32[]{:S(2)}) copy-start(bf16[1536,3,384]{2,0,1:T(8,128)(2,1)} %param.19) | copy-start | bytes 10616836
  25.3 1.9 %copy-start.1 = (bf16[224,768]{1,0:T(8,128)(2,1)}, bf16[224,768]{1,0:T(8,128)(2,1)S(1)}, u32[]{:S(2)}) copy-start(bf16[224,768]{1,0:T(8,128)(2,1)S(1)} %collective-permute-done.2.refs_1_.refs_8_.refs_9_) | copy-start | bytes 1032196
  25.3 2.6 %collective-permute-start.3 = (bf16[400,768]{1,0:T(8,128)(2,1)S(1)}, bf16[400,768]{1,0:T(8,128)(2,1)}, u32[]{:S(2)}, u32[]{:S(2)}) collective-permute-start(bf16[400,768]{1,0:T(8,128)(2,1)S(1)} %shard_map.149), channel_id=1, source_target_pairs={{0,1},{1,0},{2,3},{3,2},{4,5},{5,4},{6,7},{7,6},{8,9},{9,8},{10,11... | collective-permute-start | bytes 1843208 | tf_op jit(solution)/shard_map/ppermute | solution.py:107
  27.2 0.7 copy-start.27
  27.2 0.7 copy-start.28
  29.1 2.0 %copy-start.15 = (bf16[1536,3,384]{2,0,1:T(8,128)(2,1)S(1)}, bf16[1536,3,384]{2,0,1:T(8,128)(2,1)}, u32[]{:S(2)}) copy-start(bf16[1536,3,384]{2,0,1:T(8,128)(2,1)} %param.19) | copy-start | bytes 10616836
  31.9 3.3 %slice-start = ((s8[4718592]{0:T(1024)(128)(4,1)}), s8[4194304]{0:T(1024)(128)(4,1)S(1)}, s32[]{:S(2)}) async-start(s8[4718592]{0:T(1024)(128)(4,1)} %bitcast.35), calls=%async_computation | async-start | bytes 8388608
  32.7 2.4 %slice-start.1 = ((s8[4718592]{0:T(1024)(128)(4,1)}), s8[524288]{0:T(1024)(128)(4,1)S(1)}, s32[]{:S(2)}) async-start(s8[4718592]{0:T(1024)(128)(4,1)} %bitcast.35), calls=%async_computation.1 | async-start | bytes 1048576
  33.5 1.6 %copy-start.19 = (bf16[224,400]{1,0:T(8,128)(2,1)S(1)}, bf16[224,400]{1,0:T(8,128)(2,1)}, u32[]{:S(2)}) copy-start(bf16[224,400]{1,0:T(8,128)(2,1)} %constant.87.clone) | copy-start | bytes 537604
  33.5 1.6 %copy-start.21 = (bf16[224,400]{1,0:T(8,128)(2,1)S(1)}, bf16[224,400]{1,0:T(8,128)(2,1)}, u32[]{:S(2)}) copy-start(bf16[224,400]{1,0:T(8,128)(2,1)} %constant.88.clone) | copy-start | bytes 537604
  33.6 23.3 %collective-permute-start.8 = (bf16[400,1152]{1,0:T(8,128)(2,1)S(1)}, bf16[400,1152]{1,0:T(8,128)(2,1)S(1)}, u32[]{:S(2)}, u32[]{:S(2)}) collective-permute-start(bf16[400,1152]{1,0:T(8,128)(2,1)S(1)} %pad_maximum_fusion.refs_1_.refs_7_), channel_id=1, source_target_pairs={{0,4},{4,0},{1,5},{5,1},{2,6},{6,2},{3,7},{7,3},{8,12},{12,8},{9,1... | collective-permute-start | bytes 2764808 | tf_op jit(solution)/shard_map/ppermute | solution.py:107
  35.2 2.4 %copy-start.7 = (bf16[1536,384]{1,0:T(8,128)(2,1)S(1)}, bf16[1536,384]{1,0:T(8,128)(2,1)}, u32[]{:S(2)}) copy-start(bf16[1536,384]{1,0:T(8,128)(2,1)} %get-tuple-element.25.refs_3_) | copy-start | bytes 3538948
  36.6 1.3 copy-start.5
  36.6 1.6 %copy-start.6 = (bf16[1536,384]{1,0:T(8,128)(2,1)S(1)}, bf16[1536,384]{1,0:T(8,128)(2,1)}, u32[]{:S(2)}) copy-start(bf16[1536,384]{1,0:T(8,128)(2,1)} %get-tuple-element.24.refs_4_) | copy-start | bytes 3538948
  36.6 47.8 %collective-permute-start.7 = (bf16[400,1024]{1,0:T(8,128)(2,1)S(1)}, bf16[400,1024]{1,0:T(8,128)(2,1)}, u32[]{:S(2)}, u32[]{:S(2)}) collective-permute-start(bf16[400,1024]{1,0:T(8,128)(2,1)S(1)} %shard_map.150), channel_id=1, source_target_pairs={{0,4},{4,0},{1,5},{5,1},{2,6},{6,2},{3,7},{7,3},{8,12},{12,8},{9,1... | collective-permute-start | bytes 2457608 | tf_op jit(solution)/shard_map/ppermute | solution.py:107
  38.2 18.7 %copy-start.2 = (bf16[224,768]{1,0:T(8,128)(2,1)S(1)}, bf16[224,768]{1,0:T(8,128)(2,1)}, u32[]{:S(2)}) copy-start(bf16[224,768]{1,0:T(8,128)(2,1)} %copy-done.1) | copy-start | bytes 1032196
  45.8 13.6 %copy-start.3 = (bf16[200,1536]{1,0:T(8,128)(2,1)}, bf16[200,1536]{1,0:T(8,128)(2,1)S(1)}, u32[]{:S(2)}) copy-start(bf16[200,1536]{1,0:T(8,128)(2,1)S(1)} %get-tuple-element.14.refs_12_) | copy-start | bytes 1843204
  56.9 10.6 %copy-start.24 = (pred[1280]{0:T(1024)(128)(4,1)S(1)}, pred[1280]{0:T(1024)(128)(4,1)}, u32[]{:S(2)}) copy-start(pred[1280]{0:T(1024)(128)(4,1)} %constant.89.clone) | copy-start | bytes 3844
  57.0 10.6 %copy-start.25 = (pred[1280]{0:T(1024)(128)(4,1)S(1)}, pred[1280]{0:T(1024)(128)(4,1)}, u32[]{:S(2)}) copy-start(pred[1280]{0:T(1024)(128)(4,1)} %constant.90.clone) | copy-start | bytes 3844
  57.0 10.6 %copy-start.26 = (pred[1280]{0:T(1024)(128)(4,1)S(1)}, pred[1280]{0:T(1024)(128)(4,1)}, u32[]{:S(2)}) copy-start(pred[1280]{0:T(1024)(128)(4,1)} %constant.91.clone) | copy-start | bytes 3844
  59.4 0.7 copy-start.8
  60.2 0.7 copy-start.10
  60.9 14.5 %collective-permute-start.10 = (bf16[320,768]{1,0:T(8,128)(2,1)}, bf16[320,768]{1,0:T(8,128)(2,1)S(1)}, u32[]{:S(2)}, u32[]{:S(2)}) collective-permute-start(bf16[320,768]{1,0:T(8,128)(2,1)} %get-tuple-element.22), channel_id=1, source_target_pairs={{8,0},{16,8},{24,16},{9,1},{17,9},{25,17},{10,2},{18,10},{26,18},{... | collective-permute-start | bytes 1474568 | tf_op jit(solution)/shard_map/ppermute | solution.py:112
  62.2 14.5 %collective-permute-start.9 = (bf16[320,768]{1,0:T(8,128)(2,1)}, bf16[320,768]{1,0:T(8,128)(2,1)}, u32[]{:S(2)}, u32[]{:S(2)}) collective-permute-start(bf16[320,768]{1,0:T(8,128)(2,1)} %get-tuple-element.21), channel_id=1, source_target_pairs={{0,8},{8,16},{16,24},{1,9},{9,17},{17,25},{2,10},{10,18},{18,26},{... | collective-permute-start | bytes 1474568 | tf_op jit(solution)/shard_map/ppermute | solution.py:112
  67.6 25.5 %collective-permute-start.6 = (bf16[200,1536]{1,0:T(8,128)(2,1)}, bf16[200,1536]{1,0:T(8,128)(2,1)S(1)}, u32[]{:S(2)}, u32[]{:S(2)}) collective-permute-start(bf16[200,1536]{1,0:T(8,128)(2,1)} %copy-done.3), channel_id=1, source_target_pairs={{0,4},{4,0},{1,5},{5,1},{2,6},{6,2},{3,7},{7,3},{8,12},{12,8},{9,1... | collective-permute-start | bytes 1843208 | tf_op jit(solution)/shard_map/ppermute | solution.py:107
  76.7 1.0 copy-start.9
  77.7 1.0 copy-start.11
  84.3 1.1 copy-start.4
  84.3 10.3 %collective-permute-start.11 = (bf16[400,384]{1,0:T(8,128)(2,1)S(1)}, bf16[400,384]{1,0:T(8,128)(2,1)S(1)}, u32[]{:S(2)}, u32[]{:S(2)}) collective-permute-start(bf16[400,384]{1,0:T(8,128)(2,1)S(1)} %shard_map.153.refs_1_), channel_id=1, source_target_pairs={{0,4},{4,0},{1,5},{5,1},{2,6},{6,2},{3,7},{7,3},{8,12},{12,8},{9,1... | collective-permute-start | bytes 921608 | tf_op jit(solution)/shard_map/ppermute | solution.py:107
  87.8 4.1 %slice-start.2 = ((s8[4718592]{0:T(1024)(128)(4,1)}), s8[4194304]{0:T(1024)(128)(4,1)S(1)}, s32[]{:S(2)}) async-start(s8[4718592]{0:T(1024)(128)(4,1)} %bitcast.37), calls=%async_computation.2 | async-start | bytes 8388608
  87.8 4.1 %slice-start.3 = ((s8[4718592]{0:T(1024)(128)(4,1)}), s8[524288]{0:T(1024)(128)(4,1)S(1)}, s32[]{:S(2)}) async-start(s8[4718592]{0:T(1024)(128)(4,1)} %bitcast.37), calls=%async_computation.3 | async-start | bytes 1048576
  90.8 21.8 %collective-permute-start.17 = (bf16[200,1536]{1,0:T(8,128)(2,1)}, bf16[200,1536]{1,0:T(8,128)(2,1)}, u32[]{:S(2)}, u32[]{:S(2)}) collective-permute-start(bf16[200,1536]{1,0:T(8,128)(2,1)} %shard_map.161), channel_id=1, source_target_pairs={{0,4},{4,0},{1,5},{5,1},{2,6},{6,2},{3,7},{7,3},{8,12},{12,8},{9,1... | collective-permute-start | bytes 1843208 | tf_op jit(solution)/shard_map/ppermute | solution.py:107
  95.6 3.8 %collective-permute-start.14 = (bf16[400,768]{1,0:T(8,128)(2,1)S(1)}, bf16[400,768]{1,0:T(8,128)(2,1)S(1)}, u32[]{:S(2)}, u32[]{:S(2)}) collective-permute-start(bf16[400,768]{1,0:T(8,128)(2,1)S(1)} %fusion.29.refs_1_), channel_id=1, source_target_pairs={{0,1},{1,0},{2,3},{3,2},{4,5},{5,4},{6,7},{7,6},{8,9},{9,8},{10,11... | collective-permute-start | bytes 1843208 | tf_op jit(solution)/shard_map/ppermute | solution.py:107
  98.8 6.4 %collective-permute-start.12 = (bf16[200,768]{1,0:T(8,128)(2,1)}, bf16[200,768]{1,0:T(8,128)(2,1)}, u32[]{:S(2)}, u32[]{:S(2)}) collective-permute-start(bf16[200,768]{1,0:T(8,128)(2,1)} %fusion.50.refs_1_), channel_id=1, source_target_pairs={{0,1},{1,0},{2,3},{3,2},{4,5},{5,4},{6,7},{7,6},{8,9},{9,8},{10,11... | collective-permute-start | bytes 921608 | tf_op jit(solution)/shard_map/ppermute | solution.py:107
  99.3 4.0 %copy-start.16 = (bf16[400,768]{1,0:T(8,128)(2,1)}, bf16[400,768]{1,0:T(8,128)(2,1)S(1)}, u32[]{:S(2)}) copy-start(bf16[400,768]{1,0:T(8,128)(2,1)S(1)} %collective-permute-done.14) | copy-start | bytes 1843204
  100.3 9.9 %collective-permute-start.15 = (bf16[200,768]{1,0:T(8,128)(2,1)}, bf16[200,768]{1,0:T(8,128)(2,1)}, u32[]{:S(2)}, u32[]{:S(2)}) collective-permute-start(bf16[200,768]{1,0:T(8,128)(2,1)} %add_convert_fusion.4), channel_id=1, source_target_pairs={{0,2},{1,3},{2,0},{3,1},{4,6},{5,7},{6,4},{7,5},{8,10},{9,11},{10,... | collective-permute-start | bytes 921608 | tf_op jit(solution)/shard_map/ppermute | solution.py:107
  105.2 5.0 %copy-start.17 = (bf16[400,768]{1,0:T(8,128)(2,1)S(1)}, bf16[400,768]{1,0:T(8,128)(2,1)}, u32[]{:S(2)}) copy-start(bf16[400,768]{1,0:T(8,128)(2,1)} %copy-done.16) | copy-start | bytes 1843204
  105.2 9.0 %slice-start.4 = ((s8[4718592]{0:T(1024)(128)(4,1)}), s8[4194304]{0:T(1024)(128)(4,1)S(1)}, s32[]{:S(2)}) async-start(s8[4718592]{0:T(1024)(128)(4,1)} %bitcast.39), calls=%async_computation.4 | async-start | bytes 8388608
  106.8 9.5 %collective-permute-start.13 = (bf16[200,768]{1,0:T(8,128)(2,1)S(1)}, bf16[200,768]{1,0:T(8,128)(2,1)S(1)}, u32[]{:S(2)}, u32[]{:S(2)}) collective-permute-start(bf16[200,768]{1,0:T(8,128)(2,1)S(1)} %get-tuple-element.38), channel_id=1, source_target_pairs={{0,2},{1,3},{2,0},{3,1},{4,6},{5,7},{6,4},{7,5},{8,10},{9,11},{10,... | collective-permute-start | bytes 921608 | tf_op jit(solution)/shard_map/ppermute | solution.py:107
  110.2 4.0 %slice-start.5 = ((s8[4718592]{0:T(1024)(128)(4,1)}), s8[524288]{0:T(1024)(128)(4,1)S(1)}, s32[]{:S(2)}) async-start(s8[4718592]{0:T(1024)(128)(4,1)} %bitcast.39), calls=%async_computation.5 | async-start | bytes 1048576
  111.4 8.0 %collective-permute-start.16 = (bf16[200,768]{1,0:T(8,128)(2,1)S(1)}, bf16[200,768]{1,0:T(8,128)(2,1)S(1)}, u32[]{:S(2)}, u32[]{:S(2)}) collective-permute-start(bf16[200,768]{1,0:T(8,128)(2,1)S(1)} %add_convert_fusion.3.refs_1_), channel_id=1, source_target_pairs={{0,4},{4,0},{1,5},{5,1},{2,6},{6,2},{3,7},{7,3},{8,12},{12,8},{9,1... | collective-permute-start | bytes 921608 | tf_op jit(solution)/shard_map/ppermute | solution.py:107
  115.2 4.1 %collective-permute-start.18 = (bf16[200,768]{1,0:T(8,128)(2,1)S(1)}, bf16[200,768]{1,0:T(8,128)(2,1)S(1)}, u32[]{:S(2)}, u32[]{:S(2)}) collective-permute-start(bf16[200,768]{1,0:T(8,128)(2,1)S(1)} %fusion.51), channel_id=1, source_target_pairs={{0,1},{1,0},{2,3},{3,2},{4,5},{5,4},{6,7},{7,6},{8,9},{9,8},{10,11... | collective-permute-start | bytes 921608 | tf_op jit(solution)/shard_map/ppermute | solution.py:107
  119.5 7.1 %collective-permute-start.19 = (bf16[200,768]{1,0:T(8,128)(2,1)S(1)}, bf16[200,768]{1,0:T(8,128)(2,1)S(1)}, u32[]{:S(2)}, u32[]{:S(2)}) collective-permute-start(bf16[200,768]{1,0:T(8,128)(2,1)S(1)} %fusion.63), channel_id=1, source_target_pairs={{0,2},{1,3},{2,0},{3,1},{4,6},{5,7},{6,4},{7,5},{8,10},{9,11},{10,... | collective-permute-start | bytes 921608 | tf_op jit(solution)/shard_map/ppermute | solution.py:107

commit v5 on v4

v5 whole, which is shorter than its diff:
```python
import jax
import jax.numpy as jnp
import numpy as np
from jax import lax
from jax.experimental import pallas as pl
from jax.experimental.pallas import tpu as pltpu
from jax.sharding import PartitionSpec as P

TILE = 20


def with_halo(cells, sides, width):
    for axis, dim in sides:
        count = lax.axis_size(axis)
        ends = count - 1
        head = lax.slice_in_dim(cells, 0, width, axis=dim)
        tail = lax.slice_in_dim(cells, cells.shape[dim] - width, cells.shape[dim], axis=dim)
        cells = jnp.concatenate(
            [
                lax.ppermute(tail, axis, [(i, (i + 1) % count) for i in range(ends)]),
                cells,
                lax.ppermute(head, axis, [((i + 1) % count, i) for i in range(ends)]),
            ],
            axis=dim,
        )
    return cells


def layer_norm(vector):
    centered = vector - jnp.mean(vector, axis=-1, keepdims=True)
    variance = jnp.mean(centered * centered, axis=-1, keepdims=True)
    return centered * lax.rsqrt(variance + 1e-06)


def rms_gain(vector, scaling):
    mean_square = jnp.mean(vector * vector, axis=-1, keepdims=True)
    return vector * lax.rsqrt(mean_square + 1e-06) * scaling


def gathered_plan(
    tokens, mod_shift, mod_scale, mod_gate, w_qkv, w_mlp_in, q_gain, k_gain, w_attn_out, w_mlp_out
):
    tok_rows, model_width = tokens.shape
    tile_side = TILE
    half_side = TILE // 2
    inputs = tokens.astype(jnp.float32)
    modded = (layer_norm(inputs) * (1.0 + mod_scale) + mod_shift).astype(jnp.bfloat16)
    local_heads, head_dim = q_gain.shape
    local_width = local_heads * head_dim
    pieces = (
        lax.all_gather(w_qkv, "sx", axis=0, tiled=True),
        lax.all_gather(w_mlp_in, "sx", axis=0, tiled=True),
    )
    piece_rows = pieces[0].shape[0]
    qkv_sum = jnp.dot(
        modded, pieces[0].reshape(piece_rows, 3 * local_width), preferred_element_type=jnp.float32
    )
    mlp_sum = jnp.dot(modded, pieces[1], preferred_element_type=jnp.float32)
    qkv_parts = qkv_sum.reshape(tok_rows, 3, local_heads, head_dim)
    queries = rms_gain(qkv_parts[:, 0], q_gain).astype(jnp.bfloat16)
    key_rows = rms_gain(qkv_parts[:, 1], k_gain).astype(jnp.bfloat16)
    value_rows = qkv_parts[:, 2].astype(jnp.bfloat16)
    key_value = jnp.concatenate(
        [key_rows.reshape(tok_rows, local_width), value_rows.reshape(tok_rows, local_width)], axis=1
    )
    key_value = key_value.reshape(tile_side, tile_side, 2 * local_width)
    extended = with_halo(key_value, (("sy", 0), ("sx", 1)), half_side)
    window = extended.reshape(4 * tok_rows, 2 * local_width)
    window_keys = window[:, :local_width].reshape(4 * tok_rows, local_heads, head_dim)
    window_values = window[:, local_width:].reshape(4 * tok_rows, local_heads, head_dim)
    offsets = jnp.arange(2 * tile_side, dtype=jnp.int32)
    row_pos = lax.axis_index("sy") * tile_side - half_side + offsets
    col_pos = lax.axis_index("sx") * tile_side - half_side + offsets
    row_ok = (row_pos >= 0) & (row_pos < tile_side * lax.axis_size("sy"))
    col_ok = (col_pos >= 0) & (col_pos < tile_side * lax.axis_size("sx"))
    in_grid = (row_ok[:, None] & col_ok[None, :]).reshape(4 * tok_rows)
    scores = jnp.einsum(
        "qhd,khd->hqk", queries, window_keys, preferred_element_type=jnp.float32
    ) * head_dim ** (-0.5)
    scores = jnp.where(in_grid[None, None, :], scores, -jnp.inf)
    row_max = jnp.max(scores, axis=-1, keepdims=True)
    numerators = jnp.exp(scores - row_max)
    weights = (numerators / jnp.sum(numerators, axis=-1, keepdims=True)).astype(jnp.bfloat16)
    attended = jnp.einsum(
        "hqk,khd->qhd", weights, window_values, preferred_element_type=jnp.float32
    )
    attended = attended.astype(jnp.bfloat16).reshape(tok_rows, local_width)
    activated = jax.nn.gelu(mlp_sum, approximate=True).astype(jnp.bfloat16)
    pieces = (
        lax.all_gather(w_attn_out, "sx", axis=1, tiled=True),
        lax.all_gather(w_mlp_out, "sx", axis=1, tiled=True),
    )
    product_term = jnp.dot(attended, pieces[0], preferred_element_type=jnp.float32)
    product_term = product_term + jnp.dot(activated, pieces[1], preferred_element_type=jnp.float32)
    reduced = lax.psum_scatter(
        product_term.astype(jnp.bfloat16), "tp", scatter_dimension=1, tiled=True
    ).astype(jnp.float32)
    block_width = model_width // lax.axis_size("tp")
    first_col = lax.axis_index("tp") * block_width
    residual_part = lax.dynamic_slice_in_dim(inputs, first_col, block_width, 1)
    gate_part = lax.dynamic_slice_in_dim(mod_gate, first_col, block_width, 0)
    return (residual_part + gate_part * reduced).astype(jnp.bfloat16)


def swap(cells, axis, bit):
    count = lax.axis_size(axis)
    return lax.ppermute(cells, axis, [(i, i ^ bit) for i in range(count)])


def shift(cells, axis, step):
    count = lax.axis_size(axis)
    return lax.ppermute(
        cells, axis, [(i, i + step) for i in range(count) if 0 <= i + step < count]
    )


def dot(left, right):
    return jnp.dot(left, right, preferred_element_type=jnp.float32)


BF16, F32 = jnp.bfloat16, jnp.float32
LANES = 128
EARLY = 20_000_000
VMEM = 56
REST_VMEM = 40
POST_VMEM = 40
ROWS = 80


def width_of(total, most):
    return max(w for w in range(LANES, most + 1, LANES) if total % w == 0)


def call(body, grid, ins, outs, scratch=(), after=(), vmem=16, cost=(1000, 1000)):
    n_in, n_after = len(ins), len(after)

    def kernel(*refs):
        body(*refs[:n_in], *refs[n_in + n_after :])

    def spec(block, index):
        if block is None:
            return pl.BlockSpec(memory_space=index)
        return pl.BlockSpec(block, index)

    return pl.pallas_call(
        kernel,
        grid=(grid,),
        in_specs=[spec(b, i) for _, b, i in ins] + [pl.BlockSpec(memory_space=pl.ANY)] * n_after,
        out_specs=[spec(b, i) for _, _, b, i in outs],
        out_shape=[jax.ShapeDtypeStruct(s, d) for s, d, _, _ in outs],
        scratch_shapes=list(scratch),
        compiler_params=pltpu.CompilerParams(vmem_limit_bytes=vmem * 2**20),
        cost_estimate=pl.CostEstimate(flops=cost[0], bytes_accessed=cost[1], transcendentals=0),
    )(*[a for a, _, _ in ins], *after)


def in_order(bit, mine, other):
    return jnp.where(bit == 0, mine, other), jnp.where(bit == 0, other, mine)


def hold(cells, *earlier, cost=0):
    return pl.pallas_call(
        lambda *refs: None,
        in_specs=[pl.BlockSpec(memory_space=pl.ANY)] * (1 + len(earlier)),
        out_specs=pl.BlockSpec(memory_space=pl.ANY),
        out_shape=jax.ShapeDtypeStruct(cells.shape, cells.dtype),
        input_output_aliases={0: 0},
        compiler_params=pltpu.CompilerParams(vmem_limit_bytes=2**20),
        cost_estimate=pl.CostEstimate(flops=0, bytes_accessed=cost, transcendentals=0),
    )(cells, *earlier)


def at(*place):
    return lambda *_: place


def border_rows(tile_side):
    half = tile_side // 2
    return (half * half + 15) // 16 * 16


def border_picks(tile_side):
    half, rows = tile_side // 2, border_rows(tile_side)
    picks = np.zeros((2, 2 * rows, tile_side * tile_side), np.float32)
    for side in range(2):
        for low in range(2):
            for i in range(half):
                for j in range(half):
                    token = (low * half + i) * tile_side + j + (half if side == 0 else 0)
                    picks[side, low * rows + i * half + j, token] = 1
    return jnp.asarray(picks, BF16)


def modulate_and_heads(place, tokens, scale_row, shift_row, w_heads, after=()):
    rows, model_width = tokens.shape
    depth, width = w_heads.shape[1:]
    edge = (width - LANES) // 2
    block = max(b for b in range(16, rows + 1, 16) if rows % b == 0 and b <= ROWS)

    def body(place_ref, tokens_ref, scale_ref, shift_ref, w_heads_ref, own_ref, out_ref):
        side = place_ref[0]
        cells = tokens_ref[...].astype(F32)
        mean = jnp.mean(cells, axis=-1, keepdims=True)
        centered = cells - mean
        scaling = lax.rsqrt(jnp.mean(centered * centered, axis=-1, keepdims=True) + 1e-06)
        some = pl.ds(pl.multiple_of(side * depth, LANES), depth)
        normed = (tokens_ref[:, some].astype(F32) - mean) * scaling
        own = (normed * (1.0 + scale_ref[:, some]) + shift_ref[:, some]).astype(BF16)
        own_ref[...] = own
        theirs = pl.ds(pl.multiple_of((1 - side) * (width - edge), LANES), edge)
        for g in range(3):
            out_ref[:, g * edge : (g + 1) * edge] = dot(own, w_heads_ref[g, :, theirs]).astype(BF16)
        lane = lax.broadcasted_iota(jnp.int32, (block, LANES), 1)
        moments = jnp.zeros((block, LANES), F32)
        for first, moment in ((0, mean), (3, scaling)):
            for i in range(3):
                term = moment.astype(BF16).astype(F32)
                moments = jnp.where(lane == first + i, term, moments)
                moment = moment - term
        out_ref[:, 3 * edge :] = moments.astype(BF16)

    row = lambda i: (i, 0)
    return call(
        body, rows // block,
        [
            (place, None, pltpu.SMEM),
            (tokens, (block, model_width), row),
            (scale_row, scale_row.shape, at(0, 0)),
            (shift_row, shift_row.shape, at(0, 0)),
            (w_heads, w_heads.shape, at(0, 0, 0)),
        ],
        [
            ((rows, depth), BF16, (block, depth), row),
            ((rows, 3 * edge + LANES), BF16, (block, 3 * edge + LANES), row),
        ],
        after=after, vmem=VMEM,
    )


def border_and_hidden(place, own, picks, w_heads, hidden_weights, cut, after=()):
    rows, depth = own.shape
    half_border, width = picks.shape[1] // 2, w_heads.shape[2]

    def body(place_ref, own_ref, picks_ref, keys_ref, values_ref, w_ref, out_ref):
        taken = dot(picks_ref[place_ref[0]], own_ref[...]).astype(BF16)
        out_ref[:rows] = dot(own_ref[...], w_ref[...]).astype(BF16)
        for g, ref in enumerate((keys_ref, values_ref)):
            part = dot(taken, ref[0]).astype(BF16)
            out_ref[rows:, g * LANES : (g + 1) * LANES] = part[:half_border]
            out_ref[rows:, (2 + g) * LANES : (3 + g) * LANES] = part[half_border:]

    whole = at(0, 0)
    middle = (width - LANES) // 2 // LANES
    return call(
        body, 1,
        [(place, None, pltpu.SMEM), (own, own.shape, whole), (picks, picks.shape, at(0, 0, 0))]
        + [(w_heads, (1, depth, LANES), at(g, 0, middle)) for g in (1, 2)]
        + [(hidden_weights, (depth, cut), whole)],
        [((rows + half_border, cut), BF16, (rows + half_border, cut), whole)],
        after=after, vmem=VMEM,
    )[0]


def rest_of_first(place, own, other, picks, w_heads, hidden_weights, begin, cut, after=()):
    rows, depth = other.shape
    width, hidden = w_heads.shape[2], hidden_weights.shape[1]
    edge = (width - LANES) // 2
    border = picks.shape[1]
    block = width_of(begin, 512)
    parts = begin // block

    def body(
        place_ref, own_ref, other_ref, picks_ref, w_heads_ref, w_ref,
        qkv_ref, mine_ref, border_ref, rest_ref, a_ref, b_ref,
    ):
        side = place_ref[0]

        @pl.when(pl.program_id(0) == 0)
        def _():
            both = pl.ds(pl.multiple_of(side * edge, LANES), edge + LANES)
            mine = pl.ds(pl.multiple_of(side * (width - edge), LANES), edge)
            for g in range(3):
                qkv_ref[:, g * (edge + LANES) : (g + 1) * (edge + LANES)] = dot(own_ref[...], w_heads_ref[g, :, both])
                mine_ref[:, g * edge : (g + 1) * edge] = dot(other_ref[...], w_heads_ref[g, :, mine])
            taken = dot(picks_ref[1 - side], other_ref[...]).astype(BF16)
            for g in range(2):
                border_ref[:, g * LANES : (g + 1) * LANES] = dot(taken, w_heads_ref[1 + g, :, edge : edge + LANES])

        sums = dot(other_ref[...], w_ref[...])
        a_ref[...] = sums[:cut].astype(BF16)
        b_ref[...] = sums[cut:].astype(BF16)

        @pl.when(pl.program_id(0) >= parts)
        def _():
            rest_ref[...] = dot(own_ref[...], w_ref[...]).astype(BF16)

    whole = at(0, 0)
    column = lambda j: (0, j)
    out = lambda count, wide: ((count, wide), F32, (count, wide), whole)
    return call(
        body, hidden // block,
        [(place, None, pltpu.SMEM), (own, own.shape, whole), (other, other.shape, whole)]
        + [(a, a.shape, at(0, 0, 0)) for a in (picks, w_heads)]
        + [(hidden_weights, (depth, block), column)],
        [
            out(rows, 3 * (edge + LANES)),
            out(rows, 3 * edge),
            out(border, 2 * LANES),
            ((rows, hidden - begin), BF16, (rows, block), lambda j: (0, jnp.maximum(j - parts, 0))),
            ((cut, hidden), BF16, (cut, block), column),
            ((rows - cut, hidden), BF16, (rows - cut, block), column),
        ],
        after=after, vmem=REST_VMEM,
        cost=(
            2 * depth * (rows * 4 * width + border * 2 * LANES + rows * hidden),
            2 * depth * (2 * rows + 3 * width + hidden) + 12 * rows * width + 2 * rows * hidden,
        ),
    )


def norm_units(place, own, other, border, q_gain, k_gain, after=()):
    rows, heads, head_dim = own[0].shape[0], q_gain.shape[0], q_gain.shape[2]
    pair = heads // 2
    units = 2 * pair + 1
    half_border = border[0].shape[0] // 2
    sent_rows = (rows // 2 + 15) // 16 * 16
    sent = units * sent_rows + half_border

    def body(place_ref, *refs):
        own_refs, other_refs, border_refs = refs[:2], refs[2:4], refs[4:6]
        q_gain_ref, k_gain_ref, queries_ref, kv_ref, lower_ref, upper_ref = refs[6:]
        side = place_ref[0]
        first = side * (heads - pair)

        def head(two, index):
            some = pl.ds(pl.multiple_of(index * head_dim, LANES), head_dim)
            return sum(ref[:, some].astype(F32) for ref in two)

        def put(unit, two, p, count, index):
            q, k, v = (head(two, g * count + p) for g in range(3))
            kv = jnp.concatenate([rms_gain(k, k_gain_ref[index]), v], axis=1).astype(BF16)
            queries_ref[unit * rows : (unit + 1) * rows] = rms_gain(q, q_gain_ref[index]).astype(BF16)
            kv_ref[unit * rows : (unit + 1) * rows] = kv
            lower_ref[unit * sent_rows : (unit + 1) * sent_rows] = kv[rows - sent_rows :]
            upper_ref[unit * sent_rows : (unit + 1) * sent_rows] = kv[:sent_rows]

        for p in range(pair):
            put(2 * p, own_refs, side + p, pair + 1, first + p)
            put(2 * p + 1, other_refs, p, pair, first + p)
        put(2 * pair, own_refs, (1 - side) * pair, pair + 1, pair)
        got = border_refs[1][rows:].astype(F32)
        got = jnp.concatenate([got[:, : 2 * head_dim], got[:, 2 * head_dim : 4 * head_dim]], axis=0)
        both = border_refs[0][...] + got
        kv = [rms_gain(both[:, :head_dim], k_gain_ref[pair]), both[:, head_dim:]]
        kv = jnp.concatenate(kv, axis=1).astype(BF16)
        kv_ref[units * rows :] = kv
        upper_ref[units * sent_rows :] = kv[:half_border]
        lower_ref[units * sent_rows :] = kv[half_border:]

    whole = at(0, 0)
    out = lambda count, width: ((count, width), BF16, (count, width), whole)
    ins = [*own, *other, *border]
    return call(
        body, 1,
        [(place, None, pltpu.SMEM)]
        + [(a, a.shape, whole) for a in ins]
        + [(g, g.shape, at(0, 0, 0)) for g in (q_gain, k_gain)],
        [
            out(units * rows, head_dim),
            out(units * rows + 2 * half_border, 2 * head_dim),
            out(sent, 2 * head_dim),
            out(sent, 2 * head_dim),
        ],
        after=after, vmem=POST_VMEM,
    )


def window_codes(tile_side):
    rows, half = tile_side * tile_side, tile_side // 2
    sent_rows = (rows // 2 + 15) // 16 * 16
    extra = sent_rows - rows // 2
    column = np.arange(rows) % tile_side

    def lines(first, second):
        above = lambda on: np.concatenate([np.zeros(extra, np.int32), 2 * on[rows - rows // 2 :]])
        below = lambda on: np.concatenate([3 * on[: rows // 2], np.zeros(extra, np.int32)])
        return np.concatenate([first, second, above(first), above(second), below(first), below(second)])

    def padded(line):
        return np.pad(line, (0, -len(line) % LANES)).astype(np.float32)

    every = np.ones(rows, np.int32)
    right, left = (column >= half).astype(np.int32), (column < half).astype(np.int32)
    by_side = np.stack([
        np.stack([padded(lines(every, left)), padded(lines(right, every))]),
        np.stack([padded(lines(every, right)), padded(lines(left, every))]),
    ])
    pad = border_rows(tile_side)
    part = np.pad(np.ones(half * half, np.int32), (0, pad - half * half))
    above = np.concatenate([np.zeros(extra, np.int32), 2 * np.ones(rows // 2, np.int32), 2 * part])
    below = np.concatenate([3 * np.ones(rows // 2, np.int32), np.zeros(extra, np.int32), 3 * part])
    middle = padded(np.concatenate([every, part, part, above, below]))[None]
    return jnp.asarray(by_side), jnp.asarray(middle)


def attend(place, queries, keys_values, above, below, codes, middle_codes, heads, after=()):
    pair = heads // 2
    units = 2 * pair + 1
    head_dim = queries.shape[1]
    rows = queries.shape[0] // units
    border = keys_values.shape[0] - units * rows
    sent_rows = (above.shape[0] - border // 2) // units

    def body(place_ref, queries_ref, kv_ref, above_ref, below_ref, codes_ref, middle_ref, out_ref):
        side = place_ref[0]

        def unit_rows(ref, unit, count, size):
            return ref[unit * size : (unit + count) * size]

        def rest_rows(ref, size):
            return ref[units * size :]

        def one(unit, blocks, line, column):
            there = (line == 1) | ((line == 2) & (place_ref[2] == 1)) | ((line == 3) & (place_ref[3] == 1))
            line = jnp.where(there, 0.0, -jnp.inf)
            spare = line.shape[1] - sum(b.shape[0] for b in blocks)
            if spare:
                blocks = blocks + [jnp.zeros((spare, 2 * head_dim), BF16)]
            both = jnp.concatenate(blocks, axis=0)
            keys, values = both[:, :head_dim], both[:, head_dim:]
            mine = unit_rows(queries_ref, unit, 1, rows)
            scores = lax.dot_general(mine, keys, (((1,), (1,)), ((), ())), preferred_element_type=F32)
            scores = scores * head_dim ** (-0.5) + line
            numerators = jnp.exp(scores - jnp.max(scores, axis=-1, keepdims=True))
            total = jnp.sum(numerators, axis=-1, keepdims=True)
            got = (dot(numerators.astype(BF16), values) / total).astype(BF16)
            out_ref[:, column * head_dim : (column + 1) * head_dim] = got

        for p in range(pair):
            blocks = [
                unit_rows(kv_ref, 2 * p, 2, rows),
                unit_rows(above_ref, 2 * p, 2, sent_rows),
                unit_rows(below_ref, 2 * p, 2, sent_rows),
            ]
            one(2 * p, blocks, codes_ref[side][0:1], p)
            one(2 * p + 1, blocks, codes_ref[side][1:2], pair + 1 + p)
        blocks = [
            kv_ref[2 * pair * rows :],
            above_ref[2 * pair * sent_rows :],
            below_ref[2 * pair * sent_rows :],
        ]
        one(2 * pair, blocks, middle_ref[...], pair)

    ins = [queries, keys_values, above, below, middle_codes]
    whole = [(a, a.shape, at(0, 0)) for a in ins]
    return call(
        body, 1,
        [(place, None, pltpu.SMEM)] + whole[:4] + [(codes, codes.shape, at(0, 0, 0))] + whole[4:],
        [((rows, units * head_dim), BF16, (rows, units * head_dim), at(0, 0))],
        after=after, vmem=POST_VMEM,
    )[0]


def paired_plan(
    tokens, mod_shift, mod_scale, mod_gate, w_qkv, w_mlp_in, q_gain, k_gain, w_attn_out, w_mlp_out
):
    tok_rows, model_width = tokens.shape
    half_width, hidden = w_mlp_in.shape
    heads, head_dim = q_gain.shape
    width = heads * head_dim
    side = lax.axis_index("sx")
    part = lax.axis_index("tp")
    core, far = part % 2, part // 2
    mid = hidden // 2
    block = half_width // 2
    row = lax.axis_index("sy")
    place = jnp.stack([side, core, row > 0, row < lax.axis_size("sy") - 1]).astype(jnp.int32)
    picks = border_picks(TILE)
    q_gain, k_gain = q_gain[:, None, :], k_gain[:, None, :]

    quarter = half_width // 4
    other_first = (1 - side) * half_width + part * quarter
    sent = lax.dynamic_slice_in_dim(lax.optimization_barrier(tokens), other_first, quarter, 1)
    piece = swap(sent, "sx", 1)
    first = side * half_width
    gain_part = 1.0 + lax.dynamic_slice_in_dim(mod_scale, first, half_width, 0)
    shift_part = lax.dynamic_slice_in_dim(mod_shift, first, half_width, 0)

    def modulate(cells, pair):
        cells = (cells.astype(F32) - pair[0]) * pair[1]
        return (cells * gain_part + shift_part).astype(BF16)

    pair = heads // 2
    edge = pair * head_dim
    w_heads = jnp.transpose(w_qkv, (1, 0, 2))

    own, own_early = modulate_and_heads(place, tokens, mod_scale[None], mod_shift[None], w_heads, [sent])
    got_early = swap(own_early, "sx", 1)
    piece = hold(piece, own_early)
    pieces = in_order(far, piece, hold(swap(piece, "tp", 2), got_early))
    first_part = width_of(hidden // 3, hidden)
    own_first = border_and_hidden(place, own, picks, w_heads, w_mlp_in, first_part, [own_early, piece])
    got_first = swap(own_first, "sx", 1)
    pieces = hold(jnp.concatenate(pieces, axis=1), got_early, own_first)
    near = swap(pieces, "tp", 1)
    even, odd = in_order(core, pieces, near)
    other = jnp.concatenate([even[:, :quarter], odd[:, :quarter], even[:, quarter:], odd[:, quarter:]], axis=1)
    terms = [got_early[:, 3 * edge + i : 3 * edge + i + 1].astype(F32) for i in range(6)]
    other = modulate(other, [terms[i] + terms[i + 1] + terms[i + 2] for i in (0, 3)])
    late_first = (1 - side) * edge
    other_late = [
        dot(other, lax.dynamic_slice(w_heads, (g, 0, late_first), (1, half_width, edge + head_dim))[0]).astype(BF16)
        for g in range(3)
    ]
    other_late = jnp.concatenate(other_late, axis=1)
    got_late = swap(other_late, "sx", 1)
    cut = tok_rows // 2
    own_heads, other_heads, other_border, own_rest, other_a, other_b = rest_of_first(
        place, own, other, picks, w_heads, w_mlp_in, first_part, cut, [other_late, got_first]
    )
    got_rest = swap(own_rest, "sx", 1)
    queries, keys_values, lower, upper = norm_units(
        place, (own_heads, got_late), (other_heads, got_early), (other_border, got_first), q_gain, k_gain, [other_a]
    )
    above = shift(lower, "sy", 1)
    below = shift(upper, "sy", -1)

    sent_mlp, kept_mlp, sent_attn, kept_attn = (
        lax.dynamic_slice_in_dim(w, start * block, block, 1)
        for w in (w_mlp_out, w_attn_out)
        for start in (1 - core, core)
    )

    def activate(mine, got, *earlier):
        got = hold(got, *earlier) if earlier else got
        return hold(jax.nn.gelu(mine.astype(F32) + got.astype(F32), approximate=True).astype(BF16))

    attended = attend(place, queries, keys_values, above, below, *window_codes(TILE), heads)
    got_attended = swap(attended, "sx", 1)
    got_other_a = swap(other_a, "sx", 1)
    got_own = jnp.concatenate([got_first[:tok_rows], hold(got_rest, attended)], axis=1)
    own_hidden = jnp.concatenate([own_first[:tok_rows], own_rest], axis=1)
    other_active = activate(jnp.concatenate([other_a, other_b], axis=0), got_own)
    other_sent, other_kept = dot(other_active, sent_mlp), dot(other_active, kept_mlp)
    got_other_b = swap(hold(other_b, other_sent), "sx", 1)

    def own_part(begin, end, got, *earlier):
        active, heads_part = activate(own_hidden[begin:end], got, *earlier), own_attended[begin:end]
        return (
            (dot(active, sent_mlp) + dot(heads_part, sent_attn)).astype(BF16),
            dot(active, kept_mlp) + dot(heads_part, kept_attn),
        )

    got_attended = hold(got_attended, other_sent, other_kept, got_other_a)
    here = edge + head_dim

    def natural(mine, middle, theirs):
        return jnp.concatenate(
            [jnp.where(side == 0, mine, theirs), middle, jnp.where(side == 0, theirs, mine)], axis=1
        )

    own_attended = natural(attended[:, :edge], attended[:, edge:here], got_attended[:, here:])
    other_attended = natural(attended[:, here:], got_attended[:, edge:here], got_attended[:, :edge])
    other_sent = (other_sent + dot(other_attended, sent_attn)).astype(BF16)
    other_kept = other_kept + dot(other_attended, kept_attn)
    other_come = swap(other_sent, "tp", 1)
    own_sent_a, own_kept_a = own_part(0, cut, got_other_a, other_sent, other_kept)

    def rows_of(half):
        kept = jnp.where(half == 0, other_kept[:cut], other_kept[cut:])
        return kept + jnp.where(half == 0, other_come[:cut], other_come[cut:]).astype(F32)

    passed = rows_of(1 - far).astype(BF16)
    passed = hold(swap(passed, "tp", 2), own_sent_a, own_kept_a)
    crossing = (rows_of(far) + passed.astype(F32)).astype(BF16)
    got = swap(crossing, "sx", 1)
    own_sum_a = own_kept_a + swap(own_sent_a, "tp", 1).astype(F32)
    come_a = swap(own_sum_a.astype(BF16), "tp", 2)
    own_sent_b, own_kept_b = own_part(cut, tok_rows, got_other_b, crossing)
    own_sum_b = hold(own_kept_b, got, come_a, cost=EARLY) + swap(own_sent_b, "tp", 1).astype(F32)

    home = far == side
    come_b = swap(jnp.where(home, got, own_sum_b.astype(BF16)), "tp", 2)
    wide = got.astype(F32)
    known = jnp.concatenate(
        [
            jnp.where(home, own_sum_a + come_a.astype(F32), jnp.where(far == 0, wide, 0.0)),
            jnp.where(home, own_sum_b, jnp.where(far == 0, 0.0, wide)),
        ],
        axis=0,
    )
    first_col = hold(part[None], own_sent_a)[0] * block
    gate_part = lax.dynamic_slice_in_dim(mod_gate, first_col, block, 0)
    residual_part = lax.dynamic_slice_in_dim(tokens, first_col, block, 1).astype(F32)
    known = hold(residual_part + gate_part * known)
    late_first = jnp.where(home, 1, 1 - far) * cut
    token = lax.broadcasted_iota(jnp.int32, (tok_rows, 1), 0)
    late = (token >= late_first) & (token < late_first + cut)
    late_part = jnp.concatenate([come_b, come_b], axis=0).astype(F32)
    return (known + jnp.where(late, gate_part * late_part, 0.0)).astype(BF16)


def shards(*arrays):
    local_heads = arrays[6].shape[0]
    if lax.axis_size("sx") == 2 and lax.axis_size("tp") == 4 and local_heads % 2 and local_heads > 1 and arrays[6].shape[1] == LANES:
        return paired_plan(*arrays)
    return gathered_plan(*arrays)


def solution(mesh):
    placed = (
        P(("sy", "sx"), None),
        P(),
        P(),
        P(),
        P("sx", None, "tp"),
        P("sx", "tp"),
        P("tp", None),
        P("tp", None),
        P("tp", "sx"),
        P("tp", "sx"),
    )
    return jax.shard_map(
        shards, mesh=mesh, in_specs=placed, out_specs=P(("sy", "sx"), "tp"), check_vma=False
    )
```

time: 128 us -> 127 us (level)
  Pallas kernels: 16.7 us -> 27.5 us
  waiting for transfers between devices: 33.1 us -> 43.5 us
  other arithmetic: 19.3 us -> 11.9 us
  matrix products: 20.3 us -> 14.6 us
  starting transfers between devices: 24.4 us -> 19.9 us
  local copies, waits for them, and re-layouts: 12 us -> 7.92 us
    pallas_call x3 -> x5, Pallas kernels: 15.7 us -> 26.9 us  [call(): pl.pallas_call(kernel, grid=(grid,), in_specs=[spec(b, i) for _, b, i in...]
    ppermute x18 -> x17, waiting for transfers between devices: 25.6 us -> 35.2 us  [swap(): return lax.ppermute(cells, axis, [(i, i ^ bit) for i in range(count)])]
    dot_general x20 -> x15, matrix products: 20.3 us -> 14.6 us  [dot(): return jnp.dot(left, right, preferred_element_type=jnp.float32)]
    reduce_sum x2 -> x0, other arithmetic: 4.73 us -> none  [the longest x1 2.62 us: paired_plan(): jnp.mean(centered * centered, axis=-1, keepdims=True) + 1e-06]
    ppermute x18 -> x17, starting transfers between devices: 17.7 us -> 14.8 us  [swap(): return lax.ppermute(cells, axis, [(i, i ^ bit) for i in range(count)])]
    unnamed x70 -> x50, local copies, waits for them, and re-layouts: 7.99 us -> 5.64 us
    squeeze x1 -> x0, local copies, waits for them, and re-layouts: 1.88 us -> none  [paired_plan(): w_queries, w_keys, w_values = [w_qkv[:, group] for group in range(3)]]
    ppermute x2, starting transfers between devices: 6.63 us -> 5.1 us  [shift(): lax.ppermute(cells, axis, [(i, i + step) for i in range(count) if 0 <= i...]
  transfers between devices with their start and end apart: 20 -> 19, of which waited for: 9 -> 10; matrix products, arithmetic and copies ran while one was open for 32% -> 19% of each run, Pallas kernels for 13% -> 22%
where the time goes in v5:
time: 127 us; the launch traced here: 126 us
  waiting for transfers between devices  43.5 us (34%)
  Pallas kernels  27.5 us (22%)
  starting transfers between devices  19.9 us (16%)
  matrix products  14.6 us (11%)
  other arithmetic  11.9 us (9%)
  local copies, waits for them, and re-layouts  7.92 us (6%)
    ppermute x17, waiting for transfers between devices, swap(): return lax.ppermute(cells, axis, [(i, i ^ bit) for i in range(count)])  35.2 us
    pallas_call x5, Pallas kernels, call(): pl.pallas_call(kernel, grid=(grid,), in_specs=[spec(b, i) for _, b, i in...  26.9 us
    ppermute x17, starting transfers between devices, swap(): return lax.ppermute(cells, axis, [(i, i ^ bit) for i in range(count)])  14.8 us
    dot_general x15, matrix products, dot(): return jnp.dot(left, right, preferred_element_type=jnp.float32)  14.6 us
    ppermute x2, waiting for transfers between devices, shift(): lax.ppermute(cells, axis, [(i, i + step) for i in range(count) if 0 <= i...  8.33 us
    unnamed x50, local copies, waits for them, and re-layouts  5.64 us
    ppermute x2, starting transfers between devices, shift(): lax.ppermute(cells, axis, [(i, i + step) for i in range(count) if 0 <= i...  5.1 us
    convert_element_type x3, other arithmetic, activate(): jax.nn.gelu(mine.astype(F32) + got.astype(F32), approximate=True)  4.02 us
  transfers between devices with their start and end apart: 19, of which 10 were waited for; matrix products, arithmetic and copies ran while one was open for 19% of the time, Pallas kernels for 22%

profile of v5, /device:TPU:0, one launch (start us, length us, event | category | flops | bytes accessed | tf_op | source)
XLA Modules:
  0.0 126.4 jit_solution(3214229817427019708)
XLA Ops:
  0.0 1.1 constant_dynamic-slice_fusion.refs_5_
  1.1 3.0 %collective-permute-start = (bf16[400,384]{1,0:T(8,128)(2,1)S(1)}, bf16[400,384]{1,0:T(8,128)(2,1)}, u32[]{:S(2)}, u32[]{:S(2)}) collective-permute-start(bf16[400,384]{1,0:T(8,128)(2,1)S(1)} %constant_dynamic-slice_fusion.refs_5_), channel_id=1, source_target_pairs={{0,4},{4,0},{1,5},{5,1},{2,6},{6,2},{3,7},{7,3},{8,12},{12,8},{9,1... | collective-permute-start | bytes 921608 | tf_op jit(solution)/shard_map/ppermute | solution.py:107
  4.1 0.6 pad_add_fusion.refs_0_
  4.8 7.1 %shard_map.127 = (bf16[400,1536]{1,0:T(8,128)(2,1)}, bf16[400,512]{1,0:T(8,128)(2,1)}) custom-call(s32[4]{0:T(128)} %pad_add_fusion.refs_0_, bf16[400,3072]{1,0:T(8,128)(2,1)} %refs_1_.1, f32[1,3072]{1,0:T(1,128)} %bitcast.34, f32[1,3072]{1,0:T(1,128)} %bitcast.33, bf16[3,1536,384]{2,1,0:T(8,128)(2,1)} %bitcast.27, bf16[400,384]{1,0:T(8,128)(2,1)} %copy-done.18), custom_call_target="tpu_custom_call" | custom-call | flops 1000 | bytes 1000 | tf_op jit(solution)/shard_map/pallas_call | solution.py:145
  11.9 1.0 copy-done.6
  12.9 2.0 %collective-permute-start.1 = (bf16[400,384]{1,0:T(8,128)(2,1)}, bf16[400,384]{1,0:T(8,128)(2,1)S(1)}, u32[]{:S(2)}, u32[]{:S(2)}) collective-permute-start(bf16[400,384]{1,0:T(8,128)(2,1)} %shard_map.128.refs_7_), channel_id=1, source_target_pairs={{0,2},{1,3},{2,0},{3,1},{4,6},{5,7},{6,4},{7,5},{8,10},{9,11},{10,... | collective-permute-start | bytes 921608 | tf_op jit(solution)/shard_map/ppermute | solution.py:107
  14.9 4.5 %shard_map.129.refs_2_ = bf16[512,512]{1,0:T(8,128)(2,1)} custom-call(s32[4]{0:T(128)} %pad_add_fusion.refs_0_, bf16[400,1536]{1,0:T(8,128)(2,1)} %get-tuple-element.17.refs_1_, bf16[2,224,400]{2,1,0:T(8,128)(2,1)} %constant.75.clone.refs_2_.refs_3_, bf16[3,1536,384]{2,1,0:T(8,128)(2,1)} %bitcast.28, bf16[3,1536,384]{2,1,0:T(8,128)(2,1)} %bitcast.29, ...), custom_call_target="tpu_custom_call" | custom-call | flops 1000 | bytes 1000 | tf_op jit(solution)/shard_map/pallas_call | solution.py:145
  19.4 3.6 %collective-permute-done.2.refs_1_.refs_4_ = bf16[400,512]{1,0:T(8,128)(2,1)S(1)} collective-permute-done((bf16[400,512]{1,0:T(8,128)(2,1)}, bf16[400,512]{1,0:T(8,128)(2,1)S(1)}, u32[]{:S(2)}, u32[]{:S(2)}) %collective-permute-start.2) | collective-permute-done | bytes 409632 | tf_op jit(solution)/shard_map/ppermute | solution.py:107
  23.0 1.1 broadcast_select_fusion.3
  24.3 0.6 copy-done.19
  25.0 0.6 collective-permute-start.4
  25.6 0.4 add_reduce_fusion.1
  26.6 0.5 add_convert_fusion.refs_2_
  27.1 1.3 %copy-done.1 = bf16[1536,3,384]{2,0,1:T(8,128)(2,1)S(1)} copy-done((bf16[1536,3,384]{2,0,1:T(8,128)(2,1)S(1)}, bf16[1536,3,384]{2,0,1:T(8,128)(2,1)}, u32[]{:S(2)}) %copy-start.1) | copy-done | bytes 3538968
  28.4 0.5 convolution_convert_fusion.1
  28.9 0.5 convolution_convert_fusion.2
  29.4 0.5 convolution_convert_fusion
  30.0 1.2 collective-permute-start.7
  31.2 8.6 %collective-permute-done.4.refs_7_.refs_6_ = bf16[512,512]{1,0:T(8,128)(2,1)S(1)} collective-permute-done((bf16[512,512]{1,0:T(8,128)(2,1)S(1)}, bf16[512,512]{1,0:T(8,128)(2,1)S(1)}, u32[]{:S(2)}, u32[]{:S(2)}) %collective-permute-start.4) | collective-permute-done | bytes 524320 | tf_op jit(solution)/shard_map/ppermute | solution.py:107
  39.8 9.3 %shard_map.132 = (f32[400,768]{1,0:T(8,128)S(1)}, f32[400,384]{1,0:T(8,128)S(1)}, f32[224,256]{1,0:T(8,128)S(1)}, bf16[400,1024]{1,0:T(8,128)(2,1)}, bf16[200,15...) custom-call(s32[4]{0:T(128)S(1)} %copy-done.14, bf16[400,1536]{1,0:T(8,128)(2,1)S(1)} %copy-done.7, ...), custom_call_target="tpu_custom_call" | custom-call | flops 3951034368 | bytes 13787136 | tf_op jit(solution)/shard_map/pallas_call | solution.py:145
  49.2 0.6 collective-permute-start.6
  49.8 3.2 %collective-permute-done.7.refs_2_ = bf16[400,768]{1,0:T(8,128)(2,1)S(1)} collective-permute-done((bf16[400,768]{1,0:T(8,128)(2,1)S(1)}, bf16[400,768]{1,0:T(8,128)(2,1)S(1)}, u32[]{:S(2)}, u32[]{:S(2)}) %collective-permute-start.7) | collective-permute-done | bytes 614432 | tf_op jit(solution)/shard_map/ppermute | solution.py:107
  53.0 1.9 %shard_map.133 = (bf16[1200,128]{1,0:T(8,128)(2,1)S(1)}, bf16[1424,256]{1,0:T(8,128)(2,1)S(1)}, bf16[736,256]{1,0:T(8,128)(2,1)}, bf16[736,256]{1,0:T(8,128)(2,1)}) custom-call(s32[4]{0:T(128)S(1)} %copy-done.14, f32[400,768]{1,0:T(8,128)S(1)} %get-tuple-element.22.refs_1_, bf16[400,768]{1,0:T(8,128)(2,1)S(1)} %collective-permute-done.7.refs_2_, ...), custom_call_target="tpu_custom_call" | custom-call | flops 1000 | bytes 1000 | tf_op jit(solution)/shard_map/pallas_call | solution.py:145
  54.9 0.9 copy-done.8
  55.8 0.7 copy-done.11
  56.5 3.6 %collective-permute-start.8 = (bf16[736,256]{1,0:T(8,128)(2,1)}, bf16[736,256]{1,0:T(8,128)(2,1)S(1)}, u32[]{:S(2)}, u32[]{:S(2)}) collective-permute-start(bf16[736,256]{1,0:T(8,128)(2,1)} %get-tuple-element.27), channel_id=1, source_target_pairs={{0,8},{8,16},{16,24},{1,9},{9,17},{17,25},{2,10},{10,18},{18,26},{... | collective-permute-start | bytes 1130504 | tf_op jit(solution)/shard_map/ppermute | solution.py:112
  60.1 1.5 %collective-permute-start.9 = (bf16[736,256]{1,0:T(8,128)(2,1)}, bf16[736,256]{1,0:T(8,128)(2,1)}, u32[]{:S(2)}, u32[]{:S(2)}) collective-permute-start(bf16[736,256]{1,0:T(8,128)(2,1)} %get-tuple-element.28), channel_id=1, source_target_pairs={{8,0},{16,8},{24,16},{9,1},{17,9},{25,17},{10,2},{18,10},{26,18},{... | collective-permute-start | bytes 1130504 | tf_op jit(solution)/shard_map/ppermute | solution.py:112
  61.7 0.7 collective-permute-start.5
  62.4 4.2 %collective-permute-done.8.refs_3_ = bf16[736,256]{1,0:T(8,128)(2,1)S(1)} collective-permute-done((bf16[736,256]{1,0:T(8,128)(2,1)}, bf16[736,256]{1,0:T(8,128)(2,1)S(1)}, u32[]{:S(2)}, u32[]{:S(2)}) %collective-permute-start.8) | collective-permute-done | bytes 376864 | tf_op jit(solution)/shard_map/ppermute | solution.py:112
  66.5 4.1 %collective-permute-done.9.refs_4_ = bf16[736,256]{1,0:T(8,128)(2,1)} collective-permute-done((bf16[736,256]{1,0:T(8,128)(2,1)}, bf16[736,256]{1,0:T(8,128)(2,1)}, u32[]{:S(2)}, u32[]{:S(2)}) %collective-permute-start.9) | collective-permute-done | bytes 376864 | tf_op jit(solution)/shard_map/ppermute | solution.py:112
  70.7 0.7 copy-done.15
  71.4 4.1 %shard_map.134.refs_1_ = bf16[400,384]{1,0:T(8,128)(2,1)S(1)} custom-call(s32[4]{0:T(128)S(1)} %copy-done.14, bf16[1200,128]{1,0:T(8,128)(2,1)S(1)} %copy-done.12, bf16[1424,256]{1,0:T(8,128)(2,1)S(1)} %copy-done.9, bf16[736,256]{1,0:T(8,128)(2,1)S(1)} %collective-permute-done.8.refs_3_, bf16[736,256]{1,0:T(8,128)(2,1)} %collective-permute-done.9.refs_4_, ...), custom_call_target="tpu_custom_call" | custom-call | flops 1000 | bytes 1000 | tf_op jit(solution)/shard_map/pallas_call | solution.py:145
  75.6 0.7 collective-permute-start.10
  76.2 0.4 copy-done.4
  76.7 1.0 fusion.7.refs_0_
  77.8 2.9 %fusion.18.refs_1_ = f32[400,768]{1,0:T(8,128)S(1)} fusion(bf16[400,1536]{1,0:T(8,128)(2,1)S(1)} %shard_map.136, bf16[1536,1536]{1,0:T(8,128)(2,1)} %param.22, s32[]{:T(128)S(6)} %select_n.148), kind=kOutput, calls=%fused_computation.22 | convolution fusion | flops 943718400 | bytes 4816900 | tf_op jit(solution)/shard_map/dot_general | solution.py:118
  80.7 1.0 collective-permute-start.16
  81.7 1.1 fusion.12.refs_2_
  82.9 0.8 collective-permute-done.5.refs_3_.refs_0_
  83.7 6.6 %collective-permute-done.10.refs_0_ = bf16[400,384]{1,0:T(8,128)(2,1)S(1)} collective-permute-done((bf16[400,384]{1,0:T(8,128)(2,1)S(1)}, bf16[400,384]{1,0:T(8,128)(2,1)S(1)}, u32[]{:S(2)}, u32[]{:S(2)}) %collective-permute-start.10) | collective-permute-done | bytes 307232 | tf_op jit(solution)/shard_map/ppermute | solution.py:107
  90.4 0.5 fusion.20.refs_1_
  90.9 0.5 convolution_add_fusion.refs_2_
  91.4 1.5 %fusion.40.refs_0_ = bf16[200,1536]{1,0:T(8,128)(2,1)S(1)} fusion(bf16[200,1536]{1,0:T(8,128)(2,1)S(1)} %shard_map.138, bf16[400,512]{1,0:T(8,128)(2,1)S(1)} %slice.108, bf16[400,1024]{1,0:T(8,128)(2,1)} %get-tuple-element.19), kind=kLoop, calls=%fused_computation.38 | loop fusion | flops 4608000 | bytes 2457600 | tf_op jit(solution)/shard_map/convert_element_type | solution.py:536
  93.0 0.3 fusion.72
  93.3 0.7 fusion.53.refs_1_
  94.0 0.6 collective-permute-start.11
  95.0 1.6 %collective-permute-start.14 = (bf16[200,768]{1,0:T(8,128)(2,1)S(1)}, bf16[200,768]{1,0:T(8,128)(2,1)S(1)}, u32[]{:S(2)}, u32[]{:S(2)}) collective-permute-start(bf16[200,768]{1,0:T(8,128)(2,1)S(1)} %add_convert_fusion.3), channel_id=1, source_target_pairs={{0,2},{1,3},{2,0},{3,1},{4,6},{5,7},{6,4},{7,5},{8,10},{9,11},{10,... | collective-permute-start | bytes 921608 | tf_op jit(solution)/shard_map/ppermute | solution.py:107
  96.6 0.3 fusion.70
  96.9 1.4 %fusion.75 = (bf16[200,768]{1,0:T(8,128)(2,1)}, f32[200,768]{1,0:T(8,128)S(1)}) fusion(bf16[200,768]{1,0:T(8,128)(2,1)S(1)} %collective-permute-done.11, f32[200,768]{1,0:T(8,128)S(1)} %fusion.67, bf16[200,1536]{1,0:T(8,128)(2,1)S(1)} %shard_map.139, bf16[1536,1536]{1,0:T(8,128)(2,1)S(1)} %bitcast.32, s32[]{:T(128)S(6)} %select_n.150), kind=kOutput, calls=%fused_computation.87 | convolution fusion | flops 472473600 | bytes 4816900 | tf_op jit(solution)/shard_map/dot_general | solution.py:118
  98.4 0.5 collective-permute-start.12
  98.9 6.3 %collective-permute-done.14.refs_0_ = bf16[200,768]{1,0:T(8,128)(2,1)S(1)} collective-permute-done((bf16[200,768]{1,0:T(8,128)(2,1)S(1)}, bf16[200,768]{1,0:T(8,128)(2,1)S(1)}, u32[]{:S(2)}, u32[]{:S(2)}) %collective-permute-start.14) | collective-permute-done | bytes 307232 | tf_op jit(solution)/shard_map/ppermute | solution.py:107
  105.4 0.7 collective-permute-start.15
  106.0 1.5 %fusion.48.refs_0_ = bf16[200,1536]{1,0:T(8,128)(2,1)S(1)} fusion(bf16[200,1536]{1,0:T(8,128)(2,1)S(1)} %shard_map.143, bf16[400,1024]{1,0:T(8,128)(2,1)} %get-tuple-element.19, bf16[400,512]{1,0:T(8,128)(2,1)S(1)} %slice.108), kind=kLoop, calls=%fused_computation.46 | loop fusion | flops 4608000 | bytes 2457600 | tf_op jit(solution)/shard_map/convert_element_type | solution.py:536
  107.6 1.4 %fusion.50 = bf16[200,768]{1,0:T(8,128)(2,1)} fusion(f32[200,768]{1,0:T(8,128)S(1)} %fusion.70, bf16[200,1536]{1,0:T(8,128)(2,1)S(1)} %shard_map.144, bf16[1536,1536]{1,0:T(8,128)(2,1)S(1)} %bitcast.32, s32[]{:T(128)S(6)} %select_n.148), kind=kOutput, calls=%fused_computation.52 | convolution fusion | flops 472166400 | bytes 3895300 | tf_op jit(solution)/shard_map/dot_general | solution.py:118
  109.0 1.1 fusion.65
  110.1 0.5 shard_map.140
  111.2 0.8 dynamic_slice.38
  112.0 2.4 %fusion.30.refs_0_ = f32[200,768]{1,0:T(8,128)S(1)} fusion(f32[200,768]{1,0:T(8,128)} %fusion.65, bf16[200,1536]{1,0:T(8,128)(2,1)S(1)} %shard_map.144, bf16[1536,1536]{1,0:T(8,128)(2,1)} %param.22, s32[]{:T(128)S(6)} %select_n.150), kind=kOutput, calls=%fused_computation.30 | convolution fusion | flops 472012800 | bytes 4202500 | tf_op jit(solution)/shard_map/dot_general | solution.py:118
  114.5 1.1 fusion.77
  115.6 1.6 %collective-permute-start.18 = (bf16[200,768]{1,0:T(8,128)(2,1)S(1)}, bf16[200,768]{1,0:T(8,128)(2,1)S(1)}, u32[]{:S(2)}, u32[]{:S(2)}) collective-permute-start(bf16[200,768]{1,0:T(8,128)(2,1)S(1)} %fusion.77), channel_id=1, source_target_pairs={{0,2},{1,3},{2,0},{3,1},{4,6},{5,7},{6,4},{7,5},{8,10},{9,11},{10,... | collective-permute-start | bytes 921608 | tf_op jit(solution)/shard_map/ppermute | solution.py:107
  117.2 1.2 fusion.62
  118.4 1.2 fusion.49.refs_0_
  119.7 5.7 %collective-permute-done.18 = bf16[200,768]{1,0:T(8,128)(2,1)S(1)} collective-permute-done((bf16[200,768]{1,0:T(8,128)(2,1)S(1)}, bf16[200,768]{1,0:T(8,128)(2,1)S(1)}, u32[]{:S(2)}, u32[]{:S(2)}) %collective-permute-start.18) | collective-permute-done | bytes 307232 | tf_op jit(solution)/shard_map/ppermute | solution.py:107
  125.4 1.1 add_convert_fusion.1
  (89 shorter events, 2.0 us)
Async XLA Ops:
  0.0 90.4 %copy-start = (bf16[384,1536]{1,0:T(8,128)(2,1)S(1)}, bf16[384,1536]{1,0:T(8,128)(2,1)}, u32[]{:S(2)}) copy-start(bf16[384,1536]{1,0:T(8,128)(2,1)} %param.21) | copy-start | bytes 3538948
  1.1 3.7 %copy-start.18 = (bf16[400,384]{1,0:T(8,128)(2,1)}, bf16[400,384]{1,0:T(8,128)(2,1)S(1)}, u32[]{:S(2)}) copy-start(bf16[400,384]{1,0:T(8,128)(2,1)S(1)} %constant_dynamic-slice_fusion.refs_5_) | copy-start | bytes 921604
  1.1 10.8 %collective-permute-start = (bf16[400,384]{1,0:T(8,128)(2,1)S(1)}, bf16[400,384]{1,0:T(8,128)(2,1)}, u32[]{:S(2)}, u32[]{:S(2)}) collective-permute-start(bf16[400,384]{1,0:T(8,128)(2,1)S(1)} %constant_dynamic-slice_fusion.refs_5_), channel_id=1, source_target_pairs={{0,4},{4,0},{1,5},{5,1},{2,6},{6,2},{3,7},{7,3},{8,12},{12,8},{9,1... | collective-permute-start | bytes 921608 | tf_op jit(solution)/shard_map/ppermute | solution.py:107
  11.8 11.1 %collective-permute-start.2 = (bf16[400,512]{1,0:T(8,128)(2,1)}, bf16[400,512]{1,0:T(8,128)(2,1)S(1)}, u32[]{:S(2)}, u32[]{:S(2)}) collective-permute-start(bf16[400,512]{1,0:T(8,128)(2,1)} %get-tuple-element.18.refs_1_.refs_6_), channel_id=1, source_target_pairs={{0,4},{4,0},{1,5},{5,1},{2,6},{6,2},{3,7},{7,3},{8,12},{12,8},{9,1... | collective-permute-start | bytes 1228808 | tf_op jit(solution)/shard_map/ppermute | solution.py:107
  11.9 1.0 copy-start.6
  12.9 10.1 %collective-permute-start.1 = (bf16[400,384]{1,0:T(8,128)(2,1)}, bf16[400,384]{1,0:T(8,128)(2,1)S(1)}, u32[]{:S(2)}, u32[]{:S(2)}) collective-permute-start(bf16[400,384]{1,0:T(8,128)(2,1)} %shard_map.128.refs_7_), channel_id=1, source_target_pairs={{0,2},{1,3},{2,0},{3,1},{4,6},{5,7},{6,4},{7,5},{8,10},{9,11},{10,... | collective-permute-start | bytes 921608 | tf_op jit(solution)/shard_map/ppermute | solution.py:107
  23.0 1.2 copy-start.2
  24.1 0.7 copy-start.19
  24.2 0.8 copy-start.20
  24.2 2.1 %collective-permute-start.3 = (bf16[400,768]{1,0:T(8,128)(2,1)S(1)}, bf16[400,768]{1,0:T(8,128)(2,1)S(1)}, u32[]{:S(2)}, u32[]{:S(2)}) collective-permute-start(bf16[400,768]{1,0:T(8,128)(2,1)S(1)} %shard_map.131), channel_id=1, source_target_pairs={{0,1},{1,0},{2,3},{3,2},{4,5},{5,4},{6,7},{7,6},{8,9},{9,8},{10,11... | collective-permute-start | bytes 1843208 | tf_op jit(solution)/shard_map/ppermute | solution.py:107
  25.0 14.8 %collective-permute-start.4 = (bf16[512,512]{1,0:T(8,128)(2,1)S(1)}, bf16[512,512]{1,0:T(8,128)(2,1)S(1)}, u32[]{:S(2)}, u32[]{:S(2)}) collective-permute-start(bf16[512,512]{1,0:T(8,128)(2,1)S(1)} %copy-done.2), channel_id=1, source_target_pairs={{0,4},{4,0},{1,5},{5,1},{2,6},{6,2},{3,7},{7,3},{8,12},{12,8},{9,1... | collective-permute-start | bytes 1572872 | tf_op jit(solution)/shard_map/ppermute | solution.py:107
  26.4 2.0 %copy-start.1 = (bf16[1536,3,384]{2,0,1:T(8,128)(2,1)S(1)}, bf16[1536,3,384]{2,0,1:T(8,128)(2,1)}, u32[]{:S(2)}) copy-start(bf16[1536,3,384]{2,0,1:T(8,128)(2,1)} %param.17) | copy-start | bytes 10616836
  29.4 10.5 %copy-start.10 = (bf16[2,224,400]{2,1,0:T(8,128)(2,1)S(1)}, bf16[2,224,400]{2,1,0:T(8,128)(2,1)}, u32[]{:S(2)}) copy-start(bf16[2,224,400]{2,1,0:T(8,128)(2,1)} %constant.75.clone.refs_2_.refs_3_) | copy-start | bytes 1075204
  29.4 10.4 %copy-start.14 = (s32[4]{0:T(128)S(1)}, s32[4]{0:T(128)}, u32[]{:S(2)}) copy-start(s32[4]{0:T(128)} %pad_add_fusion.refs_0_) | copy-start | bytes 52
  29.9 9.9 %copy-start.7 = (bf16[400,1536]{1,0:T(8,128)(2,1)S(1)}, bf16[400,1536]{1,0:T(8,128)(2,1)}, u32[]{:S(2)}) copy-start(bf16[400,1536]{1,0:T(8,128)(2,1)} %get-tuple-element.17.refs_1_) | copy-start | bytes 3686404
  30.0 19.8 %copy-start.21 = (f32[3,128]{1,0:T(4,128)S(1)}, f32[3,128]{1,0:T(4,128)}, u32[]{:S(2)}) copy-start(f32[3,128]{1,0:T(4,128)} %param.19) | copy-start | bytes 4612
  30.0 19.8 %copy-start.22 = (f32[3,128]{1,0:T(4,128)S(1)}, f32[3,128]{1,0:T(4,128)}, u32[]{:S(2)}) copy-start(f32[3,128]{1,0:T(4,128)} %param.20) | copy-start | bytes 4612
  30.0 23.0 %collective-permute-start.7 = (bf16[400,768]{1,0:T(8,128)(2,1)S(1)}, bf16[400,768]{1,0:T(8,128)(2,1)S(1)}, u32[]{:S(2)}, u32[]{:S(2)}) collective-permute-start(bf16[400,768]{1,0:T(8,128)(2,1)S(1)} %pad_maximum_fusion.2.refs_6_), channel_id=1, source_target_pairs={{0,4},{4,0},{1,5},{5,1},{2,6},{6,2},{3,7},{7,3},{8,12},{12,8},{9,1... | collective-permute-start | bytes 1843208 | tf_op jit(solution)/shard_map/ppermute | solution.py:107
  39.8 13.2 %copy-start.5 = (bf16[512,512]{1,0:T(8,128)(2,1)}, bf16[512,512]{1,0:T(8,128)(2,1)S(1)}, u32[]{:S(2)}) copy-start(bf16[512,512]{1,0:T(8,128)(2,1)S(1)} %collective-permute-done.4.refs_7_.refs_6_) | copy-start | bytes 1572868
  49.2 5.7 %copy-start.3 = (bf16[200,1536]{1,0:T(8,128)(2,1)}, bf16[200,1536]{1,0:T(8,128)(2,1)S(1)}, u32[]{:S(2)}) copy-start(bf16[200,1536]{1,0:T(8,128)(2,1)S(1)} %get-tuple-element.21.refs_0_) | copy-start | bytes 1843204
  49.2 27.0 %collective-permute-start.6 = (bf16[400,1024]{1,0:T(8,128)(2,1)}, bf16[400,1024]{1,0:T(8,128)(2,1)S(1)}, u32[]{:S(2)}, u32[]{:S(2)}) collective-permute-start(bf16[400,1024]{1,0:T(8,128)(2,1)} %get-tuple-element.19), channel_id=1, source_target_pairs={{0,4},{4,0},{1,5},{5,1},{2,6},{6,2},{3,7},{7,3},{8,12},{12,8},{9,1... | collective-permute-start | bytes 2457608 | tf_op jit(solution)/shard_map/ppermute | solution.py:107
  54.9 0.9 copy-start.8
  55.8 0.7 copy-start.11
  56.5 14.2 %copy-start.13 = (f32[2,2,1664]{2,1,0:T(2,128)S(1)}, f32[2,2,1664]{2,1,0:T(2,128)}, u32[]{:S(2)}) copy-start(f32[2,2,1664]{2,1,0:T(2,128)} %constant.76.clone.refs_5_) | copy-start | bytes 79876
  56.5 10.1 %collective-permute-start.8 = (bf16[736,256]{1,0:T(8,128)(2,1)}, bf16[736,256]{1,0:T(8,128)(2,1)S(1)}, u32[]{:S(2)}, u32[]{:S(2)}) collective-permute-start(bf16[736,256]{1,0:T(8,128)(2,1)} %get-tuple-element.27), channel_id=1, source_target_pairs={{0,8},{8,16},{16,24},{1,9},{9,17},{17,25},{2,10},{10,18},{18,26},{... | collective-permute-start | bytes 1130504 | tf_op jit(solution)/shard_map/ppermute | solution.py:112
  60.1 10.6 %collective-permute-start.9 = (bf16[736,256]{1,0:T(8,128)(2,1)}, bf16[736,256]{1,0:T(8,128)(2,1)}, u32[]{:S(2)}, u32[]{:S(2)}) collective-permute-start(bf16[736,256]{1,0:T(8,128)(2,1)} %get-tuple-element.28), channel_id=1, source_target_pairs={{8,0},{16,8},{24,16},{9,1},{17,9},{25,17},{10,2},{18,10},{26,18},{... | collective-permute-start | bytes 1130504 | tf_op jit(solution)/shard_map/ppermute | solution.py:112
  61.6 9.1 %copy-start.9 = (bf16[1424,256]{1,0:T(8,128)(2,1)S(1)}, bf16[1424,256]{1,0:T(8,128)(2,1)}, u32[]{:S(2)}) copy-start(bf16[1424,256]{1,0:T(8,128)(2,1)} %copy-done.8) | copy-start | bytes 2187268
  61.6 9.1 %copy-start.12 = (bf16[1200,128]{1,0:T(8,128)(2,1)S(1)}, bf16[1200,128]{1,0:T(8,128)(2,1)}, u32[]{:S(2)}) copy-start(bf16[1200,128]{1,0:T(8,128)(2,1)} %copy-done.11) | copy-start | bytes 921604
  61.7 22.0 %collective-permute-start.5 = (bf16[200,1536]{1,0:T(8,128)(2,1)S(1)}, bf16[200,1536]{1,0:T(8,128)(2,1)S(1)}, u32[]{:S(2)}, u32[]{:S(2)}) collective-permute-start(bf16[200,1536]{1,0:T(8,128)(2,1)S(1)} %get-tuple-element.20.refs_9_), channel_id=1, source_target_pairs={{0,4},{4,0},{1,5},{5,1},{2,6},{6,2},{3,7},{7,3},{8,12},{12,8},{9,1... | collective-permute-start | bytes 1843208 | tf_op jit(solution)/shard_map/ppermute | solution.py:107
  70.7 0.7 copy-start.15
  75.5 1.1 copy-start.4
  75.6 1.2 slice-start
  75.6 14.7 %collective-permute-start.10 = (bf16[400,384]{1,0:T(8,128)(2,1)S(1)}, bf16[400,384]{1,0:T(8,128)(2,1)S(1)}, u32[]{:S(2)}, u32[]{:S(2)}) collective-permute-start(bf16[400,384]{1,0:T(8,128)(2,1)S(1)} %shard_map.134.refs_1_), channel_id=1, source_target_pairs={{0,4},{4,0},{1,5},{5,1},{2,6},{6,2},{3,7},{7,3},{8,12},{12,8},{9,1... | collective-permute-start | bytes 921608 | tf_op jit(solution)/shard_map/ppermute | solution.py:107
  77.7 4.0 %slice-start.1 = ((s8[4718592]{0:T(1024)(128)(4,1)}), s8[4194304]{0:T(1024)(128)(4,1)S(1)}, s32[]{:S(2)}) async-start(s8[4718592]{0:T(1024)(128)(4,1)} %bitcast.31), calls=%async_computation.1 | async-start | bytes 8388608
  77.8 4.0 %slice-start.2 = ((s8[4718592]{0:T(1024)(128)(4,1)}), s8[524288]{0:T(1024)(128)(4,1)S(1)}, s32[]{:S(2)}) async-start(s8[4718592]{0:T(1024)(128)(4,1)} %bitcast.31), calls=%async_computation.2 | async-start | bytes 1048576
  80.7 25.3 %collective-permute-start.16 = (bf16[200,1536]{1,0:T(8,128)(2,1)S(1)}, bf16[200,1536]{1,0:T(8,128)(2,1)S(1)}, u32[]{:S(2)}, u32[]{:S(2)}) collective-permute-start(bf16[200,1536]{1,0:T(8,128)(2,1)S(1)} %shard_map.142), channel_id=1, source_target_pairs={{0,4},{4,0},{1,5},{5,1},{2,6},{6,2},{3,7},{7,3},{8,12},{12,8},{9,1... | collective-permute-start | bytes 1843208 | tf_op jit(solution)/shard_map/ppermute | solution.py:107
  91.4 3.5 %collective-permute-start.13 = (bf16[400,768]{1,0:T(8,128)(2,1)S(1)}, bf16[400,768]{1,0:T(8,128)(2,1)S(1)}, u32[]{:S(2)}, u32[]{:S(2)}) collective-permute-start(bf16[400,768]{1,0:T(8,128)(2,1)S(1)} %fusion.20.refs_1_), channel_id=1, source_target_pairs={{0,1},{1,0},{2,3},{3,2},{4,5},{5,4},{6,7},{7,6},{8,9},{9,8},{10,11... | collective-permute-start | bytes 1843208 | tf_op jit(solution)/shard_map/ppermute | solution.py:107
  94.0 2.9 %collective-permute-start.11 = (bf16[200,768]{1,0:T(8,128)(2,1)S(1)}, bf16[200,768]{1,0:T(8,128)(2,1)S(1)}, u32[]{:S(2)}, u32[]{:S(2)}) collective-permute-start(bf16[200,768]{1,0:T(8,128)(2,1)S(1)} %fusion.53.refs_1_), channel_id=1, source_target_pairs={{0,1},{1,0},{2,3},{3,2},{4,5},{5,4},{6,7},{7,6},{8,9},{9,8},{10,11... | collective-permute-start | bytes 921608 | tf_op jit(solution)/shard_map/ppermute | solution.py:107
  95.0 10.2 %collective-permute-start.14 = (bf16[200,768]{1,0:T(8,128)(2,1)S(1)}, bf16[200,768]{1,0:T(8,128)(2,1)S(1)}, u32[]{:S(2)}, u32[]{:S(2)}) collective-permute-start(bf16[200,768]{1,0:T(8,128)(2,1)S(1)} %add_convert_fusion.3), channel_id=1, source_target_pairs={{0,2},{1,3},{2,0},{3,1},{4,6},{5,7},{6,4},{7,5},{8,10},{9,11},{10,... | collective-permute-start | bytes 921608 | tf_op jit(solution)/shard_map/ppermute | solution.py:107
  96.9 1.4 %copy-start.16 = (bf16[200,768]{1,0:T(8,128)(2,1)}, bf16[200,768]{1,0:T(8,128)(2,1)S(1)}, u32[]{:S(2)}) copy-start(bf16[200,768]{1,0:T(8,128)(2,1)S(1)} %collective-permute-done.11) | copy-start | bytes 921604
  98.4 16.1 %collective-permute-start.12 = (bf16[200,768]{1,0:T(8,128)(2,1)}, bf16[200,768]{1,0:T(8,128)(2,1)S(1)}, u32[]{:S(2)}, u32[]{:S(2)}) collective-permute-start(bf16[200,768]{1,0:T(8,128)(2,1)} %get-tuple-element.47), channel_id=1, source_target_pairs={{0,2},{1,3},{2,0},{3,1},{4,6},{5,7},{6,4},{7,5},{8,10},{9,11},{10,... | collective-permute-start | bytes 921608 | tf_op jit(solution)/shard_map/ppermute | solution.py:107
  105.4 9.1 %collective-permute-start.15 = (bf16[200,768]{1,0:T(8,128)(2,1)S(1)}, bf16[200,768]{1,0:T(8,128)(2,1)S(1)}, u32[]{:S(2)}, u32[]{:S(2)}) collective-permute-start(bf16[200,768]{1,0:T(8,128)(2,1)S(1)} %add_convert_fusion.2.refs_1_), channel_id=1, source_target_pairs={{0,4},{4,0},{1,5},{5,1},{2,6},{6,2},{3,7},{7,3},{8,12},{12,8},{9,1... | collective-permute-start | bytes 921608 | tf_op jit(solution)/shard_map/ppermute | solution.py:107
  109.0 5.5 %collective-permute-start.17 = (bf16[200,768]{1,0:T(8,128)(2,1)}, bf16[200,768]{1,0:T(8,128)(2,1)}, u32[]{:S(2)}, u32[]{:S(2)}) collective-permute-start(bf16[200,768]{1,0:T(8,128)(2,1)} %fusion.50), channel_id=1, source_target_pairs={{0,1},{1,0},{2,3},{3,2},{4,5},{5,4},{6,7},{7,6},{8,9},{9,8},{10,11... | collective-permute-start | bytes 921608 | tf_op jit(solution)/shard_map/ppermute | solution.py:107
  114.5 2.7 %copy-start.17 = (bf16[200,768]{1,0:T(8,128)(2,1)S(1)}, bf16[200,768]{1,0:T(8,128)(2,1)}, u32[]{:S(2)}) copy-start(bf16[200,768]{1,0:T(8,128)(2,1)} %copy-done.16) | copy-start | bytes 921604
  115.6 9.8 %collective-permute-start.18 = (bf16[200,768]{1,0:T(8,128)(2,1)S(1)}, bf16[200,768]{1,0:T(8,128)(2,1)S(1)}, u32[]{:S(2)}, u32[]{:S(2)}) collective-permute-start(bf16[200,768]{1,0:T(8,128)(2,1)S(1)} %fusion.77), channel_id=1, source_target_pairs={{0,2},{1,3},{2,0},{3,1},{4,6},{5,7},{6,4},{7,5},{8,10},{9,11},{10,... | collective-permute-start | bytes 921608 | tf_op jit(solution)/shard_map/ppermute | solution.py:107

commit v6 on v5

--- a/solution.py
+++ b/solution.py
@@ -497,14 +497,16 @@
     own, own_early = modulate_and_heads(place, tokens, mod_scale[None], mod_shift[None], w_heads, [sent])
     got_early = swap(own_early, "sx", 1)
     piece = hold(piece, own_early)
-    pieces = in_order(far, piece, hold(swap(piece, "tp", 2), got_early))
+    near = swap(piece, "tp", 1)
+    piece_far = hold(swap(piece, "tp", 2), got_early)
     first_part = width_of(hidden // 3, hidden)
     own_first = border_and_hidden(place, own, picks, w_heads, w_mlp_in, first_part, [own_early, piece])
     got_first = swap(own_first, "sx", 1)
-    pieces = hold(jnp.concatenate(pieces, axis=1), got_early, own_first)
-    near = swap(pieces, "tp", 1)
-    even, odd = in_order(core, pieces, near)
-    other = jnp.concatenate([even[:, :quarter], odd[:, :quarter], even[:, quarter:], odd[:, quarter:]], axis=1)
+    piece_far = hold(piece_far, own_first)
+    near_far = swap(piece_far, "tp", 1)
+    lower, upper = in_order(far, piece, piece_far), in_order(far, near, near_far)
+    quarters = [part for pair_of in zip(lower, upper) for part in in_order(core, *pair_of)]
+    other = jnp.concatenate(quarters, axis=1)
     terms = [got_early[:, 3 * edge + i : 3 * edge + i + 1].astype(F32) for i in range(6)]
     other = modulate(other, [terms[i] + terms[i + 1] + terms[i + 2] for i in (0, 3)])
     late_first = (1 - side) * edge
@@ -589,7 +591,7 @@
         ],
         axis=0,
     )
-    first_col = hold(part[None], own_sent_a)[0] * block
+    first_col = part * block
     gate_part = lax.dynamic_slice_in_dim(mod_gate, first_col, block, 0)
     residual_part = lax.dynamic_slice_in_dim(tokens, first_col, block, 1).astype(F32)
     known = hold(residual_part + gate_part * known)

time: 127 us -> 121 us (0.953)
  matrix products: 14.6 us -> 10.5 us
  other arithmetic: 11.9 us -> 10.1 us
  starting transfers between devices: 19.9 us -> 21.2 us
    dot_general x15, matrix products: 14.6 us -> 10.5 us  [dot(): return jnp.dot(left, right, preferred_element_type=jnp.float32)]
    ppermute x17 -> x18, waiting for transfers between devices: 35.2 us -> 38.5 us  [swap(): return lax.ppermute(cells, axis, [(i, i ^ bit) for i in range(count)])]
    ppermute x2, waiting for transfers between devices: 8.33 us -> 5.22 us  [shift(): lax.ppermute(cells, axis, [(i, i + step) for i in range(count) if 0 <= i...]
    ppermute x2, starting transfers between devices: 5.1 us -> 6.71 us  [shift(): lax.ppermute(cells, axis, [(i, i + step) for i in range(count) if 0 <= i...]
    unnamed x50 -> x46, local copies, waits for them, and re-layouts: 5.64 us -> 4.96 us
    ppermute x17 -> x18, starting transfers between devices: 14.8 us -> 14.5 us  [swap(): return lax.ppermute(cells, axis, [(i, i ^ bit) for i in range(count)])]
  transfers between devices with their start and end apart: 19 -> 20, of which waited for: 10 -> 12; matrix products, arithmetic and copies ran while one was open for 19% -> 17% of each run, Pallas kernels for 22% -> 22%
where the time goes in v6:
time: 121 us; the launch traced here: 120 us
  waiting for transfers between devices  43.8 us (36%)
  Pallas kernels  27 us (22%)
  starting transfers between devices  21.2 us (18%)
  matrix products  10.5 us (9%)
  other arithmetic  10.1 us (8%)
  local copies, waits for them, and re-layouts  7.15 us (6%)
    ppermute x18, waiting for transfers between devices, swap(): return lax.ppermute(cells, axis, [(i, i ^ bit) for i in range(count)])  38.5 us
    pallas_call x5, Pallas kernels, call(): pl.pallas_call(kernel, grid=(grid,), in_specs=[spec(b, i) for _, b, i in...  26.9 us
    ppermute x18, starting transfers between devices, swap(): return lax.ppermute(cells, axis, [(i, i ^ bit) for i in range(count)])  14.5 us
    dot_general x15, matrix products, dot(): return jnp.dot(left, right, preferred_element_type=jnp.float32)  10.5 us
    ppermute x2, starting transfers between devices, shift(): lax.ppermute(cells, axis, [(i, i + step) for i in range(count) if 0 <= i...  6.71 us
    ppermute x2, waiting for transfers between devices, shift(): lax.ppermute(cells, axis, [(i, i + step) for i in range(count) if 0 <= i...  5.22 us
    unnamed x46, local copies, waits for them, and re-layouts  4.96 us
    convert_element_type x3, other arithmetic, activate(): jax.nn.gelu(mine.astype(F32) + got.astype(F32), approximate=True)  4.02 us
  transfers between devices with their start and end apart: 20, of which 12 were waited for; matrix products, arithmetic and copies ran while one was open for 17% of the time, Pallas kernels for 22%

profile of v6, /device:TPU:0, one launch (start us, length us, event | category | flops | bytes accessed | tf_op | source)
XLA Modules:
  0.0 120.0 jit_solution(11762475698271866062)
XLA Ops:
  0.0 1.1 constant_dynamic-slice_fusion.refs_5_
  1.1 3.0 %collective-permute-start = (bf16[400,384]{1,0:T(8,128)(2,1)S(1)}, bf16[400,384]{1,0:T(8,128)(2,1)}, u32[]{:S(2)}, u32[]{:S(2)}) collective-permute-start(bf16[400,384]{1,0:T(8,128)(2,1)S(1)} %constant_dynamic-slice_fusion.refs_5_), channel_id=1, source_target_pairs={{0,4},{4,0},{1,5},{5,1},{2,6},{6,2},{3,7},{7,3},{8,12},{12,8},{9,1... | collective-permute-start | bytes 921608 | tf_op jit(solution)/shard_map/ppermute | solution.py:107
  4.1 0.6 pad_add_fusion.refs_0_
  4.7 7.1 %shard_map.127 = (bf16[400,1536]{1,0:T(8,128)(2,1)}, bf16[400,512]{1,0:T(8,128)(2,1)}) custom-call(s32[4]{0:T(128)} %pad_add_fusion.refs_0_, bf16[400,3072]{1,0:T(8,128)(2,1)} %refs_1_.1, f32[1,3072]{1,0:T(1,128)} %bitcast.32, f32[1,3072]{1,0:T(1,128)} %bitcast.31, bf16[3,1536,384]{2,1,0:T(8,128)(2,1)} %bitcast.25, bf16[400,384]{1,0:T(8,128)(2,1)} %copy-done.16), custom_call_target="tpu_custom_call" | custom-call | flops 1000 | bytes 1000 | tf_op jit(solution)/shard_map/pallas_call | solution.py:145
  11.9 1.0 copy-done.6
  12.9 2.0 %collective-permute-start.1 = (bf16[400,384]{1,0:T(8,128)(2,1)}, bf16[400,384]{1,0:T(8,128)(2,1)S(1)}, u32[]{:S(2)}, u32[]{:S(2)}) collective-permute-start(bf16[400,384]{1,0:T(8,128)(2,1)} %shard_map.128.refs_7_), channel_id=1, source_target_pairs={{0,2},{1,3},{2,0},{3,1},{4,6},{5,7},{6,4},{7,5},{8,10},{9,11},{10,... | collective-permute-start | bytes 921608 | tf_op jit(solution)/shard_map/ppermute | solution.py:107
  14.9 4.5 %shard_map.129.refs_1_ = bf16[512,512]{1,0:T(8,128)(2,1)} custom-call(s32[4]{0:T(128)} %pad_add_fusion.refs_0_, bf16[400,1536]{1,0:T(8,128)(2,1)} %get-tuple-element.17.refs_1_, bf16[2,224,400]{2,1,0:T(8,128)(2,1)} %constant.73.clone.refs_2_.refs_3_, bf16[3,1536,384]{2,1,0:T(8,128)(2,1)} %bitcast.26, bf16[3,1536,384]{2,1,0:T(8,128)(2,1)} %bitcast.27, ...), custom_call_target="tpu_custom_call" | custom-call | flops 1000 | bytes 1000 | tf_op jit(solution)/shard_map/pallas_call | solution.py:145
  19.3 3.6 %collective-permute-done.2.refs_1_.refs_4_ = bf16[400,512]{1,0:T(8,128)(2,1)S(1)} collective-permute-done((bf16[400,512]{1,0:T(8,128)(2,1)}, bf16[400,512]{1,0:T(8,128)(2,1)S(1)}, u32[]{:S(2)}, u32[]{:S(2)}) %collective-permute-start.2) | collective-permute-done | bytes 409632 | tf_op jit(solution)/shard_map/ppermute | solution.py:107
  23.2 0.5 collective-permute-start.5
  23.8 0.4 add_reduce_fusion.1
  24.1 0.5 collective-permute-done.4
  24.6 1.3 %broadcast_select_fusion.7 = (bf16[400,384]{1,0:T(8,128)(2,1)S(1)}, bf16[400,384]{1,0:T(8,128)(2,1)S(1)}, bf16[400,384]{1,0:T(8,128)(2,1)S(1)}, bf16[400,384]{1,0:T(8,128)(2,1)S(1)}) fusion(pred[]{:T(512)S(6)} %eq.13, bf16[400,384]{1,0:T(8,128)(2,1)} %shard_map.128.refs_7_, bf16[400,384]{1,0:T(8,128)(2,1)S(1)} %shard_map.131, pred[]{:T(512)S(6)} %eq.14, ...), kind=kLoop, calls=%fused_computation.96 | loop fusion | flops 1228800 | bytes 2457602 | tf_op jit(solution)/shard_map/jit(_where)/select_n | solution.py:158
  25.9 0.5 add_convert_fusion.refs_2_
  26.7 0.5 convolution_convert_fusion.1
  27.2 0.5 convolution_convert_fusion.2
  27.7 0.5 convolution_convert_fusion
  28.3 1.1 collective-permute-start.8
  29.4 8.5 %collective-permute-done.5.refs_7_.refs_6_ = bf16[512,512]{1,0:T(8,128)(2,1)S(1)} collective-permute-done((bf16[512,512]{1,0:T(8,128)(2,1)S(1)}, bf16[512,512]{1,0:T(8,128)(2,1)S(1)}, u32[]{:S(2)}, u32[]{:S(2)}) %collective-permute-start.5) | collective-permute-done | bytes 524320 | tf_op jit(solution)/shard_map/ppermute | solution.py:107
  38.0 9.3 %shard_map.132 = (f32[400,768]{1,0:T(8,128)S(1)}, f32[400,384]{1,0:T(8,128)S(1)}, f32[224,256]{1,0:T(8,128)S(1)}, bf16[400,1024]{1,0:T(8,128)(2,1)}, bf16[200,15...) custom-call(s32[4]{0:T(128)S(1)} %copy-done.14, bf16[400,1536]{1,0:T(8,128)(2,1)S(1)} %copy-done.7, ...), custom_call_target="tpu_custom_call" | custom-call | flops 3951034368 | bytes 13787136 | tf_op jit(solution)/shard_map/pallas_call | solution.py:145
  47.3 0.8 copy-done.3
  48.1 0.5 collective-permute-start.7
  48.7 2.4 %collective-permute-done.8.refs_2_ = bf16[400,768]{1,0:T(8,128)(2,1)S(1)} collective-permute-done((bf16[400,768]{1,0:T(8,128)(2,1)S(1)}, bf16[400,768]{1,0:T(8,128)(2,1)S(1)}, u32[]{:S(2)}, u32[]{:S(2)}) %collective-permute-start.8) | collective-permute-done | bytes 614432 | tf_op jit(solution)/shard_map/ppermute | solution.py:107
  51.1 1.9 %shard_map.133 = (bf16[1200,128]{1,0:T(8,128)(2,1)S(1)}, bf16[1424,256]{1,0:T(8,128)(2,1)S(1)}, bf16[736,256]{1,0:T(8,128)(2,1)}, bf16[736,256]{1,0:T(8,128)(2,1)}) custom-call(s32[4]{0:T(128)S(1)} %copy-done.14, f32[400,768]{1,0:T(8,128)S(1)} %get-tuple-element.22.refs_1_, bf16[400,768]{1,0:T(8,128)(2,1)S(1)} %collective-permute-done.8.refs_2_, ...), custom_call_target="tpu_custom_call" | custom-call | flops 1000 | bytes 1000 | tf_op jit(solution)/shard_map/pallas_call | solution.py:145
  53.1 0.9 copy-done.8
  53.9 0.7 copy-done.11
  54.7 1.4 %collective-permute-start.10 = (bf16[736,256]{1,0:T(8,128)(2,1)}, bf16[736,256]{1,0:T(8,128)(2,1)S(1)}, u32[]{:S(2)}, u32[]{:S(2)}) collective-permute-start(bf16[736,256]{1,0:T(8,128)(2,1)} %get-tuple-element.28), channel_id=1, source_target_pairs={{8,0},{16,8},{24,16},{9,1},{17,9},{25,17},{10,2},{18,10},{26,18},{... | collective-permute-start | bytes 1130504 | tf_op jit(solution)/shard_map/ppermute | solution.py:112
  56.1 5.3 %collective-permute-start.9 = (bf16[736,256]{1,0:T(8,128)(2,1)}, bf16[736,256]{1,0:T(8,128)(2,1)}, u32[]{:S(2)}, u32[]{:S(2)}) collective-permute-start(bf16[736,256]{1,0:T(8,128)(2,1)} %get-tuple-element.27), channel_id=1, source_target_pairs={{0,8},{8,16},{16,24},{1,9},{9,17},{17,25},{2,10},{10,18},{18,26},{... | collective-permute-start | bytes 1130504 | tf_op jit(solution)/shard_map/ppermute | solution.py:112
  61.4 0.9 dynamic_slice.31
  62.3 0.6 collective-permute-start.6
  62.8 3.9 %collective-permute-done.10.refs_4_ = bf16[736,256]{1,0:T(8,128)(2,1)S(1)} collective-permute-done((bf16[736,256]{1,0:T(8,128)(2,1)}, bf16[736,256]{1,0:T(8,128)(2,1)S(1)}, u32[]{:S(2)}, u32[]{:S(2)}) %collective-permute-start.10) | collective-permute-done | bytes 376864 | tf_op jit(solution)/shard_map/ppermute | solution.py:112
  66.8 1.3 %collective-permute-done.9.refs_3_ = bf16[736,256]{1,0:T(8,128)(2,1)} collective-permute-done((bf16[736,256]{1,0:T(8,128)(2,1)}, bf16[736,256]{1,0:T(8,128)(2,1)}, u32[]{:S(2)}, u32[]{:S(2)}) %collective-permute-start.9) | collective-permute-done | bytes 376864 | tf_op jit(solution)/shard_map/ppermute | solution.py:112
  68.1 0.7 copy-done.15
  68.8 4.2 %shard_map.134.refs_1_ = bf16[400,384]{1,0:T(8,128)(2,1)S(1)} custom-call(s32[4]{0:T(128)S(1)} %copy-done.14, bf16[1200,128]{1,0:T(8,128)(2,1)S(1)} %copy-done.12, bf16[1424,256]{1,0:T(8,128)(2,1)S(1)} %copy-done.9, bf16[736,256]{1,0:T(8,128)(2,1)} %collective-permute-done.9.refs_3_, bf16[736,256]{1,0:T(8,128)(2,1)S(1)} %collective-permute-done.10.refs_4_, ...), custom_call_target="tpu_custom_call" | custom-call | flops 1000 | bytes 1000 | tf_op jit(solution)/shard_map/pallas_call | solution.py:145
  72.9 0.6 collective-permute-start.11
  73.5 0.5 copy-done.4
  74.1 1.0 fusion.7.refs_0_
  75.2 2.9 %fusion.18.refs_1_ = f32[400,768]{1,0:T(8,128)S(1)} fusion(bf16[400,1536]{1,0:T(8,128)(2,1)S(1)} %shard_map.136, bf16[1536,1536]{1,0:T(8,128)(2,1)} %param.22, s32[]{:T(128)S(6)} %select_n.168), kind=kOutput, calls=%fused_computation.22 | convolution fusion | flops 943718400 | bytes 4816900 | tf_op jit(solution)/shard_map/dot_general | solution.py:118
  78.1 1.0 collective-permute-start.17
  79.1 1.1 fusion.12.refs_2_
  80.3 2.4 %collective-permute-done.6.refs_3_.refs_0_ = bf16[200,1536]{1,0:T(8,128)(2,1)S(1)} collective-permute-done((bf16[200,1536]{1,0:T(8,128)(2,1)S(1)}, bf16[200,1536]{1,0:T(8,128)(2,1)S(1)}, u32[]{:S(2)}, u32[]{:S(2)}) %collective-permute-start.6) | collective-permute-done | bytes 614432 | tf_op jit(solution)/shard_map/ppermute | solution.py:107
  82.7 6.6 %collective-permute-done.11.refs_0_ = bf16[400,384]{1,0:T(8,128)(2,1)S(1)} collective-permute-done((bf16[400,384]{1,0:T(8,128)(2,1)S(1)}, bf16[400,384]{1,0:T(8,128)(2,1)S(1)}, u32[]{:S(2)}, u32[]{:S(2)}) %collective-permute-start.11) | collective-permute-done | bytes 307232 | tf_op jit(solution)/shard_map/ppermute | solution.py:107
  89.4 0.5 fusion.20.refs_1_
  89.8 0.5 convolution_add_fusion.refs_2_
  90.4 1.5 %fusion.40.refs_0_ = bf16[200,1536]{1,0:T(8,128)(2,1)S(1)} fusion(bf16[200,1536]{1,0:T(8,128)(2,1)S(1)} %shard_map.138, bf16[400,512]{1,0:T(8,128)(2,1)S(1)} %slice.92, bf16[400,1024]{1,0:T(8,128)(2,1)} %get-tuple-element.19), kind=kLoop, calls=%fused_computation.38 | loop fusion | flops 4608000 | bytes 2457600 | tf_op jit(solution)/shard_map/convert_element_type | solution.py:538
  92.0 0.3 fusion.72
  92.3 0.7 fusion.53.refs_1_
  93.0 0.6 collective-permute-start.12
  93.6 0.3 fusion.67
  94.0 1.6 %collective-permute-start.15 = (bf16[200,768]{1,0:T(8,128)(2,1)S(1)}, bf16[200,768]{1,0:T(8,128)(2,1)S(1)}, u32[]{:S(2)}, u32[]{:S(2)}) collective-permute-start(bf16[200,768]{1,0:T(8,128)(2,1)S(1)} %add_convert_fusion.3), channel_id=1, source_target_pairs={{0,2},{1,3},{2,0},{3,1},{4,6},{5,7},{6,4},{7,5},{8,10},{9,11},{10,... | collective-permute-start | bytes 921608 | tf_op jit(solution)/shard_map/ppermute | solution.py:107
  95.6 0.3 fusion.70
  95.9 0.7 fusion.75
  96.6 0.6 collective-permute-start.13
  97.2 7.0 %collective-permute-done.15.refs_0_ = bf16[200,768]{1,0:T(8,128)(2,1)S(1)} collective-permute-done((bf16[200,768]{1,0:T(8,128)(2,1)S(1)}, bf16[200,768]{1,0:T(8,128)(2,1)S(1)}, u32[]{:S(2)}, u32[]{:S(2)}) %collective-permute-start.15) | collective-permute-done | bytes 307232 | tf_op jit(solution)/shard_map/ppermute | solution.py:107
  104.5 0.6 collective-permute-start.16
  105.1 1.5 %fusion.48.refs_0_ = bf16[200,1536]{1,0:T(8,128)(2,1)S(1)} fusion(bf16[200,1536]{1,0:T(8,128)(2,1)S(1)} %shard_map.142, bf16[400,1024]{1,0:T(8,128)(2,1)} %get-tuple-element.19, bf16[400,512]{1,0:T(8,128)(2,1)S(1)} %slice.92), kind=kLoop, calls=%fused_computation.46 | loop fusion | flops 4608000 | bytes 2457600 | tf_op jit(solution)/shard_map/convert_element_type | solution.py:538
  106.6 0.7 fusion.50
  107.3 0.3 fusion.65
  107.7 0.7 fusion.30.refs_0_
  108.3 1.5 %collective-permute-done.13.refs_2_ = bf16[200,768]{1,0:T(8,128)(2,1)S(1)} collective-permute-done((bf16[200,768]{1,0:T(8,128)(2,1)S(1)}, bf16[200,768]{1,0:T(8,128)(2,1)S(1)}, u32[]{:S(2)}, u32[]{:S(2)}) %collective-permute-start.13) | collective-permute-done | bytes 307232 | tf_op jit(solution)/shard_map/ppermute | solution.py:107
  109.9 2.0 %collective-permute-done.16.refs_1_ = bf16[200,768]{1,0:T(8,128)(2,1)S(1)} collective-permute-done((bf16[200,768]{1,0:T(8,128)(2,1)S(1)}, bf16[200,768]{1,0:T(8,128)(2,1)S(1)}, u32[]{:S(2)}, u32[]{:S(2)}) %collective-permute-start.16) | collective-permute-done | bytes 307232 | tf_op jit(solution)/shard_map/ppermute | solution.py:107
  112.1 1.6 %collective-permute-start.19 = (bf16[200,768]{1,0:T(8,128)(2,1)S(1)}, bf16[200,768]{1,0:T(8,128)(2,1)S(1)}, u32[]{:S(2)}, u32[]{:S(2)}) collective-permute-start(bf16[200,768]{1,0:T(8,128)(2,1)S(1)} %fusion.77), channel_id=1, source_target_pairs={{0,2},{1,3},{2,0},{3,1},{4,6},{5,7},{6,4},{7,5},{8,10},{9,11},{10,... | collective-permute-start | bytes 921608 | tf_op jit(solution)/shard_map/ppermute | solution.py:107
  113.9 1.2 %fusion.49.refs_0_ = f32[400,768]{1,0:T(8,128)S(1)} fusion(f32[200,768]{1,0:T(8,128)S(1)} %get-tuple-element.40, f32[200,768]{1,0:T(8,128)S(1)} %get-tuple-element.39, f32[768]{0:T(1024)S(1)} %dynamic_slice.31, bf16[400,3072]{1,0:T(8,128)(2,1)} %refs_1_.1, s32[]{:T(128)S(6)} %select_n.151), kind=kLoop, calls=%fused_computation.50 | loop fusion | flops 1228800 | bytes 3075076 | tf_op jit(solution)/shard_map/add | solution.py:597
  115.2 3.8 %collective-permute-done.19 = bf16[200,768]{1,0:T(8,128)(2,1)S(1)} collective-permute-done((bf16[200,768]{1,0:T(8,128)(2,1)S(1)}, bf16[200,768]{1,0:T(8,128)(2,1)S(1)}, u32[]{:S(2)}, u32[]{:S(2)}) %collective-permute-start.19) | collective-permute-done | bytes 307232 | tf_op jit(solution)/shard_map/ppermute | solution.py:107
  119.0 1.0 add_convert_fusion.1
  (83 shorter events, 1.9 us)
Async XLA Ops:
  0.0 89.4 %copy-start = (bf16[384,1536]{1,0:T(8,128)(2,1)S(1)}, bf16[384,1536]{1,0:T(8,128)(2,1)}, u32[]{:S(2)}) copy-start(bf16[384,1536]{1,0:T(8,128)(2,1)} %param.21) | copy-start | bytes 3538948
  1.1 3.6 %copy-start.16 = (bf16[400,384]{1,0:T(8,128)(2,1)}, bf16[400,384]{1,0:T(8,128)(2,1)S(1)}, u32[]{:S(2)}) copy-start(bf16[400,384]{1,0:T(8,128)(2,1)S(1)} %constant_dynamic-slice_fusion.refs_5_) | copy-start | bytes 921604
  1.1 10.8 %collective-permute-start = (bf16[400,384]{1,0:T(8,128)(2,1)S(1)}, bf16[400,384]{1,0:T(8,128)(2,1)}, u32[]{:S(2)}, u32[]{:S(2)}) collective-permute-start(bf16[400,384]{1,0:T(8,128)(2,1)S(1)} %constant_dynamic-slice_fusion.refs_5_), channel_id=1, source_target_pairs={{0,4},{4,0},{1,5},{5,1},{2,6},{6,2},{3,7},{7,3},{8,12},{12,8},{9,1... | collective-permute-start | bytes 921608 | tf_op jit(solution)/shard_map/ppermute | solution.py:107
  11.8 11.1 %collective-permute-start.2 = (bf16[400,512]{1,0:T(8,128)(2,1)}, bf16[400,512]{1,0:T(8,128)(2,1)S(1)}, u32[]{:S(2)}, u32[]{:S(2)}) collective-permute-start(bf16[400,512]{1,0:T(8,128)(2,1)} %get-tuple-element.18.refs_1_.refs_6_), channel_id=1, source_target_pairs={{0,4},{4,0},{1,5},{5,1},{2,6},{6,2},{3,7},{7,3},{8,12},{12,8},{9,1... | collective-permute-start | bytes 1228808 | tf_op jit(solution)/shard_map/ppermute | solution.py:107
  11.9 1.0 copy-start.6
  12.9 10.1 %collective-permute-start.1 = (bf16[400,384]{1,0:T(8,128)(2,1)}, bf16[400,384]{1,0:T(8,128)(2,1)S(1)}, u32[]{:S(2)}, u32[]{:S(2)}) collective-permute-start(bf16[400,384]{1,0:T(8,128)(2,1)} %shard_map.128.refs_7_), channel_id=1, source_target_pairs={{0,2},{1,3},{2,0},{3,1},{4,6},{5,7},{6,4},{7,5},{8,10},{9,11},{10,... | collective-permute-start | bytes 921608 | tf_op jit(solution)/shard_map/ppermute | solution.py:107
  14.9 9.3 %collective-permute-start.3 = (bf16[400,384]{1,0:T(8,128)(2,1)}, bf16[400,384]{1,0:T(8,128)(2,1)S(1)}, u32[]{:S(2)}, u32[]{:S(2)}) collective-permute-start(bf16[400,384]{1,0:T(8,128)(2,1)} %shard_map.128.refs_7_), channel_id=1, source_target_pairs={{0,1},{1,0},{2,3},{3,2},{4,5},{5,4},{6,7},{7,6},{8,9},{9,8},{10,11... | collective-permute-start | bytes 921608 | tf_op jit(solution)/shard_map/ppermute | solution.py:107
  19.3 3.6 %copy-start.2 = (bf16[512,512]{1,0:T(8,128)(2,1)S(1)}, bf16[512,512]{1,0:T(8,128)(2,1)}, u32[]{:S(2)}) copy-start(bf16[512,512]{1,0:T(8,128)(2,1)} %shard_map.129.refs_1_) | copy-start | bytes 1572868
  19.3 3.7 %copy-start.17 = (f32[3072]{0:T(1024)S(1)}, f32[3072]{0:T(1024)}, u32[]{:S(2)}) copy-start(f32[3072]{0:T(1024)} %param.14) | copy-start | bytes 36868
  19.3 3.8 %copy-start.18 = (f32[3072]{0:T(1024)S(1)}, f32[3072]{0:T(1024)}, u32[]{:S(2)}) copy-start(f32[3072]{0:T(1024)} %param.15) | copy-start | bytes 36868
  23.0 1.7 %collective-permute-start.4 = (bf16[400,384]{1,0:T(8,128)(2,1)S(1)}, bf16[400,384]{1,0:T(8,128)(2,1)S(1)}, u32[]{:S(2)}, u32[]{:S(2)}) collective-permute-start(bf16[400,384]{1,0:T(8,128)(2,1)S(1)} %shard_map.131), channel_id=1, source_target_pairs={{0,1},{1,0},{2,3},{3,2},{4,5},{5,4},{6,7},{7,6},{8,9},{9,8},{10,11... | collective-permute-start | bytes 921608 | tf_op jit(solution)/shard_map/ppermute | solution.py:107
  23.2 14.7 %collective-permute-start.5 = (bf16[512,512]{1,0:T(8,128)(2,1)S(1)}, bf16[512,512]{1,0:T(8,128)(2,1)S(1)}, u32[]{:S(2)}, u32[]{:S(2)}) collective-permute-start(bf16[512,512]{1,0:T(8,128)(2,1)S(1)} %copy-done.2), channel_id=1, source_target_pairs={{0,4},{4,0},{1,5},{5,1},{2,6},{6,2},{3,7},{7,3},{8,12},{12,8},{9,1... | collective-permute-start | bytes 1572872 | tf_op jit(solution)/shard_map/ppermute | solution.py:107
  24.6 2.1 %copy-start.1 = (bf16[1536,3,384]{2,0,1:T(8,128)(2,1)S(1)}, bf16[1536,3,384]{2,0,1:T(8,128)(2,1)}, u32[]{:S(2)}) copy-start(bf16[1536,3,384]{2,0,1:T(8,128)(2,1)} %param.17) | copy-start | bytes 10616836
  27.7 10.3 %copy-start.10 = (bf16[2,224,400]{2,1,0:T(8,128)(2,1)S(1)}, bf16[2,224,400]{2,1,0:T(8,128)(2,1)}, u32[]{:S(2)}) copy-start(bf16[2,224,400]{2,1,0:T(8,128)(2,1)} %constant.73.clone.refs_2_.refs_3_) | copy-start | bytes 1075204
  27.7 10.2 %copy-start.14 = (s32[4]{0:T(128)S(1)}, s32[4]{0:T(128)}, u32[]{:S(2)}) copy-start(s32[4]{0:T(128)} %pad_add_fusion.refs_0_) | copy-start | bytes 52
  28.2 9.7 %copy-start.7 = (bf16[400,1536]{1,0:T(8,128)(2,1)S(1)}, bf16[400,1536]{1,0:T(8,128)(2,1)}, u32[]{:S(2)}) copy-start(bf16[400,1536]{1,0:T(8,128)(2,1)} %get-tuple-element.17.refs_1_) | copy-start | bytes 3686404
  28.3 20.4 %copy-start.19 = (f32[3,128]{1,0:T(4,128)S(1)}, f32[3,128]{1,0:T(4,128)}, u32[]{:S(2)}) copy-start(f32[3,128]{1,0:T(4,128)} %param.19) | copy-start | bytes 4612
  28.3 20.4 %copy-start.20 = (f32[3,128]{1,0:T(4,128)S(1)}, f32[3,128]{1,0:T(4,128)}, u32[]{:S(2)}) copy-start(f32[3,128]{1,0:T(4,128)} %param.20) | copy-start | bytes 4612
  28.3 22.8 %collective-permute-start.8 = (bf16[400,768]{1,0:T(8,128)(2,1)S(1)}, bf16[400,768]{1,0:T(8,128)(2,1)S(1)}, u32[]{:S(2)}, u32[]{:S(2)}) collective-permute-start(bf16[400,768]{1,0:T(8,128)(2,1)S(1)} %pad_maximum_fusion.1.refs_6_), channel_id=1, source_target_pairs={{0,4},{4,0},{1,5},{5,1},{2,6},{6,2},{3,7},{7,3},{8,12},{12,8},{9,1... | collective-permute-start | bytes 1843208 | tf_op jit(solution)/shard_map/ppermute | solution.py:107
  38.0 13.2 %copy-start.5 = (bf16[512,512]{1,0:T(8,128)(2,1)}, bf16[512,512]{1,0:T(8,128)(2,1)S(1)}, u32[]{:S(2)}) copy-start(bf16[512,512]{1,0:T(8,128)(2,1)S(1)} %collective-permute-done.5.refs_7_.refs_6_) | copy-start | bytes 1572868
  47.3 0.8 copy-start.3
  48.1 25.4 %collective-permute-start.7 = (bf16[400,1024]{1,0:T(8,128)(2,1)}, bf16[400,1024]{1,0:T(8,128)(2,1)S(1)}, u32[]{:S(2)}, u32[]{:S(2)}) collective-permute-start(bf16[400,1024]{1,0:T(8,128)(2,1)} %get-tuple-element.19), channel_id=1, source_target_pairs={{0,4},{4,0},{1,5},{5,1},{2,6},{6,2},{3,7},{7,3},{8,12},{12,8},{9,1... | collective-permute-start | bytes 2457608 | tf_op jit(solution)/shard_map/ppermute | solution.py:107
  53.0 0.9 copy-start.8
  53.9 0.7 copy-start.11
  54.7 13.4 %copy-start.13 = (f32[2,2,1664]{2,1,0:T(2,128)S(1)}, f32[2,2,1664]{2,1,0:T(2,128)}, u32[]{:S(2)}) copy-start(f32[2,2,1664]{2,1,0:T(2,128)} %constant.74.clone.refs_5_) | copy-start | bytes 79876
  54.7 12.1 %collective-permute-start.10 = (bf16[736,256]{1,0:T(8,128)(2,1)}, bf16[736,256]{1,0:T(8,128)(2,1)S(1)}, u32[]{:S(2)}, u32[]{:S(2)}) collective-permute-start(bf16[736,256]{1,0:T(8,128)(2,1)} %get-tuple-element.28), channel_id=1, source_target_pairs={{8,0},{16,8},{24,16},{9,1},{17,9},{25,17},{10,2},{18,10},{26,18},{... | collective-permute-start | bytes 1130504 | tf_op jit(solution)/shard_map/ppermute | solution.py:112
  56.1 12.0 %collective-permute-start.9 = (bf16[736,256]{1,0:T(8,128)(2,1)}, bf16[736,256]{1,0:T(8,128)(2,1)}, u32[]{:S(2)}, u32[]{:S(2)}) collective-permute-start(bf16[736,256]{1,0:T(8,128)(2,1)} %get-tuple-element.27), channel_id=1, source_target_pairs={{0,8},{8,16},{16,24},{1,9},{9,17},{17,25},{2,10},{10,18},{18,26},{... | collective-permute-start | bytes 1130504 | tf_op jit(solution)/shard_map/ppermute | solution.py:112
  61.4 6.7 %copy-start.9 = (bf16[1424,256]{1,0:T(8,128)(2,1)S(1)}, bf16[1424,256]{1,0:T(8,128)(2,1)}, u32[]{:S(2)}) copy-start(bf16[1424,256]{1,0:T(8,128)(2,1)} %copy-done.8) | copy-start | bytes 2187268
  61.4 6.7 %copy-start.12 = (bf16[1200,128]{1,0:T(8,128)(2,1)S(1)}, bf16[1200,128]{1,0:T(8,128)(2,1)}, u32[]{:S(2)}) copy-start(bf16[1200,128]{1,0:T(8,128)(2,1)} %copy-done.11) | copy-start | bytes 921604
  62.3 20.4 %collective-permute-start.6 = (bf16[200,1536]{1,0:T(8,128)(2,1)S(1)}, bf16[200,1536]{1,0:T(8,128)(2,1)S(1)}, u32[]{:S(2)}, u32[]{:S(2)}) collective-permute-start(bf16[200,1536]{1,0:T(8,128)(2,1)S(1)} %get-tuple-element.20.refs_9_), channel_id=1, source_target_pairs={{0,4},{4,0},{1,5},{5,1},{2,6},{6,2},{3,7},{7,3},{8,12},{12,8},{9,1... | collective-permute-start | bytes 1843208 | tf_op jit(solution)/shard_map/ppermute | solution.py:107
  68.1 0.7 copy-start.15
  72.9 1.1 copy-start.4
  72.9 1.2 slice-start
  72.9 16.3 %collective-permute-start.11 = (bf16[400,384]{1,0:T(8,128)(2,1)S(1)}, bf16[400,384]{1,0:T(8,128)(2,1)S(1)}, u32[]{:S(2)}, u32[]{:S(2)}) collective-permute-start(bf16[400,384]{1,0:T(8,128)(2,1)S(1)} %shard_map.134.refs_1_), channel_id=1, source_target_pairs={{0,4},{4,0},{1,5},{5,1},{2,6},{6,2},{3,7},{7,3},{8,12},{12,8},{9,1... | collective-permute-start | bytes 921608 | tf_op jit(solution)/shard_map/ppermute | solution.py:107
  75.1 4.0 %slice-start.1 = ((s8[4718592]{0:T(1024)(128)(4,1)}), s8[4194304]{0:T(1024)(128)(4,1)S(1)}, s32[]{:S(2)}) async-start(s8[4718592]{0:T(1024)(128)(4,1)} %bitcast.29), calls=%async_computation.1 | async-start | bytes 8388608
  75.2 4.0 %slice-start.2 = ((s8[4718592]{0:T(1024)(128)(4,1)}), s8[524288]{0:T(1024)(128)(4,1)S(1)}, s32[]{:S(2)}) async-start(s8[4718592]{0:T(1024)(128)(4,1)} %bitcast.29), calls=%async_computation.2 | async-start | bytes 1048576
  78.1 26.9 %collective-permute-start.17 = (bf16[200,1536]{1,0:T(8,128)(2,1)S(1)}, bf16[200,1536]{1,0:T(8,128)(2,1)S(1)}, u32[]{:S(2)}, u32[]{:S(2)}) collective-permute-start(bf16[200,1536]{1,0:T(8,128)(2,1)S(1)} %shard_map.141), channel_id=1, source_target_pairs={{0,4},{4,0},{1,5},{5,1},{2,6},{6,2},{3,7},{7,3},{8,12},{12,8},{9,1... | collective-permute-start | bytes 1843208 | tf_op jit(solution)/shard_map/ppermute | solution.py:107
  90.3 3.5 %collective-permute-start.14 = (bf16[400,768]{1,0:T(8,128)(2,1)S(1)}, bf16[400,768]{1,0:T(8,128)(2,1)S(1)}, u32[]{:S(2)}, u32[]{:S(2)}) collective-permute-start(bf16[400,768]{1,0:T(8,128)(2,1)S(1)} %fusion.20.refs_1_), channel_id=1, source_target_pairs={{0,1},{1,0},{2,3},{3,2},{4,5},{5,4},{6,7},{7,6},{8,9},{9,8},{10,11... | collective-permute-start | bytes 1843208 | tf_op jit(solution)/shard_map/ppermute | solution.py:107
  93.0 2.9 %collective-permute-start.12 = (bf16[200,768]{1,0:T(8,128)(2,1)S(1)}, bf16[200,768]{1,0:T(8,128)(2,1)S(1)}, u32[]{:S(2)}, u32[]{:S(2)}) collective-permute-start(bf16[200,768]{1,0:T(8,128)(2,1)S(1)} %fusion.53.refs_1_), channel_id=1, source_target_pairs={{0,1},{1,0},{2,3},{3,2},{4,5},{5,4},{6,7},{7,6},{8,9},{9,8},{10,11... | collective-permute-start | bytes 921608 | tf_op jit(solution)/shard_map/ppermute | solution.py:107
  94.0 10.2 %collective-permute-start.15 = (bf16[200,768]{1,0:T(8,128)(2,1)S(1)}, bf16[200,768]{1,0:T(8,128)(2,1)S(1)}, u32[]{:S(2)}, u32[]{:S(2)}) collective-permute-start(bf16[200,768]{1,0:T(8,128)(2,1)S(1)} %add_convert_fusion.3), channel_id=1, source_target_pairs={{0,2},{1,3},{2,0},{3,1},{4,6},{5,7},{6,4},{7,5},{8,10},{9,11},{10,... | collective-permute-start | bytes 921608 | tf_op jit(solution)/shard_map/ppermute | solution.py:107
  96.6 13.2 %collective-permute-start.13 = (bf16[200,768]{1,0:T(8,128)(2,1)S(1)}, bf16[200,768]{1,0:T(8,128)(2,1)S(1)}, u32[]{:S(2)}, u32[]{:S(2)}) collective-permute-start(bf16[200,768]{1,0:T(8,128)(2,1)S(1)} %get-tuple-element.43), channel_id=1, source_target_pairs={{0,2},{1,3},{2,0},{3,1},{4,6},{5,7},{6,4},{7,5},{8,10},{9,11},{10,... | collective-permute-start | bytes 921608 | tf_op jit(solution)/shard_map/ppermute | solution.py:107
  104.5 7.5 %collective-permute-start.16 = (bf16[200,768]{1,0:T(8,128)(2,1)S(1)}, bf16[200,768]{1,0:T(8,128)(2,1)S(1)}, u32[]{:S(2)}, u32[]{:S(2)}) collective-permute-start(bf16[200,768]{1,0:T(8,128)(2,1)S(1)} %add_convert_fusion.2.refs_1_), channel_id=1, source_target_pairs={{0,4},{4,0},{1,5},{5,1},{2,6},{6,2},{3,7},{7,3},{8,12},{12,8},{9,1... | collective-permute-start | bytes 921608 | tf_op jit(solution)/shard_map/ppermute | solution.py:107
  107.3 4.7 %collective-permute-start.18 = (bf16[200,768]{1,0:T(8,128)(2,1)S(1)}, bf16[200,768]{1,0:T(8,128)(2,1)S(1)}, u32[]{:S(2)}, u32[]{:S(2)}) collective-permute-start(bf16[200,768]{1,0:T(8,128)(2,1)S(1)} %fusion.50), channel_id=1, source_target_pairs={{0,1},{1,0},{2,3},{3,2},{4,5},{5,4},{6,7},{7,6},{8,9},{9,8},{10,11... | collective-permute-start | bytes 921608 | tf_op jit(solution)/shard_map/ppermute | solution.py:107
  112.1 6.9 %collective-permute-start.19 = (bf16[200,768]{1,0:T(8,128)(2,1)S(1)}, bf16[200,768]{1,0:T(8,128)(2,1)S(1)}, u32[]{:S(2)}, u32[]{:S(2)}) collective-permute-start(bf16[200,768]{1,0:T(8,128)(2,1)S(1)} %fusion.77), channel_id=1, source_target_pairs={{0,2},{1,3},{2,0},{3,1},{4,6},{5,7},{6,4},{7,5},{8,10},{9,11},{10,... | collective-permute-start | bytes 921608 | tf_op jit(solution)/shard_map/ppermute | solution.py:107

commit v7 on v6

--- a/solution.py
+++ b/solution.py
@@ -124,7 +124,6 @@
 VMEM = 56
 REST_VMEM = 40
 POST_VMEM = 40
-ROWS = 80
 
 
 def width_of(total, most):
@@ -191,13 +190,17 @@
     return jnp.asarray(picks, BF16)
 
 
+def token_block(rows):
+    return max(b for b in range(16, LANES + 1, 16) if rows % b == 0)
+
+
 def modulate_and_heads(place, tokens, scale_row, shift_row, w_heads, after=()):
     rows, model_width = tokens.shape
     depth, width = w_heads.shape[1:]
     edge = (width - LANES) // 2
-    block = max(b for b in range(16, rows + 1, 16) if rows % b == 0 and b <= ROWS)
-
-    def body(place_ref, tokens_ref, scale_ref, shift_ref, w_heads_ref, own_ref, out_ref):
+    block = token_block(rows)
+
+    def body(place_ref, tokens_ref, scale_ref, shift_ref, w_heads_ref, own_ref, out_ref, moments_ref):
         side = place_ref[0]
         cells = tokens_ref[...].astype(F32)
         mean = jnp.mean(cells, axis=-1, keepdims=True)
@@ -210,14 +213,10 @@
         theirs = pl.ds(pl.multiple_of((1 - side) * (width - edge), LANES), edge)
         for g in range(3):
             out_ref[:, g * edge : (g + 1) * edge] = dot(own, w_heads_ref[g, :, theirs]).astype(BF16)
-        lane = lax.broadcasted_iota(jnp.int32, (block, LANES), 1)
-        moments = jnp.zeros((block, LANES), F32)
-        for first, moment in ((0, mean), (3, scaling)):
-            for i in range(3):
-                term = moment.astype(BF16).astype(F32)
-                moments = jnp.where(lane == first + i, term, moments)
-                moment = moment - term
-        out_ref[:, 3 * edge :] = moments.astype(BF16)
+        lane = lax.broadcasted_iota(jnp.int32, (LANES, LANES), 1)
+        mean, scaling = (jnp.pad(m, ((0, LANES - block), (0, 0))) for m in (mean, scaling))
+        moments = jnp.where(lane == 0, mean, jnp.where(lane == 1, scaling, 0.0))
+        moments_ref[0] = moments.T[:8]
 
     row = lambda i: (i, 0)
     return call(
@@ -231,7 +230,8 @@
         ],
         [
             ((rows, depth), BF16, (block, depth), row),
-            ((rows, 3 * edge + LANES), BF16, (block, 3 * edge + LANES), row),
+            ((rows, 3 * edge), BF16, (block, 3 * edge), row),
+            ((rows // block, 8, LANES), F32, (1, 8, LANES), lambda i: (i, 0, 0)),
         ],
         after=after, vmem=VMEM,
     )
@@ -494,11 +494,11 @@
     edge = pair * head_dim
     w_heads = jnp.transpose(w_qkv, (1, 0, 2))
 
-    own, own_early = modulate_and_heads(place, tokens, mod_scale[None], mod_shift[None], w_heads, [sent])
-    got_early = swap(own_early, "sx", 1)
+    own, own_early, moments = modulate_and_heads(place, tokens, mod_scale[None], mod_shift[None], w_heads, [sent])
+    got_early, got_moments = swap(own_early, "sx", 1), swap(moments, "sx", 1)
     piece = hold(piece, own_early)
     near = swap(piece, "tp", 1)
-    piece_far = hold(swap(piece, "tp", 2), got_early)
+    piece_far = hold(swap(piece, "tp", 2), got_early, got_moments)
     first_part = width_of(hidden // 3, hidden)
     own_first = border_and_hidden(place, own, picks, w_heads, w_mlp_in, first_part, [own_early, piece])
     got_first = swap(own_first, "sx", 1)
@@ -507,8 +507,7 @@
     lower, upper = in_order(far, piece, piece_far), in_order(far, near, near_far)
     quarters = [part for pair_of in zip(lower, upper) for part in in_order(core, *pair_of)]
     other = jnp.concatenate(quarters, axis=1)
-    terms = [got_early[:, 3 * edge + i : 3 * edge + i + 1].astype(F32) for i in range(6)]
-    other = modulate(other, [terms[i] + terms[i + 1] + terms[i + 2] for i in (0, 3)])
+    other = modulate(other, [got_moments[:, i, : token_block(tok_rows)].reshape(tok_rows, 1) for i in range(2)])
     late_first = (1 - side) * edge
     other_late = [
         dot(other, lax.dynamic_slice(w_heads, (g, 0, late_first), (1, half_width, edge + head_dim))[0]).astype(BF16)

time: 121 us -> 118 us (0.975)
  starting transfers between devices: 21.2 us -> 25.9 us
  waiting for transfers between devices: 43.8 us -> 41.4 us
  other arithmetic: 10.1 us -> 7.73 us
  local copies, waits for them, and re-layouts: 7.15 us -> 5.48 us
    ppermute x18 -> x19, starting transfers between devices: 14.5 us -> 20.1 us  [swap(): return lax.ppermute(cells, axis, [(i, i ^ bit) for i in range(count)])]
    ppermute x18 -> x19, waiting for transfers between devices: 38.5 us -> 34.1 us  [swap(): return lax.ppermute(cells, axis, [(i, i ^ bit) for i in range(count)])]
    ppermute x2, waiting for transfers between devices: 5.22 us -> 7.26 us  [shift(): lax.ppermute(cells, axis, [(i, i + step) for i in range(count) if 0 <= i...]
    convert_element_type x3, other arithmetic: 4.02 us -> 2.01 us  [activate(): jax.nn.gelu(mine.astype(F32) + got.astype(F32), approximate=True)]
    unnamed x46 -> x54, local copies, waits for them, and re-layouts: 4.96 us -> 3.2 us
  transfers between devices with their start and end apart: 20 -> 21, of which waited for: 12 -> 11; matrix products, arithmetic and copies ran while one was open for 17% -> 15% of each run, Pallas kernels for 22% -> 22%
where the time goes in v7:
time: 118 us
  waiting for transfers between devices  41.4 us (35%)
  Pallas kernels  26.4 us (22%)
  starting transfers between devices  25.9 us (22%)
  matrix products  10.5 us (9%)
  other arithmetic  7.73 us (7%)
  local copies, waits for them, and re-layouts  5.48 us (5%)
    ppermute x19, waiting for transfers between devices, swap(): return lax.ppermute(cells, axis, [(i, i ^ bit) for i in range(count)])  34.1 us
    pallas_call x5, Pallas kernels, call(): pl.pallas_call(kernel, grid=(grid,), in_specs=[spec(b, i) for _, b, i in...  26.4 us
    ppermute x19, starting transfers between devices, swap(): return lax.ppermute(cells, axis, [(i, i ^ bit) for i in range(count)])  20.1 us
    dot_general x15, matrix products, dot(): return jnp.dot(left, right, preferred_element_type=jnp.float32)  10.5 us
    ppermute x2, waiting for transfers between devices, shift(): lax.ppermute(cells, axis, [(i, i + step) for i in range(count) if 0 <= i...  7.26 us
    ppermute x2, starting transfers between devices, shift(): lax.ppermute(cells, axis, [(i, i + step) for i in range(count) if 0 <= i...  5.8 us
    unnamed x54, local copies, waits for them, and re-layouts  3.2 us
  transfers between devices with their start and end apart: 21, of which 11 were waited for; matrix products, arithmetic and copies ran while one was open for 15% of the time, Pallas kernels for 22%

profile of v7, /device:TPU:0, one launch (start us, length us, event | category | flops | bytes accessed | tf_op | source)
XLA Modules:
  0.0 117.9 jit_solution(15958550427969996468)
XLA Ops:
  0.0 1.1 constant_dynamic-slice_fusion.refs_5_
  1.1 3.0 %collective-permute-start = (bf16[400,384]{1,0:T(8,128)(2,1)S(1)}, bf16[400,384]{1,0:T(8,128)(2,1)}, u32[]{:S(2)}, u32[]{:S(2)}) collective-permute-start(bf16[400,384]{1,0:T(8,128)(2,1)S(1)} %constant_dynamic-slice_fusion.refs_5_), channel_id=1, source_target_pairs={{0,4},{4,0},{1,5},{5,1},{2,6},{6,2},{3,7},{7,3},{8,12},{12,8},{9,1... | collective-permute-start | bytes 921608 | tf_op jit(solution)/shard_map/ppermute | solution.py:107
  4.1 0.7 pad_add_fusion.refs_0_
  4.8 7.1 %shard_map.127 = (bf16[400,1536]{1,0:T(8,128)(2,1)}, bf16[400,384]{1,0:T(8,128)(2,1)}, f32[5,8,128]{2,1,0:T(8,128)}) custom-call(s32[4]{0:T(128)} %pad_add_fusion.refs_0_, bf16[400,3072]{1,0:T(8,128)(2,1)} %refs_1_.1, f32[1,3072]{1,0:T(1,128)} %bitcast.32, f32[1,3072]{1,0:T(1,128)} %bitcast.31, bf16[3,1536,384]{2,1,0:T(8,128)(2,1)} %bitcast.25, ...), custom_call_target="tpu_custom_call" | custom-call | flops 1000 | bytes 1000 | tf_op jit(solution)/shard_map/pallas_call | solution.py:144
  12.0 1.0 copy-done.8
  13.0 2.0 %collective-permute-start.1 = (bf16[400,384]{1,0:T(8,128)(2,1)}, bf16[400,384]{1,0:T(8,128)(2,1)S(1)}, u32[]{:S(2)}, u32[]{:S(2)}) collective-permute-start(bf16[400,384]{1,0:T(8,128)(2,1)} %shard_map.128.refs_7_), channel_id=1, source_target_pairs={{0,2},{1,3},{2,0},{3,1},{4,6},{5,7},{6,4},{7,5},{8,10},{9,11},{10,... | collective-permute-start | bytes 921608 | tf_op jit(solution)/shard_map/ppermute | solution.py:107
  14.9 1.5 %collective-permute-start.3 = (f32[5,8,128]{2,1,0:T(8,128)}, f32[5,8,128]{2,1,0:T(8,128)S(1)}, u32[]{:S(2)}, u32[]{:S(2)}) collective-permute-start(f32[5,8,128]{2,1,0:T(8,128)} %get-tuple-element.20), channel_id=1, source_target_pairs={{0,4},{4,0},{1,5},{5,1},{2,6},{6,2},{3,7},{7,3},{8,12},{12,8},{9,1... | collective-permute-start | bytes 61448 | tf_op jit(solution)/shard_map/ppermute | solution.py:107
  16.5 4.5 %shard_map.129.refs_1_ = bf16[512,512]{1,0:T(8,128)(2,1)} custom-call(s32[4]{0:T(128)} %pad_add_fusion.refs_0_, bf16[400,1536]{1,0:T(8,128)(2,1)} %get-tuple-element.18.refs_1_, bf16[2,224,400]{2,1,0:T(8,128)(2,1)} %constant.73.clone.refs_2_.refs_3_, bf16[3,1536,384]{2,1,0:T(8,128)(2,1)} %bitcast.26, bf16[3,1536,384]{2,1,0:T(8,128)(2,1)} %bitcast.27, ...), custom_call_target="tpu_custom_call" | custom-call | flops 1000 | bytes 1000 | tf_op jit(solution)/shard_map/pallas_call | solution.py:144
  21.0 0.4 collective-permute-done.3.refs_2_
  21.3 0.6 collective-permute-done.1.refs_0_
  22.1 0.6 collective-permute-start.5
  23.0 1.1 collective-permute-start.6
  24.1 1.3 %broadcast_select_fusion.7 = (bf16[400,384]{1,0:T(8,128)(2,1)S(1)}, bf16[400,384]{1,0:T(8,128)(2,1)S(1)}, bf16[400,384]{1,0:T(8,128)(2,1)S(1)}, bf16[400,384]{1,0:T(8,128)(2,1)S(1)}) fusion(pred[]{:T(512)S(6)} %eq.13, bf16[400,384]{1,0:T(8,128)(2,1)} %shard_map.128.refs_7_, bf16[400,384]{1,0:T(8,128)(2,1)S(1)} %shard_map.131, pred[]{:T(512)S(6)} %eq.14, ...), kind=kLoop, calls=%fused_computation.96 | loop fusion | flops 1228800 | bytes 2457602 | tf_op jit(solution)/shard_map/jit(_where)/select_n | solution.py:157
  25.4 0.5 add_convert_fusion.refs_2_
  26.0 0.3 copy-done.1
  26.2 0.5 convolution_convert_fusion.1
  26.7 0.5 convolution_convert_fusion.2
  27.2 0.5 convolution_convert_fusion
  27.8 1.3 %collective-permute-start.9 = (bf16[400,768]{1,0:T(8,128)(2,1)S(1)}, bf16[400,768]{1,0:T(8,128)(2,1)S(1)}, u32[]{:S(2)}, u32[]{:S(2)}) collective-permute-start(bf16[400,768]{1,0:T(8,128)(2,1)S(1)} %pad_maximum_fusion.1.refs_6_), channel_id=1, source_target_pairs={{0,4},{4,0},{1,5},{5,1},{2,6},{6,2},{3,7},{7,3},{8,12},{12,8},{9,1... | collective-permute-start | bytes 1843208 | tf_op jit(solution)/shard_map/ppermute | solution.py:107
  29.1 8.7 %collective-permute-done.6.refs_7_.refs_6_ = bf16[512,512]{1,0:T(8,128)(2,1)S(1)} collective-permute-done((bf16[512,512]{1,0:T(8,128)(2,1)S(1)}, bf16[512,512]{1,0:T(8,128)(2,1)S(1)}, u32[]{:S(2)}, u32[]{:S(2)}) %collective-permute-start.6) | collective-permute-done | bytes 524320 | tf_op jit(solution)/shard_map/ppermute | solution.py:107
  37.8 8.7 %shard_map.132 = (f32[400,768]{1,0:T(8,128)S(1)}, f32[400,384]{1,0:T(8,128)S(1)}, f32[224,256]{1,0:T(8,128)S(1)}, bf16[400,1024]{1,0:T(8,128)(2,1)S(1)}, bf16[20...) custom-call(s32[4]{0:T(128)S(1)} %copy-done.18, bf16[400,1536]{1,0:T(8,128)(2,1)S(1)} %copy-done.11, ...), custom_call_target="tpu_custom_call" | custom-call | flops 3951034368 | bytes 13787136 | tf_op jit(solution)/shard_map/pallas_call | solution.py:144
  46.5 1.2 collective-permute-start.8
  47.6 3.3 %collective-permute-done.9.refs_2_ = bf16[400,768]{1,0:T(8,128)(2,1)S(1)} collective-permute-done((bf16[400,768]{1,0:T(8,128)(2,1)S(1)}, bf16[400,768]{1,0:T(8,128)(2,1)S(1)}, u32[]{:S(2)}, u32[]{:S(2)}) %collective-permute-start.9) | collective-permute-done | bytes 614432 | tf_op jit(solution)/shard_map/ppermute | solution.py:107
  50.9 1.9 %shard_map.133 = (bf16[1200,128]{1,0:T(8,128)(2,1)S(1)}, bf16[1424,256]{1,0:T(8,128)(2,1)S(1)}, bf16[736,256]{1,0:T(8,128)(2,1)}, bf16[736,256]{1,0:T(8,128)(2,1)}) custom-call(s32[4]{0:T(128)S(1)} %copy-done.18, f32[400,768]{1,0:T(8,128)S(1)} %get-tuple-element.24.refs_1_, bf16[400,768]{1,0:T(8,128)(2,1)S(1)} %collective-permute-done.9.refs_2_, ...), custom_call_target="tpu_custom_call" | custom-call | flops 1000 | bytes 1000 | tf_op jit(solution)/shard_map/pallas_call | solution.py:144
  52.8 0.9 copy-done.12
  53.7 0.7 copy-done.15
  54.4 4.3 %collective-permute-start.10 = (bf16[736,256]{1,0:T(8,128)(2,1)}, bf16[736,256]{1,0:T(8,128)(2,1)}, u32[]{:S(2)}, u32[]{:S(2)}) collective-permute-start(bf16[736,256]{1,0:T(8,128)(2,1)} %get-tuple-element.29), channel_id=1, source_target_pairs={{0,8},{8,16},{16,24},{1,9},{9,17},{17,25},{2,10},{10,18},{18,26},{... | collective-permute-start | bytes 1130504 | tf_op jit(solution)/shard_map/ppermute | solution.py:112
  58.8 1.5 %collective-permute-start.11 = (bf16[736,256]{1,0:T(8,128)(2,1)}, bf16[736,256]{1,0:T(8,128)(2,1)}, u32[]{:S(2)}, u32[]{:S(2)}) collective-permute-start(bf16[736,256]{1,0:T(8,128)(2,1)} %get-tuple-element.30), channel_id=1, source_target_pairs={{8,0},{16,8},{24,16},{9,1},{17,9},{25,17},{10,2},{18,10},{26,18},{... | collective-permute-start | bytes 1130504 | tf_op jit(solution)/shard_map/ppermute | solution.py:112
  60.3 0.9 dynamic_slice.31
  61.4 1.1 collective-permute-start.7
  62.5 2.4 %collective-permute-done.10.refs_3_ = bf16[736,256]{1,0:T(8,128)(2,1)} collective-permute-done((bf16[736,256]{1,0:T(8,128)(2,1)}, bf16[736,256]{1,0:T(8,128)(2,1)}, u32[]{:S(2)}, u32[]{:S(2)}) %collective-permute-start.10) | collective-permute-done | bytes 376864 | tf_op jit(solution)/shard_map/ppermute | solution.py:112
  64.9 4.8 %collective-permute-done.11.refs_4_ = bf16[736,256]{1,0:T(8,128)(2,1)} collective-permute-done((bf16[736,256]{1,0:T(8,128)(2,1)}, bf16[736,256]{1,0:T(8,128)(2,1)}, u32[]{:S(2)}, u32[]{:S(2)}) %collective-permute-start.11) | collective-permute-done | bytes 376864 | tf_op jit(solution)/shard_map/ppermute | solution.py:112
  69.7 4.2 %shard_map.134.refs_1_ = bf16[400,384]{1,0:T(8,128)(2,1)S(1)} custom-call(s32[4]{0:T(128)S(1)} %copy-done.18, bf16[1200,128]{1,0:T(8,128)(2,1)S(1)} %copy-done.16, bf16[1424,256]{1,0:T(8,128)(2,1)S(1)} %copy-done.13, bf16[736,256]{1,0:T(8,128)(2,1)} %collective-permute-done.10.refs_3_, bf16[736,256]{1,0:T(8,128)(2,1)} %collective-permute-done.11.refs_4_, ...), custom_call_target="tpu_custom_call" | custom-call | flops 1000 | bytes 1000 | tf_op jit(solution)/shard_map/pallas_call | solution.py:144
  74.0 2.0 %collective-permute-start.12 = (bf16[400,384]{1,0:T(8,128)(2,1)S(1)}, bf16[400,384]{1,0:T(8,128)(2,1)S(1)}, u32[]{:S(2)}, u32[]{:S(2)}) collective-permute-start(bf16[400,384]{1,0:T(8,128)(2,1)S(1)} %shard_map.134.refs_1_), channel_id=1, source_target_pairs={{0,4},{4,0},{1,5},{5,1},{2,6},{6,2},{3,7},{7,3},{8,12},{12,8},{9,1... | collective-permute-start | bytes 921608 | tf_op jit(solution)/shard_map/ppermute | solution.py:107
  76.1 1.0 fusion.7.refs_0_
  77.1 2.9 %fusion.18.refs_1_ = f32[400,768]{1,0:T(8,128)S(1)} fusion(bf16[400,1536]{1,0:T(8,128)(2,1)S(1)} %shard_map.136, bf16[1536,1536]{1,0:T(8,128)(2,1)} %param.22, s32[]{:T(128)S(6)} %select_n.168), kind=kOutput, calls=%fused_computation.22 | convolution fusion | flops 943718400 | bytes 4816900 | tf_op jit(solution)/shard_map/dot_general | solution.py:118
  80.0 1.2 collective-permute-start.18
  81.2 1.1 fusion.12.refs_2_
  82.4 5.9 %collective-permute-done.12.refs_0_ = bf16[400,384]{1,0:T(8,128)(2,1)S(1)} collective-permute-done((bf16[400,384]{1,0:T(8,128)(2,1)S(1)}, bf16[400,384]{1,0:T(8,128)(2,1)S(1)}, u32[]{:S(2)}, u32[]{:S(2)}) %collective-permute-start.12) | collective-permute-done | bytes 307232 | tf_op jit(solution)/shard_map/ppermute | solution.py:107
  88.3 0.5 fusion.20.refs_1_
  88.8 0.5 convolution_add_fusion.refs_2_
  89.4 0.5 fusion.40.refs_0_
  89.9 0.3 fusion.72
  90.3 0.7 fusion.53.refs_1_
  90.9 0.6 collective-permute-start.13
  91.5 0.3 fusion.67
  92.0 1.1 collective-permute-start.16
  93.1 0.3 fusion.70
  93.4 0.7 fusion.75
  94.1 1.0 collective-permute-start.14
  95.2 7.0 %collective-permute-done.16.refs_0_ = bf16[200,768]{1,0:T(8,128)(2,1)S(1)} collective-permute-done((bf16[200,768]{1,0:T(8,128)(2,1)S(1)}, bf16[200,768]{1,0:T(8,128)(2,1)S(1)}, u32[]{:S(2)}, u32[]{:S(2)}) %collective-permute-start.16) | collective-permute-done | bytes 307232 | tf_op jit(solution)/shard_map/ppermute | solution.py:107
  102.2 0.2 add_convert_fusion.2.refs_1_
  102.4 1.1 collective-permute-start.17
  103.5 0.5 fusion.48.refs_0_
  104.0 0.7 fusion.50
  104.8 0.3 fusion.65
  105.1 0.7 fusion.30.refs_0_
  105.8 2.0 %collective-permute-done.14.refs_2_ = bf16[200,768]{1,0:T(8,128)(2,1)S(1)} collective-permute-done((bf16[200,768]{1,0:T(8,128)(2,1)S(1)}, bf16[200,768]{1,0:T(8,128)(2,1)S(1)}, u32[]{:S(2)}, u32[]{:S(2)}) %collective-permute-start.14) | collective-permute-done | bytes 307232 | tf_op jit(solution)/shard_map/ppermute | solution.py:107
  107.8 2.0 %collective-permute-done.17.refs_1_ = bf16[200,768]{1,0:T(8,128)(2,1)S(1)} collective-permute-done((bf16[200,768]{1,0:T(8,128)(2,1)S(1)}, bf16[200,768]{1,0:T(8,128)(2,1)S(1)}, u32[]{:S(2)}, u32[]{:S(2)}) %collective-permute-start.17) | collective-permute-done | bytes 307232 | tf_op jit(solution)/shard_map/ppermute | solution.py:107
  110.0 1.1 collective-permute-start.20
  111.1 0.3 fusion.62
  111.4 1.2 %fusion.49.refs_0_ = f32[400,768]{1,0:T(8,128)S(1)} fusion(f32[200,768]{1,0:T(8,128)S(1)} %get-tuple-element.42, f32[200,768]{1,0:T(8,128)S(1)} %get-tuple-element.41, f32[768]{0:T(1024)S(1)} %dynamic_slice.31, bf16[400,3072]{1,0:T(8,128)(2,1)} %refs_1_.1, s32[]{:T(128)S(6)} %select_n.151), kind=kLoop, calls=%fused_computation.50 | loop fusion | flops 1228800 | bytes 3075076 | tf_op jit(solution)/shard_map/add | solution.py:596
  112.6 4.3 %collective-permute-done.20 = bf16[200,768]{1,0:T(8,128)(2,1)S(1)} collective-permute-done((bf16[200,768]{1,0:T(8,128)(2,1)S(1)}, bf16[200,768]{1,0:T(8,128)(2,1)S(1)}, u32[]{:S(2)}, u32[]{:S(2)}) %collective-permute-start.20) | collective-permute-done | bytes 307232 | tf_op jit(solution)/shard_map/ppermute | solution.py:107
  116.9 1.0 add_convert_fusion.1
  (95 shorter events, 1.4 us)
Async XLA Ops:
  0.0 88.3 %copy-start = (bf16[384,1536]{1,0:T(8,128)(2,1)S(1)}, bf16[384,1536]{1,0:T(8,128)(2,1)}, u32[]{:S(2)}) copy-start(bf16[384,1536]{1,0:T(8,128)(2,1)} %param.21) | copy-start | bytes 3538948
  1.1 3.7 %copy-start.20 = (bf16[400,384]{1,0:T(8,128)(2,1)}, bf16[400,384]{1,0:T(8,128)(2,1)S(1)}, u32[]{:S(2)}) copy-start(bf16[400,384]{1,0:T(8,128)(2,1)S(1)} %constant_dynamic-slice_fusion.refs_5_) | copy-start | bytes 921604
  1.1 10.9 %collective-permute-start = (bf16[400,384]{1,0:T(8,128)(2,1)S(1)}, bf16[400,384]{1,0:T(8,128)(2,1)}, u32[]{:S(2)}, u32[]{:S(2)}) collective-permute-start(bf16[400,384]{1,0:T(8,128)(2,1)S(1)} %constant_dynamic-slice_fusion.refs_5_), channel_id=1, source_target_pairs={{0,4},{4,0},{1,5},{5,1},{2,6},{6,2},{3,7},{7,3},{8,12},{12,8},{9,1... | collective-permute-start | bytes 921608 | tf_op jit(solution)/shard_map/ppermute | solution.py:107
  12.0 9.4 %collective-permute-start.2 = (bf16[400,384]{1,0:T(8,128)(2,1)}, bf16[400,384]{1,0:T(8,128)(2,1)S(1)}, u32[]{:S(2)}, u32[]{:S(2)}) collective-permute-start(bf16[400,384]{1,0:T(8,128)(2,1)} %get-tuple-element.19.refs_1_.refs_6_), channel_id=1, source_target_pairs={{0,4},{4,0},{1,5},{5,1},{2,6},{6,2},{3,7},{7,3},{8,12},{12,8},{9,1... | collective-permute-start | bytes 921608 | tf_op jit(solution)/shard_map/ppermute | solution.py:107
  12.0 1.0 copy-start.8
  13.0 8.9 %collective-permute-start.1 = (bf16[400,384]{1,0:T(8,128)(2,1)}, bf16[400,384]{1,0:T(8,128)(2,1)S(1)}, u32[]{:S(2)}, u32[]{:S(2)}) collective-permute-start(bf16[400,384]{1,0:T(8,128)(2,1)} %shard_map.128.refs_7_), channel_id=1, source_target_pairs={{0,2},{1,3},{2,0},{3,1},{4,6},{5,7},{6,4},{7,5},{8,10},{9,11},{10,... | collective-permute-start | bytes 921608 | tf_op jit(solution)/shard_map/ppermute | solution.py:107
  14.9 6.4 %collective-permute-start.3 = (f32[5,8,128]{2,1,0:T(8,128)}, f32[5,8,128]{2,1,0:T(8,128)S(1)}, u32[]{:S(2)}, u32[]{:S(2)}) collective-permute-start(f32[5,8,128]{2,1,0:T(8,128)} %get-tuple-element.20), channel_id=1, source_target_pairs={{0,4},{4,0},{1,5},{5,1},{2,6},{6,2},{3,7},{7,3},{8,12},{12,8},{9,1... | collective-permute-start | bytes 61448 | tf_op jit(solution)/shard_map/ppermute | solution.py:107
  16.5 7.6 %collective-permute-start.4 = (bf16[400,384]{1,0:T(8,128)(2,1)}, bf16[400,384]{1,0:T(8,128)(2,1)S(1)}, u32[]{:S(2)}, u32[]{:S(2)}) collective-permute-start(bf16[400,384]{1,0:T(8,128)(2,1)} %shard_map.128.refs_7_), channel_id=1, source_target_pairs={{0,1},{1,0},{2,3},{3,2},{4,5},{5,4},{6,7},{7,6},{8,9},{9,8},{10,11... | collective-permute-start | bytes 921608 | tf_op jit(solution)/shard_map/ppermute | solution.py:107
  21.0 1.0 copy-start.2
  21.0 1.7 %copy-start.21 = (f32[3072]{0:T(1024)S(1)}, f32[3072]{0:T(1024)}, u32[]{:S(2)}) copy-start(f32[3072]{0:T(1024)} %param.14) | copy-start | bytes 36868
  21.0 1.7 %copy-start.22 = (f32[3072]{0:T(1024)S(1)}, f32[3072]{0:T(1024)}, u32[]{:S(2)}) copy-start(f32[3072]{0:T(1024)} %param.15) | copy-start | bytes 36868
  21.3 0.7 copy-start.9
  22.1 2.0 %collective-permute-start.5 = (bf16[400,384]{1,0:T(8,128)(2,1)S(1)}, bf16[400,384]{1,0:T(8,128)(2,1)S(1)}, u32[]{:S(2)}, u32[]{:S(2)}) collective-permute-start(bf16[400,384]{1,0:T(8,128)(2,1)S(1)} %shard_map.131), channel_id=1, source_target_pairs={{0,1},{1,0},{2,3},{3,2},{4,5},{5,4},{6,7},{7,6},{8,9},{9,8},{10,11... | collective-permute-start | bytes 921608 | tf_op jit(solution)/shard_map/ppermute | solution.py:107
  23.0 14.8 %collective-permute-start.6 = (bf16[512,512]{1,0:T(8,128)(2,1)S(1)}, bf16[512,512]{1,0:T(8,128)(2,1)S(1)}, u32[]{:S(2)}, u32[]{:S(2)}) collective-permute-start(bf16[512,512]{1,0:T(8,128)(2,1)S(1)} %copy-done.2), channel_id=1, source_target_pairs={{0,4},{4,0},{1,5},{5,1},{2,6},{6,2},{3,7},{7,3},{8,12},{12,8},{9,1... | collective-permute-start | bytes 1572872 | tf_op jit(solution)/shard_map/ppermute | solution.py:107
  24.1 2.1 %copy-start.1 = (bf16[1536,3,384]{2,0,1:T(8,128)(2,1)S(1)}, bf16[1536,3,384]{2,0,1:T(8,128)(2,1)}, u32[]{:S(2)}) copy-start(bf16[1536,3,384]{2,0,1:T(8,128)(2,1)} %param.17) | copy-start | bytes 10616836
  27.2 10.6 %copy-start.14 = (bf16[2,224,400]{2,1,0:T(8,128)(2,1)S(1)}, bf16[2,224,400]{2,1,0:T(8,128)(2,1)}, u32[]{:S(2)}) copy-start(bf16[2,224,400]{2,1,0:T(8,128)(2,1)} %constant.73.clone.refs_2_.refs_3_) | copy-start | bytes 1075204
  27.2 10.5 %copy-start.18 = (s32[4]{0:T(128)S(1)}, s32[4]{0:T(128)}, u32[]{:S(2)}) copy-start(s32[4]{0:T(128)} %pad_add_fusion.refs_0_) | copy-start | bytes 52
  27.7 10.0 %copy-start.11 = (bf16[400,1536]{1,0:T(8,128)(2,1)S(1)}, bf16[400,1536]{1,0:T(8,128)(2,1)}, u32[]{:S(2)}) copy-start(bf16[400,1536]{1,0:T(8,128)(2,1)} %get-tuple-element.18.refs_1_) | copy-start | bytes 3686404
  27.8 19.9 %copy-start.23 = (f32[3,128]{1,0:T(4,128)S(1)}, f32[3,128]{1,0:T(4,128)}, u32[]{:S(2)}) copy-start(f32[3,128]{1,0:T(4,128)} %param.19) | copy-start | bytes 4612
  27.8 19.8 %copy-start.24 = (f32[3,128]{1,0:T(4,128)S(1)}, f32[3,128]{1,0:T(4,128)}, u32[]{:S(2)}) copy-start(f32[3,128]{1,0:T(4,128)} %param.20) | copy-start | bytes 4612
  27.8 23.1 %copy-start.10 = (bf16[400,384]{1,0:T(8,128)(2,1)S(1)}, bf16[400,384]{1,0:T(8,128)(2,1)}, u32[]{:S(2)}) copy-start(bf16[400,384]{1,0:T(8,128)(2,1)} %copy-done.9) | copy-start | bytes 921604
  27.8 23.1 %collective-permute-start.9 = (bf16[400,768]{1,0:T(8,128)(2,1)S(1)}, bf16[400,768]{1,0:T(8,128)(2,1)S(1)}, u32[]{:S(2)}, u32[]{:S(2)}) collective-permute-start(bf16[400,768]{1,0:T(8,128)(2,1)S(1)} %pad_maximum_fusion.1.refs_6_), channel_id=1, source_target_pairs={{0,4},{4,0},{1,5},{5,1},{2,6},{6,2},{3,7},{7,3},{8,12},{12,8},{9,1... | collective-permute-start | bytes 1843208 | tf_op jit(solution)/shard_map/ppermute | solution.py:107
  37.8 13.2 %copy-start.7 = (bf16[512,512]{1,0:T(8,128)(2,1)}, bf16[512,512]{1,0:T(8,128)(2,1)S(1)}, u32[]{:S(2)}) copy-start(bf16[512,512]{1,0:T(8,128)(2,1)S(1)} %collective-permute-done.6.refs_7_.refs_6_) | copy-start | bytes 1572868
  46.4 6.4 %copy-start.3 = (bf16[200,1536]{1,0:T(8,128)(2,1)}, bf16[200,1536]{1,0:T(8,128)(2,1)S(1)}, u32[]{:S(2)}) copy-start(bf16[200,1536]{1,0:T(8,128)(2,1)S(1)} %get-tuple-element.23.refs_0_) | copy-start | bytes 1843204
  46.5 6.4 %copy-start.5 = (bf16[200,1536]{1,0:T(8,128)(2,1)}, bf16[200,1536]{1,0:T(8,128)(2,1)S(1)}, u32[]{:S(2)}) copy-start(bf16[200,1536]{1,0:T(8,128)(2,1)S(1)} %get-tuple-element.22.refs_9_) | copy-start | bytes 1843204
  46.5 29.6 %collective-permute-start.8 = (bf16[400,1024]{1,0:T(8,128)(2,1)S(1)}, bf16[400,1024]{1,0:T(8,128)(2,1)S(1)}, u32[]{:S(2)}, u32[]{:S(2)}) collective-permute-start(bf16[400,1024]{1,0:T(8,128)(2,1)S(1)} %get-tuple-element.21), channel_id=1, source_target_pairs={{0,4},{4,0},{1,5},{5,1},{2,6},{6,2},{3,7},{7,3},{8,12},{12,8},{9,1... | collective-permute-start | bytes 2457608 | tf_op jit(solution)/shard_map/ppermute | solution.py:107
  52.8 0.9 copy-start.12
  53.7 0.7 copy-start.15
  54.4 15.3 %copy-start.17 = (f32[2,2,1664]{2,1,0:T(2,128)S(1)}, f32[2,2,1664]{2,1,0:T(2,128)}, u32[]{:S(2)}) copy-start(f32[2,2,1664]{2,1,0:T(2,128)} %constant.74.clone.refs_5_) | copy-start | bytes 79876
  54.4 15.3 %copy-start.19 = (f32[1,1280]{1,0:T(1,128)S(1)}, f32[1,1280]{1,0:T(1,128)}, u32[]{:S(2)}) copy-start(f32[1,1280]{1,0:T(1,128)} %constant.75.clone.refs_6_) | copy-start | bytes 15364
  54.4 10.5 %collective-permute-start.10 = (bf16[736,256]{1,0:T(8,128)(2,1)}, bf16[736,256]{1,0:T(8,128)(2,1)}, u32[]{:S(2)}, u32[]{:S(2)}) collective-permute-start(bf16[736,256]{1,0:T(8,128)(2,1)} %get-tuple-element.29), channel_id=1, source_target_pairs={{0,8},{8,16},{16,24},{1,9},{9,17},{17,25},{2,10},{10,18},{18,26},{... | collective-permute-start | bytes 1130504 | tf_op jit(solution)/shard_map/ppermute | solution.py:112
  58.8 11.0 %collective-permute-start.11 = (bf16[736,256]{1,0:T(8,128)(2,1)}, bf16[736,256]{1,0:T(8,128)(2,1)}, u32[]{:S(2)}, u32[]{:S(2)}) collective-permute-start(bf16[736,256]{1,0:T(8,128)(2,1)} %get-tuple-element.30), channel_id=1, source_target_pairs={{8,0},{16,8},{24,16},{9,1},{17,9},{25,17},{10,2},{18,10},{26,18},{... | collective-permute-start | bytes 1130504 | tf_op jit(solution)/shard_map/ppermute | solution.py:112
  60.3 1.1 copy-start.6
  60.3 9.4 %copy-start.13 = (bf16[1424,256]{1,0:T(8,128)(2,1)S(1)}, bf16[1424,256]{1,0:T(8,128)(2,1)}, u32[]{:S(2)}) copy-start(bf16[1424,256]{1,0:T(8,128)(2,1)} %copy-done.12) | copy-start | bytes 2187268
  60.3 9.4 %copy-start.16 = (bf16[1200,128]{1,0:T(8,128)(2,1)S(1)}, bf16[1200,128]{1,0:T(8,128)(2,1)}, u32[]{:S(2)}) copy-start(bf16[1200,128]{1,0:T(8,128)(2,1)} %copy-done.15) | copy-start | bytes 921604
  61.4 21.0 %collective-permute-start.7 = (bf16[200,1536]{1,0:T(8,128)(2,1)S(1)}, bf16[200,1536]{1,0:T(8,128)(2,1)S(1)}, u32[]{:S(2)}, u32[]{:S(2)}) collective-permute-start(bf16[200,1536]{1,0:T(8,128)(2,1)S(1)} %copy-done.6), channel_id=1, source_target_pairs={{0,4},{4,0},{1,5},{5,1},{2,6},{6,2},{3,7},{7,3},{8,12},{12,8},{9,1... | collective-permute-start | bytes 1843208 | tf_op jit(solution)/shard_map/ppermute | solution.py:107
  74.0 2.1 %copy-start.4 = (bf16[200,1536]{1,0:T(8,128)(2,1)S(1)}, bf16[200,1536]{1,0:T(8,128)(2,1)}, u32[]{:S(2)}) copy-start(bf16[200,1536]{1,0:T(8,128)(2,1)} %copy-done.3) | copy-start | bytes 1843204
  74.0 2.0 %slice-start = ((bf16[512,512]{1,0:T(8,128)(2,1)}), bf16[400,512]{1,0:T(8,128)(2,1)S(1)}, s32[]{:S(2)}) async-start(bf16[512,512]{1,0:T(8,128)(2,1)} %copy-done.7), calls=%async_computation | async-start | bytes 819200 | tf_op jit(solution)/shard_map/slice | solution.py:542
  74.0 14.2 %collective-permute-start.12 = (bf16[400,384]{1,0:T(8,128)(2,1)S(1)}, bf16[400,384]{1,0:T(8,128)(2,1)S(1)}, u32[]{:S(2)}, u32[]{:S(2)}) collective-permute-start(bf16[400,384]{1,0:T(8,128)(2,1)S(1)} %shard_map.134.refs_1_), channel_id=1, source_target_pairs={{0,4},{4,0},{1,5},{5,1},{2,6},{6,2},{3,7},{7,3},{8,12},{12,8},{9,1... | collective-permute-start | bytes 921608 | tf_op jit(solution)/shard_map/ppermute | solution.py:107
  77.1 4.2 %slice-start.1 = ((s8[4718592]{0:T(1024)(128)(4,1)}), s8[4194304]{0:T(1024)(128)(4,1)S(1)}, s32[]{:S(2)}) async-start(s8[4718592]{0:T(1024)(128)(4,1)} %bitcast.29), calls=%async_computation.1 | async-start | bytes 8388608
  77.1 4.1 %slice-start.2 = ((s8[4718592]{0:T(1024)(128)(4,1)}), s8[524288]{0:T(1024)(128)(4,1)S(1)}, s32[]{:S(2)}) async-start(s8[4718592]{0:T(1024)(128)(4,1)} %bitcast.29), calls=%async_computation.2 | async-start | bytes 1048576
  80.0 23.5 %collective-permute-start.18 = (bf16[200,1536]{1,0:T(8,128)(2,1)S(1)}, bf16[200,1536]{1,0:T(8,128)(2,1)S(1)}, u32[]{:S(2)}, u32[]{:S(2)}) collective-permute-start(bf16[200,1536]{1,0:T(8,128)(2,1)S(1)} %shard_map.141), channel_id=1, source_target_pairs={{0,4},{4,0},{1,5},{5,1},{2,6},{6,2},{3,7},{7,3},{8,12},{12,8},{9,1... | collective-permute-start | bytes 1843208 | tf_op jit(solution)/shard_map/ppermute | solution.py:107
  89.3 2.5 %collective-permute-start.15 = (bf16[400,768]{1,0:T(8,128)(2,1)S(1)}, bf16[400,768]{1,0:T(8,128)(2,1)S(1)}, u32[]{:S(2)}, u32[]{:S(2)}) collective-permute-start(bf16[400,768]{1,0:T(8,128)(2,1)S(1)} %fusion.20.refs_1_), channel_id=1, source_target_pairs={{0,1},{1,0},{2,3},{3,2},{4,5},{5,4},{6,7},{7,6},{8,9},{9,8},{10,11... | collective-permute-start | bytes 1843208 | tf_op jit(solution)/shard_map/ppermute | solution.py:107
  90.9 2.5 %collective-permute-start.13 = (bf16[200,768]{1,0:T(8,128)(2,1)S(1)}, bf16[200,768]{1,0:T(8,128)(2,1)S(1)}, u32[]{:S(2)}, u32[]{:S(2)}) collective-permute-start(bf16[200,768]{1,0:T(8,128)(2,1)S(1)} %fusion.53.refs_1_), channel_id=1, source_target_pairs={{0,1},{1,0},{2,3},{3,2},{4,5},{5,4},{6,7},{7,6},{8,9},{9,8},{10,11... | collective-permute-start | bytes 921608 | tf_op jit(solution)/shard_map/ppermute | solution.py:107
  92.0 10.2 %collective-permute-start.16 = (bf16[200,768]{1,0:T(8,128)(2,1)S(1)}, bf16[200,768]{1,0:T(8,128)(2,1)S(1)}, u32[]{:S(2)}, u32[]{:S(2)}) collective-permute-start(bf16[200,768]{1,0:T(8,128)(2,1)S(1)} %add_convert_fusion.3), channel_id=1, source_target_pairs={{0,2},{1,3},{2,0},{3,1},{4,6},{5,7},{6,4},{7,5},{8,10},{9,11},{10,... | collective-permute-start | bytes 921608 | tf_op jit(solution)/shard_map/ppermute | solution.py:107
  94.1 13.7 %collective-permute-start.14 = (bf16[200,768]{1,0:T(8,128)(2,1)S(1)}, bf16[200,768]{1,0:T(8,128)(2,1)S(1)}, u32[]{:S(2)}, u32[]{:S(2)}) collective-permute-start(bf16[200,768]{1,0:T(8,128)(2,1)S(1)} %get-tuple-element.45), channel_id=1, source_target_pairs={{0,2},{1,3},{2,0},{3,1},{4,6},{5,7},{6,4},{7,5},{8,10},{9,11},{10,... | collective-permute-start | bytes 921608 | tf_op jit(solution)/shard_map/ppermute | solution.py:107
  102.4 7.5 %collective-permute-start.17 = (bf16[200,768]{1,0:T(8,128)(2,1)S(1)}, bf16[200,768]{1,0:T(8,128)(2,1)S(1)}, u32[]{:S(2)}, u32[]{:S(2)}) collective-permute-start(bf16[200,768]{1,0:T(8,128)(2,1)S(1)} %add_convert_fusion.2.refs_1_), channel_id=1, source_target_pairs={{0,4},{4,0},{1,5},{5,1},{2,6},{6,2},{3,7},{7,3},{8,12},{12,8},{9,1... | collective-permute-start | bytes 921608 | tf_op jit(solution)/shard_map/ppermute | solution.py:107
  104.7 5.1 %collective-permute-start.19 = (bf16[200,768]{1,0:T(8,128)(2,1)S(1)}, bf16[200,768]{1,0:T(8,128)(2,1)S(1)}, u32[]{:S(2)}, u32[]{:S(2)}) collective-permute-start(bf16[200,768]{1,0:T(8,128)(2,1)S(1)} %fusion.50), channel_id=1, source_target_pairs={{0,1},{1,0},{2,3},{3,2},{4,5},{5,4},{6,7},{7,6},{8,9},{9,8},{10,11... | collective-permute-start | bytes 921608 | tf_op jit(solution)/shard_map/ppermute | solution.py:107
  110.0 6.9 %collective-permute-start.20 = (bf16[200,768]{1,0:T(8,128)(2,1)S(1)}, bf16[200,768]{1,0:T(8,128)(2,1)S(1)}, u32[]{:S(2)}, u32[]{:S(2)}) collective-permute-start(bf16[200,768]{1,0:T(8,128)(2,1)S(1)} %fusion.77), channel_id=1, source_target_pairs={{0,2},{1,3},{2,0},{3,1},{4,6},{5,7},{6,4},{7,5},{8,10},{9,11},{10,... | collective-permute-start | bytes 921608 | tf_op jit(solution)/shard_map/ppermute | solution.py:107

commit v8 on v7

--- a/solution.py
+++ b/solution.py
@@ -194,14 +194,14 @@
     return max(b for b in range(16, LANES + 1, 16) if rows % b == 0)
 
 
-def modulate_and_heads(place, tokens, scale_row, shift_row, w_heads, after=()):
+def modulate_and_heads(tokens, scale_row, shift_row, w_heads, after=()):
     rows, model_width = tokens.shape
     depth, width = w_heads.shape[1:]
     edge = (width - LANES) // 2
     block = token_block(rows)
 
-    def body(place_ref, tokens_ref, scale_ref, shift_ref, w_heads_ref, own_ref, out_ref, moments_ref):
-        side = place_ref[0]
+    def body(tokens_ref, scale_ref, shift_ref, w_heads_ref, own_ref, out_ref, moments_ref):
+        side = lax.axis_index("sx")
         cells = tokens_ref[...].astype(F32)
         mean = jnp.mean(cells, axis=-1, keepdims=True)
         centered = cells - mean
@@ -222,7 +222,6 @@
     return call(
         body, rows // block,
         [
-            (place, None, pltpu.SMEM),
             (tokens, (block, model_width), row),
             (scale_row, scale_row.shape, at(0, 0)),
             (shift_row, shift_row.shape, at(0, 0)),
@@ -237,12 +236,12 @@
     )
 
 
-def border_and_hidden(place, own, picks, w_heads, hidden_weights, cut, after=()):
+def border_and_hidden(own, picks, w_heads, hidden_weights, cut, after=()):
     rows, depth = own.shape
     half_border, width = picks.shape[1] // 2, w_heads.shape[2]
 
-    def body(place_ref, own_ref, picks_ref, keys_ref, values_ref, w_ref, out_ref):
-        taken = dot(picks_ref[place_ref[0]], own_ref[...]).astype(BF16)
+    def body(own_ref, picks_ref, keys_ref, values_ref, w_ref, out_ref):
+        taken = dot(picks_ref[lax.axis_index("sx")], own_ref[...]).astype(BF16)
         out_ref[:rows] = dot(own_ref[...], w_ref[...]).astype(BF16)
         for g, ref in enumerate((keys_ref, values_ref)):
             part = dot(taken, ref[0]).astype(BF16)
@@ -253,7 +252,7 @@
     middle = (width - LANES) // 2 // LANES
     return call(
         body, 1,
-        [(place, None, pltpu.SMEM), (own, own.shape, whole), (picks, picks.shape, at(0, 0, 0))]
+        [(own, own.shape, whole), (picks, picks.shape, at(0, 0, 0))]
         + [(w_heads, (1, depth, LANES), at(g, 0, middle)) for g in (1, 2)]
         + [(hidden_weights, (depth, cut), whole)],
         [((rows + half_border, cut), BF16, (rows + half_border, cut), whole)],
@@ -494,13 +493,12 @@
     edge = pair * head_dim
     w_heads = jnp.transpose(w_qkv, (1, 0, 2))
 
-    own, own_early, moments = modulate_and_heads(place, tokens, mod_scale[None], mod_shift[None], w_heads, [sent])
+    own, own_early, moments = modulate_and_heads(tokens, mod_scale[None], mod_shift[None], w_heads, [sent])
     got_early, got_moments = swap(own_early, "sx", 1), swap(moments, "sx", 1)
-    piece = hold(piece, own_early)
     near = swap(piece, "tp", 1)
     piece_far = hold(swap(piece, "tp", 2), got_early, got_moments)
     first_part = width_of(hidden // 3, hidden)
-    own_first = border_and_hidden(place, own, picks, w_heads, w_mlp_in, first_part, [own_early, piece])
+    own_first = border_and_hidden(own, picks, w_heads, w_mlp_in, first_part, [moments, piece])
     got_first = swap(own_first, "sx", 1)
     piece_far = hold(piece_far, own_first)
     near_far = swap(piece_far, "tp", 1)
@@ -563,7 +561,7 @@
     own_attended = natural(attended[:, :edge], attended[:, edge:here], got_attended[:, here:])
     other_attended = natural(attended[:, here:], got_attended[:, edge:here], got_attended[:, :edge])
     other_sent = (other_sent + dot(other_attended, sent_attn)).astype(BF16)
-    other_kept = other_kept + dot(other_attended, kept_attn)
+    other_kept = other_kept + dot(hold(other_attended, other_sent), kept_attn)
     other_come = swap(other_sent, "tp", 1)
     own_sent_a, own_kept_a = own_part(0, cut, got_other_a, other_sent, other_kept)
 

time: 118 us -> 117 us (level)
  starting transfers between devices: 25.9 us -> 23.8 us
  waiting for transfers between devices: 41.4 us -> 42.7 us
    ppermute x19, starting transfers between devices: 20.1 us -> 17.9 us  [swap(): return lax.ppermute(cells, axis, [(i, i ^ bit) for i in range(count)])]
  transfers between devices with their start and end apart: 21 -> 21, of which waited for: 11 -> 10; matrix products, arithmetic and copies ran while one was open for 15% -> 15% of each run, Pallas kernels for 22% -> 23%
where the time goes in v8:
time: 117 us; the launch traced here: 116 us
  waiting for transfers between devices  42.7 us (36%)
  Pallas kernels  26.4 us (23%)
  starting transfers between devices  23.8 us (20%)
  matrix products  10.5 us (9%)
  other arithmetic  7.38 us (6%)
  local copies, waits for them, and re-layouts  5.06 us (4%)
    ppermute x19, waiting for transfers between devices, swap(): return lax.ppermute(cells, axis, [(i, i ^ bit) for i in range(count)])  34.7 us
    pallas_call x5, Pallas kernels, call(): pl.pallas_call(kernel, grid=(grid,), in_specs=[spec(b, i) for _, b, i in...  26.4 us
    ppermute x19, starting transfers between devices, swap(): return lax.ppermute(cells, axis, [(i, i ^ bit) for i in range(count)])  17.9 us
    dot_general x15, matrix products, dot(): return jnp.dot(left, right, preferred_element_type=jnp.float32)  10.5 us
    ppermute x2, waiting for transfers between devices, shift(): lax.ppermute(cells, axis, [(i, i + step) for i in range(count) if 0 <= i...  8.01 us
    ppermute x2, starting transfers between devices, shift(): lax.ppermute(cells, axis, [(i, i + step) for i in range(count) if 0 <= i...  5.81 us
    unnamed x54, local copies, waits for them, and re-layouts  2.78 us
  transfers between devices with their start and end apart: 21, of which 10 were waited for; matrix products, arithmetic and copies ran while one was open for 15% of the time, Pallas kernels for 23%

profile of v8, /device:TPU:0, one launch (start us, length us, event | category | flops | bytes accessed | tf_op | source)
XLA Modules:
  0.0 116.4 jit_solution(8426040985818241686)
XLA Ops:
  0.0 1.1 constant_dynamic-slice_fusion.refs_4_
  1.1 3.0 %collective-permute-start = (bf16[400,384]{1,0:T(8,128)(2,1)S(1)}, bf16[400,384]{1,0:T(8,128)(2,1)S(1)}, u32[]{:S(2)}, u32[]{:S(2)}) collective-permute-start(bf16[400,384]{1,0:T(8,128)(2,1)S(1)} %constant_dynamic-slice_fusion.refs_4_), channel_id=1, source_target_pairs={{0,4},{4,0},{1,5},{5,1},{2,6},{6,2},{3,7},{7,3},{8,12},{12,8},{9,1... | collective-permute-start | bytes 921608 | tf_op jit(solution)/shard_map/ppermute | solution.py:107
  4.1 7.1 %shard_map.127 = (bf16[400,1536]{1,0:T(8,128)(2,1)}, bf16[400,384]{1,0:T(8,128)(2,1)}, f32[5,8,128]{2,1,0:T(8,128)}) custom-call(bf16[400,3072]{1,0:T(8,128)(2,1)} %refs_0_.1, f32[1,3072]{1,0:T(1,128)} %bitcast.33, f32[1,3072]{1,0:T(1,128)} %bitcast.32, bf16[3,1536,384]{2,1,0:T(8,128)(2,1)} %bitcast.26, bf16[400,384]{1,0:T(8,128)(2,1)} %copy-done.18), custom_call_target="tpu_custom_call" | custom-call | flops 1000 | bytes 1000 | tf_op jit(solution)/shard_map/pallas_call | solution.py:144
  11.3 0.6 collective-permute-start.2
  11.9 1.5 %collective-permute-start.1 = (bf16[400,384]{1,0:T(8,128)(2,1)S(1)}, bf16[400,384]{1,0:T(8,128)(2,1)S(1)}, u32[]{:S(2)}, u32[]{:S(2)}) collective-permute-start(bf16[400,384]{1,0:T(8,128)(2,1)S(1)} %collective-permute-done.refs_6_), channel_id=1, source_target_pairs={{0,2},{1,3},{2,0},{3,1},{4,6},{5,7},{6,4},{7,5},{8,10},{9,11},{10,... | collective-permute-start | bytes 921608 | tf_op jit(solution)/shard_map/ppermute | solution.py:107
  13.4 1.4 %collective-permute-start.3 = (f32[5,8,128]{2,1,0:T(8,128)}, f32[5,8,128]{2,1,0:T(8,128)S(1)}, u32[]{:S(2)}, u32[]{:S(2)}) collective-permute-start(f32[5,8,128]{2,1,0:T(8,128)} %get-tuple-element.19.refs_5_), channel_id=1, source_target_pairs={{0,4},{4,0},{1,5},{5,1},{2,6},{6,2},{3,7},{7,3},{8,12},{12,8},{9,1... | collective-permute-start | bytes 61448 | tf_op jit(solution)/shard_map/ppermute | solution.py:107
  14.9 4.5 %shard_map.128.refs_1_ = bf16[512,512]{1,0:T(8,128)(2,1)} custom-call(bf16[400,1536]{1,0:T(8,128)(2,1)} %get-tuple-element.18.refs_0_.refs_1_, bf16[2,224,400]{2,1,0:T(8,128)(2,1)} %constant.73.clone.refs_1_.refs_3_, bf16[3,1536,384]{2,1,0:T(8,128)(2,1)} %bitcast.27, bf16[3,1536,384]{2,1,0:T(8,128)(2,1)} %bitcast.28, bf16[1536,1536]{1,0:T(8,128)(2,1)} %refs_5_.2, ...), custom_call_target="tpu_custom_call" | custom-call | flops 1000 | bytes 1000 | tf_op jit(solution)/shard_map/pallas_call | solution.py:144
  19.4 1.3 %collective-permute-done.3.refs_2_ = f32[5,8,128]{2,1,0:T(8,128)S(1)} collective-permute-done((f32[5,8,128]{2,1,0:T(8,128)}, f32[5,8,128]{2,1,0:T(8,128)S(1)}, u32[]{:S(2)}, u32[]{:S(2)}) %collective-permute-start.3) | collective-permute-done | bytes 20512 | tf_op jit(solution)/shard_map/ppermute | solution.py:107
  20.7 0.3 collective-permute-start.5
  21.4 0.7 collective-permute-start.6
  22.1 0.7 copy-done.20
  22.9 1.5 %broadcast_select_fusion.7 = (bf16[400,384]{1,0:T(8,128)(2,1)S(1)}, bf16[400,384]{1,0:T(8,128)(2,1)S(1)}, bf16[400,384]{1,0:T(8,128)(2,1)S(1)}, bf16[400,384]{1,0:T(8,128)(2,1)S(1)}) fusion(pred[]{:T(512)S(6)} %eq.13, bf16[400,384]{1,0:T(8,128)(2,1)} %copy-done.19, bf16[400,384]{1,0:T(8,128)(2,1)S(1)} %shard_map.130, pred[]{:T(512)S(6)} %eq.14, ...), kind=kLoop, calls=%fused_computation.96 | loop fusion | flops 1228800 | bytes 2457602 | tf_op jit(solution)/shard_map/jit(_where)/select_n | solution.py:157
  24.3 0.5 add_convert_fusion.refs_2_
  24.9 0.2 copy-done.1
  25.1 0.5 convolution_convert_fusion.1
  25.6 0.5 convolution_convert_fusion.2
  26.1 0.5 convolution_convert_fusion
  26.7 1.4 %collective-permute-start.9 = (bf16[400,768]{1,0:T(8,128)(2,1)S(1)}, bf16[400,768]{1,0:T(8,128)(2,1)S(1)}, u32[]{:S(2)}, u32[]{:S(2)}) collective-permute-start(bf16[400,768]{1,0:T(8,128)(2,1)S(1)} %pad_maximum_fusion.1.refs_6_), channel_id=1, source_target_pairs={{0,4},{4,0},{1,5},{5,1},{2,6},{6,2},{3,7},{7,3},{8,12},{12,8},{9,1... | collective-permute-start | bytes 1843208 | tf_op jit(solution)/shard_map/ppermute | solution.py:107
  28.1 8.1 %collective-permute-done.6.refs_7_.refs_6_ = bf16[512,512]{1,0:T(8,128)(2,1)S(1)} collective-permute-done((bf16[512,512]{1,0:T(8,128)(2,1)S(1)}, bf16[512,512]{1,0:T(8,128)(2,1)S(1)}, u32[]{:S(2)}, u32[]{:S(2)}) %collective-permute-start.6) | collective-permute-done | bytes 524320 | tf_op jit(solution)/shard_map/ppermute | solution.py:107
  36.1 8.7 %shard_map.131 = (f32[400,768]{1,0:T(8,128)S(1)}, f32[400,384]{1,0:T(8,128)S(1)}, f32[224,256]{1,0:T(8,128)S(1)}, bf16[400,1024]{1,0:T(8,128)(2,1)S(1)}, bf16[20...) custom-call(s32[4]{0:T(128)S(1)} %pad_add_fusion.refs_0_, bf16[400,1536]{1,0:T(8,128)(2,1)S(1)} %copy-done.10, ...), custom_call_target="tpu_custom_call" | custom-call | flops 3951034368 | bytes 13787136 | tf_op jit(solution)/shard_map/pallas_call | solution.py:144
  44.8 0.8 collective-permute-start.8
  45.7 3.6 %collective-permute-done.9.refs_2_ = bf16[400,768]{1,0:T(8,128)(2,1)S(1)} collective-permute-done((bf16[400,768]{1,0:T(8,128)(2,1)S(1)}, bf16[400,768]{1,0:T(8,128)(2,1)S(1)}, u32[]{:S(2)}, u32[]{:S(2)}) %collective-permute-start.9) | collective-permute-done | bytes 614432 | tf_op jit(solution)/shard_map/ppermute | solution.py:107
  49.3 1.9 %shard_map.132 = (bf16[1200,128]{1,0:T(8,128)(2,1)S(1)}, bf16[1424,256]{1,0:T(8,128)(2,1)S(1)}, bf16[736,256]{1,0:T(8,128)(2,1)}, bf16[736,256]{1,0:T(8,128)(2,1)}) custom-call(s32[4]{0:T(128)S(1)} %pad_add_fusion.refs_0_, f32[400,768]{1,0:T(8,128)S(1)} %get-tuple-element.24.refs_1_, bf16[400,768]{1,0:T(8,128)(2,1)S(1)} %collective-permute-done.9.refs_2_, ...), custom_call_target="tpu_custom_call" | custom-call | flops 1000 | bytes 1000 | tf_op jit(solution)/shard_map/pallas_call | solution.py:144
  51.2 0.9 copy-done.11
  52.1 0.7 copy-done.14
  52.8 4.3 %collective-permute-start.10 = (bf16[736,256]{1,0:T(8,128)(2,1)}, bf16[736,256]{1,0:T(8,128)(2,1)}, u32[]{:S(2)}, u32[]{:S(2)}) collective-permute-start(bf16[736,256]{1,0:T(8,128)(2,1)} %get-tuple-element.29), channel_id=1, source_target_pairs={{0,8},{8,16},{16,24},{1,9},{9,17},{17,25},{2,10},{10,18},{18,26},{... | collective-permute-start | bytes 1130504 | tf_op jit(solution)/shard_map/ppermute | solution.py:112
  57.2 1.5 %collective-permute-start.11 = (bf16[736,256]{1,0:T(8,128)(2,1)}, bf16[736,256]{1,0:T(8,128)(2,1)}, u32[]{:S(2)}, u32[]{:S(2)}) collective-permute-start(bf16[736,256]{1,0:T(8,128)(2,1)} %get-tuple-element.30), channel_id=1, source_target_pairs={{8,0},{16,8},{24,16},{9,1},{17,9},{25,17},{10,2},{18,10},{26,18},{... | collective-permute-start | bytes 1130504 | tf_op jit(solution)/shard_map/ppermute | solution.py:112
  58.7 0.9 dynamic_slice.31
  59.8 0.7 collective-permute-start.7
  60.5 3.2 %collective-permute-done.10.refs_3_ = bf16[736,256]{1,0:T(8,128)(2,1)} collective-permute-done((bf16[736,256]{1,0:T(8,128)(2,1)}, bf16[736,256]{1,0:T(8,128)(2,1)}, u32[]{:S(2)}, u32[]{:S(2)}) %collective-permute-start.10) | collective-permute-done | bytes 376864 | tf_op jit(solution)/shard_map/ppermute | solution.py:112
  63.6 4.8 %collective-permute-done.11.refs_4_ = bf16[736,256]{1,0:T(8,128)(2,1)} collective-permute-done((bf16[736,256]{1,0:T(8,128)(2,1)}, bf16[736,256]{1,0:T(8,128)(2,1)}, u32[]{:S(2)}, u32[]{:S(2)}) %collective-permute-start.11) | collective-permute-done | bytes 376864 | tf_op jit(solution)/shard_map/ppermute | solution.py:112
  68.5 4.2 %shard_map.133.refs_1_ = bf16[400,384]{1,0:T(8,128)(2,1)S(1)} custom-call(s32[4]{0:T(128)S(1)} %pad_add_fusion.refs_0_, bf16[1200,128]{1,0:T(8,128)(2,1)S(1)} %copy-done.15, bf16[1424,256]{1,0:T(8,128)(2,1)S(1)} %copy-done.12, bf16[736,256]{1,0:T(8,128)(2,1)} %collective-permute-done.10.refs_3_, bf16[736,256]{1,0:T(8,128)(2,1)} %collective-permute-done.11.refs_4_, ...), custom_call_target="tpu_custom_call" | custom-call | flops 1000 | bytes 1000 | tf_op jit(solution)/shard_map/pallas_call | solution.py:144
  72.8 1.4 %collective-permute-start.12 = (bf16[400,384]{1,0:T(8,128)(2,1)S(1)}, bf16[400,384]{1,0:T(8,128)(2,1)S(1)}, u32[]{:S(2)}, u32[]{:S(2)}) collective-permute-start(bf16[400,384]{1,0:T(8,128)(2,1)S(1)} %shard_map.133.refs_1_), channel_id=1, source_target_pairs={{0,4},{4,0},{1,5},{5,1},{2,6},{6,2},{3,7},{7,3},{8,12},{12,8},{9,1... | collective-permute-start | bytes 921608 | tf_op jit(solution)/shard_map/ppermute | solution.py:107
  74.2 1.0 fusion.7.refs_0_
  75.2 2.9 %fusion.18.refs_1_ = f32[400,768]{1,0:T(8,128)S(1)} fusion(bf16[400,1536]{1,0:T(8,128)(2,1)S(1)} %shard_map.135, bf16[1536,1536]{1,0:T(8,128)(2,1)} %param.22, s32[]{:T(128)S(6)} %select_n.168), kind=kOutput, calls=%fused_computation.22 | convolution fusion | flops 943718400 | bytes 4816900 | tf_op jit(solution)/shard_map/dot_general | solution.py:118
  78.2 1.2 collective-permute-start.18
  79.3 1.1 fusion.12.refs_2_
  80.5 6.1 %collective-permute-done.12.refs_0_ = bf16[400,384]{1,0:T(8,128)(2,1)S(1)} collective-permute-done((bf16[400,384]{1,0:T(8,128)(2,1)S(1)}, bf16[400,384]{1,0:T(8,128)(2,1)S(1)}, u32[]{:S(2)}, u32[]{:S(2)}) %collective-permute-start.12) | collective-permute-done | bytes 307232 | tf_op jit(solution)/shard_map/ppermute | solution.py:107
  86.7 0.5 fusion.20.refs_1_
  87.3 0.5 convolution_add_fusion.refs_2_
  87.8 0.5 fusion.40.refs_0_
  88.4 0.3 fusion.72
  88.7 0.7 fusion.53.refs_1_
  89.4 0.6 collective-permute-start.13
  89.9 0.3 fusion.67
  90.3 0.2 add_convert_fusion.3
  90.4 1.3 %collective-permute-start.16 = (bf16[200,768]{1,0:T(8,128)(2,1)S(1)}, bf16[200,768]{1,0:T(8,128)(2,1)S(1)}, u32[]{:S(2)}, u32[]{:S(2)}) collective-permute-start(bf16[200,768]{1,0:T(8,128)(2,1)S(1)} %add_convert_fusion.3), channel_id=1, source_target_pairs={{0,2},{1,3},{2,0},{3,1},{4,6},{5,7},{6,4},{7,5},{8,10},{9,11},{10,... | collective-permute-start | bytes 921608 | tf_op jit(solution)/shard_map/ppermute | solution.py:107
  91.7 0.3 fusion.70
  92.0 0.7 fusion.75
  92.7 0.9 collective-permute-start.14
  93.6 7.0 %collective-permute-done.16.refs_0_ = bf16[200,768]{1,0:T(8,128)(2,1)S(1)} collective-permute-done((bf16[200,768]{1,0:T(8,128)(2,1)S(1)}, bf16[200,768]{1,0:T(8,128)(2,1)S(1)}, u32[]{:S(2)}, u32[]{:S(2)}) %collective-permute-start.16) | collective-permute-done | bytes 307232 | tf_op jit(solution)/shard_map/ppermute | solution.py:107
  100.6 0.2 add_convert_fusion.2.refs_1_
  100.8 0.8 collective-permute-start.17
  101.6 0.5 fusion.48.refs_0_
  102.1 0.7 fusion.50
  102.9 0.3 fusion.65
  103.2 0.7 fusion.30.refs_0_
  103.9 2.4 %collective-permute-done.14.refs_2_ = bf16[200,768]{1,0:T(8,128)(2,1)S(1)} collective-permute-done((bf16[200,768]{1,0:T(8,128)(2,1)S(1)}, bf16[200,768]{1,0:T(8,128)(2,1)S(1)}, u32[]{:S(2)}, u32[]{:S(2)}) %collective-permute-start.14) | collective-permute-done | bytes 307232 | tf_op jit(solution)/shard_map/ppermute | solution.py:107
  106.3 2.0 %collective-permute-done.17.refs_1_ = bf16[200,768]{1,0:T(8,128)(2,1)S(1)} collective-permute-done((bf16[200,768]{1,0:T(8,128)(2,1)S(1)}, bf16[200,768]{1,0:T(8,128)(2,1)S(1)}, u32[]{:S(2)}, u32[]{:S(2)}) %collective-permute-start.17) | collective-permute-done | bytes 307232 | tf_op jit(solution)/shard_map/ppermute | solution.py:107
  108.4 1.3 %collective-permute-start.20 = (bf16[200,768]{1,0:T(8,128)(2,1)S(1)}, bf16[200,768]{1,0:T(8,128)(2,1)S(1)}, u32[]{:S(2)}, u32[]{:S(2)}) collective-permute-start(bf16[200,768]{1,0:T(8,128)(2,1)S(1)} %fusion.77), channel_id=1, source_target_pairs={{0,2},{1,3},{2,0},{3,1},{4,6},{5,7},{6,4},{7,5},{8,10},{9,11},{10,... | collective-permute-start | bytes 921608 | tf_op jit(solution)/shard_map/ppermute | solution.py:107
  109.7 0.3 fusion.62
  110.0 1.2 %fusion.49.refs_0_ = f32[400,768]{1,0:T(8,128)S(1)} fusion(f32[200,768]{1,0:T(8,128)S(1)} %get-tuple-element.42, f32[200,768]{1,0:T(8,128)S(1)} %get-tuple-element.41, f32[768]{0:T(1024)S(1)} %dynamic_slice.31, bf16[400,3072]{1,0:T(8,128)(2,1)} %refs_0_.1, s32[]{:T(128)S(6)} %select_n.151), kind=kLoop, calls=%fused_computation.50 | loop fusion | flops 1228800 | bytes 3075076 | tf_op jit(solution)/shard_map/add | solution.py:594
  111.2 4.1 %collective-permute-done.20 = bf16[200,768]{1,0:T(8,128)(2,1)S(1)} collective-permute-done((bf16[200,768]{1,0:T(8,128)(2,1)S(1)}, bf16[200,768]{1,0:T(8,128)(2,1)S(1)}, u32[]{:S(2)}, u32[]{:S(2)}) %collective-permute-start.20) | collective-permute-done | bytes 307232 | tf_op jit(solution)/shard_map/ppermute | solution.py:107
  115.3 1.0 add_convert_fusion.1
  (96 shorter events, 1.2 us)
Async XLA Ops:
  0.0 86.7 %copy-start = (bf16[384,1536]{1,0:T(8,128)(2,1)S(1)}, bf16[384,1536]{1,0:T(8,128)(2,1)}, u32[]{:S(2)}) copy-start(bf16[384,1536]{1,0:T(8,128)(2,1)} %param.21) | copy-start | bytes 3538948
  1.1 3.0 %copy-start.18 = (bf16[400,384]{1,0:T(8,128)(2,1)}, bf16[400,384]{1,0:T(8,128)(2,1)S(1)}, u32[]{:S(2)}) copy-start(bf16[400,384]{1,0:T(8,128)(2,1)S(1)} %constant_dynamic-slice_fusion.refs_4_) | copy-start | bytes 921604
  1.1 10.8 %collective-permute-start = (bf16[400,384]{1,0:T(8,128)(2,1)S(1)}, bf16[400,384]{1,0:T(8,128)(2,1)S(1)}, u32[]{:S(2)}, u32[]{:S(2)}) collective-permute-start(bf16[400,384]{1,0:T(8,128)(2,1)S(1)} %constant_dynamic-slice_fusion.refs_4_), channel_id=1, source_target_pairs={{0,4},{4,0},{1,5},{5,1},{2,6},{6,2},{3,7},{7,3},{8,12},{12,8},{9,1... | collective-permute-start | bytes 921608 | tf_op jit(solution)/shard_map/ppermute | solution.py:107
  4.1 10.7 %copy-start.21 = (f32[3072]{0:T(1024)S(1)}, f32[3072]{0:T(1024)}, u32[]{:S(2)}) copy-start(f32[3072]{0:T(1024)} %param.14) | copy-start | bytes 36868
  11.3 9.4 %collective-permute-start.2 = (bf16[400,384]{1,0:T(8,128)(2,1)}, bf16[400,384]{1,0:T(8,128)(2,1)S(1)}, u32[]{:S(2)}, u32[]{:S(2)}) collective-permute-start(bf16[400,384]{1,0:T(8,128)(2,1)} %get-tuple-element.20), channel_id=1, source_target_pairs={{0,4},{4,0},{1,5},{5,1},{2,6},{6,2},{3,7},{7,3},{8,12},{12,8},{9,1... | collective-permute-start | bytes 921608 | tf_op jit(solution)/shard_map/ppermute | solution.py:107
  11.9 3.0 %copy-start.19 = (bf16[400,384]{1,0:T(8,128)(2,1)}, bf16[400,384]{1,0:T(8,128)(2,1)S(1)}, u32[]{:S(2)}) copy-start(bf16[400,384]{1,0:T(8,128)(2,1)S(1)} %collective-permute-done.refs_6_) | copy-start | bytes 921604
  11.9 8.8 %collective-permute-start.1 = (bf16[400,384]{1,0:T(8,128)(2,1)S(1)}, bf16[400,384]{1,0:T(8,128)(2,1)S(1)}, u32[]{:S(2)}, u32[]{:S(2)}) collective-permute-start(bf16[400,384]{1,0:T(8,128)(2,1)S(1)} %collective-permute-done.refs_6_), channel_id=1, source_target_pairs={{0,2},{1,3},{2,0},{3,1},{4,6},{5,7},{6,4},{7,5},{8,10},{9,11},{10,... | collective-permute-start | bytes 921608 | tf_op jit(solution)/shard_map/ppermute | solution.py:107
  13.4 7.3 %collective-permute-start.3 = (f32[5,8,128]{2,1,0:T(8,128)}, f32[5,8,128]{2,1,0:T(8,128)S(1)}, u32[]{:S(2)}, u32[]{:S(2)}) collective-permute-start(f32[5,8,128]{2,1,0:T(8,128)} %get-tuple-element.19.refs_5_), channel_id=1, source_target_pairs={{0,4},{4,0},{1,5},{5,1},{2,6},{6,2},{3,7},{7,3},{8,12},{12,8},{9,1... | collective-permute-start | bytes 61448 | tf_op jit(solution)/shard_map/ppermute | solution.py:107
  14.9 7.2 %collective-permute-start.4 = (bf16[400,384]{1,0:T(8,128)(2,1)S(1)}, bf16[400,384]{1,0:T(8,128)(2,1)S(1)}, u32[]{:S(2)}, u32[]{:S(2)}) collective-permute-start(bf16[400,384]{1,0:T(8,128)(2,1)S(1)} %collective-permute-done.refs_6_), channel_id=1, source_target_pairs={{0,1},{1,0},{2,3},{3,2},{4,5},{5,4},{6,7},{7,6},{8,9},{9,8},{10,11... | collective-permute-start | bytes 921608 | tf_op jit(solution)/shard_map/ppermute | solution.py:107
  19.4 1.3 %copy-start.2 = (bf16[512,512]{1,0:T(8,128)(2,1)S(1)}, bf16[512,512]{1,0:T(8,128)(2,1)}, u32[]{:S(2)}) copy-start(bf16[512,512]{1,0:T(8,128)(2,1)} %shard_map.128.refs_1_) | copy-start | bytes 1572868
  19.4 1.7 %copy-start.22 = (f32[3072]{0:T(1024)S(1)}, f32[3072]{0:T(1024)}, u32[]{:S(2)}) copy-start(f32[3072]{0:T(1024)} %param.15) | copy-start | bytes 36868
  20.7 3.7 %copy-start.8 = (bf16[400,384]{1,0:T(8,128)(2,1)}, bf16[400,384]{1,0:T(8,128)(2,1)S(1)}, u32[]{:S(2)}) copy-start(bf16[400,384]{1,0:T(8,128)(2,1)S(1)} %collective-permute-done.2.refs_1_.refs_4_) | copy-start | bytes 921604
  20.7 2.1 %collective-permute-start.5 = (bf16[400,384]{1,0:T(8,128)(2,1)S(1)}, bf16[400,384]{1,0:T(8,128)(2,1)}, u32[]{:S(2)}, u32[]{:S(2)}) collective-permute-start(bf16[400,384]{1,0:T(8,128)(2,1)S(1)} %shard_map.130), channel_id=1, source_target_pairs={{0,1},{1,0},{2,3},{3,2},{4,5},{5,4},{6,7},{7,6},{8,9},{9,8},{10,11... | collective-permute-start | bytes 921608 | tf_op jit(solution)/shard_map/ppermute | solution.py:107
  21.4 14.8 %collective-permute-start.6 = (bf16[512,512]{1,0:T(8,128)(2,1)S(1)}, bf16[512,512]{1,0:T(8,128)(2,1)S(1)}, u32[]{:S(2)}, u32[]{:S(2)}) collective-permute-start(bf16[512,512]{1,0:T(8,128)(2,1)S(1)} %copy-done.2), channel_id=1, source_target_pairs={{0,4},{4,0},{1,5},{5,1},{2,6},{6,2},{3,7},{7,3},{8,12},{12,8},{9,1... | collective-permute-start | bytes 1572872 | tf_op jit(solution)/shard_map/ppermute | solution.py:107
  22.1 0.7 copy-start.20
  22.8 2.3 %copy-start.1 = (bf16[1536,3,384]{2,0,1:T(8,128)(2,1)S(1)}, bf16[1536,3,384]{2,0,1:T(8,128)(2,1)}, u32[]{:S(2)}) copy-start(bf16[1536,3,384]{2,0,1:T(8,128)(2,1)} %param.17) | copy-start | bytes 10616836
  26.1 10.0 %copy-start.13 = (bf16[2,224,400]{2,1,0:T(8,128)(2,1)S(1)}, bf16[2,224,400]{2,1,0:T(8,128)(2,1)}, u32[]{:S(2)}) copy-start(bf16[2,224,400]{2,1,0:T(8,128)(2,1)} %constant.73.clone.refs_1_.refs_3_) | copy-start | bytes 1075204
  26.6 9.5 %copy-start.10 = (bf16[400,1536]{1,0:T(8,128)(2,1)S(1)}, bf16[400,1536]{1,0:T(8,128)(2,1)}, u32[]{:S(2)}) copy-start(bf16[400,1536]{1,0:T(8,128)(2,1)} %get-tuple-element.18.refs_0_.refs_1_) | copy-start | bytes 3686404
  26.7 19.0 %copy-start.23 = (f32[3,128]{1,0:T(4,128)S(1)}, f32[3,128]{1,0:T(4,128)}, u32[]{:S(2)}) copy-start(f32[3,128]{1,0:T(4,128)} %param.19) | copy-start | bytes 4612
  26.7 18.9 %copy-start.24 = (f32[3,128]{1,0:T(4,128)S(1)}, f32[3,128]{1,0:T(4,128)}, u32[]{:S(2)}) copy-start(f32[3,128]{1,0:T(4,128)} %param.20) | copy-start | bytes 4612
  26.7 22.6 %copy-start.9 = (bf16[400,384]{1,0:T(8,128)(2,1)S(1)}, bf16[400,384]{1,0:T(8,128)(2,1)}, u32[]{:S(2)}) copy-start(bf16[400,384]{1,0:T(8,128)(2,1)} %copy-done.8) | copy-start | bytes 921604
  26.7 22.6 %collective-permute-start.9 = (bf16[400,768]{1,0:T(8,128)(2,1)S(1)}, bf16[400,768]{1,0:T(8,128)(2,1)S(1)}, u32[]{:S(2)}, u32[]{:S(2)}) collective-permute-start(bf16[400,768]{1,0:T(8,128)(2,1)S(1)} %pad_maximum_fusion.1.refs_6_), channel_id=1, source_target_pairs={{0,4},{4,0},{1,5},{5,1},{2,6},{6,2},{3,7},{7,3},{8,12},{12,8},{9,1... | collective-permute-start | bytes 1843208 | tf_op jit(solution)/shard_map/ppermute | solution.py:107
  36.1 13.2 %copy-start.7 = (bf16[512,512]{1,0:T(8,128)(2,1)}, bf16[512,512]{1,0:T(8,128)(2,1)S(1)}, u32[]{:S(2)}) copy-start(bf16[512,512]{1,0:T(8,128)(2,1)S(1)} %collective-permute-done.6.refs_7_.refs_6_) | copy-start | bytes 1572868
  44.8 6.4 %copy-start.3 = (bf16[200,1536]{1,0:T(8,128)(2,1)}, bf16[200,1536]{1,0:T(8,128)(2,1)S(1)}, u32[]{:S(2)}) copy-start(bf16[200,1536]{1,0:T(8,128)(2,1)S(1)} %get-tuple-element.23.refs_0_) | copy-start | bytes 1843204
  44.8 6.4 %copy-start.5 = (bf16[200,1536]{1,0:T(8,128)(2,1)}, bf16[200,1536]{1,0:T(8,128)(2,1)S(1)}, u32[]{:S(2)}) copy-start(bf16[200,1536]{1,0:T(8,128)(2,1)S(1)} %get-tuple-element.22.refs_9_) | copy-start | bytes 1843204
  44.8 29.3 %collective-permute-start.8 = (bf16[400,1024]{1,0:T(8,128)(2,1)S(1)}, bf16[400,1024]{1,0:T(8,128)(2,1)S(1)}, u32[]{:S(2)}, u32[]{:S(2)}) collective-permute-start(bf16[400,1024]{1,0:T(8,128)(2,1)S(1)} %get-tuple-element.21), channel_id=1, source_target_pairs={{0,4},{4,0},{1,5},{5,1},{2,6},{6,2},{3,7},{7,3},{8,12},{12,8},{9,1... | collective-permute-start | bytes 2457608 | tf_op jit(solution)/shard_map/ppermute | solution.py:107
  51.2 0.9 copy-start.11
  52.1 0.7 copy-start.14
  52.8 15.7 %copy-start.16 = (f32[2,2,1664]{2,1,0:T(2,128)S(1)}, f32[2,2,1664]{2,1,0:T(2,128)}, u32[]{:S(2)}) copy-start(f32[2,2,1664]{2,1,0:T(2,128)} %constant.74.clone.refs_5_) | copy-start | bytes 79876
  52.8 15.7 %copy-start.17 = (f32[1,1280]{1,0:T(1,128)S(1)}, f32[1,1280]{1,0:T(1,128)}, u32[]{:S(2)}) copy-start(f32[1,1280]{1,0:T(1,128)} %constant.75.clone.refs_6_) | copy-start | bytes 15364
  52.8 10.8 %collective-permute-start.10 = (bf16[736,256]{1,0:T(8,128)(2,1)}, bf16[736,256]{1,0:T(8,128)(2,1)}, u32[]{:S(2)}, u32[]{:S(2)}) collective-permute-start(bf16[736,256]{1,0:T(8,128)(2,1)} %get-tuple-element.29), channel_id=1, source_target_pairs={{0,8},{8,16},{16,24},{1,9},{9,17},{17,25},{2,10},{10,18},{18,26},{... | collective-permute-start | bytes 1130504 | tf_op jit(solution)/shard_map/ppermute | solution.py:112
  57.2 11.3 %collective-permute-start.11 = (bf16[736,256]{1,0:T(8,128)(2,1)}, bf16[736,256]{1,0:T(8,128)(2,1)}, u32[]{:S(2)}, u32[]{:S(2)}) collective-permute-start(bf16[736,256]{1,0:T(8,128)(2,1)} %get-tuple-element.30), channel_id=1, source_target_pairs={{8,0},{16,8},{24,16},{9,1},{17,9},{25,17},{10,2},{18,10},{26,18},{... | collective-permute-start | bytes 1130504 | tf_op jit(solution)/shard_map/ppermute | solution.py:112
  58.7 1.1 copy-start.6
  58.7 9.8 %copy-start.12 = (bf16[1424,256]{1,0:T(8,128)(2,1)S(1)}, bf16[1424,256]{1,0:T(8,128)(2,1)}, u32[]{:S(2)}) copy-start(bf16[1424,256]{1,0:T(8,128)(2,1)} %copy-done.11) | copy-start | bytes 2187268
  58.7 9.8 %copy-start.15 = (bf16[1200,128]{1,0:T(8,128)(2,1)S(1)}, bf16[1200,128]{1,0:T(8,128)(2,1)}, u32[]{:S(2)}) copy-start(bf16[1200,128]{1,0:T(8,128)(2,1)} %copy-done.14) | copy-start | bytes 921604
  59.8 20.7 %collective-permute-start.7 = (bf16[200,1536]{1,0:T(8,128)(2,1)S(1)}, bf16[200,1536]{1,0:T(8,128)(2,1)S(1)}, u32[]{:S(2)}, u32[]{:S(2)}) collective-permute-start(bf16[200,1536]{1,0:T(8,128)(2,1)S(1)} %copy-done.6), channel_id=1, source_target_pairs={{0,4},{4,0},{1,5},{5,1},{2,6},{6,2},{3,7},{7,3},{8,12},{12,8},{9,1... | collective-permute-start | bytes 1843208 | tf_op jit(solution)/shard_map/ppermute | solution.py:107
  72.8 1.4 %copy-start.4 = (bf16[200,1536]{1,0:T(8,128)(2,1)S(1)}, bf16[200,1536]{1,0:T(8,128)(2,1)}, u32[]{:S(2)}) copy-start(bf16[200,1536]{1,0:T(8,128)(2,1)} %copy-done.3) | copy-start | bytes 1843204
  72.8 1.4 %slice-start = ((bf16[512,512]{1,0:T(8,128)(2,1)}), bf16[400,512]{1,0:T(8,128)(2,1)S(1)}, s32[]{:S(2)}) async-start(bf16[512,512]{1,0:T(8,128)(2,1)} %copy-done.7), calls=%async_computation | async-start | bytes 819200 | tf_op jit(solution)/shard_map/slice | solution.py:540
  72.8 13.8 %collective-permute-start.12 = (bf16[400,384]{1,0:T(8,128)(2,1)S(1)}, bf16[400,384]{1,0:T(8,128)(2,1)S(1)}, u32[]{:S(2)}, u32[]{:S(2)}) collective-permute-start(bf16[400,384]{1,0:T(8,128)(2,1)S(1)} %shard_map.133.refs_1_), channel_id=1, source_target_pairs={{0,4},{4,0},{1,5},{5,1},{2,6},{6,2},{3,7},{7,3},{8,12},{12,8},{9,1... | collective-permute-start | bytes 921608 | tf_op jit(solution)/shard_map/ppermute | solution.py:107
  75.2 4.2 %slice-start.1 = ((s8[4718592]{0:T(1024)(128)(4,1)}), s8[4194304]{0:T(1024)(128)(4,1)S(1)}, s32[]{:S(2)}) async-start(s8[4718592]{0:T(1024)(128)(4,1)} %bitcast.30), calls=%async_computation.1 | async-start | bytes 8388608
  75.2 4.1 %slice-start.2 = ((s8[4718592]{0:T(1024)(128)(4,1)}), s8[524288]{0:T(1024)(128)(4,1)S(1)}, s32[]{:S(2)}) async-start(s8[4718592]{0:T(1024)(128)(4,1)} %bitcast.30), calls=%async_computation.2 | async-start | bytes 1048576
  78.2 23.4 %collective-permute-start.18 = (bf16[200,1536]{1,0:T(8,128)(2,1)S(1)}, bf16[200,1536]{1,0:T(8,128)(2,1)S(1)}, u32[]{:S(2)}, u32[]{:S(2)}) collective-permute-start(bf16[200,1536]{1,0:T(8,128)(2,1)S(1)} %shard_map.141), channel_id=1, source_target_pairs={{0,4},{4,0},{1,5},{5,1},{2,6},{6,2},{3,7},{7,3},{8,12},{12,8},{9,1... | collective-permute-start | bytes 1843208 | tf_op jit(solution)/shard_map/ppermute | solution.py:107
  87.2 3.0 %collective-permute-start.15 = (bf16[400,768]{1,0:T(8,128)(2,1)S(1)}, bf16[400,768]{1,0:T(8,128)(2,1)S(1)}, u32[]{:S(2)}, u32[]{:S(2)}) collective-permute-start(bf16[400,768]{1,0:T(8,128)(2,1)S(1)} %fusion.20.refs_1_), channel_id=1, source_target_pairs={{0,1},{1,0},{2,3},{3,2},{4,5},{5,4},{6,7},{7,6},{8,9},{9,8},{10,11... | collective-permute-start | bytes 1843208 | tf_op jit(solution)/shard_map/ppermute | solution.py:107
  89.4 2.6 %collective-permute-start.13 = (bf16[200,768]{1,0:T(8,128)(2,1)S(1)}, bf16[200,768]{1,0:T(8,128)(2,1)S(1)}, u32[]{:S(2)}, u32[]{:S(2)}) collective-permute-start(bf16[200,768]{1,0:T(8,128)(2,1)S(1)} %fusion.53.refs_1_), channel_id=1, source_target_pairs={{0,1},{1,0},{2,3},{3,2},{4,5},{5,4},{6,7},{7,6},{8,9},{9,8},{10,11... | collective-permute-start | bytes 921608 | tf_op jit(solution)/shard_map/ppermute | solution.py:107
  90.4 10.2 %collective-permute-start.16 = (bf16[200,768]{1,0:T(8,128)(2,1)S(1)}, bf16[200,768]{1,0:T(8,128)(2,1)S(1)}, u32[]{:S(2)}, u32[]{:S(2)}) collective-permute-start(bf16[200,768]{1,0:T(8,128)(2,1)S(1)} %add_convert_fusion.3), channel_id=1, source_target_pairs={{0,2},{1,3},{2,0},{3,1},{4,6},{5,7},{6,4},{7,5},{8,10},{9,11},{10,... | collective-permute-start | bytes 921608 | tf_op jit(solution)/shard_map/ppermute | solution.py:107
  92.7 13.5 %collective-permute-start.14 = (bf16[200,768]{1,0:T(8,128)(2,1)S(1)}, bf16[200,768]{1,0:T(8,128)(2,1)S(1)}, u32[]{:S(2)}, u32[]{:S(2)}) collective-permute-start(bf16[200,768]{1,0:T(8,128)(2,1)S(1)} %get-tuple-element.45), channel_id=1, source_target_pairs={{0,2},{1,3},{2,0},{3,1},{4,6},{5,7},{6,4},{7,5},{8,10},{9,11},{10,... | collective-permute-start | bytes 921608 | tf_op jit(solution)/shard_map/ppermute | solution.py:107
  100.8 7.5 %collective-permute-start.17 = (bf16[200,768]{1,0:T(8,128)(2,1)S(1)}, bf16[200,768]{1,0:T(8,128)(2,1)S(1)}, u32[]{:S(2)}, u32[]{:S(2)}) collective-permute-start(bf16[200,768]{1,0:T(8,128)(2,1)S(1)} %add_convert_fusion.2.refs_1_), channel_id=1, source_target_pairs={{0,4},{4,0},{1,5},{5,1},{2,6},{6,2},{3,7},{7,3},{8,12},{12,8},{9,1... | collective-permute-start | bytes 921608 | tf_op jit(solution)/shard_map/ppermute | solution.py:107
  102.8 5.5 %collective-permute-start.19 = (bf16[200,768]{1,0:T(8,128)(2,1)S(1)}, bf16[200,768]{1,0:T(8,128)(2,1)S(1)}, u32[]{:S(2)}, u32[]{:S(2)}) collective-permute-start(bf16[200,768]{1,0:T(8,128)(2,1)S(1)} %fusion.50), channel_id=1, source_target_pairs={{0,1},{1,0},{2,3},{3,2},{4,5},{5,4},{6,7},{7,6},{8,9},{9,8},{10,11... | collective-permute-start | bytes 921608 | tf_op jit(solution)/shard_map/ppermute | solution.py:107
  108.4 6.9 %collective-permute-start.20 = (bf16[200,768]{1,0:T(8,128)(2,1)S(1)}, bf16[200,768]{1,0:T(8,128)(2,1)S(1)}, u32[]{:S(2)}, u32[]{:S(2)}) collective-permute-start(bf16[200,768]{1,0:T(8,128)(2,1)S(1)} %fusion.77), channel_id=1, source_target_pairs={{0,2},{1,3},{2,0},{3,1},{4,6},{5,7},{6,4},{7,5},{8,10},{9,11},{10,... | collective-permute-start | bytes 921608 | tf_op jit(solution)/shard_map/ppermute | solution.py:107

commit v9 on v8

--- a/solution.py
+++ b/solution.py
@@ -122,7 +122,7 @@
 LANES = 128
 EARLY = 20_000_000
 VMEM = 56
-REST_VMEM = 40
+REST_VMEM = 28
 POST_VMEM = 40
 
 
@@ -496,7 +496,7 @@
     own, own_early, moments = modulate_and_heads(tokens, mod_scale[None], mod_shift[None], w_heads, [sent])
     got_early, got_moments = swap(own_early, "sx", 1), swap(moments, "sx", 1)
     near = swap(piece, "tp", 1)
-    piece_far = hold(swap(piece, "tp", 2), got_early, got_moments)
+    piece_far = hold(swap(piece, "tp", 2), got_early)
     first_part = width_of(hidden // 3, hidden)
     own_first = border_and_hidden(own, picks, w_heads, w_mlp_in, first_part, [moments, piece])
     got_first = swap(own_first, "sx", 1)

time: 117 us -> 117 us (level)
    unnamed x54 -> x58, local copies, waits for them, and re-layouts: 2.78 us -> 3.61 us
  transfers between devices with their start and end apart: 21 -> 21, of which waited for: 10 -> 11; matrix products, arithmetic and copies ran while one was open for 15% -> 15% of each run, Pallas kernels for 23% -> 22%
where the time goes in v9:
time: 117 us; the launch traced here: 116 us
  waiting for transfers between devices  42.5 us (36%)
  Pallas kernels  25.6 us (22%)
  starting transfers between devices  24 us (21%)
  matrix products  10.5 us (9%)
  other arithmetic  7.37 us (6%)
  local copies, waits for them, and re-layouts  5.89 us (5%)
    ppermute x19, waiting for transfers between devices, swap(): return lax.ppermute(cells, axis, [(i, i ^ bit) for i in range(count)])  34.7 us
    pallas_call x5, Pallas kernels, call(): pl.pallas_call(kernel, grid=(grid,), in_specs=[spec(b, i) for _, b, i in...  25.5 us
    ppermute x19, starting transfers between devices, swap(): return lax.ppermute(cells, axis, [(i, i ^ bit) for i in range(count)])  18.2 us
    dot_general x15, matrix products, dot(): return jnp.dot(left, right, preferred_element_type=jnp.float32)  10.5 us
    ppermute x2, waiting for transfers between devices, shift(): lax.ppermute(cells, axis, [(i, i + step) for i in range(count) if 0 <= i...  7.88 us
    ppermute x2, starting transfers between devices, shift(): lax.ppermute(cells, axis, [(i, i + step) for i in range(count) if 0 <= i...  5.8 us
    unnamed x58, local copies, waits for them, and re-layouts  3.61 us
  transfers between devices with their start and end apart: 21, of which 11 were waited for; matrix products, arithmetic and copies ran while one was open for 15% of the time, Pallas kernels for 22%

profile of v9, /device:TPU:0, one launch (start us, length us, event | category | flops | bytes accessed | tf_op | source)
XLA Modules:
  0.0 116.4 jit_solution(3748884382327368094)
XLA Ops:
  0.0 1.1 constant_dynamic-slice_fusion.refs_4_
  1.1 3.0 %collective-permute-start = (bf16[400,384]{1,0:T(8,128)(2,1)S(1)}, bf16[400,384]{1,0:T(8,128)(2,1)S(1)}, u32[]{:S(2)}, u32[]{:S(2)}) collective-permute-start(bf16[400,384]{1,0:T(8,128)(2,1)S(1)} %constant_dynamic-slice_fusion.refs_4_), channel_id=1, source_target_pairs={{0,4},{4,0},{1,5},{5,1},{2,6},{6,2},{3,7},{7,3},{8,12},{12,8},{9,1... | collective-permute-start | bytes 921608 | tf_op jit(solution)/shard_map/ppermute | solution.py:107
  4.1 7.1 %shard_map.127 = (bf16[400,1536]{1,0:T(8,128)(2,1)}, bf16[400,384]{1,0:T(8,128)(2,1)}, f32[5,8,128]{2,1,0:T(8,128)}) custom-call(bf16[400,3072]{1,0:T(8,128)(2,1)} %refs_0_.1, f32[1,3072]{1,0:T(1,128)} %bitcast.34, f32[1,3072]{1,0:T(1,128)} %bitcast.35, bf16[3,1536,384]{2,1,0:T(8,128)(2,1)} %bitcast.26, bf16[400,384]{1,0:T(8,128)(2,1)} %copy-done.18), custom_call_target="tpu_custom_call" | custom-call | flops 1000 | bytes 1000 | tf_op jit(solution)/shard_map/pallas_call | solution.py:144
  11.2 0.6 collective-permute-start.2
  11.9 1.5 %collective-permute-start.1 = (bf16[400,384]{1,0:T(8,128)(2,1)S(1)}, bf16[400,384]{1,0:T(8,128)(2,1)S(1)}, u32[]{:S(2)}, u32[]{:S(2)}) collective-permute-start(bf16[400,384]{1,0:T(8,128)(2,1)S(1)} %collective-permute-done.refs_6_), channel_id=1, source_target_pairs={{0,2},{1,3},{2,0},{3,1},{4,6},{5,7},{6,4},{7,5},{8,10},{9,11},{10,... | collective-permute-start | bytes 921608 | tf_op jit(solution)/shard_map/ppermute | solution.py:107
  13.4 1.4 %collective-permute-start.5 = (f32[5,8,128]{2,1,0:T(8,128)}, f32[5,8,128]{2,1,0:T(8,128)S(1)}, u32[]{:S(2)}, u32[]{:S(2)}) collective-permute-start(f32[5,8,128]{2,1,0:T(8,128)} %get-tuple-element.19.refs_5_), channel_id=1, source_target_pairs={{0,4},{4,0},{1,5},{5,1},{2,6},{6,2},{3,7},{7,3},{8,12},{12,8},{9,1... | collective-permute-start | bytes 61448 | tf_op jit(solution)/shard_map/ppermute | solution.py:107
  14.8 4.5 %shard_map.128.refs_1_ = bf16[512,512]{1,0:T(8,128)(2,1)} custom-call(bf16[400,1536]{1,0:T(8,128)(2,1)} %get-tuple-element.18.refs_0_.refs_1_, bf16[2,224,400]{2,1,0:T(8,128)(2,1)} %constant.73.clone.refs_1_.refs_3_, bf16[3,1536,384]{2,1,0:T(8,128)(2,1)} %bitcast.27, bf16[3,1536,384]{2,1,0:T(8,128)(2,1)} %bitcast.28, bf16[1536,1536]{1,0:T(8,128)(2,1)} %refs_5_.2, ...), custom_call_target="tpu_custom_call" | custom-call | flops 1000 | bytes 1000 | tf_op jit(solution)/shard_map/pallas_call | solution.py:144
  19.3 1.1 collective-permute-done.2.refs_1_.refs_4_
  20.6 0.3 collective-permute-start.4
  21.3 0.8 collective-permute-start.6
  22.2 0.7 copy-done.20
  22.9 1.5 %broadcast_select_fusion.7 = (bf16[400,384]{1,0:T(8,128)(2,1)S(1)}, bf16[400,384]{1,0:T(8,128)(2,1)S(1)}, bf16[400,384]{1,0:T(8,128)(2,1)S(1)}, bf16[400,384]{1,0:T(8,128)(2,1)S(1)}) fusion(pred[]{:T(512)S(6)} %eq.13, bf16[400,384]{1,0:T(8,128)(2,1)} %copy-done.19, bf16[400,384]{1,0:T(8,128)(2,1)S(1)} %shard_map.130, pred[]{:T(512)S(6)} %eq.14, ...), kind=kLoop, calls=%fused_computation.96 | loop fusion | flops 1228800 | bytes 2457602 | tf_op jit(solution)/shard_map/jit(_where)/select_n | solution.py:157
  24.4 0.5 add_convert_fusion.refs_2_
  24.9 0.3 copy-done.1
  25.2 0.5 convolution_convert_fusion.1
  25.7 0.5 convolution_convert_fusion.2
  26.2 0.5 convolution_convert_fusion
  26.8 1.2 %collective-permute-start.9 = (bf16[400,768]{1,0:T(8,128)(2,1)S(1)}, bf16[400,768]{1,0:T(8,128)(2,1)S(1)}, u32[]{:S(2)}, u32[]{:S(2)}) collective-permute-start(bf16[400,768]{1,0:T(8,128)(2,1)S(1)} %pad_maximum_fusion.1.refs_6_), channel_id=1, source_target_pairs={{0,4},{4,0},{1,5},{5,1},{2,6},{6,2},{3,7},{7,3},{8,12},{12,8},{9,1... | collective-permute-start | bytes 1843208 | tf_op jit(solution)/shard_map/ppermute | solution.py:107
  28.0 8.1 %collective-permute-done.6.refs_7_.refs_6_ = bf16[512,512]{1,0:T(8,128)(2,1)S(1)} collective-permute-done((bf16[512,512]{1,0:T(8,128)(2,1)S(1)}, bf16[512,512]{1,0:T(8,128)(2,1)S(1)}, u32[]{:S(2)}, u32[]{:S(2)}) %collective-permute-start.6) | collective-permute-done | bytes 524320 | tf_op jit(solution)/shard_map/ppermute | solution.py:107
  36.2 7.8 %shard_map.131 = (f32[400,768]{1,0:T(8,128)S(1)}, f32[400,384]{1,0:T(8,128)S(1)}, f32[224,256]{1,0:T(8,128)S(1)}, bf16[400,1024]{1,0:T(8,128)(2,1)S(1)}, bf16[20...) custom-call(s32[4]{0:T(128)S(1)} %pad_add_fusion.refs_0_, bf16[400,1536]{1,0:T(8,128)(2,1)S(1)} %copy-done.10, ...), custom_call_target="tpu_custom_call" | custom-call | flops 3951034368 | bytes 13787136 | tf_op jit(solution)/shard_map/pallas_call | solution.py:144
  44.0 0.8 copy-done.3
  44.8 0.8 collective-permute-start.8
  45.6 3.6 %collective-permute-done.9.refs_2_ = bf16[400,768]{1,0:T(8,128)(2,1)S(1)} collective-permute-done((bf16[400,768]{1,0:T(8,128)(2,1)S(1)}, bf16[400,768]{1,0:T(8,128)(2,1)S(1)}, u32[]{:S(2)}, u32[]{:S(2)}) %collective-permute-start.9) | collective-permute-done | bytes 614432 | tf_op jit(solution)/shard_map/ppermute | solution.py:107
  49.3 1.9 %shard_map.132 = (bf16[1200,128]{1,0:T(8,128)(2,1)S(1)}, bf16[1424,256]{1,0:T(8,128)(2,1)S(1)}, bf16[736,256]{1,0:T(8,128)(2,1)}, bf16[736,256]{1,0:T(8,128)(2,1)}) custom-call(s32[4]{0:T(128)S(1)} %pad_add_fusion.refs_0_, f32[400,768]{1,0:T(8,128)S(1)} %get-tuple-element.24.refs_1_, bf16[400,768]{1,0:T(8,128)(2,1)S(1)} %collective-permute-done.9.refs_2_, ...), custom_call_target="tpu_custom_call" | custom-call | flops 1000 | bytes 1000 | tf_op jit(solution)/shard_map/pallas_call | solution.py:144
  51.2 0.9 copy-done.11
  52.1 0.7 copy-done.14
  52.8 4.3 %collective-permute-start.10 = (bf16[736,256]{1,0:T(8,128)(2,1)}, bf16[736,256]{1,0:T(8,128)(2,1)}, u32[]{:S(2)}, u32[]{:S(2)}) collective-permute-start(bf16[736,256]{1,0:T(8,128)(2,1)} %get-tuple-element.29), channel_id=1, source_target_pairs={{0,8},{8,16},{16,24},{1,9},{9,17},{17,25},{2,10},{10,18},{18,26},{... | collective-permute-start | bytes 1130504 | tf_op jit(solution)/shard_map/ppermute | solution.py:112
  57.2 1.5 %collective-permute-start.11 = (bf16[736,256]{1,0:T(8,128)(2,1)}, bf16[736,256]{1,0:T(8,128)(2,1)}, u32[]{:S(2)}, u32[]{:S(2)}) collective-permute-start(bf16[736,256]{1,0:T(8,128)(2,1)} %get-tuple-element.30), channel_id=1, source_target_pairs={{8,0},{16,8},{24,16},{9,1},{17,9},{25,17},{10,2},{18,10},{26,18},{... | collective-permute-start | bytes 1130504 | tf_op jit(solution)/shard_map/ppermute | solution.py:112
  58.7 0.9 dynamic_slice.31
  59.8 0.8 collective-permute-start.7
  60.5 3.0 %collective-permute-done.10.refs_3_ = bf16[736,256]{1,0:T(8,128)(2,1)} collective-permute-done((bf16[736,256]{1,0:T(8,128)(2,1)}, bf16[736,256]{1,0:T(8,128)(2,1)}, u32[]{:S(2)}, u32[]{:S(2)}) %collective-permute-start.10) | collective-permute-done | bytes 376864 | tf_op jit(solution)/shard_map/ppermute | solution.py:112
  63.6 4.8 %collective-permute-done.11.refs_4_ = bf16[736,256]{1,0:T(8,128)(2,1)} collective-permute-done((bf16[736,256]{1,0:T(8,128)(2,1)}, bf16[736,256]{1,0:T(8,128)(2,1)}, u32[]{:S(2)}, u32[]{:S(2)}) %collective-permute-start.11) | collective-permute-done | bytes 376864 | tf_op jit(solution)/shard_map/ppermute | solution.py:112
  68.5 4.2 %shard_map.133.refs_1_ = bf16[400,384]{1,0:T(8,128)(2,1)S(1)} custom-call(s32[4]{0:T(128)S(1)} %pad_add_fusion.refs_0_, bf16[1200,128]{1,0:T(8,128)(2,1)S(1)} %copy-done.15, bf16[1424,256]{1,0:T(8,128)(2,1)S(1)} %copy-done.12, bf16[736,256]{1,0:T(8,128)(2,1)} %collective-permute-done.10.refs_3_, bf16[736,256]{1,0:T(8,128)(2,1)} %collective-permute-done.11.refs_4_, ...), custom_call_target="tpu_custom_call" | custom-call | flops 1000 | bytes 1000 | tf_op jit(solution)/shard_map/pallas_call | solution.py:144
  72.7 1.5 %collective-permute-start.12 = (bf16[400,384]{1,0:T(8,128)(2,1)S(1)}, bf16[400,384]{1,0:T(8,128)(2,1)S(1)}, u32[]{:S(2)}, u32[]{:S(2)}) collective-permute-start(bf16[400,384]{1,0:T(8,128)(2,1)S(1)} %shard_map.133.refs_1_), channel_id=1, source_target_pairs={{0,4},{4,0},{1,5},{5,1},{2,6},{6,2},{3,7},{7,3},{8,12},{12,8},{9,1... | collective-permute-start | bytes 921608 | tf_op jit(solution)/shard_map/ppermute | solution.py:107
  74.2 1.0 fusion.7.refs_0_
  75.2 2.9 %fusion.18.refs_1_ = f32[400,768]{1,0:T(8,128)S(1)} fusion(bf16[400,1536]{1,0:T(8,128)(2,1)S(1)} %shard_map.135, bf16[1536,1536]{1,0:T(8,128)(2,1)} %param.22, s32[]{:T(128)S(6)} %select_n.168), kind=kOutput, calls=%fused_computation.22 | convolution fusion | flops 943718400 | bytes 4816900 | tf_op jit(solution)/shard_map/dot_general | solution.py:118
  78.2 1.2 collective-permute-start.18
  79.4 1.1 fusion.12.refs_2_
  80.5 6.1 %collective-permute-done.12.refs_0_ = bf16[400,384]{1,0:T(8,128)(2,1)S(1)} collective-permute-done((bf16[400,384]{1,0:T(8,128)(2,1)S(1)}, bf16[400,384]{1,0:T(8,128)(2,1)S(1)}, u32[]{:S(2)}, u32[]{:S(2)}) %collective-permute-start.12) | collective-permute-done | bytes 307232 | tf_op jit(solution)/shard_map/ppermute | solution.py:107
  86.7 0.5 fusion.20.refs_1_
  87.3 0.5 convolution_add_fusion.refs_2_
  87.8 0.5 fusion.40.refs_0_
  88.3 0.3 fusion.72
  88.7 0.7 fusion.53.refs_1_
  89.3 0.6 collective-permute-start.13
  89.9 0.3 fusion.67
  90.4 1.2 %collective-permute-start.16 = (bf16[200,768]{1,0:T(8,128)(2,1)S(1)}, bf16[200,768]{1,0:T(8,128)(2,1)S(1)}, u32[]{:S(2)}, u32[]{:S(2)}) collective-permute-start(bf16[200,768]{1,0:T(8,128)(2,1)S(1)} %add_convert_fusion.3), channel_id=1, source_target_pairs={{0,2},{1,3},{2,0},{3,1},{4,6},{5,7},{6,4},{7,5},{8,10},{9,11},{10,... | collective-permute-start | bytes 921608 | tf_op jit(solution)/shard_map/ppermute | solution.py:107
  91.6 0.3 fusion.70
  92.0 0.7 fusion.75
  92.7 0.9 collective-permute-start.14
  93.6 7.0 %collective-permute-done.16.refs_0_ = bf16[200,768]{1,0:T(8,128)(2,1)S(1)} collective-permute-done((bf16[200,768]{1,0:T(8,128)(2,1)S(1)}, bf16[200,768]{1,0:T(8,128)(2,1)S(1)}, u32[]{:S(2)}, u32[]{:S(2)}) %collective-permute-start.16) | collective-permute-done | bytes 307232 | tf_op jit(solution)/shard_map/ppermute | solution.py:107
  100.6 0.2 add_convert_fusion.2.refs_1_
  100.8 0.9 collective-permute-start.17
  101.7 0.5 fusion.48.refs_0_
  102.2 0.7 fusion.50
  102.9 0.3 fusion.65
  103.2 0.7 fusion.30.refs_0_
  103.9 2.3 %collective-permute-done.14.refs_2_ = bf16[200,768]{1,0:T(8,128)(2,1)S(1)} collective-permute-done((bf16[200,768]{1,0:T(8,128)(2,1)S(1)}, bf16[200,768]{1,0:T(8,128)(2,1)S(1)}, u32[]{:S(2)}, u32[]{:S(2)}) %collective-permute-start.14) | collective-permute-done | bytes 307232 | tf_op jit(solution)/shard_map/ppermute | solution.py:107
  106.2 2.0 %collective-permute-done.17.refs_1_ = bf16[200,768]{1,0:T(8,128)(2,1)S(1)} collective-permute-done((bf16[200,768]{1,0:T(8,128)(2,1)S(1)}, bf16[200,768]{1,0:T(8,128)(2,1)S(1)}, u32[]{:S(2)}, u32[]{:S(2)}) %collective-permute-start.17) | collective-permute-done | bytes 307232 | tf_op jit(solution)/shard_map/ppermute | solution.py:107
  108.4 1.2 %collective-permute-start.20 = (bf16[200,768]{1,0:T(8,128)(2,1)S(1)}, bf16[200,768]{1,0:T(8,128)(2,1)S(1)}, u32[]{:S(2)}, u32[]{:S(2)}) collective-permute-start(bf16[200,768]{1,0:T(8,128)(2,1)S(1)} %fusion.77), channel_id=1, source_target_pairs={{0,2},{1,3},{2,0},{3,1},{4,6},{5,7},{6,4},{7,5},{8,10},{9,11},{10,... | collective-permute-start | bytes 921608 | tf_op jit(solution)/shard_map/ppermute | solution.py:107
  109.6 0.3 fusion.62
  109.9 1.2 %fusion.49.refs_0_ = f32[400,768]{1,0:T(8,128)S(1)} fusion(f32[200,768]{1,0:T(8,128)S(1)} %get-tuple-element.42, f32[200,768]{1,0:T(8,128)S(1)} %get-tuple-element.41, f32[768]{0:T(1024)S(1)} %dynamic_slice.31, bf16[400,3072]{1,0:T(8,128)(2,1)} %refs_0_.1, s32[]{:T(128)S(6)} %select_n.151), kind=kLoop, calls=%fused_computation.50 | loop fusion | flops 1228800 | bytes 3075076 | tf_op jit(solution)/shard_map/add | solution.py:594
  111.2 4.2 %collective-permute-done.20 = bf16[200,768]{1,0:T(8,128)(2,1)S(1)} collective-permute-done((bf16[200,768]{1,0:T(8,128)(2,1)S(1)}, bf16[200,768]{1,0:T(8,128)(2,1)S(1)}, u32[]{:S(2)}, u32[]{:S(2)}) %collective-permute-start.20) | collective-permute-done | bytes 307232 | tf_op jit(solution)/shard_map/ppermute | solution.py:107
  115.3 1.0 add_convert_fusion.1
  (101 shorter events, 1.5 us)
Async XLA Ops:
  0.0 86.7 %copy-start = (bf16[384,1536]{1,0:T(8,128)(2,1)S(1)}, bf16[384,1536]{1,0:T(8,128)(2,1)}, u32[]{:S(2)}) copy-start(bf16[384,1536]{1,0:T(8,128)(2,1)} %param.21) | copy-start | bytes 3538948
  1.1 3.0 %copy-start.18 = (bf16[400,384]{1,0:T(8,128)(2,1)}, bf16[400,384]{1,0:T(8,128)(2,1)S(1)}, u32[]{:S(2)}) copy-start(bf16[400,384]{1,0:T(8,128)(2,1)S(1)} %constant_dynamic-slice_fusion.refs_4_) | copy-start | bytes 921604
  1.1 10.8 %collective-permute-start = (bf16[400,384]{1,0:T(8,128)(2,1)S(1)}, bf16[400,384]{1,0:T(8,128)(2,1)S(1)}, u32[]{:S(2)}, u32[]{:S(2)}) collective-permute-start(bf16[400,384]{1,0:T(8,128)(2,1)S(1)} %constant_dynamic-slice_fusion.refs_4_), channel_id=1, source_target_pairs={{0,4},{4,0},{1,5},{5,1},{2,6},{6,2},{3,7},{7,3},{8,12},{12,8},{9,1... | collective-permute-start | bytes 921608 | tf_op jit(solution)/shard_map/ppermute | solution.py:107
  11.2 9.2 %collective-permute-start.2 = (bf16[400,384]{1,0:T(8,128)(2,1)}, bf16[400,384]{1,0:T(8,128)(2,1)S(1)}, u32[]{:S(2)}, u32[]{:S(2)}) collective-permute-start(bf16[400,384]{1,0:T(8,128)(2,1)} %get-tuple-element.20), channel_id=1, source_target_pairs={{0,4},{4,0},{1,5},{5,1},{2,6},{6,2},{3,7},{7,3},{8,12},{12,8},{9,1... | collective-permute-start | bytes 921608 | tf_op jit(solution)/shard_map/ppermute | solution.py:107
  11.9 2.9 %copy-start.19 = (bf16[400,384]{1,0:T(8,128)(2,1)}, bf16[400,384]{1,0:T(8,128)(2,1)S(1)}, u32[]{:S(2)}) copy-start(bf16[400,384]{1,0:T(8,128)(2,1)S(1)} %collective-permute-done.refs_6_) | copy-start | bytes 921604
  11.9 8.7 %collective-permute-start.1 = (bf16[400,384]{1,0:T(8,128)(2,1)S(1)}, bf16[400,384]{1,0:T(8,128)(2,1)S(1)}, u32[]{:S(2)}, u32[]{:S(2)}) collective-permute-start(bf16[400,384]{1,0:T(8,128)(2,1)S(1)} %collective-permute-done.refs_6_), channel_id=1, source_target_pairs={{0,2},{1,3},{2,0},{3,1},{4,6},{5,7},{6,4},{7,5},{8,10},{9,11},{10,... | collective-permute-start | bytes 921608 | tf_op jit(solution)/shard_map/ppermute | solution.py:107
  13.4 7.8 %collective-permute-start.5 = (f32[5,8,128]{2,1,0:T(8,128)}, f32[5,8,128]{2,1,0:T(8,128)S(1)}, u32[]{:S(2)}, u32[]{:S(2)}) collective-permute-start(f32[5,8,128]{2,1,0:T(8,128)} %get-tuple-element.19.refs_5_), channel_id=1, source_target_pairs={{0,4},{4,0},{1,5},{5,1},{2,6},{6,2},{3,7},{7,3},{8,12},{12,8},{9,1... | collective-permute-start | bytes 61448 | tf_op jit(solution)/shard_map/ppermute | solution.py:107
  14.8 7.4 %collective-permute-start.3 = (bf16[400,384]{1,0:T(8,128)(2,1)S(1)}, bf16[400,384]{1,0:T(8,128)(2,1)S(1)}, u32[]{:S(2)}, u32[]{:S(2)}) collective-permute-start(bf16[400,384]{1,0:T(8,128)(2,1)S(1)} %collective-permute-done.refs_6_), channel_id=1, source_target_pairs={{0,1},{1,0},{2,3},{3,2},{4,5},{5,4},{6,7},{7,6},{8,9},{9,8},{10,11... | collective-permute-start | bytes 921608 | tf_op jit(solution)/shard_map/ppermute | solution.py:107
  19.3 1.4 %copy-start.2 = (bf16[512,512]{1,0:T(8,128)(2,1)S(1)}, bf16[512,512]{1,0:T(8,128)(2,1)}, u32[]{:S(2)}) copy-start(bf16[512,512]{1,0:T(8,128)(2,1)} %shard_map.128.refs_1_) | copy-start | bytes 1572868
  19.3 1.7 %copy-start.21 = (f32[3072]{0:T(1024)S(1)}, f32[3072]{0:T(1024)}, u32[]{:S(2)}) copy-start(f32[3072]{0:T(1024)} %param.15) | copy-start | bytes 36868
  19.3 1.8 %copy-start.22 = (f32[3072]{0:T(1024)S(1)}, f32[3072]{0:T(1024)}, u32[]{:S(2)}) copy-start(f32[3072]{0:T(1024)} %param.14) | copy-start | bytes 36868
  20.4 4.0 %copy-start.8 = (bf16[400,384]{1,0:T(8,128)(2,1)}, bf16[400,384]{1,0:T(8,128)(2,1)S(1)}, u32[]{:S(2)}) copy-start(bf16[400,384]{1,0:T(8,128)(2,1)S(1)} %collective-permute-done.2.refs_1_.refs_4_) | copy-start | bytes 921604
  20.6 2.3 %collective-permute-start.4 = (bf16[400,384]{1,0:T(8,128)(2,1)S(1)}, bf16[400,384]{1,0:T(8,128)(2,1)}, u32[]{:S(2)}, u32[]{:S(2)}) collective-permute-start(bf16[400,384]{1,0:T(8,128)(2,1)S(1)} %shard_map.130), channel_id=1, source_target_pairs={{0,1},{1,0},{2,3},{3,2},{4,5},{5,4},{6,7},{7,6},{8,9},{9,8},{10,11... | collective-permute-start | bytes 921608 | tf_op jit(solution)/shard_map/ppermute | solution.py:107
  21.3 14.8 %collective-permute-start.6 = (bf16[512,512]{1,0:T(8,128)(2,1)S(1)}, bf16[512,512]{1,0:T(8,128)(2,1)S(1)}, u32[]{:S(2)}, u32[]{:S(2)}) collective-permute-start(bf16[512,512]{1,0:T(8,128)(2,1)S(1)} %copy-done.2), channel_id=1, source_target_pairs={{0,4},{4,0},{1,5},{5,1},{2,6},{6,2},{3,7},{7,3},{8,12},{12,8},{9,1... | collective-permute-start | bytes 1572872 | tf_op jit(solution)/shard_map/ppermute | solution.py:107
  22.2 0.7 copy-start.20
  22.9 2.3 %copy-start.1 = (bf16[1536,3,384]{2,0,1:T(8,128)(2,1)S(1)}, bf16[1536,3,384]{2,0,1:T(8,128)(2,1)}, u32[]{:S(2)}) copy-start(bf16[1536,3,384]{2,0,1:T(8,128)(2,1)} %param.17) | copy-start | bytes 10616836
  25.2 10.9 %slice-start = ((s8[4718592]{0:T(1024)(128)(4,1)}), s8[4194304]{0:T(1024)(128)(4,1)S(1)}, s32[]{:S(2)}) async-start(s8[4718592]{0:T(1024)(128)(4,1)} %bitcast.30), calls=%async_computation | async-start | bytes 8388608
  25.7 10.4 %slice-start.1 = ((s8[4718592]{0:T(1024)(128)(4,1)}), s8[524288]{0:T(1024)(128)(4,1)S(1)}, s32[]{:S(2)}) async-start(s8[4718592]{0:T(1024)(128)(4,1)} %bitcast.30), calls=%async_computation.1 | async-start | bytes 1048576
  26.2 9.9 %copy-start.13 = (bf16[2,224,400]{2,1,0:T(8,128)(2,1)S(1)}, bf16[2,224,400]{2,1,0:T(8,128)(2,1)}, u32[]{:S(2)}) copy-start(bf16[2,224,400]{2,1,0:T(8,128)(2,1)} %constant.73.clone.refs_1_.refs_3_) | copy-start | bytes 1075204
  26.7 9.4 %copy-start.10 = (bf16[400,1536]{1,0:T(8,128)(2,1)S(1)}, bf16[400,1536]{1,0:T(8,128)(2,1)}, u32[]{:S(2)}) copy-start(bf16[400,1536]{1,0:T(8,128)(2,1)} %get-tuple-element.18.refs_0_.refs_1_) | copy-start | bytes 3686404
  26.8 18.9 %copy-start.23 = (f32[3,128]{1,0:T(4,128)S(1)}, f32[3,128]{1,0:T(4,128)}, u32[]{:S(2)}) copy-start(f32[3,128]{1,0:T(4,128)} %param.19) | copy-start | bytes 4612
  26.8 18.8 %copy-start.24 = (f32[3,128]{1,0:T(4,128)S(1)}, f32[3,128]{1,0:T(4,128)}, u32[]{:S(2)}) copy-start(f32[3,128]{1,0:T(4,128)} %param.20) | copy-start | bytes 4612
  26.8 22.5 %copy-start.9 = (bf16[400,384]{1,0:T(8,128)(2,1)S(1)}, bf16[400,384]{1,0:T(8,128)(2,1)}, u32[]{:S(2)}) copy-start(bf16[400,384]{1,0:T(8,128)(2,1)} %copy-done.8) | copy-start | bytes 921604
  26.8 22.5 %collective-permute-start.9 = (bf16[400,768]{1,0:T(8,128)(2,1)S(1)}, bf16[400,768]{1,0:T(8,128)(2,1)S(1)}, u32[]{:S(2)}, u32[]{:S(2)}) collective-permute-start(bf16[400,768]{1,0:T(8,128)(2,1)S(1)} %pad_maximum_fusion.1.refs_6_), channel_id=1, source_target_pairs={{0,4},{4,0},{1,5},{5,1},{2,6},{6,2},{3,7},{7,3},{8,12},{12,8},{9,1... | collective-permute-start | bytes 1843208 | tf_op jit(solution)/shard_map/ppermute | solution.py:107
  36.1 13.1 %copy-start.7 = (bf16[512,512]{1,0:T(8,128)(2,1)}, bf16[512,512]{1,0:T(8,128)(2,1)S(1)}, u32[]{:S(2)}) copy-start(bf16[512,512]{1,0:T(8,128)(2,1)S(1)} %collective-permute-done.6.refs_7_.refs_6_) | copy-start | bytes 1572868
  44.0 0.8 copy-start.3
  44.8 6.4 %copy-start.5 = (bf16[200,1536]{1,0:T(8,128)(2,1)}, bf16[200,1536]{1,0:T(8,128)(2,1)S(1)}, u32[]{:S(2)}) copy-start(bf16[200,1536]{1,0:T(8,128)(2,1)S(1)} %get-tuple-element.22.refs_9_) | copy-start | bytes 1843204
  44.8 29.4 %collective-permute-start.8 = (bf16[400,1024]{1,0:T(8,128)(2,1)S(1)}, bf16[400,1024]{1,0:T(8,128)(2,1)S(1)}, u32[]{:S(2)}, u32[]{:S(2)}) collective-permute-start(bf16[400,1024]{1,0:T(8,128)(2,1)S(1)} %get-tuple-element.21), channel_id=1, source_target_pairs={{0,4},{4,0},{1,5},{5,1},{2,6},{6,2},{3,7},{7,3},{8,12},{12,8},{9,1... | collective-permute-start | bytes 2457608 | tf_op jit(solution)/shard_map/ppermute | solution.py:107
  51.2 0.9 copy-start.11
  52.1 0.7 copy-start.14
  52.8 15.6 %copy-start.16 = (f32[2,2,1664]{2,1,0:T(2,128)S(1)}, f32[2,2,1664]{2,1,0:T(2,128)}, u32[]{:S(2)}) copy-start(f32[2,2,1664]{2,1,0:T(2,128)} %constant.74.clone.refs_5_) | copy-start | bytes 79876
  52.8 15.6 %copy-start.17 = (f32[1,1280]{1,0:T(1,128)S(1)}, f32[1,1280]{1,0:T(1,128)}, u32[]{:S(2)}) copy-start(f32[1,1280]{1,0:T(1,128)} %constant.75.clone.refs_6_) | copy-start | bytes 15364
  52.8 10.8 %collective-permute-start.10 = (bf16[736,256]{1,0:T(8,128)(2,1)}, bf16[736,256]{1,0:T(8,128)(2,1)}, u32[]{:S(2)}, u32[]{:S(2)}) collective-permute-start(bf16[736,256]{1,0:T(8,128)(2,1)} %get-tuple-element.29), channel_id=1, source_target_pairs={{0,8},{8,16},{16,24},{1,9},{9,17},{17,25},{2,10},{10,18},{18,26},{... | collective-permute-start | bytes 1130504 | tf_op jit(solution)/shard_map/ppermute | solution.py:112
  57.2 11.3 %collective-permute-start.11 = (bf16[736,256]{1,0:T(8,128)(2,1)}, bf16[736,256]{1,0:T(8,128)(2,1)}, u32[]{:S(2)}, u32[]{:S(2)}) collective-permute-start(bf16[736,256]{1,0:T(8,128)(2,1)} %get-tuple-element.30), channel_id=1, source_target_pairs={{8,0},{16,8},{24,16},{9,1},{17,9},{25,17},{10,2},{18,10},{26,18},{... | collective-permute-start | bytes 1130504 | tf_op jit(solution)/shard_map/ppermute | solution.py:112
  58.7 1.1 copy-start.6
  58.7 9.8 %copy-start.12 = (bf16[1424,256]{1,0:T(8,128)(2,1)S(1)}, bf16[1424,256]{1,0:T(8,128)(2,1)}, u32[]{:S(2)}) copy-start(bf16[1424,256]{1,0:T(8,128)(2,1)} %copy-done.11) | copy-start | bytes 2187268
  58.7 9.8 %copy-start.15 = (bf16[1200,128]{1,0:T(8,128)(2,1)S(1)}, bf16[1200,128]{1,0:T(8,128)(2,1)}, u32[]{:S(2)}) copy-start(bf16[1200,128]{1,0:T(8,128)(2,1)} %copy-done.14) | copy-start | bytes 921604
  59.8 20.8 %collective-permute-start.7 = (bf16[200,1536]{1,0:T(8,128)(2,1)S(1)}, bf16[200,1536]{1,0:T(8,128)(2,1)S(1)}, u32[]{:S(2)}, u32[]{:S(2)}) collective-permute-start(bf16[200,1536]{1,0:T(8,128)(2,1)S(1)} %copy-done.6), channel_id=1, source_target_pairs={{0,4},{4,0},{1,5},{5,1},{2,6},{6,2},{3,7},{7,3},{8,12},{12,8},{9,1... | collective-permute-start | bytes 1843208 | tf_op jit(solution)/shard_map/ppermute | solution.py:107
  72.7 1.5 %copy-start.4 = (bf16[200,1536]{1,0:T(8,128)(2,1)S(1)}, bf16[200,1536]{1,0:T(8,128)(2,1)}, u32[]{:S(2)}) copy-start(bf16[200,1536]{1,0:T(8,128)(2,1)} %copy-done.3) | copy-start | bytes 1843204
  72.7 1.5 %slice-start.2 = ((bf16[512,512]{1,0:T(8,128)(2,1)}), bf16[400,512]{1,0:T(8,128)(2,1)S(1)}, s32[]{:S(2)}) async-start(bf16[512,512]{1,0:T(8,128)(2,1)} %copy-done.7), calls=%async_computation.2 | async-start | bytes 819200 | tf_op jit(solution)/shard_map/slice | solution.py:540
  72.7 13.9 %collective-permute-start.12 = (bf16[400,384]{1,0:T(8,128)(2,1)S(1)}, bf16[400,384]{1,0:T(8,128)(2,1)S(1)}, u32[]{:S(2)}, u32[]{:S(2)}) collective-permute-start(bf16[400,384]{1,0:T(8,128)(2,1)S(1)} %shard_map.133.refs_1_), channel_id=1, source_target_pairs={{0,4},{4,0},{1,5},{5,1},{2,6},{6,2},{3,7},{7,3},{8,12},{12,8},{9,1... | collective-permute-start | bytes 921608 | tf_op jit(solution)/shard_map/ppermute | solution.py:107
  75.2 4.2 %slice-start.3 = ((s8[4718592]{0:T(1024)(128)(4,1)}), s8[4194304]{0:T(1024)(128)(4,1)S(1)}, s32[]{:S(2)}) async-start(s8[4718592]{0:T(1024)(128)(4,1)} %bitcast.32), calls=%async_computation.3 | async-start | bytes 8388608
  75.2 4.1 %slice-start.4 = ((s8[4718592]{0:T(1024)(128)(4,1)}), s8[524288]{0:T(1024)(128)(4,1)S(1)}, s32[]{:S(2)}) async-start(s8[4718592]{0:T(1024)(128)(4,1)} %bitcast.32), calls=%async_computation.4 | async-start | bytes 1048576
  78.2 23.5 %collective-permute-start.18 = (bf16[200,1536]{1,0:T(8,128)(2,1)S(1)}, bf16[200,1536]{1,0:T(8,128)(2,1)S(1)}, u32[]{:S(2)}, u32[]{:S(2)}) collective-permute-start(bf16[200,1536]{1,0:T(8,128)(2,1)S(1)} %shard_map.141), channel_id=1, source_target_pairs={{0,4},{4,0},{1,5},{5,1},{2,6},{6,2},{3,7},{7,3},{8,12},{12,8},{9,1... | collective-permute-start | bytes 1843208 | tf_op jit(solution)/shard_map/ppermute | solution.py:107
  87.2 3.0 %collective-permute-start.15 = (bf16[400,768]{1,0:T(8,128)(2,1)S(1)}, bf16[400,768]{1,0:T(8,128)(2,1)S(1)}, u32[]{:S(2)}, u32[]{:S(2)}) collective-permute-start(bf16[400,768]{1,0:T(8,128)(2,1)S(1)} %fusion.20.refs_1_), channel_id=1, source_target_pairs={{0,1},{1,0},{2,3},{3,2},{4,5},{5,4},{6,7},{7,6},{8,9},{9,8},{10,11... | collective-permute-start | bytes 1843208 | tf_op jit(solution)/shard_map/ppermute | solution.py:107
  89.3 2.6 %collective-permute-start.13 = (bf16[200,768]{1,0:T(8,128)(2,1)S(1)}, bf16[200,768]{1,0:T(8,128)(2,1)S(1)}, u32[]{:S(2)}, u32[]{:S(2)}) collective-permute-start(bf16[200,768]{1,0:T(8,128)(2,1)S(1)} %fusion.53.refs_1_), channel_id=1, source_target_pairs={{0,1},{1,0},{2,3},{3,2},{4,5},{5,4},{6,7},{7,6},{8,9},{9,8},{10,11... | collective-permute-start | bytes 921608 | tf_op jit(solution)/shard_map/ppermute | solution.py:107
  90.4 10.2 %collective-permute-start.16 = (bf16[200,768]{1,0:T(8,128)(2,1)S(1)}, bf16[200,768]{1,0:T(8,128)(2,1)S(1)}, u32[]{:S(2)}, u32[]{:S(2)}) collective-permute-start(bf16[200,768]{1,0:T(8,128)(2,1)S(1)} %add_convert_fusion.3), channel_id=1, source_target_pairs={{0,2},{1,3},{2,0},{3,1},{4,6},{5,7},{6,4},{7,5},{8,10},{9,11},{10,... | collective-permute-start | bytes 921608 | tf_op jit(solution)/shard_map/ppermute | solution.py:107
  92.7 13.6 %collective-permute-start.14 = (bf16[200,768]{1,0:T(8,128)(2,1)S(1)}, bf16[200,768]{1,0:T(8,128)(2,1)S(1)}, u32[]{:S(2)}, u32[]{:S(2)}) collective-permute-start(bf16[200,768]{1,0:T(8,128)(2,1)S(1)} %get-tuple-element.45), channel_id=1, source_target_pairs={{0,2},{1,3},{2,0},{3,1},{4,6},{5,7},{6,4},{7,5},{8,10},{9,11},{10,... | collective-permute-start | bytes 921608 | tf_op jit(solution)/shard_map/ppermute | solution.py:107
  100.8 7.5 %collective-permute-start.17 = (bf16[200,768]{1,0:T(8,128)(2,1)S(1)}, bf16[200,768]{1,0:T(8,128)(2,1)S(1)}, u32[]{:S(2)}, u32[]{:S(2)}) collective-permute-start(bf16[200,768]{1,0:T(8,128)(2,1)S(1)} %add_convert_fusion.2.refs_1_), channel_id=1, source_target_pairs={{0,4},{4,0},{1,5},{5,1},{2,6},{6,2},{3,7},{7,3},{8,12},{12,8},{9,1... | collective-permute-start | bytes 921608 | tf_op jit(solution)/shard_map/ppermute | solution.py:107
  102.8 5.4 %collective-permute-start.19 = (bf16[200,768]{1,0:T(8,128)(2,1)S(1)}, bf16[200,768]{1,0:T(8,128)(2,1)S(1)}, u32[]{:S(2)}, u32[]{:S(2)}) collective-permute-start(bf16[200,768]{1,0:T(8,128)(2,1)S(1)} %fusion.50), channel_id=1, source_target_pairs={{0,1},{1,0},{2,3},{3,2},{4,5},{5,4},{6,7},{7,6},{8,9},{9,8},{10,11... | collective-permute-start | bytes 921608 | tf_op jit(solution)/shard_map/ppermute | solution.py:107
  108.4 6.9 %collective-permute-start.20 = (bf16[200,768]{1,0:T(8,128)(2,1)S(1)}, bf16[200,768]{1,0:T(8,128)(2,1)S(1)}, u32[]{:S(2)}, u32[]{:S(2)}) collective-permute-start(bf16[200,768]{1,0:T(8,128)(2,1)S(1)} %fusion.77), channel_id=1, source_target_pairs={{0,2},{1,3},{2,0},{3,1},{4,6},{5,7},{6,4},{7,5},{8,10},{9,11},{10,... | collective-permute-start | bytes 921608 | tf_op jit(solution)/shard_map/ppermute | solution.py:107

commit v10 on v9

--- a/solution.py
+++ b/solution.py
@@ -122,7 +122,7 @@
 LANES = 128
 EARLY = 20_000_000
 VMEM = 56
-REST_VMEM = 28
+REST_VMEM = 40
 POST_VMEM = 40
 
 
@@ -563,7 +563,7 @@
     other_sent = (other_sent + dot(other_attended, sent_attn)).astype(BF16)
     other_kept = other_kept + dot(hold(other_attended, other_sent), kept_attn)
     other_come = swap(other_sent, "tp", 1)
-    own_sent_a, own_kept_a = own_part(0, cut, got_other_a, other_sent, other_kept)
+    own_sent_a, own_kept_a = own_part(0, cut, got_other_a, other_sent)
 
     def rows_of(half):
         kept = jnp.where(half == 0, other_kept[:cut], other_kept[cut:])

time: 117 us -> 117 us (level)
    unnamed x58 -> x54, local copies, waits for them, and re-layouts: 3.61 us -> 2.78 us
  transfers between devices with their start and end apart: 21 -> 21, of which waited for: 11 -> 11; matrix products, arithmetic and copies ran while one was open for 15% -> 15% of each run, Pallas kernels for 22% -> 23%
where the time goes in v10:
time: 117 us; the launch traced here: 116 us
  waiting for transfers between devices  42.5 us (36%)
  Pallas kernels  26.4 us (23%)
  starting transfers between devices  24 us (21%)
  matrix products  10.5 us (9%)
  other arithmetic  7.42 us (6%)
  local copies, waits for them, and re-layouts  5.06 us (4%)
    ppermute x19, waiting for transfers between devices, swap(): return lax.ppermute(cells, axis, [(i, i ^ bit) for i in range(count)])  34.7 us
    pallas_call x5, Pallas kernels, call(): pl.pallas_call(kernel, grid=(grid,), in_specs=[spec(b, i) for _, b, i in...  26.4 us
    ppermute x19, starting transfers between devices, swap(): return lax.ppermute(cells, axis, [(i, i ^ bit) for i in range(count)])  18.2 us
    dot_general x15, matrix products, dot(): return jnp.dot(left, right, preferred_element_type=jnp.float32)  10.5 us
    ppermute x2, waiting for transfers between devices, shift(): lax.ppermute(cells, axis, [(i, i + step) for i in range(count) if 0 <= i...  7.87 us
    ppermute x2, starting transfers between devices, shift(): lax.ppermute(cells, axis, [(i, i + step) for i in range(count) if 0 <= i...  5.8 us
    unnamed x54, local copies, waits for them, and re-layouts  2.78 us
  transfers between devices with their start and end apart: 21, of which 11 were waited for; matrix products, arithmetic and copies ran while one was open for 15% of the time, Pallas kernels for 23%

profile of v10, /device:TPU:0, one launch (start us, length us, event | category | flops | bytes accessed | tf_op | source)
XLA Modules:
  0.0 116.5 jit_solution(17979746887429374506)
XLA Ops:
  0.0 1.1 constant_dynamic-slice_fusion.refs_4_
  1.1 3.0 %collective-permute-start = (bf16[400,384]{1,0:T(8,128)(2,1)S(1)}, bf16[400,384]{1,0:T(8,128)(2,1)S(1)}, u32[]{:S(2)}, u32[]{:S(2)}) collective-permute-start(bf16[400,384]{1,0:T(8,128)(2,1)S(1)} %constant_dynamic-slice_fusion.refs_4_), channel_id=1, source_target_pairs={{0,4},{4,0},{1,5},{5,1},{2,6},{6,2},{3,7},{7,3},{8,12},{12,8},{9,1... | collective-permute-start | bytes 921608 | tf_op jit(solution)/shard_map/ppermute | solution.py:107
  4.1 7.1 %shard_map.127 = (bf16[400,1536]{1,0:T(8,128)(2,1)}, bf16[400,384]{1,0:T(8,128)(2,1)}, f32[5,8,128]{2,1,0:T(8,128)}) custom-call(bf16[400,3072]{1,0:T(8,128)(2,1)} %refs_0_.1, f32[1,3072]{1,0:T(1,128)} %bitcast.32, f32[1,3072]{1,0:T(1,128)} %bitcast.33, bf16[3,1536,384]{2,1,0:T(8,128)(2,1)} %bitcast.26, bf16[400,384]{1,0:T(8,128)(2,1)} %copy-done.18), custom_call_target="tpu_custom_call" | custom-call | flops 1000 | bytes 1000 | tf_op jit(solution)/shard_map/pallas_call | solution.py:144
  11.3 0.6 collective-permute-start.2
  11.9 1.5 %collective-permute-start.1 = (bf16[400,384]{1,0:T(8,128)(2,1)S(1)}, bf16[400,384]{1,0:T(8,128)(2,1)S(1)}, u32[]{:S(2)}, u32[]{:S(2)}) collective-permute-start(bf16[400,384]{1,0:T(8,128)(2,1)S(1)} %collective-permute-done.refs_6_), channel_id=1, source_target_pairs={{0,2},{1,3},{2,0},{3,1},{4,6},{5,7},{6,4},{7,5},{8,10},{9,11},{10,... | collective-permute-start | bytes 921608 | tf_op jit(solution)/shard_map/ppermute | solution.py:107
  13.4 1.4 %collective-permute-start.5 = (f32[5,8,128]{2,1,0:T(8,128)}, f32[5,8,128]{2,1,0:T(8,128)S(1)}, u32[]{:S(2)}, u32[]{:S(2)}) collective-permute-start(f32[5,8,128]{2,1,0:T(8,128)} %get-tuple-element.19.refs_5_), channel_id=1, source_target_pairs={{0,4},{4,0},{1,5},{5,1},{2,6},{6,2},{3,7},{7,3},{8,12},{12,8},{9,1... | collective-permute-start | bytes 61448 | tf_op jit(solution)/shard_map/ppermute | solution.py:107
  14.8 4.5 %shard_map.128.refs_1_ = bf16[512,512]{1,0:T(8,128)(2,1)} custom-call(bf16[400,1536]{1,0:T(8,128)(2,1)} %get-tuple-element.18.refs_0_.refs_1_, bf16[2,224,400]{2,1,0:T(8,128)(2,1)} %constant.73.clone.refs_1_.refs_3_, bf16[3,1536,384]{2,1,0:T(8,128)(2,1)} %bitcast.27, bf16[3,1536,384]{2,1,0:T(8,128)(2,1)} %bitcast.28, bf16[1536,1536]{1,0:T(8,128)(2,1)} %refs_5_.2, ...), custom_call_target="tpu_custom_call" | custom-call | flops 1000 | bytes 1000 | tf_op jit(solution)/shard_map/pallas_call | solution.py:144
  19.3 1.1 collective-permute-done.2.refs_1_.refs_4_
  20.4 0.2 collective-permute-done.1.refs_0_
  20.6 0.3 collective-permute-start.4
  21.4 0.8 collective-permute-start.6
  22.2 0.7 copy-done.20
  22.9 1.5 %broadcast_select_fusion.7 = (bf16[400,384]{1,0:T(8,128)(2,1)S(1)}, bf16[400,384]{1,0:T(8,128)(2,1)S(1)}, bf16[400,384]{1,0:T(8,128)(2,1)S(1)}, bf16[400,384]{1,0:T(8,128)(2,1)S(1)}) fusion(pred[]{:T(512)S(6)} %eq.13, bf16[400,384]{1,0:T(8,128)(2,1)} %copy-done.19, bf16[400,384]{1,0:T(8,128)(2,1)S(1)} %shard_map.130, pred[]{:T(512)S(6)} %eq.14, ...), kind=kLoop, calls=%fused_computation.96 | loop fusion | flops 1228800 | bytes 2457602 | tf_op jit(solution)/shard_map/jit(_where)/select_n | solution.py:157
  24.4 0.5 add_convert_fusion.refs_2_
  25.0 0.2 copy-done.1
  25.2 0.5 convolution_convert_fusion.1
  25.7 0.5 convolution_convert_fusion.2
  26.2 0.5 convolution_convert_fusion
  26.8 1.3 %collective-permute-start.9 = (bf16[400,768]{1,0:T(8,128)(2,1)S(1)}, bf16[400,768]{1,0:T(8,128)(2,1)S(1)}, u32[]{:S(2)}, u32[]{:S(2)}) collective-permute-start(bf16[400,768]{1,0:T(8,128)(2,1)S(1)} %pad_maximum_fusion.1.refs_6_), channel_id=1, source_target_pairs={{0,4},{4,0},{1,5},{5,1},{2,6},{6,2},{3,7},{7,3},{8,12},{12,8},{9,1... | collective-permute-start | bytes 1843208 | tf_op jit(solution)/shard_map/ppermute | solution.py:107
  28.1 8.1 %collective-permute-done.6.refs_7_.refs_6_ = bf16[512,512]{1,0:T(8,128)(2,1)S(1)} collective-permute-done((bf16[512,512]{1,0:T(8,128)(2,1)S(1)}, bf16[512,512]{1,0:T(8,128)(2,1)S(1)}, u32[]{:S(2)}, u32[]{:S(2)}) %collective-permute-start.6) | collective-permute-done | bytes 524320 | tf_op jit(solution)/shard_map/ppermute | solution.py:107
  36.1 8.7 %shard_map.131 = (f32[400,768]{1,0:T(8,128)S(1)}, f32[400,384]{1,0:T(8,128)S(1)}, f32[224,256]{1,0:T(8,128)S(1)}, bf16[400,1024]{1,0:T(8,128)(2,1)S(1)}, bf16[20...) custom-call(s32[4]{0:T(128)S(1)} %pad_add_fusion.refs_0_, bf16[400,1536]{1,0:T(8,128)(2,1)S(1)} %copy-done.10, ...), custom_call_target="tpu_custom_call" | custom-call | flops 3951034368 | bytes 13787136 | tf_op jit(solution)/shard_map/pallas_call | solution.py:144
  44.8 0.9 collective-permute-start.8
  45.7 3.6 %collective-permute-done.9.refs_2_ = bf16[400,768]{1,0:T(8,128)(2,1)S(1)} collective-permute-done((bf16[400,768]{1,0:T(8,128)(2,1)S(1)}, bf16[400,768]{1,0:T(8,128)(2,1)S(1)}, u32[]{:S(2)}, u32[]{:S(2)}) %collective-permute-start.9) | collective-permute-done | bytes 614432 | tf_op jit(solution)/shard_map/ppermute | solution.py:107
  49.3 1.9 %shard_map.132 = (bf16[1200,128]{1,0:T(8,128)(2,1)S(1)}, bf16[1424,256]{1,0:T(8,128)(2,1)S(1)}, bf16[736,256]{1,0:T(8,128)(2,1)}, bf16[736,256]{1,0:T(8,128)(2,1)}) custom-call(s32[4]{0:T(128)S(1)} %pad_add_fusion.refs_0_, f32[400,768]{1,0:T(8,128)S(1)} %get-tuple-element.24.refs_1_, bf16[400,768]{1,0:T(8,128)(2,1)S(1)} %collective-permute-done.9.refs_2_, ...), custom_call_target="tpu_custom_call" | custom-call | flops 1000 | bytes 1000 | tf_op jit(solution)/shard_map/pallas_call | solution.py:144
  51.2 0.9 copy-done.11
  52.1 0.7 copy-done.14
  52.8 4.3 %collective-permute-start.10 = (bf16[736,256]{1,0:T(8,128)(2,1)}, bf16[736,256]{1,0:T(8,128)(2,1)}, u32[]{:S(2)}, u32[]{:S(2)}) collective-permute-start(bf16[736,256]{1,0:T(8,128)(2,1)} %get-tuple-element.29), channel_id=1, source_target_pairs={{0,8},{8,16},{16,24},{1,9},{9,17},{17,25},{2,10},{10,18},{18,26},{... | collective-permute-start | bytes 1130504 | tf_op jit(solution)/shard_map/ppermute | solution.py:112
  57.1 1.5 %collective-permute-start.11 = (bf16[736,256]{1,0:T(8,128)(2,1)}, bf16[736,256]{1,0:T(8,128)(2,1)}, u32[]{:S(2)}, u32[]{:S(2)}) collective-permute-start(bf16[736,256]{1,0:T(8,128)(2,1)} %get-tuple-element.30), channel_id=1, source_target_pairs={{8,0},{16,8},{24,16},{9,1},{17,9},{25,17},{10,2},{18,10},{26,18},{... | collective-permute-start | bytes 1130504 | tf_op jit(solution)/shard_map/ppermute | solution.py:112
  58.7 0.9 dynamic_slice.31
  59.7 0.8 collective-permute-start.7
  60.5 3.0 %collective-permute-done.10.refs_3_ = bf16[736,256]{1,0:T(8,128)(2,1)} collective-permute-done((bf16[736,256]{1,0:T(8,128)(2,1)}, bf16[736,256]{1,0:T(8,128)(2,1)}, u32[]{:S(2)}, u32[]{:S(2)}) %collective-permute-start.10) | collective-permute-done | bytes 376864 | tf_op jit(solution)/shard_map/ppermute | solution.py:112
  63.6 4.8 %collective-permute-done.11.refs_4_ = bf16[736,256]{1,0:T(8,128)(2,1)} collective-permute-done((bf16[736,256]{1,0:T(8,128)(2,1)}, bf16[736,256]{1,0:T(8,128)(2,1)}, u32[]{:S(2)}, u32[]{:S(2)}) %collective-permute-start.11) | collective-permute-done | bytes 376864 | tf_op jit(solution)/shard_map/ppermute | solution.py:112
  68.4 4.2 %shard_map.133.refs_1_ = bf16[400,384]{1,0:T(8,128)(2,1)S(1)} custom-call(s32[4]{0:T(128)S(1)} %pad_add_fusion.refs_0_, bf16[1200,128]{1,0:T(8,128)(2,1)S(1)} %copy-done.15, bf16[1424,256]{1,0:T(8,128)(2,1)S(1)} %copy-done.12, bf16[736,256]{1,0:T(8,128)(2,1)} %collective-permute-done.10.refs_3_, bf16[736,256]{1,0:T(8,128)(2,1)} %collective-permute-done.11.refs_4_, ...), custom_call_target="tpu_custom_call" | custom-call | flops 1000 | bytes 1000 | tf_op jit(solution)/shard_map/pallas_call | solution.py:144
  72.7 1.5 %collective-permute-start.12 = (bf16[400,384]{1,0:T(8,128)(2,1)S(1)}, bf16[400,384]{1,0:T(8,128)(2,1)S(1)}, u32[]{:S(2)}, u32[]{:S(2)}) collective-permute-start(bf16[400,384]{1,0:T(8,128)(2,1)S(1)} %shard_map.133.refs_1_), channel_id=1, source_target_pairs={{0,4},{4,0},{1,5},{5,1},{2,6},{6,2},{3,7},{7,3},{8,12},{12,8},{9,1... | collective-permute-start | bytes 921608 | tf_op jit(solution)/shard_map/ppermute | solution.py:107
  74.2 1.0 fusion.7.refs_0_
  75.2 2.9 %fusion.18.refs_1_ = f32[400,768]{1,0:T(8,128)S(1)} fusion(bf16[400,1536]{1,0:T(8,128)(2,1)S(1)} %shard_map.135, bf16[1536,1536]{1,0:T(8,128)(2,1)} %param.22, s32[]{:T(128)S(6)} %select_n.168), kind=kOutput, calls=%fused_computation.22 | convolution fusion | flops 943718400 | bytes 4816900 | tf_op jit(solution)/shard_map/dot_general | solution.py:118
  78.2 1.2 collective-permute-start.18
  79.4 1.1 fusion.12.refs_2_
  80.5 6.1 %collective-permute-done.12.refs_0_ = bf16[400,384]{1,0:T(8,128)(2,1)S(1)} collective-permute-done((bf16[400,384]{1,0:T(8,128)(2,1)S(1)}, bf16[400,384]{1,0:T(8,128)(2,1)S(1)}, u32[]{:S(2)}, u32[]{:S(2)}) %collective-permute-start.12) | collective-permute-done | bytes 307232 | tf_op jit(solution)/shard_map/ppermute | solution.py:107
  86.7 0.5 fusion.20.refs_1_
  87.2 0.5 fusion.40.refs_0_
  87.8 0.3 fusion.72
  88.1 0.7 fusion.53.refs_1_
  88.8 0.5 collective-permute-start.13
  89.4 0.3 fusion.68
  89.8 0.5 convolution_add_fusion
  90.4 1.2 %collective-permute-start.16 = (bf16[200,768]{1,0:T(8,128)(2,1)S(1)}, bf16[200,768]{1,0:T(8,128)(2,1)S(1)}, u32[]{:S(2)}, u32[]{:S(2)}) collective-permute-start(bf16[200,768]{1,0:T(8,128)(2,1)S(1)} %add_convert_fusion.3), channel_id=1, source_target_pairs={{0,2},{1,3},{2,0},{3,1},{4,6},{5,7},{6,4},{7,5},{8,10},{9,11},{10,... | collective-permute-start | bytes 921608 | tf_op jit(solution)/shard_map/ppermute | solution.py:107
  91.6 0.3 fusion.70
  92.0 0.7 fusion.75
  92.7 0.9 collective-permute-start.14
  93.6 7.0 %collective-permute-done.16.refs_0_ = bf16[200,768]{1,0:T(8,128)(2,1)S(1)} collective-permute-done((bf16[200,768]{1,0:T(8,128)(2,1)S(1)}, bf16[200,768]{1,0:T(8,128)(2,1)S(1)}, u32[]{:S(2)}, u32[]{:S(2)}) %collective-permute-start.16) | collective-permute-done | bytes 307232 | tf_op jit(solution)/shard_map/ppermute | solution.py:107
  100.6 0.2 add_convert_fusion.2.refs_1_
  100.9 0.9 collective-permute-start.17
  101.7 0.5 fusion.48.refs_0_
  102.2 0.7 fusion.50
  103.0 0.3 fusion.65
  103.3 0.7 fusion.30.refs_0_
  104.0 2.3 %collective-permute-done.14.refs_2_ = bf16[200,768]{1,0:T(8,128)(2,1)S(1)} collective-permute-done((bf16[200,768]{1,0:T(8,128)(2,1)S(1)}, bf16[200,768]{1,0:T(8,128)(2,1)S(1)}, u32[]{:S(2)}, u32[]{:S(2)}) %collective-permute-start.14) | collective-permute-done | bytes 307232 | tf_op jit(solution)/shard_map/ppermute | solution.py:107
  106.3 2.1 %collective-permute-done.17.refs_1_ = bf16[200,768]{1,0:T(8,128)(2,1)S(1)} collective-permute-done((bf16[200,768]{1,0:T(8,128)(2,1)S(1)}, bf16[200,768]{1,0:T(8,128)(2,1)S(1)}, u32[]{:S(2)}, u32[]{:S(2)}) %collective-permute-start.17) | collective-permute-done | bytes 307232 | tf_op jit(solution)/shard_map/ppermute | solution.py:107
  108.5 1.2 %collective-permute-start.20 = (bf16[200,768]{1,0:T(8,128)(2,1)S(1)}, bf16[200,768]{1,0:T(8,128)(2,1)S(1)}, u32[]{:S(2)}, u32[]{:S(2)}) collective-permute-start(bf16[200,768]{1,0:T(8,128)(2,1)S(1)} %fusion.77), channel_id=1, source_target_pairs={{0,2},{1,3},{2,0},{3,1},{4,6},{5,7},{6,4},{7,5},{8,10},{9,11},{10,... | collective-permute-start | bytes 921608 | tf_op jit(solution)/shard_map/ppermute | solution.py:107
  109.7 0.3 fusion.62
  110.0 1.2 %fusion.49.refs_0_ = f32[400,768]{1,0:T(8,128)S(1)} fusion(f32[200,768]{1,0:T(8,128)S(1)} %get-tuple-element.42, f32[200,768]{1,0:T(8,128)S(1)} %get-tuple-element.41, f32[768]{0:T(1024)S(1)} %dynamic_slice.31, bf16[400,3072]{1,0:T(8,128)(2,1)} %refs_0_.1, s32[]{:T(128)S(6)} %select_n.151), kind=kLoop, calls=%fused_computation.50 | loop fusion | flops 1228800 | bytes 3075076 | tf_op jit(solution)/shard_map/add | solution.py:594
  111.2 4.2 %collective-permute-done.20 = bf16[200,768]{1,0:T(8,128)(2,1)S(1)} collective-permute-done((bf16[200,768]{1,0:T(8,128)(2,1)S(1)}, bf16[200,768]{1,0:T(8,128)(2,1)S(1)}, u32[]{:S(2)}, u32[]{:S(2)}) %collective-permute-start.20) | collective-permute-done | bytes 307232 | tf_op jit(solution)/shard_map/ppermute | solution.py:107
  115.4 1.1 add_convert_fusion.1
  (96 shorter events, 1.3 us)
Async XLA Ops:
  0.0 86.7 %copy-start = (bf16[384,1536]{1,0:T(8,128)(2,1)S(1)}, bf16[384,1536]{1,0:T(8,128)(2,1)}, u32[]{:S(2)}) copy-start(bf16[384,1536]{1,0:T(8,128)(2,1)} %param.21) | copy-start | bytes 3538948
  1.1 3.0 %copy-start.18 = (bf16[400,384]{1,0:T(8,128)(2,1)}, bf16[400,384]{1,0:T(8,128)(2,1)S(1)}, u32[]{:S(2)}) copy-start(bf16[400,384]{1,0:T(8,128)(2,1)S(1)} %constant_dynamic-slice_fusion.refs_4_) | copy-start | bytes 921604
  1.1 10.8 %collective-permute-start = (bf16[400,384]{1,0:T(8,128)(2,1)S(1)}, bf16[400,384]{1,0:T(8,128)(2,1)S(1)}, u32[]{:S(2)}, u32[]{:S(2)}) collective-permute-start(bf16[400,384]{1,0:T(8,128)(2,1)S(1)} %constant_dynamic-slice_fusion.refs_4_), channel_id=1, source_target_pairs={{0,4},{4,0},{1,5},{5,1},{2,6},{6,2},{3,7},{7,3},{8,12},{12,8},{9,1... | collective-permute-start | bytes 921608 | tf_op jit(solution)/shard_map/ppermute | solution.py:107
  11.3 9.2 %collective-permute-start.2 = (bf16[400,384]{1,0:T(8,128)(2,1)}, bf16[400,384]{1,0:T(8,128)(2,1)S(1)}, u32[]{:S(2)}, u32[]{:S(2)}) collective-permute-start(bf16[400,384]{1,0:T(8,128)(2,1)} %get-tuple-element.20), channel_id=1, source_target_pairs={{0,4},{4,0},{1,5},{5,1},{2,6},{6,2},{3,7},{7,3},{8,12},{12,8},{9,1... | collective-permute-start | bytes 921608 | tf_op jit(solution)/shard_map/ppermute | solution.py:107
  11.9 2.9 %copy-start.19 = (bf16[400,384]{1,0:T(8,128)(2,1)}, bf16[400,384]{1,0:T(8,128)(2,1)S(1)}, u32[]{:S(2)}) copy-start(bf16[400,384]{1,0:T(8,128)(2,1)S(1)} %collective-permute-done.refs_6_) | copy-start | bytes 921604
  11.9 8.7 %collective-permute-start.1 = (bf16[400,384]{1,0:T(8,128)(2,1)S(1)}, bf16[400,384]{1,0:T(8,128)(2,1)S(1)}, u32[]{:S(2)}, u32[]{:S(2)}) collective-permute-start(bf16[400,384]{1,0:T(8,128)(2,1)S(1)} %collective-permute-done.refs_6_), channel_id=1, source_target_pairs={{0,2},{1,3},{2,0},{3,1},{4,6},{5,7},{6,4},{7,5},{8,10},{9,11},{10,... | collective-permute-start | bytes 921608 | tf_op jit(solution)/shard_map/ppermute | solution.py:107
  13.4 7.8 %collective-permute-start.5 = (f32[5,8,128]{2,1,0:T(8,128)}, f32[5,8,128]{2,1,0:T(8,128)S(1)}, u32[]{:S(2)}, u32[]{:S(2)}) collective-permute-start(f32[5,8,128]{2,1,0:T(8,128)} %get-tuple-element.19.refs_5_), channel_id=1, source_target_pairs={{0,4},{4,0},{1,5},{5,1},{2,6},{6,2},{3,7},{7,3},{8,12},{12,8},{9,1... | collective-permute-start | bytes 61448 | tf_op jit(solution)/shard_map/ppermute | solution.py:107
  14.8 7.4 %collective-permute-start.3 = (bf16[400,384]{1,0:T(8,128)(2,1)S(1)}, bf16[400,384]{1,0:T(8,128)(2,1)S(1)}, u32[]{:S(2)}, u32[]{:S(2)}) collective-permute-start(bf16[400,384]{1,0:T(8,128)(2,1)S(1)} %collective-permute-done.refs_6_), channel_id=1, source_target_pairs={{0,1},{1,0},{2,3},{3,2},{4,5},{5,4},{6,7},{7,6},{8,9},{9,8},{10,11... | collective-permute-start | bytes 921608 | tf_op jit(solution)/shard_map/ppermute | solution.py:107
  19.3 1.4 %copy-start.2 = (bf16[512,512]{1,0:T(8,128)(2,1)S(1)}, bf16[512,512]{1,0:T(8,128)(2,1)}, u32[]{:S(2)}) copy-start(bf16[512,512]{1,0:T(8,128)(2,1)} %shard_map.128.refs_1_) | copy-start | bytes 1572868
  19.3 1.7 %copy-start.21 = (f32[3072]{0:T(1024)S(1)}, f32[3072]{0:T(1024)}, u32[]{:S(2)}) copy-start(f32[3072]{0:T(1024)} %param.15) | copy-start | bytes 36868
  19.3 1.8 %copy-start.22 = (f32[3072]{0:T(1024)S(1)}, f32[3072]{0:T(1024)}, u32[]{:S(2)}) copy-start(f32[3072]{0:T(1024)} %param.14) | copy-start | bytes 36868
  20.4 4.0 %copy-start.8 = (bf16[400,384]{1,0:T(8,128)(2,1)}, bf16[400,384]{1,0:T(8,128)(2,1)S(1)}, u32[]{:S(2)}) copy-start(bf16[400,384]{1,0:T(8,128)(2,1)S(1)} %collective-permute-done.2.refs_1_.refs_4_) | copy-start | bytes 921604
  20.6 2.3 %collective-permute-start.4 = (bf16[400,384]{1,0:T(8,128)(2,1)S(1)}, bf16[400,384]{1,0:T(8,128)(2,1)}, u32[]{:S(2)}, u32[]{:S(2)}) collective-permute-start(bf16[400,384]{1,0:T(8,128)(2,1)S(1)} %shard_map.130), channel_id=1, source_target_pairs={{0,1},{1,0},{2,3},{3,2},{4,5},{5,4},{6,7},{7,6},{8,9},{9,8},{10,11... | collective-permute-start | bytes 921608 | tf_op jit(solution)/shard_map/ppermute | solution.py:107
  21.4 14.8 %collective-permute-start.6 = (bf16[512,512]{1,0:T(8,128)(2,1)S(1)}, bf16[512,512]{1,0:T(8,128)(2,1)S(1)}, u32[]{:S(2)}, u32[]{:S(2)}) collective-permute-start(bf16[512,512]{1,0:T(8,128)(2,1)S(1)} %copy-done.2), channel_id=1, source_target_pairs={{0,4},{4,0},{1,5},{5,1},{2,6},{6,2},{3,7},{7,3},{8,12},{12,8},{9,1... | collective-permute-start | bytes 1572872 | tf_op jit(solution)/shard_map/ppermute | solution.py:107
  22.2 0.7 copy-start.20
  22.9 2.3 %copy-start.1 = (bf16[1536,3,384]{2,0,1:T(8,128)(2,1)S(1)}, bf16[1536,3,384]{2,0,1:T(8,128)(2,1)}, u32[]{:S(2)}) copy-start(bf16[1536,3,384]{2,0,1:T(8,128)(2,1)} %param.17) | copy-start | bytes 10616836
  26.2 9.9 %copy-start.13 = (bf16[2,224,400]{2,1,0:T(8,128)(2,1)S(1)}, bf16[2,224,400]{2,1,0:T(8,128)(2,1)}, u32[]{:S(2)}) copy-start(bf16[2,224,400]{2,1,0:T(8,128)(2,1)} %constant.73.clone.refs_1_.refs_3_) | copy-start | bytes 1075204
  26.7 9.4 %copy-start.10 = (bf16[400,1536]{1,0:T(8,128)(2,1)S(1)}, bf16[400,1536]{1,0:T(8,128)(2,1)}, u32[]{:S(2)}) copy-start(bf16[400,1536]{1,0:T(8,128)(2,1)} %get-tuple-element.18.refs_0_.refs_1_) | copy-start | bytes 3686404
  26.8 19.0 %copy-start.23 = (f32[3,128]{1,0:T(4,128)S(1)}, f32[3,128]{1,0:T(4,128)}, u32[]{:S(2)}) copy-start(f32[3,128]{1,0:T(4,128)} %param.19) | copy-start | bytes 4612
  26.8 18.9 %copy-start.24 = (f32[3,128]{1,0:T(4,128)S(1)}, f32[3,128]{1,0:T(4,128)}, u32[]{:S(2)}) copy-start(f32[3,128]{1,0:T(4,128)} %param.20) | copy-start | bytes 4612
  26.8 22.5 %copy-start.9 = (bf16[400,384]{1,0:T(8,128)(2,1)S(1)}, bf16[400,384]{1,0:T(8,128)(2,1)}, u32[]{:S(2)}) copy-start(bf16[400,384]{1,0:T(8,128)(2,1)} %copy-done.8) | copy-start | bytes 921604
  26.8 22.5 %collective-permute-start.9 = (bf16[400,768]{1,0:T(8,128)(2,1)S(1)}, bf16[400,768]{1,0:T(8,128)(2,1)S(1)}, u32[]{:S(2)}, u32[]{:S(2)}) collective-permute-start(bf16[400,768]{1,0:T(8,128)(2,1)S(1)} %pad_maximum_fusion.1.refs_6_), channel_id=1, source_target_pairs={{0,4},{4,0},{1,5},{5,1},{2,6},{6,2},{3,7},{7,3},{8,12},{12,8},{9,1... | collective-permute-start | bytes 1843208 | tf_op jit(solution)/shard_map/ppermute | solution.py:107
  36.1 13.2 %copy-start.7 = (bf16[512,512]{1,0:T(8,128)(2,1)}, bf16[512,512]{1,0:T(8,128)(2,1)S(1)}, u32[]{:S(2)}) copy-start(bf16[512,512]{1,0:T(8,128)(2,1)S(1)} %collective-permute-done.6.refs_7_.refs_6_) | copy-start | bytes 1572868
  44.8 6.4 %copy-start.3 = (bf16[200,1536]{1,0:T(8,128)(2,1)}, bf16[200,1536]{1,0:T(8,128)(2,1)S(1)}, u32[]{:S(2)}) copy-start(bf16[200,1536]{1,0:T(8,128)(2,1)S(1)} %get-tuple-element.23.refs_0_) | copy-start | bytes 1843204
  44.8 6.4 %copy-start.5 = (bf16[200,1536]{1,0:T(8,128)(2,1)}, bf16[200,1536]{1,0:T(8,128)(2,1)S(1)}, u32[]{:S(2)}) copy-start(bf16[200,1536]{1,0:T(8,128)(2,1)S(1)} %get-tuple-element.22.refs_9_) | copy-start | bytes 1843204
  44.8 29.4 %collective-permute-start.8 = (bf16[400,1024]{1,0:T(8,128)(2,1)S(1)}, bf16[400,1024]{1,0:T(8,128)(2,1)S(1)}, u32[]{:S(2)}, u32[]{:S(2)}) collective-permute-start(bf16[400,1024]{1,0:T(8,128)(2,1)S(1)} %get-tuple-element.21), channel_id=1, source_target_pairs={{0,4},{4,0},{1,5},{5,1},{2,6},{6,2},{3,7},{7,3},{8,12},{12,8},{9,1... | collective-permute-start | bytes 2457608 | tf_op jit(solution)/shard_map/ppermute | solution.py:107
  51.2 0.9 copy-start.11
  52.1 0.7 copy-start.14
  52.8 15.6 %copy-start.16 = (f32[2,2,1664]{2,1,0:T(2,128)S(1)}, f32[2,2,1664]{2,1,0:T(2,128)}, u32[]{:S(2)}) copy-start(f32[2,2,1664]{2,1,0:T(2,128)} %constant.74.clone.refs_5_) | copy-start | bytes 79876
  52.8 15.6 %copy-start.17 = (f32[1,1280]{1,0:T(1,128)S(1)}, f32[1,1280]{1,0:T(1,128)}, u32[]{:S(2)}) copy-start(f32[1,1280]{1,0:T(1,128)} %constant.75.clone.refs_6_) | copy-start | bytes 15364
  52.8 10.8 %collective-permute-start.10 = (bf16[736,256]{1,0:T(8,128)(2,1)}, bf16[736,256]{1,0:T(8,128)(2,1)}, u32[]{:S(2)}, u32[]{:S(2)}) collective-permute-start(bf16[736,256]{1,0:T(8,128)(2,1)} %get-tuple-element.29), channel_id=1, source_target_pairs={{0,8},{8,16},{16,24},{1,9},{9,17},{17,25},{2,10},{10,18},{18,26},{... | collective-permute-start | bytes 1130504 | tf_op jit(solution)/shard_map/ppermute | solution.py:112
  57.1 11.3 %collective-permute-start.11 = (bf16[736,256]{1,0:T(8,128)(2,1)}, bf16[736,256]{1,0:T(8,128)(2,1)}, u32[]{:S(2)}, u32[]{:S(2)}) collective-permute-start(bf16[736,256]{1,0:T(8,128)(2,1)} %get-tuple-element.30), channel_id=1, source_target_pairs={{8,0},{16,8},{24,16},{9,1},{17,9},{25,17},{10,2},{18,10},{26,18},{... | collective-permute-start | bytes 1130504 | tf_op jit(solution)/shard_map/ppermute | solution.py:112
  58.6 1.1 copy-start.6
  58.7 9.8 %copy-start.12 = (bf16[1424,256]{1,0:T(8,128)(2,1)S(1)}, bf16[1424,256]{1,0:T(8,128)(2,1)}, u32[]{:S(2)}) copy-start(bf16[1424,256]{1,0:T(8,128)(2,1)} %copy-done.11) | copy-start | bytes 2187268
  58.7 9.8 %copy-start.15 = (bf16[1200,128]{1,0:T(8,128)(2,1)S(1)}, bf16[1200,128]{1,0:T(8,128)(2,1)}, u32[]{:S(2)}) copy-start(bf16[1200,128]{1,0:T(8,128)(2,1)} %copy-done.14) | copy-start | bytes 921604
  59.7 20.8 %collective-permute-start.7 = (bf16[200,1536]{1,0:T(8,128)(2,1)S(1)}, bf16[200,1536]{1,0:T(8,128)(2,1)S(1)}, u32[]{:S(2)}, u32[]{:S(2)}) collective-permute-start(bf16[200,1536]{1,0:T(8,128)(2,1)S(1)} %copy-done.6), channel_id=1, source_target_pairs={{0,4},{4,0},{1,5},{5,1},{2,6},{6,2},{3,7},{7,3},{8,12},{12,8},{9,1... | collective-permute-start | bytes 1843208 | tf_op jit(solution)/shard_map/ppermute | solution.py:107
  72.7 1.5 %copy-start.4 = (bf16[200,1536]{1,0:T(8,128)(2,1)S(1)}, bf16[200,1536]{1,0:T(8,128)(2,1)}, u32[]{:S(2)}) copy-start(bf16[200,1536]{1,0:T(8,128)(2,1)} %copy-done.3) | copy-start | bytes 1843204
  72.7 1.5 %slice-start = ((bf16[512,512]{1,0:T(8,128)(2,1)}), bf16[400,512]{1,0:T(8,128)(2,1)S(1)}, s32[]{:S(2)}) async-start(bf16[512,512]{1,0:T(8,128)(2,1)} %copy-done.7), calls=%async_computation | async-start | bytes 819200 | tf_op jit(solution)/shard_map/slice | solution.py:540
  72.7 13.9 %collective-permute-start.12 = (bf16[400,384]{1,0:T(8,128)(2,1)S(1)}, bf16[400,384]{1,0:T(8,128)(2,1)S(1)}, u32[]{:S(2)}, u32[]{:S(2)}) collective-permute-start(bf16[400,384]{1,0:T(8,128)(2,1)S(1)} %shard_map.133.refs_1_), channel_id=1, source_target_pairs={{0,4},{4,0},{1,5},{5,1},{2,6},{6,2},{3,7},{7,3},{8,12},{12,8},{9,1... | collective-permute-start | bytes 921608 | tf_op jit(solution)/shard_map/ppermute | solution.py:107
  75.2 4.2 %slice-start.1 = ((s8[4718592]{0:T(1024)(128)(4,1)}), s8[4194304]{0:T(1024)(128)(4,1)S(1)}, s32[]{:S(2)}) async-start(s8[4718592]{0:T(1024)(128)(4,1)} %bitcast.30), calls=%async_computation.1 | async-start | bytes 8388608
  75.2 4.1 %slice-start.2 = ((s8[4718592]{0:T(1024)(128)(4,1)}), s8[524288]{0:T(1024)(128)(4,1)S(1)}, s32[]{:S(2)}) async-start(s8[4718592]{0:T(1024)(128)(4,1)} %bitcast.30), calls=%async_computation.2 | async-start | bytes 1048576
  78.2 23.5 %collective-permute-start.18 = (bf16[200,1536]{1,0:T(8,128)(2,1)S(1)}, bf16[200,1536]{1,0:T(8,128)(2,1)S(1)}, u32[]{:S(2)}, u32[]{:S(2)}) collective-permute-start(bf16[200,1536]{1,0:T(8,128)(2,1)S(1)} %shard_map.141), channel_id=1, source_target_pairs={{0,4},{4,0},{1,5},{5,1},{2,6},{6,2},{3,7},{7,3},{8,12},{12,8},{9,1... | collective-permute-start | bytes 1843208 | tf_op jit(solution)/shard_map/ppermute | solution.py:107
  87.2 3.1 %collective-permute-start.15 = (bf16[400,768]{1,0:T(8,128)(2,1)S(1)}, bf16[400,768]{1,0:T(8,128)(2,1)S(1)}, u32[]{:S(2)}, u32[]{:S(2)}) collective-permute-start(bf16[400,768]{1,0:T(8,128)(2,1)S(1)} %fusion.20.refs_1_), channel_id=1, source_target_pairs={{0,1},{1,0},{2,3},{3,2},{4,5},{5,4},{6,7},{7,6},{8,9},{9,8},{10,11... | collective-permute-start | bytes 1843208 | tf_op jit(solution)/shard_map/ppermute | solution.py:107
  88.8 3.1 %collective-permute-start.13 = (bf16[200,768]{1,0:T(8,128)(2,1)S(1)}, bf16[200,768]{1,0:T(8,128)(2,1)S(1)}, u32[]{:S(2)}, u32[]{:S(2)}) collective-permute-start(bf16[200,768]{1,0:T(8,128)(2,1)S(1)} %fusion.53.refs_1_), channel_id=1, source_target_pairs={{0,1},{1,0},{2,3},{3,2},{4,5},{5,4},{6,7},{7,6},{8,9},{9,8},{10,11... | collective-permute-start | bytes 921608 | tf_op jit(solution)/shard_map/ppermute | solution.py:107
  90.4 10.2 %collective-permute-start.16 = (bf16[200,768]{1,0:T(8,128)(2,1)S(1)}, bf16[200,768]{1,0:T(8,128)(2,1)S(1)}, u32[]{:S(2)}, u32[]{:S(2)}) collective-permute-start(bf16[200,768]{1,0:T(8,128)(2,1)S(1)} %add_convert_fusion.3), channel_id=1, source_target_pairs={{0,2},{1,3},{2,0},{3,1},{4,6},{5,7},{6,4},{7,5},{8,10},{9,11},{10,... | collective-permute-start | bytes 921608 | tf_op jit(solution)/shard_map/ppermute | solution.py:107
  92.7 13.6 %collective-permute-start.14 = (bf16[200,768]{1,0:T(8,128)(2,1)S(1)}, bf16[200,768]{1,0:T(8,128)(2,1)S(1)}, u32[]{:S(2)}, u32[]{:S(2)}) collective-permute-start(bf16[200,768]{1,0:T(8,128)(2,1)S(1)} %get-tuple-element.45), channel_id=1, source_target_pairs={{0,2},{1,3},{2,0},{3,1},{4,6},{5,7},{6,4},{7,5},{8,10},{9,11},{10,... | collective-permute-start | bytes 921608 | tf_op jit(solution)/shard_map/ppermute | solution.py:107
  100.9 7.5 %collective-permute-start.17 = (bf16[200,768]{1,0:T(8,128)(2,1)S(1)}, bf16[200,768]{1,0:T(8,128)(2,1)S(1)}, u32[]{:S(2)}, u32[]{:S(2)}) collective-permute-start(bf16[200,768]{1,0:T(8,128)(2,1)S(1)} %add_convert_fusion.2.refs_1_), channel_id=1, source_target_pairs={{0,4},{4,0},{1,5},{5,1},{2,6},{6,2},{3,7},{7,3},{8,12},{12,8},{9,1... | collective-permute-start | bytes 921608 | tf_op jit(solution)/shard_map/ppermute | solution.py:107
  102.9 5.5 %collective-permute-start.19 = (bf16[200,768]{1,0:T(8,128)(2,1)S(1)}, bf16[200,768]{1,0:T(8,128)(2,1)S(1)}, u32[]{:S(2)}, u32[]{:S(2)}) collective-permute-start(bf16[200,768]{1,0:T(8,128)(2,1)S(1)} %fusion.50), channel_id=1, source_target_pairs={{0,1},{1,0},{2,3},{3,2},{4,5},{5,4},{6,7},{7,6},{8,9},{9,8},{10,11... | collective-permute-start | bytes 921608 | tf_op jit(solution)/shard_map/ppermute | solution.py:107
  108.5 6.9 %collective-permute-start.20 = (bf16[200,768]{1,0:T(8,128)(2,1)S(1)}, bf16[200,768]{1,0:T(8,128)(2,1)S(1)}, u32[]{:S(2)}, u32[]{:S(2)}) collective-permute-start(bf16[200,768]{1,0:T(8,128)(2,1)S(1)} %fusion.77), channel_id=1, source_target_pairs={{0,2},{1,3},{2,0},{3,1},{4,6},{5,7},{6,4},{7,5},{8,10},{9,11},{10,... | collective-permute-start | bytes 921608 | tf_op jit(solution)/shard_map/ppermute | solution.py:107
